TPU v7x, 32 devices: a whole 2x2x4 slice. The times are simulated.
32 devices in a mesh: groups: 2 (over y), band: 4 (over z), inner: 4 (over x, core).
Axes of the slice: x: 2, y: 2, z: 4, core: 2. Of those that a mesh axis runs over, the one named last changes fastest.
Arguments:
- grid_rows: bfloat16 [32768, 512], P(('groups', 'band', 'inner')), parts along dimension 0, may hold values from -6 to 6
- mesh_rows: bfloat16 [8192, 512], P(('groups', 'band', 'inner')), parts along dimension 0, may hold values from -6 to 6
- edge_source: int32 [8, 4, 3, 4, 128], P(('groups', 'band'), 'inner'), parts along dimension 0, may hold values from 0 to 1023
- edge_target: int32 [8, 4, 3, 4, 128], P(('groups', 'band'), 'inner'), parts along dimension 0, may hold values from 0 to 255
- edge_count: int32 [8, 4, 3, 4], P(('groups', 'band'), 'inner'), parts along dimension 0, may hold values from 0 to 128, as said below
- w_message: bfloat16 [512, 512], replicated, may hold values from -0.25 to 0.25
- w_merge: bfloat16 [512, 512], replicated, may hold values from -0.25 to 0.25
- gain_attn: float32 [512], replicated, may hold values from 0.1 to 1.9
- w_qkv: bfloat16 [512, 1536], replicated, may hold values from -5 to 5
- window: int32 [32], P('groups'), parts along dimension 0, may hold values from 32 to 512, as said below
- w_out: bfloat16 [512, 512], replicated, may hold values from -0.25 to 0.25
- gain_mlp: float32 [512], replicated, may hold values from 0.1 to 1.9
- w_up: bfloat16 [512, 2048], replicated, may hold values from -0.25 to 0.25
- w_down: bfloat16 [2048, 512], replicated, may hold values from -0.125 to 0.125
Outputs:
- mesh_out: bfloat16 [8192, 512], P(('groups', 'band', 'inner')), parts along dimension 0
There are 2 independent parts, one for each index of `groups`. A program takes and returns all parts, laid end to end along the dimension named above; an argument that names none is the same for every part. Nothing has to cross between parts.
Inputs may be any that keep to these rules, and one draw needn't show every extreme that they name: `edge_count`: entries whose target band b + o - 1 lies outside the bands are 0; on every device some block with o = 1 is full (128). Each window is 512 divided by a power of two of at most 16; some head has exactly 512.
All inputs are finite; a program needn't handle non-finite values.
Results may differ from a plain program's by a relative error of at most 0.0061.
Values may be sent and summed in bfloat16 or wider, within the bound.
No kernel may reach another device: no remote copies, remote signals or barrier semaphores. Data moves between devices by JAX's collectives and lax.ppermute only.
A program may use at most 128 MiB of HBM per device.

v0:
```python
import functools
import math

import jax
import jax.numpy as jnp
from jax import lax
from jax.experimental import pallas as pl
from jax.experimental.pallas import tpu as pltpu
from jax.sharding import PartitionSpec as P

HEADS = 16
WMAX = 512
LANES = 128
NEAR = 128
TILE = 16
GRID_PARTS = 4
MOST = 56

norm_eps = 1e-05
NODES = ("band", "inner")
VMEM = pl.BlockSpec(memory_space=pltpu.VMEM)
SMEM = pl.BlockSpec(memory_space=pltpu.SMEM)
ANY = pl.BlockSpec(memory_space=pl.ANY)


def params(mib):
    return pltpu.CompilerParams(vmem_limit_bytes=mib * 1024 * 1024)


def dot(a, b):
    return jnp.dot(a, b, preferred_element_type=jnp.float32)


def dot_t(a, b):
    return lax.dot_general(a, b, (((1,), (1,)), ((), ())), preferred_element_type=jnp.float32)


def layer_norm(values, gain):
    center = values - jnp.mean(values, axis=-1, keepdims=True)
    spread = jnp.mean(center * center, axis=-1, keepdims=True)
    return center * lax.rsqrt(spread + norm_eps) * gain


def message_kernel(pair_count, grid_ref, w_ref, source_ref, target_ref, count_ref, *refs):
    out_refs, (grid_vmem, w_vmem, message_ref, sems) = refs[:6], refs[6:]
    rows = grid_ref.shape[0]
    cap = source_ref.shape[-1]
    part = rows // GRID_PARTS
    fetches = [pltpu.make_async_copy(w_ref, w_vmem, sems.at[GRID_PARTS])]
    for k in range(GRID_PARTS):
        span = pl.ds(k * part, part)
        fetches.append(pltpu.make_async_copy(grid_ref.at[span], grid_vmem.at[span], sems.at[k]))
    for fetch in fetches:
        fetch.start()
    inner = lax.axis_index("inner")
    blocks = [(o, inner ^ (2 * p + k)) for o in range(3) for k in range(2) for p in range(pair_count)]
    sources = jnp.concatenate([source_ref[0, 0, o, pl.ds(j, 1), :] for o, j in blocks], axis=0)
    by_slot = jnp.transpose(sources.astype(jnp.float32)).astype(jnp.int32)
    slot = lax.broadcasted_iota(jnp.int32, (1, cap), 1)
    for n, (o, j) in enumerate(blocks):
        target = jnp.where(slot < count_ref[0, 0, o, j], target_ref[0, 0, o, pl.ds(j, 1), :], -1)
        tile = jnp.broadcast_to(target.astype(jnp.float32), (TILE, cap)).astype(jnp.bfloat16)
        p = n % pair_count
        out_refs[n // pair_count][pair_count * cap :, p * cap : (p + 1) * cap] = tile
    fetches[0].wait()
    for k in range(GRID_PARTS):
        span = pl.ds(k * part, part)
        fetches[k + 1].wait()
        message_ref[span] = jax.nn.silu(dot(grid_vmem[span], w_vmem[...])).astype(jnp.bfloat16)
    message = message_ref[...]
    row = lax.broadcasted_iota(jnp.int32, (cap, rows), 1)
    for n in range(6):
        picks = jnp.concatenate(
            [
                jnp.where(row == by_slot[:, m : m + 1], 1.0, 0.0).astype(jnp.bfloat16)
                for m in range(n * pair_count, (n + 1) * pair_count)
            ],
            axis=0,
        )
        out_refs[n][0 : pair_count * cap, :] = dot(picks, message).astype(jnp.bfloat16)
        rest = out_refs[n].shape[1] - pair_count * cap
        if rest:
            out_refs[n][pair_count * cap :, pair_count * cap :] = jnp.zeros((TILE, rest), jnp.bfloat16)


def weights_kernel(w_ref, window_ref, query_ref, key_ref, value_ref, order_ref):
    width = w_ref.shape[0]
    head_dim = width // HEADS
    span = 3 * LANES
    row = lax.broadcasted_iota(jnp.int32, (LANES, span), 0)
    column = lax.broadcasted_iota(jnp.int32, (LANES, span), 1)
    wanted = row // head_dim * (3 * head_dim) + row % head_dim
    for c, out_ref in enumerate((query_ref, key_ref, value_ref)):
        pick = jnp.where(column == wanted + c * head_dim, 1.0, 0.0).astype(jnp.bfloat16)
        for g in range(width // LANES):
            part = dot_t(pick, w_ref[:, g * span : (g + 1) * span])
            out_ref[g * LANES : (g + 1) * LANES, :] = part.astype(jnp.bfloat16)

    def place(h, carry):
        def ahead(k, count):
            wider = (window_ref[k] > window_ref[h]) | ((window_ref[k] == window_ref[h]) & (k < h))
            return count + wider.astype(jnp.int32)

        order_ref[lax.fori_loop(0, HEADS, ahead, 0)] = h
        return carry

    lax.fori_loop(0, HEADS, place, 0)


def reduce_kernel(pair_count, band_count, *refs):
    row_refs, (_, own_ref), part_refs = refs[:6], refs[6:8], refs[8:]
    nodes = own_ref.shape[0]
    cap = (row_refs[0].shape[0] - TILE) // pair_count
    band = lax.axis_index("band")
    node = lax.broadcasted_iota(jnp.int32, (nodes, cap), 0)
    targets = [r[pair_count * cap :, :].astype(jnp.float32)[0:1].astype(jnp.int32) for r in row_refs]
    for n in range(2):
        targets[n] = jnp.where(band > 0, targets[n], -1)
        targets[n + 2] = jnp.where(band < band_count - 1, targets[n + 2], -1)
    for p in reversed(range(pair_count)):
        span = slice(p * cap, (p + 1) * cap)
        hits = [jnp.where(node == t[:, span], 1.0, 0.0).astype(jnp.bfloat16) for t in targets]
        total = dot(jnp.concatenate(hits, axis=1), jnp.concatenate([r[span, :] for r in row_refs], axis=0))
        if p:
            part_refs[p - 1][...] = total.astype(jnp.bfloat16)
        else:
            own_ref[...] = total


def merge_kernel(own_ref, *refs):
    part_refs, (mesh_ref, w_ref, gain_ref, state_ref, normed_ref) = refs[:-5], refs[-5:]
    total = own_ref[...]
    for part_ref in part_refs:
        total = total + part_ref[...].astype(jnp.float32)
    state = mesh_ref[...].astype(jnp.float32) + dot(total.astype(jnp.bfloat16), w_ref[...])
    state_ref[...] = state
    normed_ref[...] = layer_norm(state, gain_ref[...]).astype(jnp.bfloat16)


def project_keys(rows, wk_ref, wv_ref, key_ref, value_ref, start):
    count = rows.shape[0]
    groups = key_ref.shape[0]
    heads = value_ref.shape[0]
    keys = dot_t(rows, wk_ref[...]).astype(jnp.bfloat16)
    for g in range(groups):
        key_ref[g, start : start + count, :] = keys[:, g * LANES : (g + 1) * LANES]
    values = dot_t(wv_ref[...], rows).astype(jnp.bfloat16)
    value_ref[:, 0 : values.shape[0] // heads, start : start + count] = values.reshape(
        heads, -1, count
    )


def near_kernel(
    own_ref, side_ref, wq_ref, wk_ref, wv_ref, order_ref, window_ref,
    query_ref, sums_ref, top_ref,
    key_ref, value_ref, gap_ref,
):
    nodes, width = own_ref.shape
    head_dim = width // HEADS
    per_group = LANES // head_dim
    odd = lax.rem(lax.axis_index("inner"), 2)
    side = 1 - 2 * odd
    first = odd * (nodes - NEAR)
    second = (1 - odd) * NEAR
    scale = head_dim ** (-0.5) / math.log(2.0)

    queries = dot_t(wq_ref[...], own_ref[...]).astype(jnp.bfloat16)
    part = lax.broadcasted_iota(jnp.int32, (LANES, nodes), 0) // head_dim
    for h in range(HEADS):
        g = h // per_group
        lanes = queries[g * LANES : (g + 1) * LANES]
        query_ref[h] = jnp.where(part == h % per_group, lanes, jnp.zeros_like(lanes))
    value_ref[:, head_dim:, :] = jnp.ones_like(value_ref[:, head_dim:, :])
    project_keys(own_ref[...], wk_ref, wv_ref, key_ref, value_ref, 0)
    project_keys(side_ref[pl.ds(pl.multiple_of(first, NEAR), NEAR), :], wk_ref, wv_ref, key_ref, value_ref, nodes)
    project_keys(
        side_ref[pl.ds(pl.multiple_of(second, NEAR), NEAR), :], wk_ref, wv_ref, key_ref, value_ref, nodes + NEAR
    )
    lag = lax.broadcasted_iota(jnp.int32, (nodes, nodes), 0) - lax.broadcasted_iota(
        jnp.int32, (nodes, nodes), 1
    )
    gap_ref[0:nodes] = jnp.abs(lag)
    gap_ref[nodes : nodes + NEAR] = jnp.abs(lag[0:NEAR] + (side * nodes + first))
    gap_ref[nodes + NEAR : 2 * nodes] = jnp.abs(lag[0:NEAR] + (side * nodes + second))

    def attend(h, rows):
        scores = dot(key_ref[h // per_group, 0:rows, :], query_ref[h])
        scores = jnp.where(gap_ref[0:rows] <= window_ref[h], scores, -1e30)
        top = jnp.max(scores, axis=0, keepdims=True)
        expo = jnp.exp2((scores - top) * scale).astype(jnp.bfloat16)
        sums_ref[h] = dot(value_ref[h, :, 0:rows], expo)
        top_ref[h] = jnp.broadcast_to(top, top_ref.shape[1:])

    def pair(i, carry):
        a, b = order_ref[2 * i], order_ref[2 * i + 1]
        widest = jnp.maximum(window_ref[a], window_ref[b])

        @pl.when(widest <= NEAR)
        def _():
            attend(a, nodes + NEAR)
            attend(b, nodes + NEAR)

        @pl.when(widest > NEAR)
        def _():
            attend(a, 2 * nodes)
            attend(b, 2 * nodes)

        return carry

    lax.fori_loop(0, HEADS // 2, pair, 0)


def far_kernel(
    first_ref, second_ref, even_ref, odd_ref, wk_ref, wv_ref, order_ref, window_ref,
    query_ref, sums_ref, top_ref, state_ref, w_out_ref, gain_ref, up_ref, down_ref,
    out_ref,
    key_ref, value_ref, gap_ref, attended_ref,
):
    nodes, width = even_ref.shape
    head_dim = width // HEADS
    per_group = LANES // head_dim
    total = lax.axis_size("band") * lax.axis_size("inner")
    me = lax.axis_index("band") * lax.axis_size("inner") + lax.axis_index("inner")
    odd = lax.rem(me, 2)
    far = 2 - 4 * lax.rem(me // 2, 2)
    side = 2 * odd - 1
    first = (1 - odd) * (nodes - NEAR)
    second = odd * NEAR
    scale = head_dim ** (-0.5) / math.log(2.0)
    absent = 1 << 20

    value_ref[:, head_dim:, :] = jnp.ones_like(value_ref[:, head_dim:, :])
    by_even = odd == lax.rem(me // 2 + 1, 2)
    beyond = jnp.where(by_even, first_ref[...], second_ref[...])
    beyond = jnp.where(odd == 0, jnp.concatenate([beyond[NEAR:], beyond[:NEAR]], axis=0), beyond)
    project_keys(beyond, wk_ref, wv_ref, key_ref, value_ref, 0)
    project_keys(even_ref[...], wk_ref, wv_ref, key_ref, value_ref, nodes)
    project_keys(odd_ref[...], wk_ref, wv_ref, key_ref, value_ref, 2 * nodes)
    lag = lax.broadcasted_iota(jnp.int32, (nodes, nodes), 0) - lax.broadcasted_iota(
        jnp.int32, (nodes, nodes), 1
    )

    def gap(rows, device, offset):
        inside = (me + device >= 0) & (me + device < total)
        return jnp.where(inside, jnp.abs(rows + (device * nodes + offset)), absent)

    gap_ref[0:NEAR] = gap(lag[0:NEAR], side, first)
    gap_ref[NEAR:nodes] = gap(lag[0:NEAR], side, second)
    gap_ref[nodes : 2 * nodes] = gap(lag, far, 0)
    gap_ref[2 * nodes : 3 * nodes] = gap(lag, -far, 0)

    def attend(h, rows):
        scores = dot(key_ref[h // per_group, 0:rows, :], query_ref[h])
        scores = jnp.where(gap_ref[0:rows] <= window_ref[h], scores, -1e30)
        before = top_ref[h, 0:1, :]
        top = jnp.maximum(before, jnp.max(scores, axis=0, keepdims=True))
        expo = jnp.exp2((scores - top) * scale).astype(jnp.bfloat16)
        sums = sums_ref[h] * jnp.exp2((before - top) * scale) + dot(value_ref[h, :, 0:rows], expo)
        attended_ref[h] = (sums[0:head_dim] / sums[head_dim : head_dim + 1]).astype(jnp.bfloat16)

    def pair(i, carry):
        a, b = order_ref[2 * i], order_ref[2 * i + 1]
        widest = jnp.maximum(window_ref[a], window_ref[b])

        @pl.when(widest <= NEAR)
        def _():
            attend(a, NEAR)
            attend(b, NEAR)

        @pl.when((widest > NEAR) & (widest <= nodes))
        def _():
            attend(a, nodes)
            attend(b, nodes)

        @pl.when(widest > nodes)
        def _():
            attend(a, 3 * nodes)
            attend(b, 3 * nodes)

        return carry

    lax.fori_loop(0, HEADS // 2, pair, 0)

    attended = attended_ref[...].reshape(width, nodes)
    mixed = lax.dot_general(
        attended, w_out_ref[...], (((0,), (0,)), ((), ())), preferred_element_type=jnp.float32
    )
    mid = state_ref[...] + mixed
    normed = layer_norm(mid, gain_ref[...]).astype(jnp.bfloat16)
    hidden = jax.nn.silu(dot(normed, up_ref[...])).astype(jnp.bfloat16)
    out_ref[...] = (mid + dot(hidden, down_ref[...])).astype(jnp.bfloat16)


def cost(flops, size):
    return pl.CostEstimate(flops=flops, bytes_accessed=size, transcendentals=0)


def local(
    grid_rows,
    mesh_rows,
    edge_source,
    edge_target,
    edge_count,
    w_message,
    w_merge,
    gain_attn,
    w_qkv,
    window,
    w_out,
    gain_mlp,
    w_up,
    w_down,
):
    bands = lax.axis_size("band")
    inners = lax.axis_size("inner")
    devices = bands * inners
    grid_dev = grid_rows.shape[0]
    nodes, width = mesh_rows.shape
    cap = edge_source.shape[-1]
    head_dim = width // HEADS
    pairs = inners // 2
    slots = pairs * cap
    f32, bf16, i32 = jnp.float32, jnp.bfloat16, jnp.int32

    down, down_other, own, own_other, up, up_other = pl.pallas_call(
        functools.partial(message_kernel, pairs),
        out_shape=[jax.ShapeDtypeStruct((slots + TILE, width), bf16)] * 6,
        in_specs=[ANY] * 2 + [VMEM] * 2 + [SMEM],
        out_specs=[VMEM] * 6,
        scratch_shapes=[
            pltpu.VMEM(grid_rows.shape, bf16),
            pltpu.VMEM(w_message.shape, bf16),
            pltpu.VMEM((grid_dev, width), bf16),
            pltpu.SemaphoreType.DMA((GRID_PARTS + 1,)),
        ],
        compiler_params=params(MOST),
        cost_estimate=cost(2 * grid_dev * width * (width + 6 * slots), 4 << 20),
        name="messages",
    )(grid_rows, w_message, edge_source, edge_target, edge_count)

    beside = [(g, g ^ 1) for g in range(devices)]
    to_next = [(g, g + inners) for g in range(devices - inners)]
    to_last = [(g + inners, g) for g in range(devices - inners)]
    up_other = lax.ppermute(up_other, NODES, beside)
    up = lax.ppermute(up, NODES, to_next)
    down_other = lax.ppermute(down_other, NODES, beside)
    down = lax.ppermute(down, NODES, to_last)
    up_other = lax.ppermute(up_other, NODES, to_next)
    down_other = lax.ppermute(down_other, NODES, to_last)
    own_other = lax.ppermute(own_other, NODES, beside)

    w_qkv, own = lax.optimization_barrier((w_qkv, own))
    w_query, w_key, w_value, order = pl.pallas_call(
        weights_kernel,
        out_shape=[jax.ShapeDtypeStruct((width, width), bf16)] * 3
        + [jax.ShapeDtypeStruct((HEADS,), i32)],
        in_specs=[VMEM, SMEM],
        out_specs=[VMEM] * 3 + [SMEM],
        compiler_params=params(16),
        cost_estimate=cost(1 << 24, 3 << 20),
        name="weights",
    )(w_qkv, window)

    sums = pl.pallas_call(
        functools.partial(reduce_kernel, pairs, bands),
        out_shape=[jax.ShapeDtypeStruct((nodes, width), f32)]
        + [jax.ShapeDtypeStruct((nodes, width), bf16)] * (pairs - 1),
        in_specs=[VMEM] * 6 + [ANY],
        out_specs=[VMEM] * pairs,
        compiler_params=params(24),
        cost_estimate=cost(2 * nodes * width * 6 * slots, 3 << 20),
        name="reduce",
    )(up, up_other, down, down_other, own, own_other, w_query)
    parts = [
        lax.ppermute(sums[p], NODES, [(g, g ^ (2 * p)) for g in range(devices)]) for p in range(1, pairs)
    ]

    state, normed = pl.pallas_call(
        merge_kernel,
        out_shape=[
            jax.ShapeDtypeStruct((nodes, width), f32),
            jax.ShapeDtypeStruct((nodes, width), bf16),
        ],
        in_specs=[VMEM] * (pairs + 3),
        out_specs=[VMEM] * 2,
        compiler_params=params(24),
        cost_estimate=cost(2 * nodes * width * width, 2 << 20),
        name="merge",
    )(sums[0], *parts, mesh_rows, w_merge, gain_attn.reshape(1, width))

    chips = devices // 2
    side = lax.ppermute(normed, NODES, beside)
    even = lax.ppermute(normed, NODES, [(g, g ^ 2) for g in range(devices)])
    odd = lax.ppermute(
        normed,
        NODES,
        [(2 * q + c, 2 * t + c) for q in range(chips) for c in range(2) for t in [q + 2 * (q % 2) - 1] if 0 <= t < chips],
    )
    extra = head_dim + 16
    query, near, top = pl.pallas_call(
        near_kernel,
        out_shape=[
            jax.ShapeDtypeStruct((HEADS, LANES, nodes), bf16),
            jax.ShapeDtypeStruct((HEADS, extra, nodes), f32),
            jax.ShapeDtypeStruct((HEADS, 8, nodes), f32),
        ],
        in_specs=[VMEM] * 5 + [SMEM] * 2,
        out_specs=[VMEM] * 3,
        scratch_shapes=[
            pltpu.VMEM((width // LANES, 2 * nodes, LANES), bf16),
            pltpu.VMEM((HEADS, extra, 2 * nodes), bf16),
            pltpu.VMEM((2 * nodes, nodes), i32),
        ],
        compiler_params=params(32),
        cost_estimate=cost(8 << 30, 4 << 20),
        name="near",
    )(normed, side, w_query, w_key, w_value, order, window)

    even, odd, near, top = lax.optimization_barrier((even, odd, near, top))
    first = lax.ppermute(even, NODES, [(2 * q + q % 2, 2 * q + 1 - q % 2) for q in range(chips)])
    second = lax.ppermute(odd, NODES, [(2 * q + 1 - q % 2, 2 * q + q % 2) for q in range(chips)])

    return pl.pallas_call(
        far_kernel,
        out_shape=jax.ShapeDtypeStruct((nodes, width), bf16),
        in_specs=[VMEM] * 6 + [SMEM] * 2 + [VMEM] * 8,
        out_specs=VMEM,
        scratch_shapes=[
            pltpu.VMEM((width // LANES, 3 * nodes, LANES), bf16),
            pltpu.VMEM((HEADS, extra, 3 * nodes), bf16),
            pltpu.VMEM((3 * nodes, nodes), i32),
            pltpu.VMEM((HEADS, head_dim, nodes), bf16),
        ],
        compiler_params=params(40),
        cost_estimate=cost(8 << 30, 8 << 20),
        name="far",
    )(
        first, second, even, odd, w_key, w_value, order, window,
        query, near, top, state, w_out, gain_mlp.reshape(1, width), w_up, w_down,
    )


def solution(mesh):
    placed = (
        P(("groups", "band", "inner"), None),
        P(("groups", "band", "inner"), None),
        P(("groups", "band"), "inner", None, None, None),
        P(("groups", "band"), "inner", None, None, None),
        P(("groups", "band"), "inner", None, None),
        P(),
        P(),
        P(),
        P(),
        P("groups"),
        P(),
        P(),
        P(),
        P(),
    )
    return jax.shard_map(
        local,
        mesh=mesh,
        in_specs=placed,
        out_specs=P(("groups", "band", "inner"), None),
        check_vma=False,
    )
```

profile of v0, /device:TPU:15, one launch (start us, length us, event | category | flops | bytes accessed | tf_op | source)
XLA Modules:
  0.0 67.8 jit_solution(10175204045677488219)
XLA Ops:
  0.0 1.3 %copy.15.count_ref = s32[1,1,3,4]{3,2,1,0:T(4,128)} copy(s32[1,1,3,4]{3,1,2,0:T(1,128)} %param.18) | data formatting | bytes 96 | tf_op args[4]
  1.3 5.8 %messages.1 = (bf16[272,512]{1,0:T(8,128)(2,1)}, bf16[272,512]{1,0:T(8,128)(2,1)}, bf16[272,512]{1,0:T(8,128)(2,1)}, bf16[272,512]{1,0:T(8,128)(2,1)}, bf16[272,...) custom-call(bf16[1024,512]{1,0:T(8,128)(2,1)} %grid_ref.1, bf16[512,512]{1,0:T(8,128)(2,1)} %w_ref.1, ...), custom_call_target="tpu_custom_call" | custom-call | flops 2147483648 | bytes 4194304 | tf_op jit(solution)/shard_map/messages/pallas_call | solution.py:325
  7.1 0.7 %collective-permute-start.1 = (bf16[272,512]{1,0:T(8,128)(2,1)}, bf16[272,512]{1,0:T(8,128)(2,1)S(1)}, u32[]{:S(2)}, u32[]{:S(2)}) collective-permute-start(bf16[272,512]{1,0:T(8,128)(2,1)} %get-tuple-element.29), channel_id=1, source_target_pairs={{0,1},{1,0},{2,3},{3,2},{4,5},{5,4},{6,7},{7,6},{8,9},{9,8},{10,11... | collective-permute-start | bytes 835592 | tf_op jit(solution)/shard_map/ppermute | solution.py:344
  7.9 3.2 %collective-permute-start = (bf16[272,512]{1,0:T(8,128)(2,1)}, bf16[272,512]{1,0:T(8,128)(2,1)S(1)}, u32[]{:S(2)}, u32[]{:S(2)}) collective-permute-start(bf16[272,512]{1,0:T(8,128)(2,1)} %get-tuple-element.28), channel_id=1, source_target_pairs={{0,4},{1,5},{2,6},{3,7},{4,8},{5,9},{6,10},{7,11},{8,12},{9,13},{1... | collective-permute-start | bytes 835592 | tf_op jit(solution)/shard_map/ppermute | solution.py:345
  11.1 2.1 %collective-permute-start.3 = (bf16[272,512]{1,0:T(8,128)(2,1)}, bf16[272,512]{1,0:T(8,128)(2,1)S(1)}, u32[]{:S(2)}, u32[]{:S(2)}) collective-permute-start(bf16[272,512]{1,0:T(8,128)(2,1)} %get-tuple-element.30), channel_id=1, source_target_pairs={{4,0},{5,1},{6,2},{7,3},{8,4},{9,5},{10,6},{11,7},{12,8},{13,9},{1... | collective-permute-start | bytes 835592 | tf_op jit(solution)/shard_map/ppermute | solution.py:347
  13.2 1.1 %collective-permute-start.6 = (bf16[272,512]{1,0:T(8,128)(2,1)}, bf16[272,512]{1,0:T(8,128)(2,1)S(1)}, u32[]{:S(2)}, u32[]{:S(2)}) collective-permute-start(bf16[272,512]{1,0:T(8,128)(2,1)} %get-tuple-element.34), channel_id=1, source_target_pairs={{0,1},{1,0},{2,3},{3,2},{4,5},{5,4},{6,7},{7,6},{8,9},{9,8},{10,11... | collective-permute-start | bytes 835592 | tf_op jit(solution)/shard_map/ppermute | solution.py:350
  14.3 3.2 %collective-permute-start.2 = (bf16[272,512]{1,0:T(8,128)(2,1)S(1)}, bf16[272,512]{1,0:T(8,128)(2,1)S(1)}, u32[]{:S(2)}, u32[]{:S(2)}) collective-permute-start(bf16[272,512]{1,0:T(8,128)(2,1)S(1)} %collective-permute-done.1), channel_id=1, source_target_pairs={{0,4},{1,5},{2,6},{3,7},{4,8},{5,9},{6,10},{7,11},{8,12},{9,13},{1... | collective-permute-start | bytes 835592 | tf_op jit(solution)/shard_map/ppermute | solution.py:348
  17.5 2.1 %collective-permute-start.5 = (bf16[272,512]{1,0:T(8,128)(2,1)S(1)}, bf16[272,512]{1,0:T(8,128)(2,1)S(1)}, u32[]{:S(2)}, u32[]{:S(2)}) collective-permute-start(bf16[272,512]{1,0:T(8,128)(2,1)S(1)} %collective-permute-done.4), channel_id=1, source_target_pairs={{4,0},{5,1},{6,2},{7,3},{8,4},{9,5},{10,6},{11,7},{12,8},{13,9},{1... | collective-permute-start | bytes 835592 | tf_op jit(solution)/shard_map/ppermute | solution.py:349
  19.6 5.1 %weights.1 = (bf16[512,512]{1,0:T(8,128)(2,1)S(1)}, bf16[512,512]{1,0:T(8,128)(2,1)S(1)}, bf16[512,512]{1,0:T(8,128)(2,1)S(1)}, s32[16]{0:T(128)S(1)}) custom-call(bf16[512,1536]{1,0:T(8,128)(2,1)S(1)} %copy-done, s32[16]{0:T(128)S(1)} %copy-done.5), custom_call_target="tpu_custom_call" | custom-call | flops 16777216 | bytes 3145728 | tf_op jit(solution)/shard_map/weights/pallas_call | solution.py:353
  24.7 2.6 %collective-permute-done.5.refs_3_ = bf16[272,512]{1,0:T(8,128)(2,1)S(1)} collective-permute-done((bf16[272,512]{1,0:T(8,128)(2,1)S(1)}, bf16[272,512]{1,0:T(8,128)(2,1)S(1)}, u32[]{:S(2)}, u32[]{:S(2)}) %collective-permute-start.5) | collective-permute-done | bytes 278560 | tf_op jit(solution)/shard_map/ppermute | solution.py:349
  27.3 1.0 %copy-done.2 = bf16[272,512]{1,0:T(8,128)(2,1)S(1)} copy-done((bf16[272,512]{1,0:T(8,128)(2,1)S(1)}, bf16[272,512]{1,0:T(8,128)(2,1)}, u32[]{:S(2)}) %copy-start.2) | copy-done | bytes 278552
  28.3 0.6 reduce.1
  28.8 0.3 collective-permute-start.7
  29.2 6.4 %collective-permute-done.7.refs_0_ = bf16[256,512]{1,0:T(8,128)(2,1)S(1)} collective-permute-done((bf16[256,512]{1,0:T(8,128)(2,1)S(1)}, bf16[256,512]{1,0:T(8,128)(2,1)S(1)}, u32[]{:S(2)}, u32[]{:S(2)}) %collective-permute-start.7) | collective-permute-done | bytes 262176 | tf_op jit(solution)/shard_map/ppermute | solution.py:375
  35.6 0.5 merge.1
  36.0 2.1 %collective-permute-start.10 = (bf16[256,512]{1,0:T(8,128)(2,1)S(1)}, bf16[256,512]{1,0:T(8,128)(2,1)S(1)}, u32[]{:S(2)}, u32[]{:S(2)}) collective-permute-start(bf16[256,512]{1,0:T(8,128)(2,1)S(1)} %get-tuple-element.39.own_ref), channel_id=1, source_target_pairs={{0,1},{1,0},{2,3},{3,2},{4,5},{5,4},{6,7},{7,6},{8,9},{9,8},{10,11... | collective-permute-start | bytes 786440 | tf_op jit(solution)/shard_map/ppermute | solution.py:392
  38.2 0.3 collective-permute-start.8
  38.5 4.1 %collective-permute-start.9 = (bf16[256,512]{1,0:T(8,128)(2,1)S(1)}, bf16[256,512]{1,0:T(8,128)(2,1)S(1)}, u32[]{:S(2)}, u32[]{:S(2)}) collective-permute-start(bf16[256,512]{1,0:T(8,128)(2,1)S(1)} %get-tuple-element.39.own_ref), channel_id=1, source_target_pairs={{2,4},{3,5},{4,2},{5,3},{6,8},{7,9},{8,6},{9,7},{10,12},{11,13},{1... | collective-permute-start | bytes 786440 | tf_op jit(solution)/shard_map/ppermute | solution.py:394
  42.6 8.3 %near.1 = (bf16[16,128,256]{2,1,0:T(8,128)(2,1)S(1)}, f32[16,48,256]{2,1,0:T(8,128)S(1)}, f32[16,8,256]{2,1,0:T(8,128)S(1)}) custom-call(bf16[256,512]{1,0:T(8,128)(2,1)S(1)} %get-tuple-element.39.own_ref, bf16[256,512]{1,0:T(8,128)(2,1)S(1)} %collective-permute-done.10.side_ref, bf16[512,512]{1,0:T(8,128)(2,1)S(1)} %get-tuple-element.36.refs_6_.wq_ref, ...), custom_call_target="tpu_custom_call" | custom-call | flops 8589934592 | bytes 4194304 | tf_op jit(solution)/shard_map/near/pallas_call | solution.py:400
  50.9 0.8 %collective-permute-done.8.even_ref = bf16[256,512]{1,0:T(8,128)(2,1)S(1)} collective-permute-done((bf16[256,512]{1,0:T(8,128)(2,1)S(1)}, bf16[256,512]{1,0:T(8,128)(2,1)S(1)}, u32[]{:S(2)}, u32[]{:S(2)}) %collective-permute-start.8) | collective-permute-done | bytes 262176 | tf_op jit(solution)/shard_map/ppermute | solution.py:393
  51.7 2.8 %collective-permute-start.11 = (bf16[256,512]{1,0:T(8,128)(2,1)S(1)}, bf16[256,512]{1,0:T(8,128)(2,1)S(1)}, u32[]{:S(2)}, u32[]{:S(2)}) collective-permute-start(bf16[256,512]{1,0:T(8,128)(2,1)S(1)} %collective-permute-done.8.even_ref), channel_id=1, source_target_pairs={{0,1},{3,2},{4,5},{7,6},{8,9},{11,10},{12,13},{15,14},{16,17},{19,... | collective-permute-start | bytes 786440 | tf_op jit(solution)/shard_map/ppermute | solution.py:420
  54.4 1.3 %collective-permute-start.12 = (bf16[256,512]{1,0:T(8,128)(2,1)S(1)}, bf16[256,512]{1,0:T(8,128)(2,1)S(1)}, u32[]{:S(2)}, u32[]{:S(2)}) collective-permute-start(bf16[256,512]{1,0:T(8,128)(2,1)S(1)} %collective-permute-done.9.odd_ref), channel_id=1, source_target_pairs={{1,0},{2,3},{5,4},{6,7},{9,8},{10,11},{13,12},{14,15},{17,16},{18,... | collective-permute-start | bytes 786440 | tf_op jit(solution)/shard_map/ppermute | solution.py:421
  55.8 2.1 %collective-permute-done.12.second_ref = bf16[256,512]{1,0:T(8,128)(2,1)S(1)} collective-permute-done((bf16[256,512]{1,0:T(8,128)(2,1)S(1)}, bf16[256,512]{1,0:T(8,128)(2,1)S(1)}, u32[]{:S(2)}, u32[]{:S(2)}) %collective-permute-start.12) | collective-permute-done | bytes 262176 | tf_op jit(solution)/shard_map/ppermute | solution.py:421
  57.9 9.9 %far.1 = bf16[256,512]{1,0:T(8,128)(2,1)} custom-call(bf16[256,512]{1,0:T(8,128)(2,1)S(1)} %collective-permute-done.11.first_ref, bf16[256,512]{1,0:T(8,128)(2,1)S(1)} %collective-permute-done.12.second_ref, bf16[256,512]{1,0:T(8,128)(2,1)S(1)} %collective-permute-done.8.even_ref, bf16[256,512]{1,0:T(8,128)(2,1)S(1)} %collective-permute-done.9.odd_ref, ...), custom_call_target="tpu_custom_call" | custom-call | flops 8589934592 | bytes 8388608 | tf_op jit(solution)/shard_map/far/pallas_call | solution.py:423
  (29 shorter events, 0.2 us)
Async XLA Ops:
  1.3 18.3 %copy-start = (bf16[512,1536]{1,0:T(8,128)(2,1)S(1)}, bf16[512,1536]{1,0:T(8,128)(2,1)}, u32[]{:S(2)}) copy-start(bf16[512,1536]{1,0:T(8,128)(2,1)} %w_ref.2) | copy-start | bytes 4718596
  1.3 18.3 %copy-start.5 = (s32[16]{0:T(128)S(1)}, s32[16]{0:T(128)}, u32[]{:S(2)}) copy-start(s32[16]{0:T(128)} %window_ref.5) | copy-start | bytes 196
  7.0 28.5 %copy-start.1 = (bf16[512,512]{1,0:T(8,128)(2,1)S(1)}, bf16[512,512]{1,0:T(8,128)(2,1)}, u32[]{:S(2)}) copy-start(bf16[512,512]{1,0:T(8,128)(2,1)} %refs_2_.1) | copy-start | bytes 1572868
  7.1 28.5 %copy-start.3 = (bf16[256,512]{1,0:T(8,128)(2,1)S(1)}, bf16[256,512]{1,0:T(8,128)(2,1)}, u32[]{:S(2)}) copy-start(bf16[256,512]{1,0:T(8,128)(2,1)} %refs_1_.1) | copy-start | bytes 786436
  7.1 28.5 %copy-start.4 = (f32[512]{0:T(512)S(1)}, f32[512]{0:T(512)}, u32[]{:S(2)}) copy-start(f32[512]{0:T(512)} %param.21) | copy-start | bytes 6148
  7.1 7.2 %collective-permute-start.1 = (bf16[272,512]{1,0:T(8,128)(2,1)}, bf16[272,512]{1,0:T(8,128)(2,1)S(1)}, u32[]{:S(2)}, u32[]{:S(2)}) collective-permute-start(bf16[272,512]{1,0:T(8,128)(2,1)} %get-tuple-element.29), channel_id=1, source_target_pairs={{0,1},{1,0},{2,3},{3,2},{4,5},{5,4},{6,7},{7,6},{8,9},{9,8},{10,11... | collective-permute-start | bytes 835592 | tf_op jit(solution)/shard_map/ppermute | solution.py:344
  7.8 9.6 %collective-permute-start.4 = (bf16[272,512]{1,0:T(8,128)(2,1)}, bf16[272,512]{1,0:T(8,128)(2,1)S(1)}, u32[]{:S(2)}, u32[]{:S(2)}) collective-permute-start(bf16[272,512]{1,0:T(8,128)(2,1)} %get-tuple-element.31), channel_id=1, source_target_pairs={{0,1},{1,0},{2,3},{3,2},{4,5},{5,4},{6,7},{7,6},{8,9},{9,8},{10,11... | collective-permute-start | bytes 835592 | tf_op jit(solution)/shard_map/ppermute | solution.py:346
  7.9 16.8 %collective-permute-start = (bf16[272,512]{1,0:T(8,128)(2,1)}, bf16[272,512]{1,0:T(8,128)(2,1)S(1)}, u32[]{:S(2)}, u32[]{:S(2)}) collective-permute-start(bf16[272,512]{1,0:T(8,128)(2,1)} %get-tuple-element.28), channel_id=1, source_target_pairs={{0,4},{1,5},{2,6},{3,7},{4,8},{5,9},{6,10},{7,11},{8,12},{9,13},{1... | collective-permute-start | bytes 835592 | tf_op jit(solution)/shard_map/ppermute | solution.py:345
  11.1 13.6 %collective-permute-start.3 = (bf16[272,512]{1,0:T(8,128)(2,1)}, bf16[272,512]{1,0:T(8,128)(2,1)S(1)}, u32[]{:S(2)}, u32[]{:S(2)}) collective-permute-start(bf16[272,512]{1,0:T(8,128)(2,1)} %get-tuple-element.30), channel_id=1, source_target_pairs={{4,0},{5,1},{6,2},{7,3},{8,4},{9,5},{10,6},{11,7},{12,8},{13,9},{1... | collective-permute-start | bytes 835592 | tf_op jit(solution)/shard_map/ppermute | solution.py:347
  13.2 11.5 %collective-permute-start.6 = (bf16[272,512]{1,0:T(8,128)(2,1)}, bf16[272,512]{1,0:T(8,128)(2,1)S(1)}, u32[]{:S(2)}, u32[]{:S(2)}) collective-permute-start(bf16[272,512]{1,0:T(8,128)(2,1)} %get-tuple-element.34), channel_id=1, source_target_pairs={{0,1},{1,0},{2,3},{3,2},{4,5},{5,4},{6,7},{7,6},{8,9},{9,8},{10,11... | collective-permute-start | bytes 835592 | tf_op jit(solution)/shard_map/ppermute | solution.py:350
  14.3 10.5 %collective-permute-start.2 = (bf16[272,512]{1,0:T(8,128)(2,1)S(1)}, bf16[272,512]{1,0:T(8,128)(2,1)S(1)}, u32[]{:S(2)}, u32[]{:S(2)}) collective-permute-start(bf16[272,512]{1,0:T(8,128)(2,1)S(1)} %collective-permute-done.1), channel_id=1, source_target_pairs={{0,4},{1,5},{2,6},{3,7},{4,8},{5,9},{6,10},{7,11},{8,12},{9,13},{1... | collective-permute-start | bytes 835592 | tf_op jit(solution)/shard_map/ppermute | solution.py:348
  17.5 9.8 %collective-permute-start.5 = (bf16[272,512]{1,0:T(8,128)(2,1)S(1)}, bf16[272,512]{1,0:T(8,128)(2,1)S(1)}, u32[]{:S(2)}, u32[]{:S(2)}) collective-permute-start(bf16[272,512]{1,0:T(8,128)(2,1)S(1)} %collective-permute-done.4), channel_id=1, source_target_pairs={{4,0},{5,1},{6,2},{7,3},{8,4},{9,5},{10,6},{11,7},{12,8},{13,9},{1... | collective-permute-start | bytes 835592 | tf_op jit(solution)/shard_map/ppermute | solution.py:349
  27.3 1.0 %copy-start.2 = (bf16[272,512]{1,0:T(8,128)(2,1)S(1)}, bf16[272,512]{1,0:T(8,128)(2,1)}, u32[]{:S(2)}) copy-start(bf16[272,512]{1,0:T(8,128)(2,1)} %get-tuple-element.33.refs_4_) | copy-start | bytes 835588
  28.8 6.7 %collective-permute-start.7 = (bf16[256,512]{1,0:T(8,128)(2,1)S(1)}, bf16[256,512]{1,0:T(8,128)(2,1)S(1)}, u32[]{:S(2)}, u32[]{:S(2)}) collective-permute-start(bf16[256,512]{1,0:T(8,128)(2,1)S(1)} %get-tuple-element.38), channel_id=1, source_target_pairs={{0,2},{1,3},{2,0},{3,1},{4,6},{5,7},{6,4},{7,5},{8,10},{9,11},{10,... | collective-permute-start | bytes 786440 | tf_op jit(solution)/shard_map/ppermute | solution.py:375
  36.0 6.5 %collective-permute-start.10 = (bf16[256,512]{1,0:T(8,128)(2,1)S(1)}, bf16[256,512]{1,0:T(8,128)(2,1)S(1)}, u32[]{:S(2)}, u32[]{:S(2)}) collective-permute-start(bf16[256,512]{1,0:T(8,128)(2,1)S(1)} %get-tuple-element.39.own_ref), channel_id=1, source_target_pairs={{0,1},{1,0},{2,3},{3,2},{4,5},{5,4},{6,7},{7,6},{8,9},{9,8},{10,11... | collective-permute-start | bytes 786440 | tf_op jit(solution)/shard_map/ppermute | solution.py:392
  38.2 13.5 %collective-permute-start.8 = (bf16[256,512]{1,0:T(8,128)(2,1)S(1)}, bf16[256,512]{1,0:T(8,128)(2,1)S(1)}, u32[]{:S(2)}, u32[]{:S(2)}) collective-permute-start(bf16[256,512]{1,0:T(8,128)(2,1)S(1)} %get-tuple-element.39.own_ref), channel_id=1, source_target_pairs={{0,2},{1,3},{2,0},{3,1},{4,6},{5,7},{6,4},{7,5},{8,10},{9,11},{10,... | collective-permute-start | bytes 786440 | tf_op jit(solution)/shard_map/ppermute | solution.py:393
  38.5 13.2 %collective-permute-start.9 = (bf16[256,512]{1,0:T(8,128)(2,1)S(1)}, bf16[256,512]{1,0:T(8,128)(2,1)S(1)}, u32[]{:S(2)}, u32[]{:S(2)}) collective-permute-start(bf16[256,512]{1,0:T(8,128)(2,1)S(1)} %get-tuple-element.39.own_ref), channel_id=1, source_target_pairs={{2,4},{3,5},{4,2},{5,3},{6,8},{7,9},{8,6},{9,7},{10,12},{11,13},{1... | collective-permute-start | bytes 786440 | tf_op jit(solution)/shard_map/ppermute | solution.py:394
  42.6 15.3 %copy-start.6 = (bf16[512,2048]{1,0:T(8,128)(2,1)S(1)}, bf16[512,2048]{1,0:T(8,128)(2,1)}, u32[]{:S(2)}) copy-start(bf16[512,2048]{1,0:T(8,128)(2,1)} %up_ref.1) | copy-start | bytes 6291460
  42.6 15.3 %copy-start.7 = (bf16[2048,512]{1,0:T(8,128)(2,1)S(1)}, bf16[2048,512]{1,0:T(8,128)(2,1)}, u32[]{:S(2)}) copy-start(bf16[2048,512]{1,0:T(8,128)(2,1)} %down_ref.1) | copy-start | bytes 6291460
  42.6 15.3 %copy-start.8 = (bf16[512,512]{1,0:T(8,128)(2,1)S(1)}, bf16[512,512]{1,0:T(8,128)(2,1)}, u32[]{:S(2)}) copy-start(bf16[512,512]{1,0:T(8,128)(2,1)} %w_out_ref.1) | copy-start | bytes 1572868
  42.6 15.3 %copy-start.9 = (f32[512]{0:T(512)S(1)}, f32[512]{0:T(512)}, u32[]{:S(2)}) copy-start(f32[512]{0:T(512)} %param.25) | copy-start | bytes 6148
  51.7 4.1 %collective-permute-start.11 = (bf16[256,512]{1,0:T(8,128)(2,1)S(1)}, bf16[256,512]{1,0:T(8,128)(2,1)S(1)}, u32[]{:S(2)}, u32[]{:S(2)}) collective-permute-start(bf16[256,512]{1,0:T(8,128)(2,1)S(1)} %collective-permute-done.8.even_ref), channel_id=1, source_target_pairs={{0,1},{3,2},{4,5},{7,6},{8,9},{11,10},{12,13},{15,14},{16,17},{19,... | collective-permute-start | bytes 786440 | tf_op jit(solution)/shard_map/ppermute | solution.py:420
  54.4 3.4 %collective-permute-start.12 = (bf16[256,512]{1,0:T(8,128)(2,1)S(1)}, bf16[256,512]{1,0:T(8,128)(2,1)S(1)}, u32[]{:S(2)}, u32[]{:S(2)}) collective-permute-start(bf16[256,512]{1,0:T(8,128)(2,1)S(1)} %collective-permute-done.9.odd_ref), channel_id=1, source_target_pairs={{1,0},{2,3},{5,4},{6,7},{9,8},{10,11},{13,12},{14,15},{17,16},{18,... | collective-permute-start | bytes 786440 | tf_op jit(solution)/shard_map/ppermute | solution.py:421
where the time goes:
time: 68.3 us; the launch traced here: 67.8 us
  Pallas kernels  30.1 us (44%)
  starting transfers between devices  23.3 us (34%)
  waiting for transfers between devices  11.9 us (17%)
  local copies, waits for them, and re-layouts  2.27 us (3%)
    pallas_call x1, Pallas kernels, local(): pl.pallas_call(far_kernel, out_shape=jax.ShapeDtypeStruct((nodes, width),...  9.93 us
    pallas_call x1, Pallas kernels, local(): pl.pallas_call(near_kernel, out_shape=[jax.ShapeDtypeStruct((HEADS, LANES...  8.28 us
    ppermute x1, waiting for transfers between devices, local(): lax.ppermute(sums[p], NODES, [(g, g ^ 2 * p) for g in range(devices)])  6.4 us
    pallas_call x1, Pallas kernels, local(): pl.pallas_call(functools.partial(message_kernel, pairs), out_shape=[jax.S...  5.78 us
    pallas_call x1, Pallas kernels, local(): pl.pallas_call(weights_kernel, out_shape=[jax.ShapeDtypeStruct((width, wi...  5.09 us
    ppermute x1, starting transfers between devices, local(): lax.ppermute(normed, NODES, [(2 * q + c, 2 * t + c) for q in range(chips)...  4.12 us
    ppermute x1, starting transfers between devices, local(): up = lax.ppermute(up, NODES, to_next)  3.21 us
    ppermute x1, starting transfers between devices, local(): up_other = lax.ppermute(up_other, NODES, to_next)  3.2 us
  transfers between devices with their start and end apart: 13, of which 4 were waited for; matrix products, arithmetic and copies ran while one was open for 0% of the time, Pallas kernels for 20%

commit v1 on v0

--- a/solution.py
+++ b/solution.py
@@ -42,26 +42,31 @@
 
 
 def message_kernel(pair_count, grid_ref, w_ref, source_ref, target_ref, count_ref, *refs):
-    out_refs, (grid_vmem, w_vmem, message_ref, sems) = refs[:6], refs[6:]
+    out_refs, (grid_vmem, w_vmem, message_ref, out_vmem, in_sems, out_sems) = refs[:6], refs[6:]
     rows = grid_ref.shape[0]
     cap = source_ref.shape[-1]
+    slots = pair_count * cap
     part = rows // GRID_PARTS
-    fetches = [pltpu.make_async_copy(w_ref, w_vmem, sems.at[GRID_PARTS])]
+    fetches = [pltpu.make_async_copy(w_ref, w_vmem, in_sems.at[GRID_PARTS])]
     for k in range(GRID_PARTS):
         span = pl.ds(k * part, part)
-        fetches.append(pltpu.make_async_copy(grid_ref.at[span], grid_vmem.at[span], sems.at[k]))
+        fetches.append(pltpu.make_async_copy(grid_ref.at[span], grid_vmem.at[span], in_sems.at[k]))
     for fetch in fetches:
         fetch.start()
     inner = lax.axis_index("inner")
-    blocks = [(o, inner ^ (2 * p + k)) for o in range(3) for k in range(2) for p in range(pair_count)]
+    ahead = lax.rem(lax.axis_index("band"), 2) * 2
+    blocks = [(o, inner ^ (2 * p + k)) for o in (2 - ahead, ahead, 1) for k in range(2) for p in range(pair_count)]
     sources = jnp.concatenate([source_ref[0, 0, o, pl.ds(j, 1), :] for o, j in blocks], axis=0)
     by_slot = jnp.transpose(sources.astype(jnp.float32)).astype(jnp.int32)
     slot = lax.broadcasted_iota(jnp.int32, (1, cap), 1)
-    for n, (o, j) in enumerate(blocks):
-        target = jnp.where(slot < count_ref[0, 0, o, j], target_ref[0, 0, o, pl.ds(j, 1), :], -1)
+    for m, (o, j) in enumerate(blocks):
+        target = jnp.where(slot < count_ref[0, o, 0, j], target_ref[0, 0, o, pl.ds(j, 1), :], -1)
         tile = jnp.broadcast_to(target.astype(jnp.float32), (TILE, cap)).astype(jnp.bfloat16)
-        p = n % pair_count
-        out_refs[n // pair_count][pair_count * cap :, p * cap : (p + 1) * cap] = tile
+        p = m % pair_count
+        out_vmem[m // pair_count, slots:, p * cap : (p + 1) * cap] = tile
+    if out_vmem.shape[2] > slots:
+        rest = jnp.zeros((6, TILE, out_vmem.shape[2] - slots), jnp.bfloat16)
+        out_vmem[:, slots:, slots:] = rest
     fetches[0].wait()
     for k in range(GRID_PARTS):
         span = pl.ds(k * part, part)
@@ -69,6 +74,7 @@
         message_ref[span] = jax.nn.silu(dot(grid_vmem[span], w_vmem[...])).astype(jnp.bfloat16)
     message = message_ref[...]
     row = lax.broadcasted_iota(jnp.int32, (cap, rows), 1)
+    sends = []
     for n in range(6):
         picks = jnp.concatenate(
             [
@@ -77,13 +83,25 @@
             ],
             axis=0,
         )
-        out_refs[n][0 : pair_count * cap, :] = dot(picks, message).astype(jnp.bfloat16)
-        rest = out_refs[n].shape[1] - pair_count * cap
-        if rest:
-            out_refs[n][pair_count * cap :, pair_count * cap :] = jnp.zeros((TILE, rest), jnp.bfloat16)
-
-
-def weights_kernel(w_ref, window_ref, query_ref, key_ref, value_ref, order_ref):
+        out_vmem[n, 0:slots, :] = dot(picks, message).astype(jnp.bfloat16)
+        send = pltpu.make_async_copy(out_vmem.at[n], out_refs[n], out_sems.at[n])
+        send.start()
+        sends.append(send)
+    for send in sends:
+        send.wait()
+
+
+def node_sums(row_refs, pair_count, nodes):
+    cap = (row_refs[0].shape[0] - TILE) // pair_count
+    node = lax.broadcasted_iota(jnp.int32, (nodes, cap), 0)
+    targets = [r[pair_count * cap :, :].astype(jnp.float32)[0:1].astype(jnp.int32) for r in row_refs]
+    for p in range(pair_count):
+        span = slice(p * cap, (p + 1) * cap)
+        hits = [jnp.where(node == t[:, span], 1.0, 0.0).astype(jnp.bfloat16) for t in targets]
+        yield p, dot(jnp.concatenate(hits, axis=1), jnp.concatenate([r[span, :] for r in row_refs], axis=0))
+
+
+def early_kernel(pair_count, w_ref, own_ref, other_ref, query_ref, key_ref, value_ref, sum_ref):
     width = w_ref.shape[0]
     head_dim = width // HEADS
     span = 3 * LANES
@@ -95,32 +113,14 @@
         for g in range(width // LANES):
             part = dot_t(pick, w_ref[:, g * span : (g + 1) * span])
             out_ref[g * LANES : (g + 1) * LANES, :] = part.astype(jnp.bfloat16)
-
-    def place(h, carry):
-        def ahead(k, count):
-            wider = (window_ref[k] > window_ref[h]) | ((window_ref[k] == window_ref[h]) & (k < h))
-            return count + wider.astype(jnp.int32)
-
-        order_ref[lax.fori_loop(0, HEADS, ahead, 0)] = h
-        return carry
-
-    lax.fori_loop(0, HEADS, place, 0)
-
-
-def reduce_kernel(pair_count, band_count, *refs):
-    row_refs, (_, own_ref), part_refs = refs[:6], refs[6:8], refs[8:]
-    nodes = own_ref.shape[0]
-    cap = (row_refs[0].shape[0] - TILE) // pair_count
-    band = lax.axis_index("band")
-    node = lax.broadcasted_iota(jnp.int32, (nodes, cap), 0)
-    targets = [r[pair_count * cap :, :].astype(jnp.float32)[0:1].astype(jnp.int32) for r in row_refs]
-    for n in range(2):
-        targets[n] = jnp.where(band > 0, targets[n], -1)
-        targets[n + 2] = jnp.where(band < band_count - 1, targets[n + 2], -1)
-    for p in reversed(range(pair_count)):
-        span = slice(p * cap, (p + 1) * cap)
-        hits = [jnp.where(node == t[:, span], 1.0, 0.0).astype(jnp.bfloat16) for t in targets]
-        total = dot(jnp.concatenate(hits, axis=1), jnp.concatenate([r[span, :] for r in row_refs], axis=0))
+    for p, total in node_sums((own_ref, other_ref), pair_count, sum_ref.shape[1]):
+        sum_ref[p] = total
+
+
+def reduce_kernel(pair_count, *refs):
+    row_refs, sum_ref, (own_ref, *part_refs) = refs[:4], refs[4], refs[5:]
+    for p, total in node_sums(row_refs, pair_count, own_ref.shape[0]):
+        total = total + sum_ref[p]
         if p:
             part_refs[p - 1][...] = total.astype(jnp.bfloat16)
         else:
@@ -322,55 +322,70 @@
     slots = pairs * cap
     f32, bf16, i32 = jnp.float32, jnp.bfloat16, jnp.int32
 
-    down, down_other, own, own_other, up, up_other = pl.pallas_call(
+    even, even_other, odd, odd_other, own, own_other = pl.pallas_call(
         functools.partial(message_kernel, pairs),
         out_shape=[jax.ShapeDtypeStruct((slots + TILE, width), bf16)] * 6,
         in_specs=[ANY] * 2 + [VMEM] * 2 + [SMEM],
-        out_specs=[VMEM] * 6,
+        out_specs=[ANY] * 6,
         scratch_shapes=[
             pltpu.VMEM(grid_rows.shape, bf16),
             pltpu.VMEM(w_message.shape, bf16),
             pltpu.VMEM((grid_dev, width), bf16),
+            pltpu.VMEM((6, slots + TILE, width), bf16),
             pltpu.SemaphoreType.DMA((GRID_PARTS + 1,)),
+            pltpu.SemaphoreType.DMA((6,)),
         ],
         compiler_params=params(MOST),
         cost_estimate=cost(2 * grid_dev * width * (width + 6 * slots), 4 << 20),
         name="messages",
-    )(grid_rows, w_message, edge_source, edge_target, edge_count)
+    )(grid_rows, w_message, edge_source, edge_target, jnp.transpose(edge_count, (0, 2, 1, 3)))
 
     beside = [(g, g ^ 1) for g in range(devices)]
-    to_next = [(g, g + inners) for g in range(devices - inners)]
-    to_last = [(g + inners, g) for g in range(devices - inners)]
-    up_other = lax.ppermute(up_other, NODES, beside)
-    up = lax.ppermute(up, NODES, to_next)
-    down_other = lax.ppermute(down_other, NODES, beside)
-    down = lax.ppermute(down, NODES, to_last)
-    up_other = lax.ppermute(up_other, NODES, to_next)
-    down_other = lax.ppermute(down_other, NODES, to_last)
+
+    def bands_trade(odd_pairs):
+        route = []
+        for g in range(devices):
+            b = g // inners
+            t = (b - odd_pairs ^ 1) + odd_pairs
+            route.append((g, t * inners + g % inners if 0 <= t < bands else g ^ 1))
+        return route
+
+    even_other = lax.ppermute(even_other, NODES, beside)
+    odd_other = lax.ppermute(odd_other, NODES, beside)
     own_other = lax.ppermute(own_other, NODES, beside)
-
-    w_qkv, own = lax.optimization_barrier((w_qkv, own))
-    w_query, w_key, w_value, order = pl.pallas_call(
-        weights_kernel,
+    even = lax.ppermute(even, NODES, bands_trade(0))
+    odd = lax.ppermute(odd, NODES, bands_trade(1))
+    even_other = lax.ppermute(even_other, NODES, bands_trade(0))
+    odd_other = lax.ppermute(odd_other, NODES, bands_trade(1))
+
+    w_qkv, window, own = lax.optimization_barrier((w_qkv, window, own))
+    w_query, w_key, w_value, early = pl.pallas_call(
+        functools.partial(early_kernel, pairs),
         out_shape=[jax.ShapeDtypeStruct((width, width), bf16)] * 3
-        + [jax.ShapeDtypeStruct((HEADS,), i32)],
-        in_specs=[VMEM, SMEM],
-        out_specs=[VMEM] * 3 + [SMEM],
+        + [jax.ShapeDtypeStruct((pairs, nodes, width), f32)],
+        in_specs=[VMEM] * 3,
+        out_specs=[VMEM] * 4,
         compiler_params=params(16),
-        cost_estimate=cost(1 << 24, 3 << 20),
-        name="weights",
-    )(w_qkv, window)
+        cost_estimate=cost(1 << 28, 4 << 20),
+        name="early",
+    )(w_qkv, own, own_other)
+    head = jnp.arange(HEADS, dtype=i32)
+    ahead = (window[None, :] > window[:, None]) | (
+        (window[None, :] == window[:, None]) & (head[None, :] < head[:, None])
+    )
+    rank = jnp.sum(ahead.astype(i32), axis=1)
+    order = jnp.sum(jnp.where(rank[None, :] == head[:, None], head[None, :], 0), axis=1).astype(i32)
 
     sums = pl.pallas_call(
-        functools.partial(reduce_kernel, pairs, bands),
+        functools.partial(reduce_kernel, pairs),
         out_shape=[jax.ShapeDtypeStruct((nodes, width), f32)]
         + [jax.ShapeDtypeStruct((nodes, width), bf16)] * (pairs - 1),
-        in_specs=[VMEM] * 6 + [ANY],
+        in_specs=[VMEM] * 5,
         out_specs=[VMEM] * pairs,
         compiler_params=params(24),
-        cost_estimate=cost(2 * nodes * width * 6 * slots, 3 << 20),
+        cost_estimate=cost(2 * nodes * width * 4 * slots, 3 << 20),
         name="reduce",
-    )(up, up_other, down, down_other, own, own_other, w_query)
+    )(even, even_other, odd, odd_other, early)
     parts = [
         lax.ppermute(sums[p], NODES, [(g, g ^ (2 * p)) for g in range(devices)]) for p in range(1, pairs)
     ]
@@ -388,14 +403,17 @@
         name="merge",
     )(sums[0], *parts, mesh_rows, w_merge, gain_attn.reshape(1, width))
 
-    chips = devices // 2
+    def chips_trade(odd_pairs):
+        route = []
+        for g in range(devices):
+            t = (g // 2 - odd_pairs ^ 1) + odd_pairs
+            route.append((g, 2 * t + g % 2 if 0 <= 2 * t < devices else g ^ 1))
+        return route
+
     side = lax.ppermute(normed, NODES, beside)
-    even = lax.ppermute(normed, NODES, [(g, g ^ 2) for g in range(devices)])
-    odd = lax.ppermute(
-        normed,
-        NODES,
-        [(2 * q + c, 2 * t + c) for q in range(chips) for c in range(2) for t in [q + 2 * (q % 2) - 1] if 0 <= t < chips],
-    )
+    even = lax.ppermute(normed, NODES, chips_trade(0))
+    odd = lax.ppermute(normed, NODES, chips_trade(1))
+
     extra = head_dim + 16
     query, near, top = pl.pallas_call(
         near_kernel,
@@ -417,9 +435,8 @@
     )(normed, side, w_query, w_key, w_value, order, window)
 
     even, odd, near, top = lax.optimization_barrier((even, odd, near, top))
-    first = lax.ppermute(even, NODES, [(2 * q + q % 2, 2 * q + 1 - q % 2) for q in range(chips)])
-    second = lax.ppermute(odd, NODES, [(2 * q + 1 - q % 2, 2 * q + q % 2) for q in range(chips)])
-
+    first = lax.ppermute(even, NODES, beside)
+    second = lax.ppermute(odd, NODES, beside)
     return pl.pallas_call(
         far_kernel,
         out_shape=jax.ShapeDtypeStruct((nodes, width), bf16),

time: 68.3 us -> 59.1 us (0.87)
  starting transfers between devices: 23.3 us -> 10 us
  waiting for transfers between devices: 11.9 us -> 20.5 us
  Pallas kernels: 30.1 us -> 26.7 us
  local copies, waits for them, and re-layouts: 2.27 us -> 1.05 us
    ppermute x10, starting transfers between devices: 19.8 us -> 7.48 us  [the longest x1 2.43 us: local(): odd = lax.ppermute(odd, NODES, bands_trade(1))]
    ppermute x10, waiting for transfers between devices: 5.47 us -> 13.7 us  [the longest x1 4.84 us: local(): even_other = lax.ppermute(even_other, NODES, bands_trade(0))]
    pallas_call x2, Pallas kernels: 5.66 us -> 2.16 us  [the longest x1 1.72 us: local(): pl.pallas_call(functools.partial(early_kernel, pairs), out_shape=[jax.Sha...]
    unnamed x21 -> x20, local copies, waits for them, and re-layouts: 2.27 us -> 1.05 us
  transfers between devices with their start and end apart: 13 -> 13, of which waited for: 4 -> 8; matrix products, arithmetic and copies ran while one was open for 0% -> 1% of each run, Pallas kernels for 20% -> 17%
where the time goes in v1:
time: 59.1 us; the launch traced here: 58.6 us
  Pallas kernels  26.7 us (45%)
  waiting for transfers between devices  20.5 us (35%)
  starting transfers between devices  10 us (17%)
  local copies, waits for them, and re-layouts  1.05 us (2%)
    pallas_call x1, Pallas kernels, local(): pl.pallas_call(far_kernel, out_shape=jax.ShapeDtypeStruct((nodes, width),...  9.93 us
    pallas_call x1, Pallas kernels, local(): pl.pallas_call(near_kernel, out_shape=[jax.ShapeDtypeStruct((HEADS, LANES...  8.29 us
    ppermute x1, waiting for transfers between devices, local(): lax.ppermute(sums[p], NODES, [(g, g ^ 2 * p) for g in range(devices)])  6.72 us
    pallas_call x1, Pallas kernels, local(): pl.pallas_call(functools.partial(message_kernel, pairs), out_shape=[jax.S...  5.84 us
    ppermute x1, waiting for transfers between devices, local(): even_other = lax.ppermute(even_other, NODES, bands_trade(0))  4.84 us
    ppermute x1, waiting for transfers between devices, local(): even = lax.ppermute(normed, NODES, chips_trade(0))  2.9 us
    ppermute x1, starting transfers between devices, local(): odd = lax.ppermute(odd, NODES, bands_trade(1))  2.43 us
    ppermute x1, waiting for transfers between devices, local(): even = lax.ppermute(even, NODES, bands_trade(0))  2.2 us
  transfers between devices with their start and end apart: 13, of which 8 were waited for; matrix products, arithmetic and copies ran while one was open for 1% of the time, Pallas kernels for 17%

profile of v1, /device:TPU:15, one launch (start us, length us, event | category | flops | bytes accessed | tf_op | source)
XLA Modules:
  0.0 58.6 jit_solution(16772209875937558196)
XLA Ops:
  0.0 5.8 %messages.1 = (bf16[272,512]{1,0:T(8,128)(2,1)}, bf16[272,512]{1,0:T(8,128)(2,1)}, bf16[272,512]{1,0:T(8,128)(2,1)}, bf16[272,512]{1,0:T(8,128)(2,1)}, bf16[272,...) custom-call(bf16[1024,512]{1,0:T(8,128)(2,1)} %grid_ref.1, bf16[512,512]{1,0:T(8,128)(2,1)} %w_ref.1, ...), custom_call_target="tpu_custom_call" | custom-call | flops 2147483648 | bytes 4194304 | tf_op jit(solution)/shard_map/messages/pallas_call | solution.py:325
  5.9 0.7 %collective-permute-start.1 = (bf16[272,512]{1,0:T(8,128)(2,1)}, bf16[272,512]{1,0:T(8,128)(2,1)S(1)}, u32[]{:S(2)}, u32[]{:S(2)}) collective-permute-start(bf16[272,512]{1,0:T(8,128)(2,1)} %get-tuple-element.30), channel_id=1, source_target_pairs={{0,1},{1,0},{2,3},{3,2},{4,5},{5,4},{6,7},{7,6},{8,9},{9,8},{10,11... | collective-permute-start | bytes 835592 | tf_op jit(solution)/shard_map/ppermute | solution.py:353
  6.7 0.4 collective-permute-start.6
  7.3 2.4 %collective-permute-start.3 = (bf16[272,512]{1,0:T(8,128)(2,1)}, bf16[272,512]{1,0:T(8,128)(2,1)S(1)}, u32[]{:S(2)}, u32[]{:S(2)}) collective-permute-start(bf16[272,512]{1,0:T(8,128)(2,1)} %get-tuple-element.31), channel_id=1, source_target_pairs={{0,1},{1,0},{2,3},{3,2},{4,8},{5,9},{6,10},{7,11},{8,4},{9,5},{10,... | collective-permute-start | bytes 835592 | tf_op jit(solution)/shard_map/ppermute | solution.py:357
  9.7 0.9 %collective-permute-start.5 = (bf16[272,512]{1,0:T(8,128)(2,1)S(1)}, bf16[272,512]{1,0:T(8,128)(2,1)S(1)}, u32[]{:S(2)}, u32[]{:S(2)}) collective-permute-start(bf16[272,512]{1,0:T(8,128)(2,1)S(1)} %collective-permute-done.4), channel_id=1, source_target_pairs={{0,1},{1,0},{2,3},{3,2},{4,8},{5,9},{6,10},{7,11},{8,4},{9,5},{10,... | collective-permute-start | bytes 835592 | tf_op jit(solution)/shard_map/ppermute | solution.py:359
  10.6 1.0 %copy-done.2 = bf16[272,512]{1,0:T(8,128)(2,1)S(1)} copy-done((bf16[272,512]{1,0:T(8,128)(2,1)S(1)}, bf16[272,512]{1,0:T(8,128)(2,1)}, u32[]{:S(2)}) %copy-start.2) | copy-done | bytes 278552
  11.6 1.7 %early.1 = (bf16[512,512]{1,0:T(8,128)(2,1)S(1)}, bf16[512,512]{1,0:T(8,128)(2,1)S(1)}, bf16[512,512]{1,0:T(8,128)(2,1)S(1)}, f32[2,256,512]{2,1,0:T(8,128)S(1)}) custom-call(bf16[512,1536]{1,0:T(8,128)(2,1)S(1)} %copy-done, bf16[272,512]{1,0:T(8,128)(2,1)S(1)} %copy-done.2, bf16[272,512]{1,0:T(8,128)(2,1)S(1)} %collective-permute-done.6.other_ref), custom_call_target="tpu_custom_call" | custom-call | flops 268435456 | bytes 4194304 | tf_op jit(solution)/shard_map/early/pallas_call | solution.py:362
  13.4 2.2 %collective-permute-done.refs_0_ = bf16[272,512]{1,0:T(8,128)(2,1)S(1)} collective-permute-done((bf16[272,512]{1,0:T(8,128)(2,1)}, bf16[272,512]{1,0:T(8,128)(2,1)S(1)}, u32[]{:S(2)}, u32[]{:S(2)}) %collective-permute-start) | collective-permute-done | bytes 278560 | tf_op jit(solution)/shard_map/ppermute | solution.py:356
  15.6 1.1 %collective-permute-done.3.refs_2_ = bf16[272,512]{1,0:T(8,128)(2,1)S(1)} collective-permute-done((bf16[272,512]{1,0:T(8,128)(2,1)}, bf16[272,512]{1,0:T(8,128)(2,1)S(1)}, u32[]{:S(2)}, u32[]{:S(2)}) %collective-permute-start.3) | collective-permute-done | bytes 278560 | tf_op jit(solution)/shard_map/ppermute | solution.py:357
  16.7 4.8 %collective-permute-done.2.refs_1_ = bf16[272,512]{1,0:T(8,128)(2,1)S(1)} collective-permute-done((bf16[272,512]{1,0:T(8,128)(2,1)S(1)}, bf16[272,512]{1,0:T(8,128)(2,1)S(1)}, u32[]{:S(2)}, u32[]{:S(2)}) %collective-permute-start.2) | collective-permute-done | bytes 278560 | tf_op jit(solution)/shard_map/ppermute | solution.py:358
  21.5 1.1 %collective-permute-done.5.refs_3_ = bf16[272,512]{1,0:T(8,128)(2,1)S(1)} collective-permute-done((bf16[272,512]{1,0:T(8,128)(2,1)S(1)}, bf16[272,512]{1,0:T(8,128)(2,1)S(1)}, u32[]{:S(2)}, u32[]{:S(2)}) %collective-permute-start.5) | collective-permute-done | bytes 278560 | tf_op jit(solution)/shard_map/ppermute | solution.py:359
  22.7 0.4 reduce.1
  23.1 0.3 collective-permute-start.7
  23.4 6.7 %collective-permute-done.7.refs_0_ = bf16[256,512]{1,0:T(8,128)(2,1)S(1)} collective-permute-done((bf16[256,512]{1,0:T(8,128)(2,1)S(1)}, bf16[256,512]{1,0:T(8,128)(2,1)S(1)}, u32[]{:S(2)}, u32[]{:S(2)}) %collective-permute-start.7) | collective-permute-done | bytes 262176 | tf_op jit(solution)/shard_map/ppermute | solution.py:390
  30.1 0.5 merge.1
  30.6 1.8 %collective-permute-start.10 = (bf16[256,512]{1,0:T(8,128)(2,1)S(1)}, bf16[256,512]{1,0:T(8,128)(2,1)S(1)}, u32[]{:S(2)}, u32[]{:S(2)}) collective-permute-start(bf16[256,512]{1,0:T(8,128)(2,1)S(1)} %get-tuple-element.40.own_ref), channel_id=1, source_target_pairs={{0,1},{1,0},{2,3},{3,2},{4,5},{5,4},{6,7},{7,6},{8,9},{9,8},{10,11... | collective-permute-start | bytes 786440 | tf_op jit(solution)/shard_map/ppermute | solution.py:413
  32.7 0.3 collective-permute-start.8
  33.1 2.1 %collective-permute-start.9 = (bf16[256,512]{1,0:T(8,128)(2,1)S(1)}, bf16[256,512]{1,0:T(8,128)(2,1)S(1)}, u32[]{:S(2)}, u32[]{:S(2)}) collective-permute-start(bf16[256,512]{1,0:T(8,128)(2,1)S(1)} %get-tuple-element.40.own_ref), channel_id=1, source_target_pairs={{0,1},{1,0},{2,4},{3,5},{4,2},{5,3},{6,8},{7,9},{8,6},{9,7},{10,12... | collective-permute-start | bytes 786440 | tf_op jit(solution)/shard_map/ppermute | solution.py:415
  35.2 8.3 %near.1 = (bf16[16,128,256]{2,1,0:T(8,128)(2,1)S(1)}, f32[16,48,256]{2,1,0:T(8,128)S(1)}, f32[16,8,256]{2,1,0:T(8,128)S(1)}) custom-call(bf16[256,512]{1,0:T(8,128)(2,1)S(1)} %get-tuple-element.40.own_ref, bf16[256,512]{1,0:T(8,128)(2,1)S(1)} %collective-permute-done.10.side_ref, bf16[512,512]{1,0:T(8,128)(2,1)S(1)} %get-tuple-element.41.wq_ref, ...), custom_call_target="tpu_custom_call" | custom-call | flops 8589934592 | bytes 4194304 | tf_op jit(solution)/shard_map/near/pallas_call | solution.py:418
  43.4 2.9 %collective-permute-done.8.even_ref = bf16[256,512]{1,0:T(8,128)(2,1)S(1)} collective-permute-done((bf16[256,512]{1,0:T(8,128)(2,1)S(1)}, bf16[256,512]{1,0:T(8,128)(2,1)S(1)}, u32[]{:S(2)}, u32[]{:S(2)}) %collective-permute-start.8) | collective-permute-done | bytes 262176 | tf_op jit(solution)/shard_map/ppermute | solution.py:414
  46.3 0.8 %collective-permute-start.11 = (bf16[256,512]{1,0:T(8,128)(2,1)S(1)}, bf16[256,512]{1,0:T(8,128)(2,1)S(1)}, u32[]{:S(2)}, u32[]{:S(2)}) collective-permute-start(bf16[256,512]{1,0:T(8,128)(2,1)S(1)} %collective-permute-done.8.even_ref), channel_id=1, source_target_pairs={{0,1},{1,0},{2,3},{3,2},{4,5},{5,4},{6,7},{7,6},{8,9},{9,8},{10,11... | collective-permute-start | bytes 786440 | tf_op jit(solution)/shard_map/ppermute | solution.py:438
  47.2 1.2 %collective-permute-done.11.first_ref = bf16[256,512]{1,0:T(8,128)(2,1)S(1)} collective-permute-done((bf16[256,512]{1,0:T(8,128)(2,1)S(1)}, bf16[256,512]{1,0:T(8,128)(2,1)S(1)}, u32[]{:S(2)}, u32[]{:S(2)}) %collective-permute-start.11) | collective-permute-done | bytes 262176 | tf_op jit(solution)/shard_map/ppermute | solution.py:438
  48.3 0.4 collective-permute-done.12.second_ref
  48.7 9.9 %far.1 = bf16[256,512]{1,0:T(8,128)(2,1)} custom-call(bf16[256,512]{1,0:T(8,128)(2,1)S(1)} %collective-permute-done.11.first_ref, bf16[256,512]{1,0:T(8,128)(2,1)S(1)} %collective-permute-done.12.second_ref, bf16[256,512]{1,0:T(8,128)(2,1)S(1)} %collective-permute-done.8.even_ref, bf16[256,512]{1,0:T(8,128)(2,1)S(1)} %collective-permute-done.9.odd_ref, ...), custom_call_target="tpu_custom_call" | custom-call | flops 8589934592 | bytes 8388608 | tf_op jit(solution)/shard_map/far/pallas_call | solution.py:440
  (30 shorter events, 0.6 us)
Async XLA Ops:
  0.0 10.6 %copy-start = (bf16[512,1536]{1,0:T(8,128)(2,1)S(1)}, bf16[512,1536]{1,0:T(8,128)(2,1)}, u32[]{:S(2)}) copy-start(bf16[512,1536]{1,0:T(8,128)(2,1)} %w_ref.2) | copy-start | bytes 4718596
  5.9 3.9 %collective-permute-start.1 = (bf16[272,512]{1,0:T(8,128)(2,1)}, bf16[272,512]{1,0:T(8,128)(2,1)S(1)}, u32[]{:S(2)}, u32[]{:S(2)}) collective-permute-start(bf16[272,512]{1,0:T(8,128)(2,1)} %get-tuple-element.30), channel_id=1, source_target_pairs={{0,1},{1,0},{2,3},{3,2},{4,5},{5,4},{6,7},{7,6},{8,9},{9,8},{10,11... | collective-permute-start | bytes 835592 | tf_op jit(solution)/shard_map/ppermute | solution.py:353
  6.6 3.1 %collective-permute-start.4 = (bf16[272,512]{1,0:T(8,128)(2,1)}, bf16[272,512]{1,0:T(8,128)(2,1)S(1)}, u32[]{:S(2)}, u32[]{:S(2)}) collective-permute-start(bf16[272,512]{1,0:T(8,128)(2,1)} %get-tuple-element.32), channel_id=1, source_target_pairs={{0,1},{1,0},{2,3},{3,2},{4,5},{5,4},{6,7},{7,6},{8,9},{9,8},{10,11... | collective-permute-start | bytes 835592 | tf_op jit(solution)/shard_map/ppermute | solution.py:354
  6.7 3.9 %collective-permute-start.6 = (bf16[272,512]{1,0:T(8,128)(2,1)}, bf16[272,512]{1,0:T(8,128)(2,1)S(1)}, u32[]{:S(2)}, u32[]{:S(2)}) collective-permute-start(bf16[272,512]{1,0:T(8,128)(2,1)} %get-tuple-element.36), channel_id=1, source_target_pairs={{0,1},{1,0},{2,3},{3,2},{4,5},{5,4},{6,7},{7,6},{8,9},{9,8},{10,11... | collective-permute-start | bytes 835592 | tf_op jit(solution)/shard_map/ppermute | solution.py:355
  7.1 8.4 %collective-permute-start = (bf16[272,512]{1,0:T(8,128)(2,1)}, bf16[272,512]{1,0:T(8,128)(2,1)S(1)}, u32[]{:S(2)}, u32[]{:S(2)}) collective-permute-start(bf16[272,512]{1,0:T(8,128)(2,1)} %get-tuple-element.29), channel_id=1, source_target_pairs={{0,4},{1,5},{2,6},{3,7},{4,0},{5,1},{6,2},{7,3},{8,12},{9,13},{10,... | collective-permute-start | bytes 835592 | tf_op jit(solution)/shard_map/ppermute | solution.py:356
  7.3 9.4 %collective-permute-start.3 = (bf16[272,512]{1,0:T(8,128)(2,1)}, bf16[272,512]{1,0:T(8,128)(2,1)S(1)}, u32[]{:S(2)}, u32[]{:S(2)}) collective-permute-start(bf16[272,512]{1,0:T(8,128)(2,1)} %get-tuple-element.31), channel_id=1, source_target_pairs={{0,1},{1,0},{2,3},{3,2},{4,8},{5,9},{6,10},{7,11},{8,4},{9,5},{10,... | collective-permute-start | bytes 835592 | tf_op jit(solution)/shard_map/ppermute | solution.py:357
  9.7 11.8 %collective-permute-start.2 = (bf16[272,512]{1,0:T(8,128)(2,1)S(1)}, bf16[272,512]{1,0:T(8,128)(2,1)S(1)}, u32[]{:S(2)}, u32[]{:S(2)}) collective-permute-start(bf16[272,512]{1,0:T(8,128)(2,1)S(1)} %collective-permute-done.1), channel_id=1, source_target_pairs={{0,4},{1,5},{2,6},{3,7},{4,0},{5,1},{6,2},{7,3},{8,12},{9,13},{10,... | collective-permute-start | bytes 835592 | tf_op jit(solution)/shard_map/ppermute | solution.py:358
  9.7 12.9 %collective-permute-start.5 = (bf16[272,512]{1,0:T(8,128)(2,1)S(1)}, bf16[272,512]{1,0:T(8,128)(2,1)S(1)}, u32[]{:S(2)}, u32[]{:S(2)}) collective-permute-start(bf16[272,512]{1,0:T(8,128)(2,1)S(1)} %collective-permute-done.4), channel_id=1, source_target_pairs={{0,1},{1,0},{2,3},{3,2},{4,8},{5,9},{6,10},{7,11},{8,4},{9,5},{10,... | collective-permute-start | bytes 835592 | tf_op jit(solution)/shard_map/ppermute | solution.py:359
  10.6 19.6 %copy-start.1 = (bf16[512,512]{1,0:T(8,128)(2,1)S(1)}, bf16[512,512]{1,0:T(8,128)(2,1)}, u32[]{:S(2)}) copy-start(bf16[512,512]{1,0:T(8,128)(2,1)} %refs_2_.1) | copy-start | bytes 1572868
  10.6 1.0 %copy-start.2 = (bf16[272,512]{1,0:T(8,128)(2,1)S(1)}, bf16[272,512]{1,0:T(8,128)(2,1)}, u32[]{:S(2)}) copy-start(bf16[272,512]{1,0:T(8,128)(2,1)} %get-tuple-element.35.own_ref) | copy-start | bytes 835588
  11.6 18.5 %copy-start.3 = (bf16[256,512]{1,0:T(8,128)(2,1)S(1)}, bf16[256,512]{1,0:T(8,128)(2,1)}, u32[]{:S(2)}) copy-start(bf16[256,512]{1,0:T(8,128)(2,1)} %refs_1_.1) | copy-start | bytes 786436
  11.6 18.5 %copy-start.4 = (f32[512]{0:T(512)S(1)}, f32[512]{0:T(512)}, u32[]{:S(2)}) copy-start(f32[512]{0:T(512)} %param.21) | copy-start | bytes 6148
  13.3 19.1 %copy-start.9 = (s32[16]{0:T(128)S(1)}, s32[16]{0:T(128)}, u32[]{:S(2)}) copy-start(s32[16]{0:T(128)} %window_ref.1) | copy-start | bytes 196
  23.1 7.0 %collective-permute-start.7 = (bf16[256,512]{1,0:T(8,128)(2,1)S(1)}, bf16[256,512]{1,0:T(8,128)(2,1)S(1)}, u32[]{:S(2)}, u32[]{:S(2)}) collective-permute-start(bf16[256,512]{1,0:T(8,128)(2,1)S(1)} %get-tuple-element.39), channel_id=1, source_target_pairs={{0,2},{1,3},{2,0},{3,1},{4,6},{5,7},{6,4},{7,5},{8,10},{9,11},{10,... | collective-permute-start | bytes 786440 | tf_op jit(solution)/shard_map/ppermute | solution.py:390
  30.6 4.5 %collective-permute-start.10 = (bf16[256,512]{1,0:T(8,128)(2,1)S(1)}, bf16[256,512]{1,0:T(8,128)(2,1)S(1)}, u32[]{:S(2)}, u32[]{:S(2)}) collective-permute-start(bf16[256,512]{1,0:T(8,128)(2,1)S(1)} %get-tuple-element.40.own_ref), channel_id=1, source_target_pairs={{0,1},{1,0},{2,3},{3,2},{4,5},{5,4},{6,7},{7,6},{8,9},{9,8},{10,11... | collective-permute-start | bytes 786440 | tf_op jit(solution)/shard_map/ppermute | solution.py:413
  32.7 13.6 %collective-permute-start.8 = (bf16[256,512]{1,0:T(8,128)(2,1)S(1)}, bf16[256,512]{1,0:T(8,128)(2,1)S(1)}, u32[]{:S(2)}, u32[]{:S(2)}) collective-permute-start(bf16[256,512]{1,0:T(8,128)(2,1)S(1)} %get-tuple-element.40.own_ref), channel_id=1, source_target_pairs={{0,2},{1,3},{2,0},{3,1},{4,6},{5,7},{6,4},{7,5},{8,10},{9,11},{10,... | collective-permute-start | bytes 786440 | tf_op jit(solution)/shard_map/ppermute | solution.py:414
  33.1 13.3 %collective-permute-start.9 = (bf16[256,512]{1,0:T(8,128)(2,1)S(1)}, bf16[256,512]{1,0:T(8,128)(2,1)S(1)}, u32[]{:S(2)}, u32[]{:S(2)}) collective-permute-start(bf16[256,512]{1,0:T(8,128)(2,1)S(1)} %get-tuple-element.40.own_ref), channel_id=1, source_target_pairs={{0,1},{1,0},{2,4},{3,5},{4,2},{5,3},{6,8},{7,9},{8,6},{9,7},{10,12... | collective-permute-start | bytes 786440 | tf_op jit(solution)/shard_map/ppermute | solution.py:415
  35.1 13.6 %copy-start.5 = (bf16[512,2048]{1,0:T(8,128)(2,1)S(1)}, bf16[512,2048]{1,0:T(8,128)(2,1)}, u32[]{:S(2)}) copy-start(bf16[512,2048]{1,0:T(8,128)(2,1)} %up_ref.1) | copy-start | bytes 6291460
  35.1 13.6 %copy-start.6 = (bf16[2048,512]{1,0:T(8,128)(2,1)S(1)}, bf16[2048,512]{1,0:T(8,128)(2,1)}, u32[]{:S(2)}) copy-start(bf16[2048,512]{1,0:T(8,128)(2,1)} %down_ref.1) | copy-start | bytes 6291460
  35.1 13.6 %copy-start.7 = (bf16[512,512]{1,0:T(8,128)(2,1)S(1)}, bf16[512,512]{1,0:T(8,128)(2,1)}, u32[]{:S(2)}) copy-start(bf16[512,512]{1,0:T(8,128)(2,1)} %w_out_ref.1) | copy-start | bytes 1572868
  35.1 13.6 %copy-start.8 = (f32[512]{0:T(512)S(1)}, f32[512]{0:T(512)}, u32[]{:S(2)}) copy-start(f32[512]{0:T(512)} %param.25) | copy-start | bytes 6148
  46.3 2.0 %collective-permute-start.11 = (bf16[256,512]{1,0:T(8,128)(2,1)S(1)}, bf16[256,512]{1,0:T(8,128)(2,1)S(1)}, u32[]{:S(2)}, u32[]{:S(2)}) collective-permute-start(bf16[256,512]{1,0:T(8,128)(2,1)S(1)} %collective-permute-done.8.even_ref), channel_id=1, source_target_pairs={{0,1},{1,0},{2,3},{3,2},{4,5},{5,4},{6,7},{7,6},{8,9},{9,8},{10,11... | collective-permute-start | bytes 786440 | tf_op jit(solution)/shard_map/ppermute | solution.py:438
  47.1 1.5 %collective-permute-start.12 = (bf16[256,512]{1,0:T(8,128)(2,1)S(1)}, bf16[256,512]{1,0:T(8,128)(2,1)S(1)}, u32[]{:S(2)}, u32[]{:S(2)}) collective-permute-start(bf16[256,512]{1,0:T(8,128)(2,1)S(1)} %collective-permute-done.9.odd_ref), channel_id=1, source_target_pairs={{0,1},{1,0},{2,3},{3,2},{4,5},{5,4},{6,7},{7,6},{8,9},{9,8},{10,11... | collective-permute-start | bytes 786440 | tf_op jit(solution)/shard_map/ppermute | solution.py:439

commit v2 on v1

--- a/solution.py
+++ b/solution.py
@@ -15,6 +15,7 @@
 TILE = 16
 GRID_PARTS = 4
 MOST = 56
+GROUP = 4
 
 norm_eps = 1e-05
 NODES = ("band", "inner")
@@ -183,31 +184,32 @@
     gap_ref[nodes : nodes + NEAR] = jnp.abs(lag[0:NEAR] + (side * nodes + first))
     gap_ref[nodes + NEAR : 2 * nodes] = jnp.abs(lag[0:NEAR] + (side * nodes + second))
 
-    def attend(h, rows):
-        scores = dot(key_ref[h // per_group, 0:rows, :], query_ref[h])
-        scores = jnp.where(gap_ref[0:rows] <= window_ref[h], scores, -1e30)
-        top = jnp.max(scores, axis=0, keepdims=True)
-        expo = jnp.exp2((scores - top) * scale).astype(jnp.bfloat16)
-        sums_ref[h] = dot(value_ref[h, :, 0:rows], expo)
-        top_ref[h] = jnp.broadcast_to(top, top_ref.shape[1:])
-
-    def pair(i, carry):
-        a, b = order_ref[2 * i], order_ref[2 * i + 1]
-        widest = jnp.maximum(window_ref[a], window_ref[b])
+    def attend(heads, rows):
+        scores = [dot(key_ref[h // per_group, 0:rows, :], query_ref[h]) for h in heads]
+        scores = [
+            jnp.where(gap_ref[0:rows] <= window_ref[h], x, -1e30) for h, x in zip(heads, scores)
+        ]
+        tops = [jnp.max(x, axis=0, keepdims=True) for x in scores]
+        expos = [jnp.exp2((x - top) * scale).astype(jnp.bfloat16) for x, top in zip(scores, tops)]
+        for h, top, expo in zip(heads, tops, expos):
+            sums_ref[h] = dot(value_ref[h, :, 0:rows], expo)
+            top_ref[h] = jnp.broadcast_to(top, top_ref.shape[1:])
+
+    def together(i, carry):
+        heads = [order_ref[GROUP * i + k] for k in range(GROUP)]
+        widest = functools.reduce(jnp.maximum, [window_ref[h] for h in heads])
 
         @pl.when(widest <= NEAR)
         def _():
-            attend(a, nodes + NEAR)
-            attend(b, nodes + NEAR)
+            attend(heads, nodes + NEAR)
 
         @pl.when(widest > NEAR)
         def _():
-            attend(a, 2 * nodes)
-            attend(b, 2 * nodes)
+            attend(heads, 2 * nodes)
 
         return carry
 
-    lax.fori_loop(0, HEADS // 2, pair, 0)
+    lax.fori_loop(0, HEADS // GROUP, together, 0)
 
 
 def far_kernel(
@@ -249,37 +251,37 @@
     gap_ref[nodes : 2 * nodes] = gap(lag, far, 0)
     gap_ref[2 * nodes : 3 * nodes] = gap(lag, -far, 0)
 
-    def attend(h, rows):
-        scores = dot(key_ref[h // per_group, 0:rows, :], query_ref[h])
-        scores = jnp.where(gap_ref[0:rows] <= window_ref[h], scores, -1e30)
-        before = top_ref[h, 0:1, :]
-        top = jnp.maximum(before, jnp.max(scores, axis=0, keepdims=True))
-        expo = jnp.exp2((scores - top) * scale).astype(jnp.bfloat16)
-        sums = sums_ref[h] * jnp.exp2((before - top) * scale) + dot(value_ref[h, :, 0:rows], expo)
-        attended_ref[h] = (sums[0:head_dim] / sums[head_dim : head_dim + 1]).astype(jnp.bfloat16)
-
-    def pair(i, carry):
-        a, b = order_ref[2 * i], order_ref[2 * i + 1]
-        widest = jnp.maximum(window_ref[a], window_ref[b])
+    def attend(heads, rows):
+        scores = [dot(key_ref[h // per_group, 0:rows, :], query_ref[h]) for h in heads]
+        scores = [
+            jnp.where(gap_ref[0:rows] <= window_ref[h], x, -1e30) for h, x in zip(heads, scores)
+        ]
+        olds = [top_ref[h, 0:1, :] for h in heads]
+        tops = [jnp.maximum(old, jnp.max(x, axis=0, keepdims=True)) for old, x in zip(olds, scores)]
+        expos = [jnp.exp2((x - top) * scale).astype(jnp.bfloat16) for x, top in zip(scores, tops)]
+        for h, old, top, expo in zip(heads, olds, tops, expos):
+            sums = sums_ref[h] * jnp.exp2((old - top) * scale) + dot(value_ref[h, :, 0:rows], expo)
+            attended_ref[h] = (sums[0:head_dim] / sums[head_dim : head_dim + 1]).astype(jnp.bfloat16)
+
+    def together(i, carry):
+        heads = [order_ref[GROUP * i + k] for k in range(GROUP)]
+        widest = functools.reduce(jnp.maximum, [window_ref[h] for h in heads])
 
         @pl.when(widest <= NEAR)
         def _():
-            attend(a, NEAR)
-            attend(b, NEAR)
+            attend(heads, NEAR)
 
         @pl.when((widest > NEAR) & (widest <= nodes))
         def _():
-            attend(a, nodes)
-            attend(b, nodes)
+            attend(heads, nodes)
 
         @pl.when(widest > nodes)
         def _():
-            attend(a, 3 * nodes)
-            attend(b, 3 * nodes)
+            attend(heads, 3 * nodes)
 
         return carry
 
-    lax.fori_loop(0, HEADS // 2, pair, 0)
+    lax.fori_loop(0, HEADS // GROUP, together, 0)
 
     attended = attended_ref[...].reshape(width, nodes)
     mixed = lax.dot_general(

time: 59.1 us -> 56.3 us (0.953)
  Pallas kernels: 26.7 us -> 20.5 us
  waiting for transfers between devices: 20.5 us -> 23.7 us
    pallas_call x1, Pallas kernels: 8.29 us -> 5.03 us  [local(): pl.pallas_call(near_kernel, out_shape=[jax.ShapeDtypeStruct((HEADS, LANES...]
    ppermute x1, waiting for transfers between devices: 2.9 us -> 6.15 us  [local(): even = lax.ppermute(normed, NODES, chips_trade(0))]
    pallas_call x1, Pallas kernels: 9.93 us -> 7.03 us  [local(): pl.pallas_call(far_kernel, out_shape=jax.ShapeDtypeStruct((nodes, width),...]
  transfers between devices with their start and end apart: 13 -> 13, of which waited for: 8 -> 8; matrix products, arithmetic and copies ran while one was open for 1% -> 1% of each run, Pallas kernels for 17% -> 12%
where the time goes in v2:
time: 56.3 us; the launch traced here: 55.7 us
  waiting for transfers between devices  23.7 us (42%)
  Pallas kernels  20.5 us (36%)
  starting transfers between devices  10 us (18%)
  local copies, waits for them, and re-layouts  1.05 us (2%)
    pallas_call x1, Pallas kernels, local(): pl.pallas_call(far_kernel, out_shape=jax.ShapeDtypeStruct((nodes, width),...  7.03 us
    ppermute x1, waiting for transfers between devices, local(): lax.ppermute(sums[p], NODES, [(g, g ^ 2 * p) for g in range(devices)])  6.72 us
    ppermute x1, waiting for transfers between devices, local(): even = lax.ppermute(normed, NODES, chips_trade(0))  6.15 us
    pallas_call x1, Pallas kernels, local(): pl.pallas_call(functools.partial(message_kernel, pairs), out_shape=[jax.S...  5.84 us
    pallas_call x1, Pallas kernels, local(): pl.pallas_call(near_kernel, out_shape=[jax.ShapeDtypeStruct((HEADS, LANES...  5.03 us
    ppermute x1, waiting for transfers between devices, local(): even_other = lax.ppermute(even_other, NODES, bands_trade(0))  4.84 us
    ppermute x1, starting transfers between devices, local(): odd = lax.ppermute(odd, NODES, bands_trade(1))  2.43 us
    ppermute x1, waiting for transfers between devices, local(): even = lax.ppermute(even, NODES, bands_trade(0))  2.2 us
  transfers between devices with their start and end apart: 13, of which 8 were waited for; matrix products, arithmetic and copies ran while one was open for 1% of the time, Pallas kernels for 12%

profile of v2, /device:TPU:15, one launch (start us, length us, event | category | flops | bytes accessed | tf_op | source)
XLA Modules:
  0.0 55.7 jit_solution(11404206528279114736)
XLA Ops:
  0.0 5.8 %messages.1 = (bf16[272,512]{1,0:T(8,128)(2,1)}, bf16[272,512]{1,0:T(8,128)(2,1)}, bf16[272,512]{1,0:T(8,128)(2,1)}, bf16[272,512]{1,0:T(8,128)(2,1)}, bf16[272,...) custom-call(bf16[1024,512]{1,0:T(8,128)(2,1)} %grid_ref.1, bf16[512,512]{1,0:T(8,128)(2,1)} %w_ref.1, ...), custom_call_target="tpu_custom_call" | custom-call | flops 2147483648 | bytes 4194304 | tf_op jit(solution)/shard_map/messages/pallas_call | solution.py:327
  5.9 0.7 %collective-permute-start.1 = (bf16[272,512]{1,0:T(8,128)(2,1)}, bf16[272,512]{1,0:T(8,128)(2,1)S(1)}, u32[]{:S(2)}, u32[]{:S(2)}) collective-permute-start(bf16[272,512]{1,0:T(8,128)(2,1)} %get-tuple-element.30), channel_id=1, source_target_pairs={{0,1},{1,0},{2,3},{3,2},{4,5},{5,4},{6,7},{7,6},{8,9},{9,8},{10,11... | collective-permute-start | bytes 835592 | tf_op jit(solution)/shard_map/ppermute | solution.py:355
  6.7 0.4 collective-permute-start.6
  7.3 2.4 %collective-permute-start.3 = (bf16[272,512]{1,0:T(8,128)(2,1)}, bf16[272,512]{1,0:T(8,128)(2,1)S(1)}, u32[]{:S(2)}, u32[]{:S(2)}) collective-permute-start(bf16[272,512]{1,0:T(8,128)(2,1)} %get-tuple-element.31), channel_id=1, source_target_pairs={{0,1},{1,0},{2,3},{3,2},{4,8},{5,9},{6,10},{7,11},{8,4},{9,5},{10,... | collective-permute-start | bytes 835592 | tf_op jit(solution)/shard_map/ppermute | solution.py:359
  9.7 0.9 %collective-permute-start.5 = (bf16[272,512]{1,0:T(8,128)(2,1)S(1)}, bf16[272,512]{1,0:T(8,128)(2,1)S(1)}, u32[]{:S(2)}, u32[]{:S(2)}) collective-permute-start(bf16[272,512]{1,0:T(8,128)(2,1)S(1)} %collective-permute-done.4), channel_id=1, source_target_pairs={{0,1},{1,0},{2,3},{3,2},{4,8},{5,9},{6,10},{7,11},{8,4},{9,5},{10,... | collective-permute-start | bytes 835592 | tf_op jit(solution)/shard_map/ppermute | solution.py:361
  10.6 1.0 %copy-done.2 = bf16[272,512]{1,0:T(8,128)(2,1)S(1)} copy-done((bf16[272,512]{1,0:T(8,128)(2,1)S(1)}, bf16[272,512]{1,0:T(8,128)(2,1)}, u32[]{:S(2)}) %copy-start.2) | copy-done | bytes 278552
  11.6 1.7 %early.1 = (bf16[512,512]{1,0:T(8,128)(2,1)S(1)}, bf16[512,512]{1,0:T(8,128)(2,1)S(1)}, bf16[512,512]{1,0:T(8,128)(2,1)S(1)}, f32[2,256,512]{2,1,0:T(8,128)S(1)}) custom-call(bf16[512,1536]{1,0:T(8,128)(2,1)S(1)} %copy-done, bf16[272,512]{1,0:T(8,128)(2,1)S(1)} %copy-done.2, bf16[272,512]{1,0:T(8,128)(2,1)S(1)} %collective-permute-done.6.other_ref), custom_call_target="tpu_custom_call" | custom-call | flops 268435456 | bytes 4194304 | tf_op jit(solution)/shard_map/early/pallas_call | solution.py:364
  13.4 2.2 %collective-permute-done.refs_0_ = bf16[272,512]{1,0:T(8,128)(2,1)S(1)} collective-permute-done((bf16[272,512]{1,0:T(8,128)(2,1)}, bf16[272,512]{1,0:T(8,128)(2,1)S(1)}, u32[]{:S(2)}, u32[]{:S(2)}) %collective-permute-start) | collective-permute-done | bytes 278560 | tf_op jit(solution)/shard_map/ppermute | solution.py:358
  15.6 1.1 %collective-permute-done.3.refs_2_ = bf16[272,512]{1,0:T(8,128)(2,1)S(1)} collective-permute-done((bf16[272,512]{1,0:T(8,128)(2,1)}, bf16[272,512]{1,0:T(8,128)(2,1)S(1)}, u32[]{:S(2)}, u32[]{:S(2)}) %collective-permute-start.3) | collective-permute-done | bytes 278560 | tf_op jit(solution)/shard_map/ppermute | solution.py:359
  16.7 4.8 %collective-permute-done.2.refs_1_ = bf16[272,512]{1,0:T(8,128)(2,1)S(1)} collective-permute-done((bf16[272,512]{1,0:T(8,128)(2,1)S(1)}, bf16[272,512]{1,0:T(8,128)(2,1)S(1)}, u32[]{:S(2)}, u32[]{:S(2)}) %collective-permute-start.2) | collective-permute-done | bytes 278560 | tf_op jit(solution)/shard_map/ppermute | solution.py:360
  21.5 1.1 %collective-permute-done.5.refs_3_ = bf16[272,512]{1,0:T(8,128)(2,1)S(1)} collective-permute-done((bf16[272,512]{1,0:T(8,128)(2,1)S(1)}, bf16[272,512]{1,0:T(8,128)(2,1)S(1)}, u32[]{:S(2)}, u32[]{:S(2)}) %collective-permute-start.5) | collective-permute-done | bytes 278560 | tf_op jit(solution)/shard_map/ppermute | solution.py:361
  22.7 0.4 reduce.1
  23.1 0.3 collective-permute-start.7
  23.4 6.7 %collective-permute-done.7.refs_0_ = bf16[256,512]{1,0:T(8,128)(2,1)S(1)} collective-permute-done((bf16[256,512]{1,0:T(8,128)(2,1)S(1)}, bf16[256,512]{1,0:T(8,128)(2,1)S(1)}, u32[]{:S(2)}, u32[]{:S(2)}) %collective-permute-start.7) | collective-permute-done | bytes 262176 | tf_op jit(solution)/shard_map/ppermute | solution.py:392
  30.1 0.5 merge.1
  30.6 1.8 %collective-permute-start.10 = (bf16[256,512]{1,0:T(8,128)(2,1)S(1)}, bf16[256,512]{1,0:T(8,128)(2,1)S(1)}, u32[]{:S(2)}, u32[]{:S(2)}) collective-permute-start(bf16[256,512]{1,0:T(8,128)(2,1)S(1)} %get-tuple-element.40.own_ref), channel_id=1, source_target_pairs={{0,1},{1,0},{2,3},{3,2},{4,5},{5,4},{6,7},{7,6},{8,9},{9,8},{10,11... | collective-permute-start | bytes 786440 | tf_op jit(solution)/shard_map/ppermute | solution.py:415
  32.7 0.3 collective-permute-start.8
  33.1 2.1 %collective-permute-start.9 = (bf16[256,512]{1,0:T(8,128)(2,1)S(1)}, bf16[256,512]{1,0:T(8,128)(2,1)S(1)}, u32[]{:S(2)}, u32[]{:S(2)}) collective-permute-start(bf16[256,512]{1,0:T(8,128)(2,1)S(1)} %get-tuple-element.40.own_ref), channel_id=1, source_target_pairs={{0,1},{1,0},{2,4},{3,5},{4,2},{5,3},{6,8},{7,9},{8,6},{9,7},{10,12... | collective-permute-start | bytes 786440 | tf_op jit(solution)/shard_map/ppermute | solution.py:417
  35.2 5.0 %near.1 = (bf16[16,128,256]{2,1,0:T(8,128)(2,1)S(1)}, f32[16,48,256]{2,1,0:T(8,128)S(1)}, f32[16,8,256]{2,1,0:T(8,128)S(1)}) custom-call(bf16[256,512]{1,0:T(8,128)(2,1)S(1)} %get-tuple-element.40.own_ref, bf16[256,512]{1,0:T(8,128)(2,1)S(1)} %collective-permute-done.10.side_ref, bf16[512,512]{1,0:T(8,128)(2,1)S(1)} %get-tuple-element.41.wq_ref, ...), custom_call_target="tpu_custom_call" | custom-call | flops 8589934592 | bytes 4194304 | tf_op jit(solution)/shard_map/near/pallas_call | solution.py:420
  40.2 6.2 %collective-permute-done.8.even_ref = bf16[256,512]{1,0:T(8,128)(2,1)S(1)} collective-permute-done((bf16[256,512]{1,0:T(8,128)(2,1)S(1)}, bf16[256,512]{1,0:T(8,128)(2,1)S(1)}, u32[]{:S(2)}, u32[]{:S(2)}) %collective-permute-start.8) | collective-permute-done | bytes 262176 | tf_op jit(solution)/shard_map/ppermute | solution.py:416
  46.3 0.8 %collective-permute-start.11 = (bf16[256,512]{1,0:T(8,128)(2,1)S(1)}, bf16[256,512]{1,0:T(8,128)(2,1)S(1)}, u32[]{:S(2)}, u32[]{:S(2)}) collective-permute-start(bf16[256,512]{1,0:T(8,128)(2,1)S(1)} %collective-permute-done.8.even_ref), channel_id=1, source_target_pairs={{0,1},{1,0},{2,3},{3,2},{4,5},{5,4},{6,7},{7,6},{8,9},{9,8},{10,11... | collective-permute-start | bytes 786440 | tf_op jit(solution)/shard_map/ppermute | solution.py:440
  47.2 1.2 %collective-permute-done.11.first_ref = bf16[256,512]{1,0:T(8,128)(2,1)S(1)} collective-permute-done((bf16[256,512]{1,0:T(8,128)(2,1)S(1)}, bf16[256,512]{1,0:T(8,128)(2,1)S(1)}, u32[]{:S(2)}, u32[]{:S(2)}) %collective-permute-start.11) | collective-permute-done | bytes 262176 | tf_op jit(solution)/shard_map/ppermute | solution.py:440
  48.3 0.4 collective-permute-done.12.second_ref
  48.7 7.0 %far.1 = bf16[256,512]{1,0:T(8,128)(2,1)} custom-call(bf16[256,512]{1,0:T(8,128)(2,1)S(1)} %collective-permute-done.11.first_ref, bf16[256,512]{1,0:T(8,128)(2,1)S(1)} %collective-permute-done.12.second_ref, bf16[256,512]{1,0:T(8,128)(2,1)S(1)} %collective-permute-done.8.even_ref, bf16[256,512]{1,0:T(8,128)(2,1)S(1)} %collective-permute-done.9.odd_ref, ...), custom_call_target="tpu_custom_call" | custom-call | flops 8589934592 | bytes 8388608 | tf_op jit(solution)/shard_map/far/pallas_call | solution.py:442
  (30 shorter events, 0.6 us)
Async XLA Ops:
  0.0 10.6 %copy-start = (bf16[512,1536]{1,0:T(8,128)(2,1)S(1)}, bf16[512,1536]{1,0:T(8,128)(2,1)}, u32[]{:S(2)}) copy-start(bf16[512,1536]{1,0:T(8,128)(2,1)} %w_ref.2) | copy-start | bytes 4718596
  5.9 3.9 %collective-permute-start.1 = (bf16[272,512]{1,0:T(8,128)(2,1)}, bf16[272,512]{1,0:T(8,128)(2,1)S(1)}, u32[]{:S(2)}, u32[]{:S(2)}) collective-permute-start(bf16[272,512]{1,0:T(8,128)(2,1)} %get-tuple-element.30), channel_id=1, source_target_pairs={{0,1},{1,0},{2,3},{3,2},{4,5},{5,4},{6,7},{7,6},{8,9},{9,8},{10,11... | collective-permute-start | bytes 835592 | tf_op jit(solution)/shard_map/ppermute | solution.py:355
  6.6 3.1 %collective-permute-start.4 = (bf16[272,512]{1,0:T(8,128)(2,1)}, bf16[272,512]{1,0:T(8,128)(2,1)S(1)}, u32[]{:S(2)}, u32[]{:S(2)}) collective-permute-start(bf16[272,512]{1,0:T(8,128)(2,1)} %get-tuple-element.32), channel_id=1, source_target_pairs={{0,1},{1,0},{2,3},{3,2},{4,5},{5,4},{6,7},{7,6},{8,9},{9,8},{10,11... | collective-permute-start | bytes 835592 | tf_op jit(solution)/shard_map/ppermute | solution.py:356
  6.7 3.9 %collective-permute-start.6 = (bf16[272,512]{1,0:T(8,128)(2,1)}, bf16[272,512]{1,0:T(8,128)(2,1)S(1)}, u32[]{:S(2)}, u32[]{:S(2)}) collective-permute-start(bf16[272,512]{1,0:T(8,128)(2,1)} %get-tuple-element.36), channel_id=1, source_target_pairs={{0,1},{1,0},{2,3},{3,2},{4,5},{5,4},{6,7},{7,6},{8,9},{9,8},{10,11... | collective-permute-start | bytes 835592 | tf_op jit(solution)/shard_map/ppermute | solution.py:357
  7.1 8.4 %collective-permute-start = (bf16[272,512]{1,0:T(8,128)(2,1)}, bf16[272,512]{1,0:T(8,128)(2,1)S(1)}, u32[]{:S(2)}, u32[]{:S(2)}) collective-permute-start(bf16[272,512]{1,0:T(8,128)(2,1)} %get-tuple-element.29), channel_id=1, source_target_pairs={{0,4},{1,5},{2,6},{3,7},{4,0},{5,1},{6,2},{7,3},{8,12},{9,13},{10,... | collective-permute-start | bytes 835592 | tf_op jit(solution)/shard_map/ppermute | solution.py:358
  7.3 9.4 %collective-permute-start.3 = (bf16[272,512]{1,0:T(8,128)(2,1)}, bf16[272,512]{1,0:T(8,128)(2,1)S(1)}, u32[]{:S(2)}, u32[]{:S(2)}) collective-permute-start(bf16[272,512]{1,0:T(8,128)(2,1)} %get-tuple-element.31), channel_id=1, source_target_pairs={{0,1},{1,0},{2,3},{3,2},{4,8},{5,9},{6,10},{7,11},{8,4},{9,5},{10,... | collective-permute-start | bytes 835592 | tf_op jit(solution)/shard_map/ppermute | solution.py:359
  9.7 11.8 %collective-permute-start.2 = (bf16[272,512]{1,0:T(8,128)(2,1)S(1)}, bf16[272,512]{1,0:T(8,128)(2,1)S(1)}, u32[]{:S(2)}, u32[]{:S(2)}) collective-permute-start(bf16[272,512]{1,0:T(8,128)(2,1)S(1)} %collective-permute-done.1), channel_id=1, source_target_pairs={{0,4},{1,5},{2,6},{3,7},{4,0},{5,1},{6,2},{7,3},{8,12},{9,13},{10,... | collective-permute-start | bytes 835592 | tf_op jit(solution)/shard_map/ppermute | solution.py:360
  9.7 12.9 %collective-permute-start.5 = (bf16[272,512]{1,0:T(8,128)(2,1)S(1)}, bf16[272,512]{1,0:T(8,128)(2,1)S(1)}, u32[]{:S(2)}, u32[]{:S(2)}) collective-permute-start(bf16[272,512]{1,0:T(8,128)(2,1)S(1)} %collective-permute-done.4), channel_id=1, source_target_pairs={{0,1},{1,0},{2,3},{3,2},{4,8},{5,9},{6,10},{7,11},{8,4},{9,5},{10,... | collective-permute-start | bytes 835592 | tf_op jit(solution)/shard_map/ppermute | solution.py:361
  10.6 19.6 %copy-start.1 = (bf16[512,512]{1,0:T(8,128)(2,1)S(1)}, bf16[512,512]{1,0:T(8,128)(2,1)}, u32[]{:S(2)}) copy-start(bf16[512,512]{1,0:T(8,128)(2,1)} %refs_2_.1) | copy-start | bytes 1572868
  10.6 1.0 %copy-start.2 = (bf16[272,512]{1,0:T(8,128)(2,1)S(1)}, bf16[272,512]{1,0:T(8,128)(2,1)}, u32[]{:S(2)}) copy-start(bf16[272,512]{1,0:T(8,128)(2,1)} %get-tuple-element.35.own_ref) | copy-start | bytes 835588
  11.6 18.5 %copy-start.3 = (bf16[256,512]{1,0:T(8,128)(2,1)S(1)}, bf16[256,512]{1,0:T(8,128)(2,1)}, u32[]{:S(2)}) copy-start(bf16[256,512]{1,0:T(8,128)(2,1)} %refs_1_.1) | copy-start | bytes 786436
  11.6 18.5 %copy-start.4 = (f32[512]{0:T(512)S(1)}, f32[512]{0:T(512)}, u32[]{:S(2)}) copy-start(f32[512]{0:T(512)} %param.21) | copy-start | bytes 6148
  13.3 19.1 %copy-start.9 = (s32[16]{0:T(128)S(1)}, s32[16]{0:T(128)}, u32[]{:S(2)}) copy-start(s32[16]{0:T(128)} %window_ref.1) | copy-start | bytes 196
  23.1 7.0 %collective-permute-start.7 = (bf16[256,512]{1,0:T(8,128)(2,1)S(1)}, bf16[256,512]{1,0:T(8,128)(2,1)S(1)}, u32[]{:S(2)}, u32[]{:S(2)}) collective-permute-start(bf16[256,512]{1,0:T(8,128)(2,1)S(1)} %get-tuple-element.39), channel_id=1, source_target_pairs={{0,2},{1,3},{2,0},{3,1},{4,6},{5,7},{6,4},{7,5},{8,10},{9,11},{10,... | collective-permute-start | bytes 786440 | tf_op jit(solution)/shard_map/ppermute | solution.py:392
  30.6 4.5 %collective-permute-start.10 = (bf16[256,512]{1,0:T(8,128)(2,1)S(1)}, bf16[256,512]{1,0:T(8,128)(2,1)S(1)}, u32[]{:S(2)}, u32[]{:S(2)}) collective-permute-start(bf16[256,512]{1,0:T(8,128)(2,1)S(1)} %get-tuple-element.40.own_ref), channel_id=1, source_target_pairs={{0,1},{1,0},{2,3},{3,2},{4,5},{5,4},{6,7},{7,6},{8,9},{9,8},{10,11... | collective-permute-start | bytes 786440 | tf_op jit(solution)/shard_map/ppermute | solution.py:415
  32.7 13.6 %collective-permute-start.8 = (bf16[256,512]{1,0:T(8,128)(2,1)S(1)}, bf16[256,512]{1,0:T(8,128)(2,1)S(1)}, u32[]{:S(2)}, u32[]{:S(2)}) collective-permute-start(bf16[256,512]{1,0:T(8,128)(2,1)S(1)} %get-tuple-element.40.own_ref), channel_id=1, source_target_pairs={{0,2},{1,3},{2,0},{3,1},{4,6},{5,7},{6,4},{7,5},{8,10},{9,11},{10,... | collective-permute-start | bytes 786440 | tf_op jit(solution)/shard_map/ppermute | solution.py:416
  33.1 13.3 %collective-permute-start.9 = (bf16[256,512]{1,0:T(8,128)(2,1)S(1)}, bf16[256,512]{1,0:T(8,128)(2,1)S(1)}, u32[]{:S(2)}, u32[]{:S(2)}) collective-permute-start(bf16[256,512]{1,0:T(8,128)(2,1)S(1)} %get-tuple-element.40.own_ref), channel_id=1, source_target_pairs={{0,1},{1,0},{2,4},{3,5},{4,2},{5,3},{6,8},{7,9},{8,6},{9,7},{10,12... | collective-permute-start | bytes 786440 | tf_op jit(solution)/shard_map/ppermute | solution.py:417
  35.1 13.6 %copy-start.5 = (bf16[512,2048]{1,0:T(8,128)(2,1)S(1)}, bf16[512,2048]{1,0:T(8,128)(2,1)}, u32[]{:S(2)}) copy-start(bf16[512,2048]{1,0:T(8,128)(2,1)} %up_ref.1) | copy-start | bytes 6291460
  35.1 13.6 %copy-start.6 = (bf16[2048,512]{1,0:T(8,128)(2,1)S(1)}, bf16[2048,512]{1,0:T(8,128)(2,1)}, u32[]{:S(2)}) copy-start(bf16[2048,512]{1,0:T(8,128)(2,1)} %down_ref.1) | copy-start | bytes 6291460
  35.1 13.6 %copy-start.7 = (bf16[512,512]{1,0:T(8,128)(2,1)S(1)}, bf16[512,512]{1,0:T(8,128)(2,1)}, u32[]{:S(2)}) copy-start(bf16[512,512]{1,0:T(8,128)(2,1)} %w_out_ref.1) | copy-start | bytes 1572868
  35.1 13.6 %copy-start.8 = (f32[512]{0:T(512)S(1)}, f32[512]{0:T(512)}, u32[]{:S(2)}) copy-start(f32[512]{0:T(512)} %param.25) | copy-start | bytes 6148
  46.3 2.0 %collective-permute-start.11 = (bf16[256,512]{1,0:T(8,128)(2,1)S(1)}, bf16[256,512]{1,0:T(8,128)(2,1)S(1)}, u32[]{:S(2)}, u32[]{:S(2)}) collective-permute-start(bf16[256,512]{1,0:T(8,128)(2,1)S(1)} %collective-permute-done.8.even_ref), channel_id=1, source_target_pairs={{0,1},{1,0},{2,3},{3,2},{4,5},{5,4},{6,7},{7,6},{8,9},{9,8},{10,11... | collective-permute-start | bytes 786440 | tf_op jit(solution)/shard_map/ppermute | solution.py:440
  47.1 1.5 %collective-permute-start.12 = (bf16[256,512]{1,0:T(8,128)(2,1)S(1)}, bf16[256,512]{1,0:T(8,128)(2,1)S(1)}, u32[]{:S(2)}, u32[]{:S(2)}) collective-permute-start(bf16[256,512]{1,0:T(8,128)(2,1)S(1)} %collective-permute-done.9.odd_ref), channel_id=1, source_target_pairs={{0,1},{1,0},{2,3},{3,2},{4,5},{5,4},{6,7},{7,6},{8,9},{9,8},{10,11... | collective-permute-start | bytes 786440 | tf_op jit(solution)/shard_map/ppermute | solution.py:441

commit v3 on v2

--- a/solution.py
+++ b/solution.py
@@ -13,6 +13,7 @@
 LANES = 128
 NEAR = 128
 TILE = 16
+CAP = 128
 GRID_PARTS = 4
 MOST = 56
 GROUP = 4
@@ -42,11 +43,34 @@
     return center * lax.rsqrt(spread + norm_eps) * gain
 
 
+def band_offsets():
+    ahead = lax.rem(lax.axis_index("band"), 2) * 2
+    return 2 - ahead, ahead, 1
+
+
+def slot_columns(source_ref, blocks):
+    sources = jnp.concatenate([source_ref[0, 0, o, pl.ds(j, 1), :] for o, j in blocks], axis=0)
+    return jnp.transpose(sources.astype(jnp.float32)).astype(jnp.int32)
+
+
+def target_tile(target_ref, count_ref, blocks, lanes):
+    cap = target_ref.shape[-1]
+    slot = lax.broadcasted_iota(jnp.int32, (1, cap), 1)
+    targets = [
+        jnp.where(slot < count_ref[0, o, 0, j], target_ref[0, 0, o, pl.ds(j, 1), :], -1) for o, j in blocks
+    ]
+    targets.append(jnp.full((TILE - len(blocks), cap), -1, jnp.int32))
+    tile = jnp.concatenate(targets, axis=0).astype(jnp.float32).astype(jnp.bfloat16)
+    return jnp.concatenate([tile] * (lanes // cap), axis=1)
+
+
 def message_kernel(pair_count, grid_ref, w_ref, source_ref, target_ref, count_ref, *refs):
-    out_refs, (grid_vmem, w_vmem, message_ref, out_vmem, in_sems, out_sems) = refs[:6], refs[6:]
+    count = 4 + 2 * pair_count
+    out_refs, out_vmems = refs[:count], refs[count : 2 * count]
+    grid_vmem, w_vmem, message_ref, in_sems, out_sems = refs[2 * count :]
     rows = grid_ref.shape[0]
     cap = source_ref.shape[-1]
-    slots = pair_count * cap
+    half = w_ref.shape[1] // 2
     part = rows // GRID_PARTS
     fetches = [pltpu.make_async_copy(w_ref, w_vmem, in_sems.at[GRID_PARTS])]
     for k in range(GRID_PARTS):
@@ -55,54 +79,60 @@
     for fetch in fetches:
         fetch.start()
     inner = lax.axis_index("inner")
-    ahead = lax.rem(lax.axis_index("band"), 2) * 2
-    blocks = [(o, inner ^ (2 * p + k)) for o in (2 - ahead, ahead, 1) for k in range(2) for p in range(pair_count)]
-    sources = jnp.concatenate([source_ref[0, 0, o, pl.ds(j, 1), :] for o, j in blocks], axis=0)
-    by_slot = jnp.transpose(sources.astype(jnp.float32)).astype(jnp.int32)
-    slot = lax.broadcasted_iota(jnp.int32, (1, cap), 1)
-    for m, (o, j) in enumerate(blocks):
-        target = jnp.where(slot < count_ref[0, o, 0, j], target_ref[0, 0, o, pl.ds(j, 1), :], -1)
-        tile = jnp.broadcast_to(target.astype(jnp.float32), (TILE, cap)).astype(jnp.bfloat16)
-        p = m % pair_count
-        out_vmem[m // pair_count, slots:, p * cap : (p + 1) * cap] = tile
-    if out_vmem.shape[2] > slots:
-        rest = jnp.zeros((6, TILE, out_vmem.shape[2] - slots), jnp.bfloat16)
-        out_vmem[:, slots:, slots:] = rest
+    offsets = band_offsets()
+    keys = [(t, p, k) for t in range(3) for p in range(pair_count) for k in range(2)]
+    place = {(t, p, k): (offsets[t], inner ^ (2 * p + k)) for t, p, k in keys}
+    by_slot = slot_columns(source_ref, [place[key] for key in keys])
+    left, right = slice(0, half), slice(half, 2 * half)
+    runs = [[([(t, p, k) for p in range(pair_count)], left)] for t in range(2) for k in range(2)]
+    runs += [[([(t, p, k) for t in range(3)], right)] for p in range(1, pair_count) for k in range(2)]
+    runs += [
+        [([(2, p, k) for p in range(pair_count)], left), ([(t, 0, k) for t in range(3)], right)] for k in range(2)
+    ]
+    for out_vmem, parts in zip(out_vmems, runs):
+        start = 0
+        for chosen, _ in parts:
+            start += len(chosen) * cap
+            out_vmem[start : start + TILE, :] = target_tile(target_ref, count_ref, [place[key] for key in chosen], half)
+            start += TILE
     fetches[0].wait()
     for k in range(GRID_PARTS):
         span = pl.ds(k * part, part)
         fetches[k + 1].wait()
         message_ref[span] = jax.nn.silu(dot(grid_vmem[span], w_vmem[...])).astype(jnp.bfloat16)
-    message = message_ref[...]
     row = lax.broadcasted_iota(jnp.int32, (cap, rows), 1)
+    picks = {
+        key: jnp.where(row == by_slot[:, m : m + 1], 1.0, 0.0).astype(jnp.bfloat16) for m, key in enumerate(keys)
+    }
     sends = []
-    for n in range(6):
-        picks = jnp.concatenate(
-            [
-                jnp.where(row == by_slot[:, m : m + 1], 1.0, 0.0).astype(jnp.bfloat16)
-                for m in range(n * pair_count, (n + 1) * pair_count)
-            ],
-            axis=0,
-        )
-        out_vmem[n, 0:slots, :] = dot(picks, message).astype(jnp.bfloat16)
-        send = pltpu.make_async_copy(out_vmem.at[n], out_refs[n], out_sems.at[n])
+    for n, parts in enumerate(runs):
+        start = 0
+        for chosen, lanes in parts:
+            taken = dot(jnp.concatenate([picks[key] for key in chosen], axis=0), message_ref[:, lanes])
+            out_vmems[n][start : start + len(chosen) * cap, :] = taken.astype(jnp.bfloat16)
+            start += len(chosen) * cap + TILE
+        send = pltpu.make_async_copy(out_vmems[n], out_refs[n], out_sems.at[n])
         send.start()
         sends.append(send)
     for send in sends:
         send.wait()
 
 
-def node_sums(row_refs, pair_count, nodes):
-    cap = (row_refs[0].shape[0] - TILE) // pair_count
+def node_sums(arrays, nodes):
+    count = arrays[0][2]
+    cap = CAP
     node = lax.broadcasted_iota(jnp.int32, (nodes, cap), 0)
-    targets = [r[pair_count * cap :, :].astype(jnp.float32)[0:1].astype(jnp.int32) for r in row_refs]
-    for p in range(pair_count):
-        span = slice(p * cap, (p + 1) * cap)
-        hits = [jnp.where(node == t[:, span], 1.0, 0.0).astype(jnp.bfloat16) for t in targets]
-        yield p, dot(jnp.concatenate(hits, axis=1), jnp.concatenate([r[span, :] for r in row_refs], axis=0))
-
-
-def early_kernel(pair_count, w_ref, own_ref, other_ref, query_ref, key_ref, value_ref, sum_ref):
+    targets = [
+        ref[start + count * cap : start + count * cap + TILE, 0:cap].astype(jnp.float32).astype(jnp.int32)
+        for ref, start, _ in arrays
+    ]
+    for n in range(count):
+        hits = [jnp.where(node == t[n : n + 1], 1.0, 0.0).astype(jnp.bfloat16) for t in targets]
+        rows = [ref[start + n * cap : start + (n + 1) * cap, :] for ref, start, _ in arrays]
+        yield n, dot(jnp.concatenate(hits, axis=1), jnp.concatenate(rows, axis=0))
+
+
+def early_kernel(pair_count, w_ref, own_ref, other_ref, query_ref, key_ref, value_ref, left_ref, right_ref):
     width = w_ref.shape[0]
     head_dim = width // HEADS
     span = 3 * LANES
@@ -114,26 +144,28 @@
         for g in range(width // LANES):
             part = dot_t(pick, w_ref[:, g * span : (g + 1) * span])
             out_ref[g * LANES : (g + 1) * LANES, :] = part.astype(jnp.bfloat16)
-    for p, total in node_sums((own_ref, other_ref), pair_count, sum_ref.shape[1]):
-        sum_ref[p] = total
-
-
-def reduce_kernel(pair_count, *refs):
-    row_refs, sum_ref, (own_ref, *part_refs) = refs[:4], refs[4], refs[5:]
-    for p, total in node_sums(row_refs, pair_count, own_ref.shape[0]):
-        total = total + sum_ref[p]
-        if p:
-            part_refs[p - 1][...] = total.astype(jnp.bfloat16)
-        else:
-            own_ref[...] = total
-
-
-def merge_kernel(own_ref, *refs):
-    part_refs, (mesh_ref, w_ref, gain_ref, state_ref, normed_ref) = refs[:-5], refs[-5:]
-    total = own_ref[...]
-    for part_ref in part_refs:
-        total = total + part_ref[...].astype(jnp.float32)
-    state = mesh_ref[...].astype(jnp.float32) + dot(total.astype(jnp.bfloat16), w_ref[...])
+    start = 0
+    for sum_ref in (left_ref, right_ref):
+        count, nodes, _ = sum_ref.shape
+        for n, total in node_sums([(own_ref, start, count), (other_ref, start, count)], nodes):
+            sum_ref[n] = total
+        start += count * CAP + TILE
+
+
+def sums_kernel(array_count, kept, *refs):
+    row_refs, early_ref, out_refs = refs[:array_count], refs[array_count], refs[array_count + 1 :]
+    count, nodes, _ = early_ref.shape
+    for n, total in node_sums([(r, 0, count) for r in row_refs], nodes):
+        total = total + early_ref[n]
+        out_refs[n][...] = total if n == kept else total.astype(jnp.bfloat16)
+
+
+def merge_kernel(*refs):
+    *part_refs, right_ref, even_ref, odd_ref, mesh_ref, w_ref, gain_ref, state_ref, normed_ref = refs
+    left = functools.reduce(jnp.add, [r[...].astype(jnp.float32) for r in part_refs])
+    right = right_ref[...] + even_ref[...].astype(jnp.float32) + odd_ref[...].astype(jnp.float32)
+    total = jnp.concatenate([left, right], axis=1).astype(jnp.bfloat16)
+    state = mesh_ref[...].astype(jnp.float32) + dot(total, w_ref[...])
     state_ref[...] = state
     normed_ref[...] = layer_norm(state, gain_ref[...]).astype(jnp.bfloat16)
 
@@ -321,27 +353,31 @@
     cap = edge_source.shape[-1]
     head_dim = width // HEADS
     pairs = inners // 2
-    slots = pairs * cap
+    half = width // 2
     f32, bf16, i32 = jnp.float32, jnp.bfloat16, jnp.int32
-
-    even, even_other, odd, odd_other, own, own_other = pl.pallas_call(
+    edges = (edge_source, edge_target, jnp.transpose(edge_count, (0, 2, 1, 3)))
+
+    def rows_of(*blocks):
+        return jax.ShapeDtypeStruct((sum(n * cap + TILE for n in blocks), half), bf16)
+
+    outgoing = [rows_of(pairs)] * 4 + [rows_of(3)] * (2 * pairs - 2) + [rows_of(pairs, 3)] * 2
+    even, even_other, odd, odd_other, *cross, here, here_other = pl.pallas_call(
         functools.partial(message_kernel, pairs),
-        out_shape=[jax.ShapeDtypeStruct((slots + TILE, width), bf16)] * 6,
+        out_shape=outgoing,
         in_specs=[ANY] * 2 + [VMEM] * 2 + [SMEM],
-        out_specs=[ANY] * 6,
-        scratch_shapes=[
+        out_specs=[ANY] * len(outgoing),
+        scratch_shapes=[pltpu.VMEM(a.shape, bf16) for a in outgoing]
+        + [
             pltpu.VMEM(grid_rows.shape, bf16),
             pltpu.VMEM(w_message.shape, bf16),
             pltpu.VMEM((grid_dev, width), bf16),
-            pltpu.VMEM((6, slots + TILE, width), bf16),
             pltpu.SemaphoreType.DMA((GRID_PARTS + 1,)),
-            pltpu.SemaphoreType.DMA((6,)),
+            pltpu.SemaphoreType.DMA((len(outgoing),)),
         ],
         compiler_params=params(MOST),
-        cost_estimate=cost(2 * grid_dev * width * (width + 6 * slots), 4 << 20),
+        cost_estimate=cost(2 * grid_dev * width * (width + 3 * inners * cap), 4 << 20),
         name="messages",
-    )(grid_rows, w_message, edge_source, edge_target, jnp.transpose(edge_count, (0, 2, 1, 3)))
-
+    )(grid_rows, w_message, *edges)
     beside = [(g, g ^ 1) for g in range(devices)]
 
     def bands_trade(odd_pairs):
@@ -352,25 +388,31 @@
             route.append((g, t * inners + g % inners if 0 <= t < bands else g ^ 1))
         return route
 
+    def chip_trade(p):
+        return [(g, g ^ (2 * p)) for g in range(devices)]
+
     even_other = lax.ppermute(even_other, NODES, beside)
+    cross_other = [lax.ppermute(c, NODES, beside) for c in cross[1::2]]
     odd_other = lax.ppermute(odd_other, NODES, beside)
-    own_other = lax.ppermute(own_other, NODES, beside)
+    cross = [lax.ppermute(c, NODES, chip_trade(p + 1)) for p, c in enumerate(cross[0::2])]
     even = lax.ppermute(even, NODES, bands_trade(0))
     odd = lax.ppermute(odd, NODES, bands_trade(1))
+    cross_other = [lax.ppermute(c, NODES, chip_trade(p + 1)) for p, c in enumerate(cross_other)]
     even_other = lax.ppermute(even_other, NODES, bands_trade(0))
     odd_other = lax.ppermute(odd_other, NODES, bands_trade(1))
-
-    w_qkv, window, own = lax.optimization_barrier((w_qkv, window, own))
-    w_query, w_key, w_value, early = pl.pallas_call(
+    here_other = lax.ppermute(here_other, NODES, beside)
+
+    w_qkv, window, here = lax.optimization_barrier((w_qkv, window, here))
+    w_query, w_key, w_value, early_left, early_right = pl.pallas_call(
         functools.partial(early_kernel, pairs),
         out_shape=[jax.ShapeDtypeStruct((width, width), bf16)] * 3
-        + [jax.ShapeDtypeStruct((pairs, nodes, width), f32)],
+        + [jax.ShapeDtypeStruct((n, nodes, half), f32) for n in (pairs, 3)],
         in_specs=[VMEM] * 3,
-        out_specs=[VMEM] * 4,
-        compiler_params=params(16),
+        out_specs=[VMEM] * 5,
+        compiler_params=params(24),
         cost_estimate=cost(1 << 28, 4 << 20),
         name="early",
-    )(w_qkv, own, own_other)
+    )(w_qkv, here, here_other)
     head = jnp.arange(HEADS, dtype=i32)
     ahead = (window[None, :] > window[:, None]) | (
         (window[None, :] == window[:, None]) & (head[None, :] < head[:, None])
@@ -378,19 +420,23 @@
     rank = jnp.sum(ahead.astype(i32), axis=1)
     order = jnp.sum(jnp.where(rank[None, :] == head[:, None], head[None, :], 0), axis=1).astype(i32)
 
-    sums = pl.pallas_call(
-        functools.partial(reduce_kernel, pairs),
-        out_shape=[jax.ShapeDtypeStruct((nodes, width), f32)]
-        + [jax.ShapeDtypeStruct((nodes, width), bf16)] * (pairs - 1),
-        in_specs=[VMEM] * 5,
-        out_specs=[VMEM] * pairs,
-        compiler_params=params(24),
-        cost_estimate=cost(2 * nodes * width * 4 * slots, 3 << 20),
-        name="reduce",
-    )(even, even_other, odd, odd_other, early)
-    parts = [
-        lax.ppermute(sums[p], NODES, [(g, g ^ (2 * p)) for g in range(devices)]) for p in range(1, pairs)
-    ]
+    def sums(arrays, early, kept, name):
+        count = early.shape[0]
+        return pl.pallas_call(
+            functools.partial(sums_kernel, len(arrays), kept),
+            out_shape=[jax.ShapeDtypeStruct((nodes, half), f32 if n == kept else bf16) for n in range(count)],
+            in_specs=[VMEM] * (len(arrays) + 1),
+            out_specs=[VMEM] * count,
+            compiler_params=params(24),
+            cost_estimate=cost(2 * nodes * half * len(arrays) * count * cap, 2 << 20),
+            name=name,
+        )(*arrays, early)
+
+    left, *parts = sums([even, even_other, odd, odd_other], early_left, 0, "left")
+    parts = [lax.ppermute(part, NODES, chip_trade(p + 1)) for p, part in enumerate(parts)]
+    to_even, to_odd, right = sums([*cross, *cross_other], early_right, 2, "right")
+    from_even = lax.ppermute(to_even, NODES, bands_trade(0))
+    from_odd = lax.ppermute(to_odd, NODES, bands_trade(1))
 
     state, normed = pl.pallas_call(
         merge_kernel,
@@ -398,12 +444,12 @@
             jax.ShapeDtypeStruct((nodes, width), f32),
             jax.ShapeDtypeStruct((nodes, width), bf16),
         ],
-        in_specs=[VMEM] * (pairs + 3),
+        in_specs=[VMEM] * (pairs + 6),
         out_specs=[VMEM] * 2,
         compiler_params=params(24),
         cost_estimate=cost(2 * nodes * width * width, 2 << 20),
         name="merge",
-    )(sums[0], *parts, mesh_rows, w_merge, gain_attn.reshape(1, width))
+    )(left, *parts, right, from_even, from_odd, mesh_rows, w_merge, gain_attn.reshape(1, width))
 
     def chips_trade(odd_pairs):
         route = []

time: 56.3 us -> 52.5 us (0.933)
  waiting for transfers between devices: 23.7 us -> 13.1 us
  starting transfers between devices: 10 us -> 16.3 us
    ppermute x1, waiting for transfers between devices: 4.84 us -> 0.01 us  [local(): even_other = lax.ppermute(even_other, NODES, bands_trade(0))]
    ppermute x2 -> x7, starting transfers between devices: 0.75 us -> 5.26 us  [the longest x1 2.58 us: local(): from_odd = lax.ppermute(to_odd, NODES, bands_trade(1))]
    ppermute x2 -> x7, waiting for transfers between devices: 6.73 us -> 3.94 us  [the longest x1 1.52 us: local(): from_even = lax.ppermute(to_even, NODES, bands_trade(0))]
    ppermute x1, starting transfers between devices: 0.86 us -> 2.42 us  [local(): odd_other = lax.ppermute(odd_other, NODES, bands_trade(1))]
    ppermute x1, waiting for transfers between devices: 2.2 us -> 0.86 us  [local(): even = lax.ppermute(even, NODES, bands_trade(0))]
    ppermute x1, waiting for transfers between devices: 0.01 us -> 1.22 us  [local(): even_other = lax.ppermute(even_other, NODES, beside)]
    ppermute x1, starting transfers between devices: 2.43 us -> 1.3 us  [local(): odd = lax.ppermute(odd, NODES, bands_trade(1))]
    ppermute x1, waiting for transfers between devices: 1.13 us -> 0.01 us  [local(): odd = lax.ppermute(odd, NODES, bands_trade(1))]
  transfers between devices with their start and end apart: 13 -> 18, of which waited for: 8 -> 9; matrix products, arithmetic and copies ran while one was open for 1% -> 1% of each run, Pallas kernels for 12% -> 14%
where the time goes in v3:
time: 52.5 us; the launch traced here: 51.6 us
  Pallas kernels  20.7 us (39%)
  starting transfers between devices  16.3 us (31%)
  waiting for transfers between devices  13.1 us (25%)
  local copies, waits for them, and re-layouts  1.02 us (2%)
    pallas_call x1, Pallas kernels, local(): pl.pallas_call(far_kernel, out_shape=jax.ShapeDtypeStruct((nodes, width),...  7.03 us
    pallas_call x1, Pallas kernels, local(): pl.pallas_call(functools.partial(message_kernel, pairs), out_shape=outgoi...  5.86 us
    ppermute x1, waiting for transfers between devices, local(): even = lax.ppermute(normed, NODES, chips_trade(0))  5.37 us
    pallas_call x1, Pallas kernels, local(): pl.pallas_call(near_kernel, out_shape=[jax.ShapeDtypeStruct((HEADS, LANES...  5.21 us
    ppermute x1, starting transfers between devices, local(): side = lax.ppermute(normed, NODES, beside)  2.69 us
    ppermute x1, starting transfers between devices, local(): odd = lax.ppermute(normed, NODES, chips_trade(1))  2.67 us
    ppermute x1, starting transfers between devices, local(): from_odd = lax.ppermute(to_odd, NODES, bands_trade(1))  2.58 us
    ppermute x1, starting transfers between devices, local(): odd_other = lax.ppermute(odd_other, NODES, bands_trade(1))  2.42 us
  transfers between devices with their start and end apart: 18, of which 9 were waited for; matrix products, arithmetic and copies ran while one was open for 1% of the time, Pallas kernels for 14%

profile of v3, /device:TPU:15, one launch (start us, length us, event | category | flops | bytes accessed | tf_op | source)
XLA Modules:
  0.0 51.6 jit_solution(15010837011197479489)
XLA Ops:
  0.0 5.9 %messages.1 = (bf16[272,256]{1,0:T(8,128)(2,1)}, bf16[272,256]{1,0:T(8,128)(2,1)}, bf16[272,256]{1,0:T(8,128)(2,1)}, bf16[272,256]{1,0:T(8,128)(2,1)}, bf16[400,...) custom-call(bf16[1024,512]{1,0:T(8,128)(2,1)} %grid_ref.1, ...), custom_call_target="tpu_custom_call" | custom-call | flops 2147483648 | bytes 4194304 | tf_op jit(solution)/shard_map/messages/pallas_call | solution.py:364
  5.9 0.7 %collective-permute-start.6 = (bf16[672,256]{1,0:T(8,128)(2,1)}, bf16[672,256]{1,0:T(8,128)(2,1)S(1)}, u32[]{:S(2)}, u32[]{:S(2)}) collective-permute-start(bf16[672,256]{1,0:T(8,128)(2,1)} %get-tuple-element.42), channel_id=1, source_target_pairs={{0,1},{1,0},{2,3},{3,2},{4,5},{5,4},{6,7},{7,6},{8,9},{9,8},{10,11... | collective-permute-start | bytes 1032200 | tf_op jit(solution)/shard_map/ppermute | solution.py:403
  6.7 0.4 collective-permute-start.1
  7.4 1.2 %collective-permute-done.1 = bf16[272,256]{1,0:T(8,128)(2,1)S(1)} collective-permute-done((bf16[272,256]{1,0:T(8,128)(2,1)}, bf16[272,256]{1,0:T(8,128)(2,1)S(1)}, u32[]{:S(2)}, u32[]{:S(2)}) %collective-permute-start.1) | collective-permute-done | bytes 139296 | tf_op jit(solution)/shard_map/ppermute | solution.py:394
  8.9 1.2 %collective-permute-start.10 = (bf16[400,256]{1,0:T(8,128)(2,1)S(1)}, bf16[400,256]{1,0:T(8,128)(2,1)S(1)}, u32[]{:S(2)}, u32[]{:S(2)}) collective-permute-start(bf16[400,256]{1,0:T(8,128)(2,1)S(1)} %collective-permute-done.9), channel_id=1, source_target_pairs={{0,2},{1,3},{2,0},{3,1},{4,6},{5,7},{6,4},{7,5},{8,10},{9,11},{10,... | collective-permute-start | bytes 614408 | tf_op jit(solution)/shard_map/ppermute | solution.py:400
  10.1 1.3 %collective-permute-start.3 = (bf16[272,256]{1,0:T(8,128)(2,1)}, bf16[272,256]{1,0:T(8,128)(2,1)S(1)}, u32[]{:S(2)}, u32[]{:S(2)}) collective-permute-start(bf16[272,256]{1,0:T(8,128)(2,1)} %get-tuple-element.37), channel_id=1, source_target_pairs={{0,1},{1,0},{2,3},{3,2},{4,8},{5,9},{6,10},{7,11},{8,4},{9,5},{10,... | collective-permute-start | bytes 417800 | tf_op jit(solution)/shard_map/ppermute | solution.py:399
  11.4 0.9 %collective-permute-done.refs_0_ = bf16[272,256]{1,0:T(8,128)(2,1)S(1)} collective-permute-done((bf16[272,256]{1,0:T(8,128)(2,1)}, bf16[272,256]{1,0:T(8,128)(2,1)S(1)}, u32[]{:S(2)}, u32[]{:S(2)}) %collective-permute-start) | collective-permute-done | bytes 139296 | tf_op jit(solution)/shard_map/ppermute | solution.py:398
  12.4 2.4 %collective-permute-start.5 = (bf16[272,256]{1,0:T(8,128)(2,1)S(1)}, bf16[272,256]{1,0:T(8,128)(2,1)S(1)}, u32[]{:S(2)}, u32[]{:S(2)}) collective-permute-start(bf16[272,256]{1,0:T(8,128)(2,1)S(1)} %collective-permute-done.4), channel_id=1, source_target_pairs={{0,1},{1,0},{2,3},{3,2},{4,8},{5,9},{6,10},{7,11},{8,4},{9,5},{10,... | collective-permute-start | bytes 417800 | tf_op jit(solution)/shard_map/ppermute | solution.py:402
  14.8 1.0 %copy-done.2 = bf16[672,256]{1,0:T(8,128)(2,1)S(1)} copy-done((bf16[672,256]{1,0:T(8,128)(2,1)S(1)}, bf16[672,256]{1,0:T(8,128)(2,1)}, u32[]{:S(2)}) %copy-start.2) | copy-done | bytes 344088
  15.8 1.6 %early.1 = (bf16[512,512]{1,0:T(8,128)(2,1)S(1)}, bf16[512,512]{1,0:T(8,128)(2,1)S(1)}, bf16[512,512]{1,0:T(8,128)(2,1)S(1)}, f32[2,256,256]{2,1,0:T(8,128)S(1)}, f32[3,256,256]{2,1,0:T(8,128)S(1)}) custom-call(bf16[512,1536]{1,0:T(8,128)(2,1)S(1)} %copy-done, bf16[672,256]{1,0:T(8,128)(2,1)S(1)} %copy-done.2, ...), custom_call_target="tpu_custom_call" | custom-call | flops 268435456 | bytes 4194304 | tf_op jit(solution)/shard_map/early/pallas_call | solution.py:406
  17.9 0.3 collective-permute-start.7
  18.2 1.3 %collective-permute-done.10.refs_1_ = bf16[400,256]{1,0:T(8,128)(2,1)S(1)} collective-permute-done((bf16[400,256]{1,0:T(8,128)(2,1)S(1)}, bf16[400,256]{1,0:T(8,128)(2,1)S(1)}, u32[]{:S(2)}, u32[]{:S(2)}) %collective-permute-start.10) | collective-permute-done | bytes 204832 | tf_op jit(solution)/shard_map/ppermute | solution.py:400
  19.9 2.6 %collective-permute-start.12 = (bf16[256,256]{1,0:T(8,128)(2,1)S(1)}, bf16[256,256]{1,0:T(8,128)(2,1)S(1)}, u32[]{:S(2)}, u32[]{:S(2)}) collective-permute-start(bf16[256,256]{1,0:T(8,128)(2,1)S(1)} %get-tuple-element.51), channel_id=1, source_target_pairs={{0,1},{1,0},{2,3},{3,2},{4,8},{5,9},{6,10},{7,11},{8,4},{9,5},{10,... | collective-permute-start | bytes 393224 | tf_op jit(solution)/shard_map/ppermute | solution.py:439
  22.4 1.5 %collective-permute-done.11.refs_3_ = bf16[256,256]{1,0:T(8,128)(2,1)S(1)} collective-permute-done((bf16[256,256]{1,0:T(8,128)(2,1)S(1)}, bf16[256,256]{1,0:T(8,128)(2,1)S(1)}, u32[]{:S(2)}, u32[]{:S(2)}) %collective-permute-start.11) | collective-permute-done | bytes 131104 | tf_op jit(solution)/shard_map/ppermute | solution.py:438
  24.0 1.1 %collective-permute-done.12.refs_4_ = bf16[256,256]{1,0:T(8,128)(2,1)S(1)} collective-permute-done((bf16[256,256]{1,0:T(8,128)(2,1)S(1)}, bf16[256,256]{1,0:T(8,128)(2,1)S(1)}, u32[]{:S(2)}, u32[]{:S(2)}) %collective-permute-start.12) | collective-permute-done | bytes 131104 | tf_op jit(solution)/shard_map/ppermute | solution.py:439
  25.1 0.5 merge.1
  25.6 2.7 %collective-permute-start.15 = (bf16[256,512]{1,0:T(8,128)(2,1)S(1)}, bf16[256,512]{1,0:T(8,128)(2,1)S(1)}, u32[]{:S(2)}, u32[]{:S(2)}) collective-permute-start(bf16[256,512]{1,0:T(8,128)(2,1)S(1)} %get-tuple-element.52.own_ref), channel_id=1, source_target_pairs={{0,1},{1,0},{2,3},{3,2},{4,5},{5,4},{6,7},{7,6},{8,9},{9,8},{10,11... | collective-permute-start | bytes 786440 | tf_op jit(solution)/shard_map/ppermute | solution.py:461
  28.9 2.7 %collective-permute-start.14 = (bf16[256,512]{1,0:T(8,128)(2,1)S(1)}, bf16[256,512]{1,0:T(8,128)(2,1)S(1)}, u32[]{:S(2)}, u32[]{:S(2)}) collective-permute-start(bf16[256,512]{1,0:T(8,128)(2,1)S(1)} %get-tuple-element.52.own_ref), channel_id=1, source_target_pairs={{0,1},{1,0},{2,4},{3,5},{4,2},{5,3},{6,8},{7,9},{8,6},{9,7},{10,12... | collective-permute-start | bytes 786440 | tf_op jit(solution)/shard_map/ppermute | solution.py:463
  31.6 5.2 %near.1 = (bf16[16,128,256]{2,1,0:T(8,128)(2,1)S(1)}, f32[16,48,256]{2,1,0:T(8,128)S(1)}, f32[16,8,256]{2,1,0:T(8,128)S(1)}) custom-call(bf16[256,512]{1,0:T(8,128)(2,1)S(1)} %get-tuple-element.52.own_ref, bf16[256,512]{1,0:T(8,128)(2,1)S(1)} %collective-permute-done.15.side_ref, bf16[512,512]{1,0:T(8,128)(2,1)S(1)} %get-tuple-element.53.wq_ref, ...), custom_call_target="tpu_custom_call" | custom-call | flops 8589934592 | bytes 4194304 | tf_op jit(solution)/shard_map/near/pallas_call | solution.py:466
  36.8 5.4 %collective-permute-done.13.even_ref = bf16[256,512]{1,0:T(8,128)(2,1)S(1)} collective-permute-done((bf16[256,512]{1,0:T(8,128)(2,1)S(1)}, bf16[256,512]{1,0:T(8,128)(2,1)S(1)}, u32[]{:S(2)}, u32[]{:S(2)}) %collective-permute-start.13) | collective-permute-done | bytes 262176 | tf_op jit(solution)/shard_map/ppermute | solution.py:462
  42.2 0.8 %collective-permute-start.16 = (bf16[256,512]{1,0:T(8,128)(2,1)S(1)}, bf16[256,512]{1,0:T(8,128)(2,1)S(1)}, u32[]{:S(2)}, u32[]{:S(2)}) collective-permute-start(bf16[256,512]{1,0:T(8,128)(2,1)S(1)} %collective-permute-done.13.even_ref), channel_id=1, source_target_pairs={{0,1},{1,0},{2,3},{3,2},{4,5},{5,4},{6,7},{7,6},{8,9},{9,8},{10,11... | collective-permute-start | bytes 786440 | tf_op jit(solution)/shard_map/ppermute | solution.py:486
  43.0 1.2 %collective-permute-done.16.first_ref = bf16[256,512]{1,0:T(8,128)(2,1)S(1)} collective-permute-done((bf16[256,512]{1,0:T(8,128)(2,1)S(1)}, bf16[256,512]{1,0:T(8,128)(2,1)S(1)}, u32[]{:S(2)}, u32[]{:S(2)}) %collective-permute-start.16) | collective-permute-done | bytes 262176 | tf_op jit(solution)/shard_map/ppermute | solution.py:486
  44.1 0.4 collective-permute-done.17.second_ref
  44.5 7.0 %far.1 = bf16[256,512]{1,0:T(8,128)(2,1)} custom-call(bf16[256,512]{1,0:T(8,128)(2,1)S(1)} %collective-permute-done.16.first_ref, bf16[256,512]{1,0:T(8,128)(2,1)S(1)} %collective-permute-done.17.second_ref, bf16[256,512]{1,0:T(8,128)(2,1)S(1)} %collective-permute-done.13.even_ref, bf16[256,512]{1,0:T(8,128)(2,1)S(1)} %collective-permute-done.14.odd_ref, ...), custom_call_target="tpu_custom_call" | custom-call | flops 8589934592 | bytes 8388608 | tf_op jit(solution)/shard_map/far/pallas_call | solution.py:488
  (41 shorter events, 2.2 us)
Async XLA Ops:
  0.0 14.8 %copy-start = (bf16[512,1536]{1,0:T(8,128)(2,1)S(1)}, bf16[512,1536]{1,0:T(8,128)(2,1)}, u32[]{:S(2)}) copy-start(bf16[512,1536]{1,0:T(8,128)(2,1)} %w_ref.2) | copy-start | bytes 4718596
  5.9 6.5 %collective-permute-start.6 = (bf16[672,256]{1,0:T(8,128)(2,1)}, bf16[672,256]{1,0:T(8,128)(2,1)S(1)}, u32[]{:S(2)}, u32[]{:S(2)}) collective-permute-start(bf16[672,256]{1,0:T(8,128)(2,1)} %get-tuple-element.42), channel_id=1, source_target_pairs={{0,1},{1,0},{2,3},{3,2},{4,5},{5,4},{6,7},{7,6},{8,9},{9,8},{10,11... | collective-permute-start | bytes 1032200 | tf_op jit(solution)/shard_map/ppermute | solution.py:403
  6.6 2.2 %collective-permute-start.9 = (bf16[400,256]{1,0:T(8,128)(2,1)}, bf16[400,256]{1,0:T(8,128)(2,1)S(1)}, u32[]{:S(2)}, u32[]{:S(2)}) collective-permute-start(bf16[400,256]{1,0:T(8,128)(2,1)} %get-tuple-element.47), channel_id=1, source_target_pairs={{0,1},{1,0},{2,3},{3,2},{4,5},{5,4},{6,7},{7,6},{8,9},{9,8},{10,11... | collective-permute-start | bytes 614408 | tf_op jit(solution)/shard_map/ppermute | solution.py:395
  6.7 1.9 %collective-permute-start.1 = (bf16[272,256]{1,0:T(8,128)(2,1)}, bf16[272,256]{1,0:T(8,128)(2,1)S(1)}, u32[]{:S(2)}, u32[]{:S(2)}) collective-permute-start(bf16[272,256]{1,0:T(8,128)(2,1)} %get-tuple-element.36), channel_id=1, source_target_pairs={{0,1},{1,0},{2,3},{3,2},{4,5},{5,4},{6,7},{7,6},{8,9},{9,8},{10,11... | collective-permute-start | bytes 417800 | tf_op jit(solution)/shard_map/ppermute | solution.py:394
  7.1 2.9 %collective-permute-start.4 = (bf16[272,256]{1,0:T(8,128)(2,1)}, bf16[272,256]{1,0:T(8,128)(2,1)S(1)}, u32[]{:S(2)}, u32[]{:S(2)}) collective-permute-start(bf16[272,256]{1,0:T(8,128)(2,1)} %get-tuple-element.38), channel_id=1, source_target_pairs={{0,1},{1,0},{2,3},{3,2},{4,5},{5,4},{6,7},{7,6},{8,9},{9,8},{10,11... | collective-permute-start | bytes 417800 | tf_op jit(solution)/shard_map/ppermute | solution.py:396
  7.2 5.0 %collective-permute-start = (bf16[272,256]{1,0:T(8,128)(2,1)}, bf16[272,256]{1,0:T(8,128)(2,1)S(1)}, u32[]{:S(2)}, u32[]{:S(2)}) collective-permute-start(bf16[272,256]{1,0:T(8,128)(2,1)} %get-tuple-element.35), channel_id=1, source_target_pairs={{0,4},{1,5},{2,6},{3,7},{4,0},{5,1},{6,2},{7,3},{8,12},{9,13},{10,... | collective-permute-start | bytes 417800 | tf_op jit(solution)/shard_map/ppermute | solution.py:398
  8.6 9.6 %collective-permute-start.8 = (bf16[400,256]{1,0:T(8,128)(2,1)}, bf16[400,256]{1,0:T(8,128)(2,1)S(1)}, u32[]{:S(2)}, u32[]{:S(2)}) collective-permute-start(bf16[400,256]{1,0:T(8,128)(2,1)} %get-tuple-element.46), channel_id=1, source_target_pairs={{0,2},{1,3},{2,0},{3,1},{4,6},{5,7},{6,4},{7,5},{8,10},{9,11},{10,... | collective-permute-start | bytes 614408 | tf_op jit(solution)/shard_map/ppermute | solution.py:397
  8.9 10.6 %collective-permute-start.10 = (bf16[400,256]{1,0:T(8,128)(2,1)S(1)}, bf16[400,256]{1,0:T(8,128)(2,1)S(1)}, u32[]{:S(2)}, u32[]{:S(2)}) collective-permute-start(bf16[400,256]{1,0:T(8,128)(2,1)S(1)} %collective-permute-done.9), channel_id=1, source_target_pairs={{0,2},{1,3},{2,0},{3,1},{4,6},{5,7},{6,4},{7,5},{8,10},{9,11},{10,... | collective-permute-start | bytes 614408 | tf_op jit(solution)/shard_map/ppermute | solution.py:400
  10.1 7.3 %collective-permute-start.3 = (bf16[272,256]{1,0:T(8,128)(2,1)}, bf16[272,256]{1,0:T(8,128)(2,1)S(1)}, u32[]{:S(2)}, u32[]{:S(2)}) collective-permute-start(bf16[272,256]{1,0:T(8,128)(2,1)} %get-tuple-element.37), channel_id=1, source_target_pairs={{0,1},{1,0},{2,3},{3,2},{4,8},{5,9},{6,10},{7,11},{8,4},{9,5},{10,... | collective-permute-start | bytes 417800 | tf_op jit(solution)/shard_map/ppermute | solution.py:399
  12.2 5.2 %collective-permute-start.2 = (bf16[272,256]{1,0:T(8,128)(2,1)S(1)}, bf16[272,256]{1,0:T(8,128)(2,1)S(1)}, u32[]{:S(2)}, u32[]{:S(2)}) collective-permute-start(bf16[272,256]{1,0:T(8,128)(2,1)S(1)} %collective-permute-done.1), channel_id=1, source_target_pairs={{0,4},{1,5},{2,6},{3,7},{4,0},{5,1},{6,2},{7,3},{8,12},{9,13},{10,... | collective-permute-start | bytes 417800 | tf_op jit(solution)/shard_map/ppermute | solution.py:401
  12.4 5.2 %collective-permute-start.5 = (bf16[272,256]{1,0:T(8,128)(2,1)S(1)}, bf16[272,256]{1,0:T(8,128)(2,1)S(1)}, u32[]{:S(2)}, u32[]{:S(2)}) collective-permute-start(bf16[272,256]{1,0:T(8,128)(2,1)S(1)} %collective-permute-done.4), channel_id=1, source_target_pairs={{0,1},{1,0},{2,3},{3,2},{4,8},{5,9},{6,10},{7,11},{8,4},{9,5},{10,... | collective-permute-start | bytes 417800 | tf_op jit(solution)/shard_map/ppermute | solution.py:402
  17.4 10.9 %copy-start.9 = (s32[16]{0:T(128)S(1)}, s32[16]{0:T(128)}, u32[]{:S(2)}) copy-start(s32[16]{0:T(128)} %window_ref.1) | copy-start | bytes 196
  17.9 4.6 %collective-permute-start.7 = (bf16[256,256]{1,0:T(8,128)(2,1)S(1)}, bf16[256,256]{1,0:T(8,128)(2,1)S(1)}, u32[]{:S(2)}, u32[]{:S(2)}) collective-permute-start(bf16[256,256]{1,0:T(8,128)(2,1)S(1)} %get-tuple-element.45), channel_id=1, source_target_pairs={{0,2},{1,3},{2,0},{3,1},{4,6},{5,7},{6,4},{7,5},{8,10},{9,11},{10,... | collective-permute-start | bytes 393224 | tf_op jit(solution)/shard_map/ppermute | solution.py:436
  19.8 4.2 %collective-permute-start.11 = (bf16[256,256]{1,0:T(8,128)(2,1)S(1)}, bf16[256,256]{1,0:T(8,128)(2,1)S(1)}, u32[]{:S(2)}, u32[]{:S(2)}) collective-permute-start(bf16[256,256]{1,0:T(8,128)(2,1)S(1)} %get-tuple-element.50), channel_id=1, source_target_pairs={{0,4},{1,5},{2,6},{3,7},{4,0},{5,1},{6,2},{7,3},{8,12},{9,13},{10,... | collective-permute-start | bytes 393224 | tf_op jit(solution)/shard_map/ppermute | solution.py:438
  19.9 5.2 %collective-permute-start.12 = (bf16[256,256]{1,0:T(8,128)(2,1)S(1)}, bf16[256,256]{1,0:T(8,128)(2,1)S(1)}, u32[]{:S(2)}, u32[]{:S(2)}) collective-permute-start(bf16[256,256]{1,0:T(8,128)(2,1)S(1)} %get-tuple-element.51), channel_id=1, source_target_pairs={{0,1},{1,0},{2,3},{3,2},{4,8},{5,9},{6,10},{7,11},{8,4},{9,5},{10,... | collective-permute-start | bytes 393224 | tf_op jit(solution)/shard_map/ppermute | solution.py:439
  25.6 6.0 %collective-permute-start.15 = (bf16[256,512]{1,0:T(8,128)(2,1)S(1)}, bf16[256,512]{1,0:T(8,128)(2,1)S(1)}, u32[]{:S(2)}, u32[]{:S(2)}) collective-permute-start(bf16[256,512]{1,0:T(8,128)(2,1)S(1)} %get-tuple-element.52.own_ref), channel_id=1, source_target_pairs={{0,1},{1,0},{2,3},{3,2},{4,5},{5,4},{6,7},{7,6},{8,9},{9,8},{10,11... | collective-permute-start | bytes 786440 | tf_op jit(solution)/shard_map/ppermute | solution.py:461
  28.6 13.6 %collective-permute-start.13 = (bf16[256,512]{1,0:T(8,128)(2,1)S(1)}, bf16[256,512]{1,0:T(8,128)(2,1)S(1)}, u32[]{:S(2)}, u32[]{:S(2)}) collective-permute-start(bf16[256,512]{1,0:T(8,128)(2,1)S(1)} %get-tuple-element.52.own_ref), channel_id=1, source_target_pairs={{0,2},{1,3},{2,0},{3,1},{4,6},{5,7},{6,4},{7,5},{8,10},{9,11},{10,... | collective-permute-start | bytes 786440 | tf_op jit(solution)/shard_map/ppermute | solution.py:462
  28.9 13.3 %collective-permute-start.14 = (bf16[256,512]{1,0:T(8,128)(2,1)S(1)}, bf16[256,512]{1,0:T(8,128)(2,1)S(1)}, u32[]{:S(2)}, u32[]{:S(2)}) collective-permute-start(bf16[256,512]{1,0:T(8,128)(2,1)S(1)} %get-tuple-element.52.own_ref), channel_id=1, source_target_pairs={{0,1},{1,0},{2,4},{3,5},{4,2},{5,3},{6,8},{7,9},{8,6},{9,7},{10,12... | collective-permute-start | bytes 786440 | tf_op jit(solution)/shard_map/ppermute | solution.py:463
  31.6 13.0 %copy-start.5 = (bf16[512,2048]{1,0:T(8,128)(2,1)S(1)}, bf16[512,2048]{1,0:T(8,128)(2,1)}, u32[]{:S(2)}) copy-start(bf16[512,2048]{1,0:T(8,128)(2,1)} %up_ref.1) | copy-start | bytes 6291460
  31.6 13.0 %copy-start.6 = (bf16[2048,512]{1,0:T(8,128)(2,1)S(1)}, bf16[2048,512]{1,0:T(8,128)(2,1)}, u32[]{:S(2)}) copy-start(bf16[2048,512]{1,0:T(8,128)(2,1)} %down_ref.1) | copy-start | bytes 6291460
  31.6 13.0 %copy-start.7 = (bf16[512,512]{1,0:T(8,128)(2,1)S(1)}, bf16[512,512]{1,0:T(8,128)(2,1)}, u32[]{:S(2)}) copy-start(bf16[512,512]{1,0:T(8,128)(2,1)} %w_out_ref.1) | copy-start | bytes 1572868
  31.6 13.0 %copy-start.8 = (f32[512]{0:T(512)S(1)}, f32[512]{0:T(512)}, u32[]{:S(2)}) copy-start(f32[512]{0:T(512)} %param.25) | copy-start | bytes 6148
  42.2 2.0 %collective-permute-start.16 = (bf16[256,512]{1,0:T(8,128)(2,1)S(1)}, bf16[256,512]{1,0:T(8,128)(2,1)S(1)}, u32[]{:S(2)}, u32[]{:S(2)}) collective-permute-start(bf16[256,512]{1,0:T(8,128)(2,1)S(1)} %collective-permute-done.13.even_ref), channel_id=1, source_target_pairs={{0,1},{1,0},{2,3},{3,2},{4,5},{5,4},{6,7},{7,6},{8,9},{9,8},{10,11... | collective-permute-start | bytes 786440 | tf_op jit(solution)/shard_map/ppermute | solution.py:486
  43.0 1.5 %collective-permute-start.17 = (bf16[256,512]{1,0:T(8,128)(2,1)S(1)}, bf16[256,512]{1,0:T(8,128)(2,1)S(1)}, u32[]{:S(2)}, u32[]{:S(2)}) collective-permute-start(bf16[256,512]{1,0:T(8,128)(2,1)S(1)} %collective-permute-done.14.odd_ref), channel_id=1, source_target_pairs={{0,1},{1,0},{2,3},{3,2},{4,5},{5,4},{6,7},{7,6},{8,9},{9,8},{10,11... | collective-permute-start | bytes 786440 | tf_op jit(solution)/shard_map/ppermute | solution.py:487
  (4 other events, 28.8 us)

commit v4 on v3

--- a/solution.py
+++ b/solution.py
@@ -161,13 +161,16 @@
 
 
 def merge_kernel(*refs):
-    *part_refs, right_ref, even_ref, odd_ref, mesh_ref, w_ref, gain_ref, state_ref, normed_ref = refs
+    *part_refs, right_ref, even_ref, odd_ref, mesh_ref, w_ref, gain_ref, state_ref, normed_ref, top_ref, bottom_ref = refs
     left = functools.reduce(jnp.add, [r[...].astype(jnp.float32) for r in part_refs])
     right = right_ref[...] + even_ref[...].astype(jnp.float32) + odd_ref[...].astype(jnp.float32)
     total = jnp.concatenate([left, right], axis=1).astype(jnp.bfloat16)
     state = mesh_ref[...].astype(jnp.float32) + dot(total, w_ref[...])
     state_ref[...] = state
-    normed_ref[...] = layer_norm(state, gain_ref[...]).astype(jnp.bfloat16)
+    normed = layer_norm(state, gain_ref[...]).astype(jnp.bfloat16)
+    normed_ref[...] = normed
+    top_ref[...] = normed[:NEAR]
+    bottom_ref[...] = normed[NEAR:]
 
 
 def project_keys(rows, wk_ref, wv_ref, key_ref, value_ref, start):
@@ -244,77 +247,96 @@
     lax.fori_loop(0, HEADS // GROUP, together, 0)
 
 
-def far_kernel(
-    first_ref, second_ref, even_ref, odd_ref, wk_ref, wv_ref, order_ref, window_ref,
-    query_ref, sums_ref, top_ref, state_ref, w_out_ref, gain_ref, up_ref, down_ref,
-    out_ref,
-    key_ref, value_ref, gap_ref, attended_ref,
+def more_attention(
+    by_pair, other_top, other_bottom, block_top, block_bottom, wk_ref, wv_ref, order_ref, window_ref,
+    query_ref, sums_ref, top_ref, key_ref, value_ref, gap_ref, store,
 ):
-    nodes, width = even_ref.shape
-    head_dim = width // HEADS
+    cap = block_top.shape[0]
+    nodes = 2 * cap
+    head_dim = wv_ref.shape[0] // HEADS
     per_group = LANES // head_dim
     total = lax.axis_size("band") * lax.axis_size("inner")
     me = lax.axis_index("band") * lax.axis_size("inner") + lax.axis_index("inner")
     odd = lax.rem(me, 2)
-    far = 2 - 4 * lax.rem(me // 2, 2)
-    side = 2 * odd - 1
-    first = (1 - odd) * (nodes - NEAR)
-    second = odd * NEAR
+    chip_odd = lax.rem(me // 2, 2)
+    ahead = (1 - 2 * chip_odd) * (1 if by_pair else -1)
+    closer = odd == (ahead + 1) // 2
     scale = head_dim ** (-0.5) / math.log(2.0)
-    absent = 1 << 20
 
     value_ref[:, head_dim:, :] = jnp.ones_like(value_ref[:, head_dim:, :])
-    by_even = odd == lax.rem(me // 2 + 1, 2)
-    beyond = jnp.where(by_even, first_ref[...], second_ref[...])
-    beyond = jnp.where(odd == 0, jnp.concatenate([beyond[NEAR:], beyond[:NEAR]], axis=0), beyond)
-    project_keys(beyond, wk_ref, wv_ref, key_ref, value_ref, 0)
-    project_keys(even_ref[...], wk_ref, wv_ref, key_ref, value_ref, nodes)
-    project_keys(odd_ref[...], wk_ref, wv_ref, key_ref, value_ref, 2 * nodes)
     lag = lax.broadcasted_iota(jnp.int32, (nodes, nodes), 0) - lax.broadcasted_iota(
         jnp.int32, (nodes, nodes), 1
     )
 
     def gap(rows, device, offset):
         inside = (me + device >= 0) & (me + device < total)
-        return jnp.where(inside, jnp.abs(rows + (device * nodes + offset)), absent)
-
-    gap_ref[0:NEAR] = gap(lag[0:NEAR], side, first)
-    gap_ref[NEAR:nodes] = gap(lag[0:NEAR], side, second)
-    gap_ref[nodes : 2 * nodes] = gap(lag, far, 0)
-    gap_ref[2 * nodes : 3 * nodes] = gap(lag, -far, 0)
-
-    def attend(heads, rows):
-        scores = [dot(key_ref[h // per_group, 0:rows, :], query_ref[h]) for h in heads]
+        return jnp.where(inside, jnp.abs(rows + (device * nodes + offset)), 1 << 20)
+
+    @pl.when(closer)
+    def _():
+        top, bottom = other_top[...], other_bottom[...]
+        project_keys(jnp.where(odd == 1, top, bottom), wk_ref, wv_ref, key_ref, value_ref, 0)
+        project_keys(jnp.where(odd == 1, bottom, top), wk_ref, wv_ref, key_ref, value_ref, cap)
+        gap_ref[0:cap] = gap(lag[0:cap], ahead, (1 - odd) * cap)
+        gap_ref[cap:nodes] = gap(lag[0:cap], ahead, odd * cap)
+
+    project_keys(block_top[...], wk_ref, wv_ref, key_ref, value_ref, nodes)
+    project_keys(block_bottom[...], wk_ref, wv_ref, key_ref, value_ref, nodes + cap)
+    gap_ref[nodes : 2 * nodes] = gap(lag, 2 * ahead, 0)
+
+    def attend(heads, start, stop):
+        olds = [top_ref[h, 0:1, :] for h in heads]
+        if start == stop:
+            for h, old in zip(heads, olds):
+                store(h, sums_ref[h], old)
+            return
+        scores = [dot(key_ref[h // per_group, start:stop, :], query_ref[h]) for h in heads]
         scores = [
-            jnp.where(gap_ref[0:rows] <= window_ref[h], x, -1e30) for h, x in zip(heads, scores)
+            jnp.where(gap_ref[start:stop] <= window_ref[h], x, -1e30) for h, x in zip(heads, scores)
         ]
-        olds = [top_ref[h, 0:1, :] for h in heads]
         tops = [jnp.maximum(old, jnp.max(x, axis=0, keepdims=True)) for old, x in zip(olds, scores)]
         expos = [jnp.exp2((x - top) * scale).astype(jnp.bfloat16) for x, top in zip(scores, tops)]
         for h, old, top, expo in zip(heads, olds, tops, expos):
-            sums = sums_ref[h] * jnp.exp2((old - top) * scale) + dot(value_ref[h, :, 0:rows], expo)
-            attended_ref[h] = (sums[0:head_dim] / sums[head_dim : head_dim + 1]).astype(jnp.bfloat16)
+            sums = sums_ref[h] * jnp.exp2((old - top) * scale) + dot(value_ref[h, :, start:stop], expo)
+            store(h, sums, top)
 
     def together(i, carry):
         heads = [order_ref[GROUP * i + k] for k in range(GROUP)]
         widest = functools.reduce(jnp.maximum, [window_ref[h] for h in heads])
-
-        @pl.when(widest <= NEAR)
-        def _():
-            attend(heads, NEAR)
-
-        @pl.when((widest > NEAR) & (widest <= nodes))
-        def _():
-            attend(heads, nodes)
-
-        @pl.when(widest > nodes)
-        def _():
-            attend(heads, 3 * nodes)
-
+        cases = (
+            (closer & (widest <= cap), 0, cap),
+            (closer & (widest > cap) & (widest <= nodes), 0, nodes),
+            (closer & (widest > nodes), 0, 2 * nodes),
+            (jnp.logical_not(closer) & (widest > nodes), nodes, 2 * nodes),
+            (jnp.logical_not(closer) & (widest <= nodes), 0, 0),
+        )
+        for case, start, stop in cases:
+            pl.when(case)(functools.partial(attend, heads, start, stop))
         return carry
 
     lax.fori_loop(0, HEADS // GROUP, together, 0)
 
+
+def mid_kernel(*refs):
+    operands, (sums_out, top_out), scratch = refs[:11], refs[11:13], refs[13:]
+
+    def store(h, sums, top):
+        sums_out[h] = sums
+        top_out[h] = jnp.broadcast_to(top, top_out.shape[1:])
+
+    more_attention(True, *operands, *scratch, store)
+
+
+def far_kernel(*refs):
+    operands, rest = refs[:11], refs[11:]
+    state_ref, w_out_ref, gain_ref, up_ref, down_ref, out_ref, attended_ref, *scratch = rest
+    nodes, width = out_ref.shape
+    head_dim = width // HEADS
+
+    def store(h, sums, top):
+        attended_ref[h] = (sums[0:head_dim] / sums[head_dim : head_dim + 1]).astype(jnp.bfloat16)
+
+    more_attention(False, *operands, *scratch, store)
     attended = attended_ref[...].reshape(width, nodes)
     mixed = lax.dot_general(
         attended, w_out_ref[...], (((0,), (0,)), ((), ())), preferred_element_type=jnp.float32
@@ -438,14 +460,12 @@
     from_even = lax.ppermute(to_even, NODES, bands_trade(0))
     from_odd = lax.ppermute(to_odd, NODES, bands_trade(1))
 
-    state, normed = pl.pallas_call(
+    state, normed, top_rows, bottom_rows = pl.pallas_call(
         merge_kernel,
-        out_shape=[
-            jax.ShapeDtypeStruct((nodes, width), f32),
-            jax.ShapeDtypeStruct((nodes, width), bf16),
-        ],
+        out_shape=[jax.ShapeDtypeStruct((nodes, width), f32)]
+        + [jax.ShapeDtypeStruct((n, width), bf16) for n in (nodes, NEAR, nodes - NEAR)],
         in_specs=[VMEM] * (pairs + 6),
-        out_specs=[VMEM] * 2,
+        out_specs=[VMEM] * 4,
         compiler_params=params(24),
         cost_estimate=cost(2 * nodes * width * width, 2 << 20),
         name="merge",
@@ -459,8 +479,8 @@
         return route
 
     side = lax.ppermute(normed, NODES, beside)
-    even = lax.ppermute(normed, NODES, chips_trade(0))
-    odd = lax.ppermute(normed, NODES, chips_trade(1))
+    pair_top = lax.ppermute(top_rows, NODES, chips_trade(0))
+    pair_bottom = lax.ppermute(bottom_rows, NODES, chips_trade(0))
 
     extra = head_dim + 16
     query, near, top = pl.pallas_call(
@@ -482,25 +502,56 @@
         name="near",
     )(normed, side, w_query, w_key, w_value, order, window)
 
-    even, odd, near, top = lax.optimization_barrier((even, odd, near, top))
-    first = lax.ppermute(even, NODES, beside)
-    second = lax.ppermute(odd, NODES, beside)
+    top_rows, bottom_rows, pair_top, pair_bottom, near, top = lax.optimization_barrier(
+        (top_rows, bottom_rows, pair_top, pair_bottom, near, top)
+    )
+    other_top = lax.ppermute(top_rows, NODES, chips_trade(1))
+    if pairs == 2:
+        route = []
+        for g in range(devices):
+            x = g // 2 % 2
+            t = g + inners * (1 - 2 * x)
+            route.append((g, t if 0 <= t < devices else g ^ 2))
+        other_bottom = lax.ppermute(pair_bottom, NODES, route)
+    else:
+        other_bottom = lax.ppermute(bottom_rows, NODES, chips_trade(1))
+    beside_top = lax.ppermute(pair_top, NODES, beside)
+    beside_bottom = lax.ppermute(pair_bottom, NODES, beside)
+
+    weights = (w_key, w_value, order, window)
+    scratch = [
+        pltpu.VMEM((width // LANES, 2 * nodes, LANES), bf16),
+        pltpu.VMEM((HEADS, extra, 2 * nodes), bf16),
+        pltpu.VMEM((2 * nodes, nodes), i32),
+    ]
+    near, top = pl.pallas_call(
+        mid_kernel,
+        out_shape=[
+            jax.ShapeDtypeStruct((HEADS, extra, nodes), f32),
+            jax.ShapeDtypeStruct((HEADS, 8, nodes), f32),
+        ],
+        in_specs=[VMEM] * 6 + [SMEM] * 2 + [VMEM] * 3,
+        out_specs=[VMEM] * 2,
+        scratch_shapes=scratch,
+        compiler_params=params(32),
+        cost_estimate=cost(4 << 30, 4 << 20),
+        name="mid",
+    )(beside_top, beside_bottom, pair_top, pair_bottom, *weights, query, near, top)
+
+    other_top, other_bottom, near, top = lax.optimization_barrier((other_top, other_bottom, near, top))
+    beside_top = lax.ppermute(other_top, NODES, beside)
+    beside_bottom = lax.ppermute(other_bottom, NODES, beside)
     return pl.pallas_call(
         far_kernel,
         out_shape=jax.ShapeDtypeStruct((nodes, width), bf16),
         in_specs=[VMEM] * 6 + [SMEM] * 2 + [VMEM] * 8,
         out_specs=VMEM,
-        scratch_shapes=[
-            pltpu.VMEM((width // LANES, 3 * nodes, LANES), bf16),
-            pltpu.VMEM((HEADS, extra, 3 * nodes), bf16),
-            pltpu.VMEM((3 * nodes, nodes), i32),
-            pltpu.VMEM((HEADS, head_dim, nodes), bf16),
-        ],
+        scratch_shapes=[pltpu.VMEM((HEADS, head_dim, nodes), bf16)] + scratch,
         compiler_params=params(40),
         cost_estimate=cost(8 << 30, 8 << 20),
         name="far",
     )(
-        first, second, even, odd, w_key, w_value, order, window,
+        beside_top, beside_bottom, other_top, other_bottom, *weights,
         query, near, top, state, w_out, gain_mlp.reshape(1, width), w_up, w_down,
     )
 

time: 52.5 us -> 58.3 us (1.11)
  the two profiles are of different devices: /device:TPU:15 before, /device:TPU:3 now
where the time goes in v4:
time: 58.3 us; the launch traced here: 57.9 us
  starting transfers between devices  25.6 us (44%)
  Pallas kernels  23.7 us (41%)
  waiting for transfers between devices  7.08 us (12%)
  local copies, waits for them, and re-layouts  1.02 us (2%)
    pallas_call x1, Pallas kernels, local(): pl.pallas_call(far_kernel, out_shape=jax.ShapeDtypeStruct((nodes, width),...  7.37 us
    pallas_call x1, Pallas kernels, local(): pl.pallas_call(functools.partial(message_kernel, pairs), out_shape=outgoi...  5.86 us
    pallas_call x1, Pallas kernels, local(): pl.pallas_call(near_kernel, out_shape=[jax.ShapeDtypeStruct((HEADS, LANES...  5.02 us
    ppermute x1, starting transfers between devices, local(): beside_top = lax.ppermute(other_top, NODES, beside)  3.16 us
    ppermute x1, waiting for transfers between devices, local(): even = lax.ppermute(even, NODES, bands_trade(0))  3.01 us
    ppermute x1, starting transfers between devices, local(): other_top = lax.ppermute(top_rows, NODES, chips_trade(1))  2.98 us
    pallas_call x1, Pallas kernels, local(): pl.pallas_call(mid_kernel, out_shape=[jax.ShapeDtypeStruct((HEADS, extra,...  2.85 us
    ppermute x1, starting transfers between devices, local(): odd_other = lax.ppermute(odd_other, NODES, bands_trade(1))  2.39 us
  transfers between devices with their start and end apart: 22, of which 8 were waited for; matrix products, arithmetic and copies ran while one was open for 1% of the time, Pallas kernels for 17%

profile of v4, /device:TPU:3, one launch (start us, length us, event | category | flops | bytes accessed | tf_op | source)
XLA Modules:
  0.0 57.9 jit_solution(5099575706460454292)
XLA Ops:
  0.0 5.9 %messages.1 = (bf16[272,256]{1,0:T(8,128)(2,1)}, bf16[272,256]{1,0:T(8,128)(2,1)}, bf16[272,256]{1,0:T(8,128)(2,1)}, bf16[272,256]{1,0:T(8,128)(2,1)}, bf16[400,...) custom-call(bf16[1024,512]{1,0:T(8,128)(2,1)} %grid_ref.1, ...), custom_call_target="tpu_custom_call" | custom-call | flops 2147483648 | bytes 4194304 | tf_op jit(solution)/shard_map/messages/pallas_call | solution.py:386
  5.9 0.7 %collective-permute-start.6 = (bf16[672,256]{1,0:T(8,128)(2,1)}, bf16[672,256]{1,0:T(8,128)(2,1)S(1)}, u32[]{:S(2)}, u32[]{:S(2)}) collective-permute-start(bf16[672,256]{1,0:T(8,128)(2,1)} %get-tuple-element.51), channel_id=1, source_target_pairs={{0,1},{1,0},{2,3},{3,2},{4,5},{5,4},{6,7},{7,6},{8,9},{9,8},{10,11... | collective-permute-start | bytes 1032200 | tf_op jit(solution)/shard_map/ppermute | solution.py:425
  6.7 1.3 %collective-permute-start = (bf16[272,256]{1,0:T(8,128)(2,1)}, bf16[272,256]{1,0:T(8,128)(2,1)S(1)}, u32[]{:S(2)}, u32[]{:S(2)}) collective-permute-start(bf16[272,256]{1,0:T(8,128)(2,1)} %get-tuple-element.44), channel_id=1, source_target_pairs={{0,4},{1,5},{2,6},{3,7},{4,0},{5,1},{6,2},{7,3},{8,12},{9,13},{10,... | collective-permute-start | bytes 417800 | tf_op jit(solution)/shard_map/ppermute | solution.py:420
  8.0 0.7 %collective-permute-start.1 = (bf16[272,256]{1,0:T(8,128)(2,1)}, bf16[272,256]{1,0:T(8,128)(2,1)S(1)}, u32[]{:S(2)}, u32[]{:S(2)}) collective-permute-start(bf16[272,256]{1,0:T(8,128)(2,1)} %get-tuple-element.45), channel_id=1, source_target_pairs={{0,1},{1,0},{2,3},{3,2},{4,5},{5,4},{6,7},{7,6},{8,9},{9,8},{10,11... | collective-permute-start | bytes 417800 | tf_op jit(solution)/shard_map/ppermute | solution.py:416
  8.7 3.0 %collective-permute-done.refs_0_ = bf16[272,256]{1,0:T(8,128)(2,1)S(1)} collective-permute-done((bf16[272,256]{1,0:T(8,128)(2,1)}, bf16[272,256]{1,0:T(8,128)(2,1)S(1)}, u32[]{:S(2)}, u32[]{:S(2)}) %collective-permute-start) | collective-permute-done | bytes 139296 | tf_op jit(solution)/shard_map/ppermute | solution.py:420
  12.1 1.1 %collective-permute-start.10 = (bf16[400,256]{1,0:T(8,128)(2,1)S(1)}, bf16[400,256]{1,0:T(8,128)(2,1)S(1)}, u32[]{:S(2)}, u32[]{:S(2)}) collective-permute-start(bf16[400,256]{1,0:T(8,128)(2,1)S(1)} %collective-permute-done.9), channel_id=1, source_target_pairs={{0,2},{1,3},{2,0},{3,1},{4,6},{5,7},{6,4},{7,5},{8,10},{9,11},{10,... | collective-permute-start | bytes 614408 | tf_op jit(solution)/shard_map/ppermute | solution.py:422
  13.2 1.8 %collective-permute-start.3 = (bf16[272,256]{1,0:T(8,128)(2,1)}, bf16[272,256]{1,0:T(8,128)(2,1)S(1)}, u32[]{:S(2)}, u32[]{:S(2)}) collective-permute-start(bf16[272,256]{1,0:T(8,128)(2,1)} %get-tuple-element.46), channel_id=1, source_target_pairs={{0,1},{1,0},{2,3},{3,2},{4,8},{5,9},{6,10},{7,11},{8,4},{9,5},{10,... | collective-permute-start | bytes 417800 | tf_op jit(solution)/shard_map/ppermute | solution.py:421
  15.0 0.8 %collective-permute-start.2 = (bf16[272,256]{1,0:T(8,128)(2,1)S(1)}, bf16[272,256]{1,0:T(8,128)(2,1)S(1)}, u32[]{:S(2)}, u32[]{:S(2)}) collective-permute-start(bf16[272,256]{1,0:T(8,128)(2,1)S(1)} %collective-permute-done.1), channel_id=1, source_target_pairs={{0,4},{1,5},{2,6},{3,7},{4,0},{5,1},{6,2},{7,3},{8,12},{9,13},{10,... | collective-permute-start | bytes 417800 | tf_op jit(solution)/shard_map/ppermute | solution.py:423
  15.8 2.4 %collective-permute-start.5 = (bf16[272,256]{1,0:T(8,128)(2,1)S(1)}, bf16[272,256]{1,0:T(8,128)(2,1)S(1)}, u32[]{:S(2)}, u32[]{:S(2)}) collective-permute-start(bf16[272,256]{1,0:T(8,128)(2,1)S(1)} %collective-permute-done.4), channel_id=1, source_target_pairs={{0,1},{1,0},{2,3},{3,2},{4,8},{5,9},{6,10},{7,11},{8,4},{9,5},{10,... | collective-permute-start | bytes 417800 | tf_op jit(solution)/shard_map/ppermute | solution.py:424
  18.2 1.0 %copy-done.2 = bf16[672,256]{1,0:T(8,128)(2,1)S(1)} copy-done((bf16[672,256]{1,0:T(8,128)(2,1)S(1)}, bf16[672,256]{1,0:T(8,128)(2,1)}, u32[]{:S(2)}) %copy-start.2) | copy-done | bytes 344088
  19.2 1.6 %early.1 = (bf16[512,512]{1,0:T(8,128)(2,1)S(1)}, bf16[512,512]{1,0:T(8,128)(2,1)S(1)}, bf16[512,512]{1,0:T(8,128)(2,1)S(1)}, f32[2,256,256]{2,1,0:T(8,128)S(1)}, f32[3,256,256]{2,1,0:T(8,128)S(1)}) custom-call(bf16[512,1536]{1,0:T(8,128)(2,1)S(1)} %copy-done, bf16[672,256]{1,0:T(8,128)(2,1)S(1)} %copy-done.2, ...), custom_call_target="tpu_custom_call" | custom-call | flops 268435456 | bytes 4194304 | tf_op jit(solution)/shard_map/early/pallas_call | solution.py:428
  21.9 2.2 %collective-permute-start.11 = (bf16[256,256]{1,0:T(8,128)(2,1)S(1)}, bf16[256,256]{1,0:T(8,128)(2,1)S(1)}, u32[]{:S(2)}, u32[]{:S(2)}) collective-permute-start(bf16[256,256]{1,0:T(8,128)(2,1)S(1)} %get-tuple-element.59), channel_id=1, source_target_pairs={{0,4},{1,5},{2,6},{3,7},{4,0},{5,1},{6,2},{7,3},{8,12},{9,13},{10,... | collective-permute-start | bytes 393224 | tf_op jit(solution)/shard_map/ppermute | solution.py:460
  24.1 2.1 %collective-permute-start.12 = (bf16[256,256]{1,0:T(8,128)(2,1)S(1)}, bf16[256,256]{1,0:T(8,128)(2,1)S(1)}, u32[]{:S(2)}, u32[]{:S(2)}) collective-permute-start(bf16[256,256]{1,0:T(8,128)(2,1)S(1)} %get-tuple-element.60), channel_id=1, source_target_pairs={{0,1},{1,0},{2,3},{3,2},{4,8},{5,9},{6,10},{7,11},{8,4},{9,5},{10,... | collective-permute-start | bytes 393224 | tf_op jit(solution)/shard_map/ppermute | solution.py:461
  27.6 2.1 %collective-permute-start.15 = (bf16[256,512]{1,0:T(8,128)(2,1)S(1)}, bf16[256,512]{1,0:T(8,128)(2,1)S(1)}, u32[]{:S(2)}, u32[]{:S(2)}) collective-permute-start(bf16[256,512]{1,0:T(8,128)(2,1)S(1)} %get-tuple-element.63.own_ref), channel_id=1, source_target_pairs={{0,1},{1,0},{2,3},{3,2},{4,5},{5,4},{6,7},{7,6},{8,9},{9,8},{10,11... | collective-permute-start | bytes 786440 | tf_op jit(solution)/shard_map/ppermute | solution.py:481
  30.0 1.2 %collective-permute-start.13 = (bf16[128,512]{1,0:T(8,128)(2,1)S(1)}, bf16[128,512]{1,0:T(8,128)(2,1)S(1)}, u32[]{:S(2)}, u32[]{:S(2)}) collective-permute-start(bf16[128,512]{1,0:T(8,128)(2,1)S(1)} %get-tuple-element.70), channel_id=1, source_target_pairs={{0,2},{1,3},{2,0},{3,1},{4,6},{5,7},{6,4},{7,5},{8,10},{9,11},{10,... | collective-permute-start | bytes 393224 | tf_op jit(solution)/shard_map/ppermute | solution.py:482
  31.5 5.0 %near.1 = (bf16[16,128,256]{2,1,0:T(8,128)(2,1)S(1)}, f32[16,48,256]{2,1,0:T(8,128)S(1)}, f32[16,8,256]{2,1,0:T(8,128)S(1)}) custom-call(bf16[256,512]{1,0:T(8,128)(2,1)S(1)} %get-tuple-element.63.own_ref, bf16[256,512]{1,0:T(8,128)(2,1)S(1)} %collective-permute-done.15.side_ref, bf16[512,512]{1,0:T(8,128)(2,1)S(1)} %get-tuple-element.64.wq_ref, ...), custom_call_target="tpu_custom_call" | custom-call | flops 8589934592 | bytes 4194304 | tf_op jit(solution)/shard_map/near/pallas_call | solution.py:486
  36.6 1.4 %collective-permute-done.14.refs_3_ = bf16[128,512]{1,0:T(8,128)(2,1)S(1)} collective-permute-done((bf16[128,512]{1,0:T(8,128)(2,1)S(1)}, bf16[128,512]{1,0:T(8,128)(2,1)S(1)}, u32[]{:S(2)}, u32[]{:S(2)}) %collective-permute-start.14) | collective-permute-done | bytes 131104 | tf_op jit(solution)/shard_map/ppermute | solution.py:483
  38.0 0.8 %collective-permute-start.18 = (bf16[128,512]{1,0:T(8,128)(2,1)S(1)}, bf16[128,512]{1,0:T(8,128)(2,1)S(1)}, u32[]{:S(2)}, u32[]{:S(2)}) collective-permute-start(bf16[128,512]{1,0:T(8,128)(2,1)S(1)} %collective-permute-done.13.refs_2_), channel_id=1, source_target_pairs={{0,1},{1,0},{2,3},{3,2},{4,5},{5,4},{6,7},{7,6},{8,9},{9,8},{10,11... | collective-permute-start | bytes 393224 | tf_op jit(solution)/shard_map/ppermute | solution.py:518
  38.8 1.2 %collective-permute-start.17 = (bf16[128,512]{1,0:T(8,128)(2,1)S(1)}, bf16[128,512]{1,0:T(8,128)(2,1)S(1)}, u32[]{:S(2)}, u32[]{:S(2)}) collective-permute-start(bf16[128,512]{1,0:T(8,128)(2,1)S(1)} %collective-permute-done.14.refs_3_), channel_id=1, source_target_pairs={{0,4},{1,5},{2,0},{3,1},{4,8},{5,9},{6,2},{7,3},{8,12},{9,13},{10,... | collective-permute-start | bytes 393224 | tf_op jit(solution)/shard_map/ppermute | solution.py:515
  39.9 3.0 %collective-permute-start.16 = (bf16[128,512]{1,0:T(8,128)(2,1)S(1)}, bf16[128,512]{1,0:T(8,128)(2,1)S(1)}, u32[]{:S(2)}, u32[]{:S(2)}) collective-permute-start(bf16[128,512]{1,0:T(8,128)(2,1)S(1)} %get-tuple-element.70), channel_id=1, source_target_pairs={{0,1},{1,0},{2,4},{3,5},{4,2},{5,3},{6,8},{7,9},{8,6},{9,7},{10,12... | collective-permute-start | bytes 393224 | tf_op jit(solution)/shard_map/ppermute | solution.py:508
  43.0 2.9 %mid.1 = (f32[16,48,256]{2,1,0:T(8,128)S(1)}, f32[16,8,256]{2,1,0:T(8,128)S(1)}) custom-call(bf16[128,512]{1,0:T(8,128)(2,1)S(1)} %collective-permute-done.18.refs_0_, bf16[128,512]{1,0:T(8,128)(2,1)S(1)} %collective-permute-done.19.refs_1_, bf16[128,512]{1,0:T(8,128)(2,1)S(1)} %collective-permute-done.13.refs_2_, ...), custom_call_target="tpu_custom_call" | custom-call | flops 4294967296 | bytes 4194304 | tf_op jit(solution)/shard_map/mid/pallas_call | solution.py:527
  46.0 3.2 %collective-permute-start.20 = (bf16[128,512]{1,0:T(8,128)(2,1)S(1)}, bf16[128,512]{1,0:T(8,128)(2,1)S(1)}, u32[]{:S(2)}, u32[]{:S(2)}) collective-permute-start(bf16[128,512]{1,0:T(8,128)(2,1)S(1)} %collective-permute-done.16.refs_2_), channel_id=1, source_target_pairs={{0,1},{1,0},{2,3},{3,2},{4,5},{5,4},{6,7},{7,6},{8,9},{9,8},{10,11... | collective-permute-start | bytes 393224 | tf_op jit(solution)/shard_map/ppermute | solution.py:542
  49.3 0.9 %collective-permute-done.20.refs_0_ = bf16[128,512]{1,0:T(8,128)(2,1)S(1)} collective-permute-done((bf16[128,512]{1,0:T(8,128)(2,1)S(1)}, bf16[128,512]{1,0:T(8,128)(2,1)S(1)}, u32[]{:S(2)}, u32[]{:S(2)}) %collective-permute-start.20) | collective-permute-done | bytes 131104 | tf_op jit(solution)/shard_map/ppermute | solution.py:542
  50.6 7.4 %far.1 = bf16[256,512]{1,0:T(8,128)(2,1)} custom-call(bf16[128,512]{1,0:T(8,128)(2,1)S(1)} %collective-permute-done.20.refs_0_, bf16[128,512]{1,0:T(8,128)(2,1)S(1)} %collective-permute-done.21.refs_1_, bf16[128,512]{1,0:T(8,128)(2,1)S(1)} %collective-permute-done.16.refs_2_, bf16[128,512]{1,0:T(8,128)(2,1)S(1)} %collective-permute-done.17.refs_3_, ...), custom_call_target="tpu_custom_call" | custom-call | flops 8589934592 | bytes 8388608 | tf_op jit(solution)/shard_map/far/pallas_call | solution.py:544
  (50 shorter events, 4.4 us)
Async XLA Ops:
  0.0 18.2 %copy-start = (bf16[512,1536]{1,0:T(8,128)(2,1)S(1)}, bf16[512,1536]{1,0:T(8,128)(2,1)}, u32[]{:S(2)}) copy-start(bf16[512,1536]{1,0:T(8,128)(2,1)} %w_ref.2) | copy-start | bytes 4718596
  5.9 9.9 %collective-permute-start.6 = (bf16[672,256]{1,0:T(8,128)(2,1)}, bf16[672,256]{1,0:T(8,128)(2,1)S(1)}, u32[]{:S(2)}, u32[]{:S(2)}) collective-permute-start(bf16[672,256]{1,0:T(8,128)(2,1)} %get-tuple-element.51), channel_id=1, source_target_pairs={{0,1},{1,0},{2,3},{3,2},{4,5},{5,4},{6,7},{7,6},{8,9},{9,8},{10,11... | collective-permute-start | bytes 1032200 | tf_op jit(solution)/shard_map/ppermute | solution.py:425
  6.6 5.5 %collective-permute-start.9 = (bf16[400,256]{1,0:T(8,128)(2,1)}, bf16[400,256]{1,0:T(8,128)(2,1)S(1)}, u32[]{:S(2)}, u32[]{:S(2)}) collective-permute-start(bf16[400,256]{1,0:T(8,128)(2,1)} %get-tuple-element.56), channel_id=1, source_target_pairs={{0,1},{1,0},{2,3},{3,2},{4,5},{5,4},{6,7},{7,6},{8,9},{9,8},{10,11... | collective-permute-start | bytes 614408 | tf_op jit(solution)/shard_map/ppermute | solution.py:417
  6.7 5.0 %collective-permute-start = (bf16[272,256]{1,0:T(8,128)(2,1)}, bf16[272,256]{1,0:T(8,128)(2,1)S(1)}, u32[]{:S(2)}, u32[]{:S(2)}) collective-permute-start(bf16[272,256]{1,0:T(8,128)(2,1)} %get-tuple-element.44), channel_id=1, source_target_pairs={{0,4},{1,5},{2,6},{3,7},{4,0},{5,1},{6,2},{7,3},{8,12},{9,13},{10,... | collective-permute-start | bytes 417800 | tf_op jit(solution)/shard_map/ppermute | solution.py:420
  8.0 5.2 %collective-permute-start.1 = (bf16[272,256]{1,0:T(8,128)(2,1)}, bf16[272,256]{1,0:T(8,128)(2,1)S(1)}, u32[]{:S(2)}, u32[]{:S(2)}) collective-permute-start(bf16[272,256]{1,0:T(8,128)(2,1)} %get-tuple-element.45), channel_id=1, source_target_pairs={{0,1},{1,0},{2,3},{3,2},{4,5},{5,4},{6,7},{7,6},{8,9},{9,8},{10,11... | collective-permute-start | bytes 417800 | tf_op jit(solution)/shard_map/ppermute | solution.py:416
  8.7 6.3 %collective-permute-start.4 = (bf16[272,256]{1,0:T(8,128)(2,1)}, bf16[272,256]{1,0:T(8,128)(2,1)S(1)}, u32[]{:S(2)}, u32[]{:S(2)}) collective-permute-start(bf16[272,256]{1,0:T(8,128)(2,1)} %get-tuple-element.47), channel_id=1, source_target_pairs={{0,1},{1,0},{2,3},{3,2},{4,5},{5,4},{6,7},{7,6},{8,9},{9,8},{10,11... | collective-permute-start | bytes 417800 | tf_op jit(solution)/shard_map/ppermute | solution.py:418
  11.7 9.7 %collective-permute-start.8 = (bf16[400,256]{1,0:T(8,128)(2,1)}, bf16[400,256]{1,0:T(8,128)(2,1)S(1)}, u32[]{:S(2)}, u32[]{:S(2)}) collective-permute-start(bf16[400,256]{1,0:T(8,128)(2,1)} %get-tuple-element.55), channel_id=1, source_target_pairs={{0,2},{1,3},{2,0},{3,1},{4,6},{5,7},{6,4},{7,5},{8,10},{9,11},{10,... | collective-permute-start | bytes 614408 | tf_op jit(solution)/shard_map/ppermute | solution.py:419
  12.1 9.5 %collective-permute-start.10 = (bf16[400,256]{1,0:T(8,128)(2,1)S(1)}, bf16[400,256]{1,0:T(8,128)(2,1)S(1)}, u32[]{:S(2)}, u32[]{:S(2)}) collective-permute-start(bf16[400,256]{1,0:T(8,128)(2,1)S(1)} %collective-permute-done.9), channel_id=1, source_target_pairs={{0,2},{1,3},{2,0},{3,1},{4,6},{5,7},{6,4},{7,5},{8,10},{9,11},{10,... | collective-permute-start | bytes 614408 | tf_op jit(solution)/shard_map/ppermute | solution.py:422
  13.2 7.6 %collective-permute-start.3 = (bf16[272,256]{1,0:T(8,128)(2,1)}, bf16[272,256]{1,0:T(8,128)(2,1)S(1)}, u32[]{:S(2)}, u32[]{:S(2)}) collective-permute-start(bf16[272,256]{1,0:T(8,128)(2,1)} %get-tuple-element.46), channel_id=1, source_target_pairs={{0,1},{1,0},{2,3},{3,2},{4,8},{5,9},{6,10},{7,11},{8,4},{9,5},{10,... | collective-permute-start | bytes 417800 | tf_op jit(solution)/shard_map/ppermute | solution.py:421
  15.0 5.8 %collective-permute-start.2 = (bf16[272,256]{1,0:T(8,128)(2,1)S(1)}, bf16[272,256]{1,0:T(8,128)(2,1)S(1)}, u32[]{:S(2)}, u32[]{:S(2)}) collective-permute-start(bf16[272,256]{1,0:T(8,128)(2,1)S(1)} %collective-permute-done.1), channel_id=1, source_target_pairs={{0,4},{1,5},{2,6},{3,7},{4,0},{5,1},{6,2},{7,3},{8,12},{9,13},{10,... | collective-permute-start | bytes 417800 | tf_op jit(solution)/shard_map/ppermute | solution.py:423
  15.8 5.0 %collective-permute-start.5 = (bf16[272,256]{1,0:T(8,128)(2,1)S(1)}, bf16[272,256]{1,0:T(8,128)(2,1)S(1)}, u32[]{:S(2)}, u32[]{:S(2)}) collective-permute-start(bf16[272,256]{1,0:T(8,128)(2,1)S(1)} %collective-permute-done.4), channel_id=1, source_target_pairs={{0,1},{1,0},{2,3},{3,2},{4,8},{5,9},{6,10},{7,11},{8,4},{9,5},{10,... | collective-permute-start | bytes 417800 | tf_op jit(solution)/shard_map/ppermute | solution.py:424
  20.7 9.0 %copy-start.9 = (s32[16]{0:T(128)S(1)}, s32[16]{0:T(128)}, u32[]{:S(2)}) copy-start(s32[16]{0:T(128)} %refs_7_.1) | copy-start | bytes 196
  21.1 5.0 %collective-permute-start.7 = (bf16[256,256]{1,0:T(8,128)(2,1)S(1)}, bf16[256,256]{1,0:T(8,128)(2,1)S(1)}, u32[]{:S(2)}, u32[]{:S(2)}) collective-permute-start(bf16[256,256]{1,0:T(8,128)(2,1)S(1)} %get-tuple-element.54), channel_id=1, source_target_pairs={{0,2},{1,3},{2,0},{3,1},{4,6},{5,7},{6,4},{7,5},{8,10},{9,11},{10,... | collective-permute-start | bytes 393224 | tf_op jit(solution)/shard_map/ppermute | solution.py:458
  21.9 4.8 %collective-permute-start.11 = (bf16[256,256]{1,0:T(8,128)(2,1)S(1)}, bf16[256,256]{1,0:T(8,128)(2,1)S(1)}, u32[]{:S(2)}, u32[]{:S(2)}) collective-permute-start(bf16[256,256]{1,0:T(8,128)(2,1)S(1)} %get-tuple-element.59), channel_id=1, source_target_pairs={{0,4},{1,5},{2,6},{3,7},{4,0},{5,1},{6,2},{7,3},{8,12},{9,13},{10,... | collective-permute-start | bytes 393224 | tf_op jit(solution)/shard_map/ppermute | solution.py:460
  24.1 3.0 %collective-permute-start.12 = (bf16[256,256]{1,0:T(8,128)(2,1)S(1)}, bf16[256,256]{1,0:T(8,128)(2,1)S(1)}, u32[]{:S(2)}, u32[]{:S(2)}) collective-permute-start(bf16[256,256]{1,0:T(8,128)(2,1)S(1)} %get-tuple-element.60), channel_id=1, source_target_pairs={{0,1},{1,0},{2,3},{3,2},{4,8},{5,9},{6,10},{7,11},{8,4},{9,5},{10,... | collective-permute-start | bytes 393224 | tf_op jit(solution)/shard_map/ppermute | solution.py:461
  27.6 3.9 %collective-permute-start.15 = (bf16[256,512]{1,0:T(8,128)(2,1)S(1)}, bf16[256,512]{1,0:T(8,128)(2,1)S(1)}, u32[]{:S(2)}, u32[]{:S(2)}) collective-permute-start(bf16[256,512]{1,0:T(8,128)(2,1)S(1)} %get-tuple-element.63.own_ref), channel_id=1, source_target_pairs={{0,1},{1,0},{2,3},{3,2},{4,5},{5,4},{6,7},{7,6},{8,9},{9,8},{10,11... | collective-permute-start | bytes 786440 | tf_op jit(solution)/shard_map/ppermute | solution.py:481
  30.0 6.6 %collective-permute-start.13 = (bf16[128,512]{1,0:T(8,128)(2,1)S(1)}, bf16[128,512]{1,0:T(8,128)(2,1)S(1)}, u32[]{:S(2)}, u32[]{:S(2)}) collective-permute-start(bf16[128,512]{1,0:T(8,128)(2,1)S(1)} %get-tuple-element.70), channel_id=1, source_target_pairs={{0,2},{1,3},{2,0},{3,1},{4,6},{5,7},{6,4},{7,5},{8,10},{9,11},{10,... | collective-permute-start | bytes 393224 | tf_op jit(solution)/shard_map/ppermute | solution.py:482
  31.2 6.8 %collective-permute-start.14 = (bf16[128,512]{1,0:T(8,128)(2,1)S(1)}, bf16[128,512]{1,0:T(8,128)(2,1)S(1)}, u32[]{:S(2)}, u32[]{:S(2)}) collective-permute-start(bf16[128,512]{1,0:T(8,128)(2,1)S(1)} %get-tuple-element.62), channel_id=1, source_target_pairs={{0,2},{1,3},{2,0},{3,1},{4,6},{5,7},{6,4},{7,5},{8,10},{9,11},{10,... | collective-permute-start | bytes 393224 | tf_op jit(solution)/shard_map/ppermute | solution.py:483
  38.0 4.9 %collective-permute-start.18 = (bf16[128,512]{1,0:T(8,128)(2,1)S(1)}, bf16[128,512]{1,0:T(8,128)(2,1)S(1)}, u32[]{:S(2)}, u32[]{:S(2)}) collective-permute-start(bf16[128,512]{1,0:T(8,128)(2,1)S(1)} %collective-permute-done.13.refs_2_), channel_id=1, source_target_pairs={{0,1},{1,0},{2,3},{3,2},{4,5},{5,4},{6,7},{7,6},{8,9},{9,8},{10,11... | collective-permute-start | bytes 393224 | tf_op jit(solution)/shard_map/ppermute | solution.py:518
  38.8 4.1 %collective-permute-start.19 = (bf16[128,512]{1,0:T(8,128)(2,1)S(1)}, bf16[128,512]{1,0:T(8,128)(2,1)S(1)}, u32[]{:S(2)}, u32[]{:S(2)}) collective-permute-start(bf16[128,512]{1,0:T(8,128)(2,1)S(1)} %collective-permute-done.14.refs_3_), channel_id=1, source_target_pairs={{0,1},{1,0},{2,3},{3,2},{4,5},{5,4},{6,7},{7,6},{8,9},{9,8},{10,11... | collective-permute-start | bytes 393224 | tf_op jit(solution)/shard_map/ppermute | solution.py:519
  38.8 7.2 %collective-permute-start.17 = (bf16[128,512]{1,0:T(8,128)(2,1)S(1)}, bf16[128,512]{1,0:T(8,128)(2,1)S(1)}, u32[]{:S(2)}, u32[]{:S(2)}) collective-permute-start(bf16[128,512]{1,0:T(8,128)(2,1)S(1)} %collective-permute-done.14.refs_3_), channel_id=1, source_target_pairs={{0,4},{1,5},{2,0},{3,1},{4,8},{5,9},{6,2},{7,3},{8,12},{9,13},{10,... | collective-permute-start | bytes 393224 | tf_op jit(solution)/shard_map/ppermute | solution.py:515
  39.9 6.1 %collective-permute-start.16 = (bf16[128,512]{1,0:T(8,128)(2,1)S(1)}, bf16[128,512]{1,0:T(8,128)(2,1)S(1)}, u32[]{:S(2)}, u32[]{:S(2)}) collective-permute-start(bf16[128,512]{1,0:T(8,128)(2,1)S(1)} %get-tuple-element.70), channel_id=1, source_target_pairs={{0,1},{1,0},{2,4},{3,5},{4,2},{5,3},{6,8},{7,9},{8,6},{9,7},{10,12... | collective-permute-start | bytes 393224 | tf_op jit(solution)/shard_map/ppermute | solution.py:508
  46.0 4.2 %collective-permute-start.20 = (bf16[128,512]{1,0:T(8,128)(2,1)S(1)}, bf16[128,512]{1,0:T(8,128)(2,1)S(1)}, u32[]{:S(2)}, u32[]{:S(2)}) collective-permute-start(bf16[128,512]{1,0:T(8,128)(2,1)S(1)} %collective-permute-done.16.refs_2_), channel_id=1, source_target_pairs={{0,1},{1,0},{2,3},{3,2},{4,5},{5,4},{6,7},{7,6},{8,9},{9,8},{10,11... | collective-permute-start | bytes 393224 | tf_op jit(solution)/shard_map/ppermute | solution.py:542
  49.2 1.3 %collective-permute-start.21 = (bf16[128,512]{1,0:T(8,128)(2,1)S(1)}, bf16[128,512]{1,0:T(8,128)(2,1)S(1)}, u32[]{:S(2)}, u32[]{:S(2)}) collective-permute-start(bf16[128,512]{1,0:T(8,128)(2,1)S(1)} %collective-permute-done.17.refs_3_), channel_id=1, source_target_pairs={{0,1},{1,0},{2,3},{3,2},{4,5},{5,4},{6,7},{7,6},{8,9},{9,8},{10,11... | collective-permute-start | bytes 393224 | tf_op jit(solution)/shard_map/ppermute | solution.py:543
  (8 other events, 55.2 us)

commit v5 on v3

--- a/solution.py
+++ b/solution.py
@@ -105,9 +105,9 @@
         key: jnp.where(row == by_slot[:, m : m + 1], 1.0, 0.0).astype(jnp.bfloat16) for m, key in enumerate(keys)
     }
     sends = []
-    for n, parts in enumerate(runs):
+    for n in reversed(range(count)):
         start = 0
-        for chosen, lanes in parts:
+        for chosen, lanes in runs[n]:
             taken = dot(jnp.concatenate([picks[key] for key in chosen], axis=0), message_ref[:, lanes])
             out_vmems[n][start : start + len(chosen) * cap, :] = taken.astype(jnp.bfloat16)
             start += len(chosen) * cap + TILE
@@ -136,14 +136,19 @@
     width = w_ref.shape[0]
     head_dim = width // HEADS
     span = 3 * LANES
-    row = lax.broadcasted_iota(jnp.int32, (LANES, span), 0)
-    column = lax.broadcasted_iota(jnp.int32, (LANES, span), 1)
-    wanted = row // head_dim * (3 * head_dim) + row % head_dim
-    for c, out_ref in enumerate((query_ref, key_ref, value_ref)):
-        pick = jnp.where(column == wanted + c * head_dim, 1.0, 0.0).astype(jnp.bfloat16)
-        for g in range(width // LANES):
-            part = dot_t(pick, w_ref[:, g * span : (g + 1) * span])
-            out_ref[g * LANES : (g + 1) * LANES, :] = part.astype(jnp.bfloat16)
+    def pick(c, along):
+        shape = (LANES, span) if along else (span, LANES)
+        to = lax.broadcasted_iota(jnp.int32, shape, 1 - along)
+        column = lax.broadcasted_iota(jnp.int32, shape, along)
+        wanted = to // head_dim * (3 * head_dim) + to % head_dim + c * head_dim
+        return jnp.where(column == wanted, 1.0, 0.0).astype(jnp.bfloat16)
+
+    for g in range(width // LANES):
+        columns = w_ref[:, g * span : (g + 1) * span]
+        part = slice(g * LANES, (g + 1) * LANES)
+        query_ref[part, :] = dot_t(pick(0, 1), columns).astype(jnp.bfloat16)
+        key_ref[:, part] = dot(columns, pick(1, 0)).astype(jnp.bfloat16)
+        value_ref[part, :] = dot_t(pick(2, 1), columns).astype(jnp.bfloat16)
     start = 0
     for sum_ref in (left_ref, right_ref):
         count, nodes, _ = sum_ref.shape
@@ -174,7 +179,7 @@
     count = rows.shape[0]
     groups = key_ref.shape[0]
     heads = value_ref.shape[0]
-    keys = dot_t(rows, wk_ref[...]).astype(jnp.bfloat16)
+    keys = dot(rows, wk_ref[...]).astype(jnp.bfloat16)
     for g in range(groups):
         key_ref[g, start : start + count, :] = keys[:, g * LANES : (g + 1) * LANES]
     values = dot_t(wv_ref[...], rows).astype(jnp.bfloat16)
@@ -244,13 +249,21 @@
     lax.fori_loop(0, HEADS // GROUP, together, 0)
 
 
+def outer_kernel(even_ref, odd_ref, wk_ref, wv_ref, key_ref, value_ref):
+    nodes, width = even_ref.shape
+    head_dim = width // HEADS
+    value_ref[:, head_dim:, :] = jnp.ones_like(value_ref[:, head_dim:, :])
+    project_keys(even_ref[...], wk_ref, wv_ref, key_ref, value_ref, 0)
+    project_keys(odd_ref[...], wk_ref, wv_ref, key_ref, value_ref, nodes)
+
+
 def far_kernel(
-    first_ref, second_ref, even_ref, odd_ref, wk_ref, wv_ref, order_ref, window_ref,
+    first_ref, second_ref, far_key_ref, far_value_ref, wk_ref, wv_ref, order_ref, window_ref,
     query_ref, sums_ref, top_ref, state_ref, w_out_ref, gain_ref, up_ref, down_ref,
     out_ref,
     key_ref, value_ref, gap_ref, attended_ref,
 ):
-    nodes, width = even_ref.shape
+    nodes, width = first_ref.shape
     head_dim = width // HEADS
     per_group = LANES // head_dim
     total = lax.axis_size("band") * lax.axis_size("inner")
@@ -268,8 +281,6 @@
     beyond = jnp.where(by_even, first_ref[...], second_ref[...])
     beyond = jnp.where(odd == 0, jnp.concatenate([beyond[NEAR:], beyond[:NEAR]], axis=0), beyond)
     project_keys(beyond, wk_ref, wv_ref, key_ref, value_ref, 0)
-    project_keys(even_ref[...], wk_ref, wv_ref, key_ref, value_ref, nodes)
-    project_keys(odd_ref[...], wk_ref, wv_ref, key_ref, value_ref, 2 * nodes)
     lag = lax.broadcasted_iota(jnp.int32, (nodes, nodes), 0) - lax.broadcasted_iota(
         jnp.int32, (nodes, nodes), 1
     )
@@ -284,7 +295,13 @@
     gap_ref[2 * nodes : 3 * nodes] = gap(lag, -far, 0)
 
     def attend(heads, rows):
-        scores = [dot(key_ref[h // per_group, 0:rows, :], query_ref[h]) for h in heads]
+        close = min(rows, nodes)
+        scores = [dot(key_ref[h // per_group, 0:close, :], query_ref[h]) for h in heads]
+        if rows > close:
+            scores = [
+                jnp.concatenate([x, dot(far_key_ref[h // per_group], query_ref[h])], axis=0)
+                for h, x in zip(heads, scores)
+            ]
         scores = [
             jnp.where(gap_ref[0:rows] <= window_ref[h], x, -1e30) for h, x in zip(heads, scores)
         ]
@@ -292,7 +309,10 @@
         tops = [jnp.maximum(old, jnp.max(x, axis=0, keepdims=True)) for old, x in zip(olds, scores)]
         expos = [jnp.exp2((x - top) * scale).astype(jnp.bfloat16) for x, top in zip(scores, tops)]
         for h, old, top, expo in zip(heads, olds, tops, expos):
-            sums = sums_ref[h] * jnp.exp2((old - top) * scale) + dot(value_ref[h, :, 0:rows], expo)
+            sums = sums_ref[h] * jnp.exp2((old - top) * scale)
+            sums += dot(value_ref[h, :, 0:close], expo[0:close])
+            if rows > close:
+                sums += dot(far_value_ref[h], expo[close:])
             attended_ref[h] = (sums[0:head_dim] / sums[head_dim : head_dim + 1]).astype(jnp.bfloat16)
 
     def together(i, carry):
@@ -380,26 +400,22 @@
     )(grid_rows, w_message, *edges)
     beside = [(g, g ^ 1) for g in range(devices)]
 
-    def bands_trade(odd_pairs):
+    def bands_trade(odd_pairs, k=0):
         route = []
         for g in range(devices):
             b = g // inners
             t = (b - odd_pairs ^ 1) + odd_pairs
-            route.append((g, t * inners + g % inners if 0 <= t < bands else g ^ 1))
+            route.append((g, t * inners + (g % inners ^ k) if 0 <= t < bands else g ^ 1))
         return route
 
-    def chip_trade(p):
-        return [(g, g ^ (2 * p)) for g in range(devices)]
-
-    even_other = lax.ppermute(even_other, NODES, beside)
-    cross_other = [lax.ppermute(c, NODES, beside) for c in cross[1::2]]
-    odd_other = lax.ppermute(odd_other, NODES, beside)
-    cross = [lax.ppermute(c, NODES, chip_trade(p + 1)) for p, c in enumerate(cross[0::2])]
+    def chip_trade(p, k=0):
+        return [(g, g ^ (2 * p + k)) for g in range(devices)]
+
+    cross = [lax.ppermute(c, NODES, chip_trade(n // 2 + 1, n % 2)) for n, c in enumerate(cross)]
     even = lax.ppermute(even, NODES, bands_trade(0))
     odd = lax.ppermute(odd, NODES, bands_trade(1))
-    cross_other = [lax.ppermute(c, NODES, chip_trade(p + 1)) for p, c in enumerate(cross_other)]
-    even_other = lax.ppermute(even_other, NODES, bands_trade(0))
-    odd_other = lax.ppermute(odd_other, NODES, bands_trade(1))
+    even_other = lax.ppermute(even_other, NODES, bands_trade(0, 1))
+    odd_other = lax.ppermute(odd_other, NODES, bands_trade(1, 1))
     here_other = lax.ppermute(here_other, NODES, beside)
 
     w_qkv, window, here = lax.optimization_barrier((w_qkv, window, here))
@@ -434,7 +450,7 @@
 
     left, *parts = sums([even, even_other, odd, odd_other], early_left, 0, "left")
     parts = [lax.ppermute(part, NODES, chip_trade(p + 1)) for p, part in enumerate(parts)]
-    to_even, to_odd, right = sums([*cross, *cross_other], early_right, 2, "right")
+    to_even, to_odd, right = sums(cross, early_right, 2, "right")
     from_even = lax.ppermute(to_even, NODES, bands_trade(0))
     from_odd = lax.ppermute(to_odd, NODES, bands_trade(1))
 
@@ -485,14 +501,27 @@
     even, odd, near, top = lax.optimization_barrier((even, odd, near, top))
     first = lax.ppermute(even, NODES, beside)
     second = lax.ppermute(odd, NODES, beside)
+    keys, values = pl.pallas_call(
+        outer_kernel,
+        out_shape=[
+            jax.ShapeDtypeStruct((width // LANES, 2 * nodes, LANES), bf16),
+            jax.ShapeDtypeStruct((HEADS, extra, 2 * nodes), bf16),
+        ],
+        in_specs=[VMEM] * 4,
+        out_specs=[VMEM] * 2,
+        compiler_params=params(16),
+        cost_estimate=cost(8 * nodes * width * width, 3 << 20),
+        name="outer",
+    )(even, odd, w_key, w_value)
+
     return pl.pallas_call(
         far_kernel,
         out_shape=jax.ShapeDtypeStruct((nodes, width), bf16),
         in_specs=[VMEM] * 6 + [SMEM] * 2 + [VMEM] * 8,
         out_specs=VMEM,
         scratch_shapes=[
-            pltpu.VMEM((width // LANES, 3 * nodes, LANES), bf16),
-            pltpu.VMEM((HEADS, extra, 3 * nodes), bf16),
+            pltpu.VMEM((width // LANES, nodes, LANES), bf16),
+            pltpu.VMEM((HEADS, extra, nodes), bf16),
             pltpu.VMEM((3 * nodes, nodes), i32),
             pltpu.VMEM((HEADS, head_dim, nodes), bf16),
         ],
@@ -500,7 +529,7 @@
         cost_estimate=cost(8 << 30, 8 << 20),
         name="far",
     )(
-        first, second, even, odd, w_key, w_value, order, window,
+        first, second, keys, values, w_key, w_value, order, window,
         query, near, top, state, w_out, gain_mlp.reshape(1, width), w_up, w_down,
     )
 

time: 52.5 us -> 52.4 us (level)
  starting transfers between devices: 16.3 us -> 12.2 us
  waiting for transfers between devices: 13.1 us -> 16.8 us
    ppermute x1, waiting for transfers between devices: 0.01 us -> 3.63 us  [local(): lax.ppermute(part, NODES, chip_trade(p + 1))]
    ppermute x1, starting transfers between devices: 2.69 us -> 0.79 us  [local(): side = lax.ppermute(normed, NODES, beside)]
    ppermute x1, starting transfers between devices: 2.67 us -> 1 us  [local(): odd = lax.ppermute(normed, NODES, chips_trade(1))]
    ppermute x1, starting transfers between devices: 2.58 us -> 1.08 us  [local(): from_odd = lax.ppermute(to_odd, NODES, bands_trade(1))]
    ppermute x1, waiting for transfers between devices: 0.86 us -> 2.23 us  [local(): even = lax.ppermute(even, NODES, bands_trade(0))]
    ppermute x1, waiting for transfers between devices: 1.52 us -> 0.46 us  [local(): from_even = lax.ppermute(to_even, NODES, bands_trade(0))]
    ppermute x1, waiting for transfers between devices: 1.13 us -> 0.08 us  [local(): from_odd = lax.ppermute(to_odd, NODES, bands_trade(1))]
    ppermute x1, starting transfers between devices: 0.32 us -> 1.26 us  [local(): even = lax.ppermute(normed, NODES, chips_trade(0))]
  transfers between devices with their start and end apart: 18 -> 15, of which waited for: 9 -> 8; matrix products, arithmetic and copies ran while one was open for 1% -> 1% of each run, Pallas kernels for 14% -> 15%
where the time goes in v5:
time: 52.4 us; the launch traced here: 51.4 us
  Pallas kernels  20.9 us (40%)
  waiting for transfers between devices  16.8 us (32%)
  starting transfers between devices  12.2 us (23%)
  local copies, waits for them, and re-layouts  1.02 us (2%)
    pallas_call x1, Pallas kernels, local(): pl.pallas_call(far_kernel, out_shape=jax.ShapeDtypeStruct((nodes, width),...  6.7 us
    ppermute x1, waiting for transfers between devices, local(): even = lax.ppermute(normed, NODES, chips_trade(0))  6.12 us
    pallas_call x1, Pallas kernels, local(): pl.pallas_call(functools.partial(message_kernel, pairs), out_shape=outgoi...  5.79 us
    pallas_call x1, Pallas kernels, local(): pl.pallas_call(near_kernel, out_shape=[jax.ShapeDtypeStruct((HEADS, LANES...  5.19 us
    ppermute x1, waiting for transfers between devices, local(): lax.ppermute(part, NODES, chip_trade(p + 1))  3.63 us
    ppermute x1, waiting for transfers between devices, local(): odd_other = lax.ppermute(odd_other, NODES, bands_trade(1, 1))  3.43 us
    ppermute x1, waiting for transfers between devices, local(): even = lax.ppermute(even, NODES, bands_trade(0))  2.23 us
    ppermute x2, starting transfers between devices, local(): lax.ppermute(c, NODES, chip_trade(n // 2 + 1, n % 2))  1.97 us
  transfers between devices with their start and end apart: 15, of which 8 were waited for; matrix products, arithmetic and copies ran while one was open for 1% of the time, Pallas kernels for 15%

profile of v5, /device:TPU:15, one launch (start us, length us, event | category | flops | bytes accessed | tf_op | source)
XLA Modules:
  0.0 51.4 jit_solution(11325051778656222726)
XLA Ops:
  0.0 5.8 %messages.1 = (bf16[272,256]{1,0:T(8,128)(2,1)}, bf16[272,256]{1,0:T(8,128)(2,1)}, bf16[272,256]{1,0:T(8,128)(2,1)}, bf16[272,256]{1,0:T(8,128)(2,1)}, bf16[400,...) custom-call(bf16[1024,512]{1,0:T(8,128)(2,1)} %grid_ref.1, ...), custom_call_target="tpu_custom_call" | custom-call | flops 2147483648 | bytes 4194304 | tf_op jit(solution)/shard_map/messages/pallas_call | solution.py:384
  5.8 0.7 %collective-permute-start.4 = (bf16[672,256]{1,0:T(8,128)(2,1)}, bf16[672,256]{1,0:T(8,128)(2,1)S(1)}, u32[]{:S(2)}, u32[]{:S(2)}) collective-permute-start(bf16[672,256]{1,0:T(8,128)(2,1)} %get-tuple-element.44), channel_id=1, source_target_pairs={{0,1},{1,0},{2,3},{3,2},{4,5},{5,4},{6,7},{7,6},{8,9},{9,8},{10,11... | collective-permute-start | bytes 1032200 | tf_op jit(solution)/shard_map/ppermute | solution.py:419
  7.0 1.7 %collective-permute-start.7 = (bf16[400,256]{1,0:T(8,128)(2,1)}, bf16[400,256]{1,0:T(8,128)(2,1)S(1)}, u32[]{:S(2)}, u32[]{:S(2)}) collective-permute-start(bf16[400,256]{1,0:T(8,128)(2,1)} %get-tuple-element.49), channel_id=1, source_target_pairs={{0,3},{1,2},{2,1},{3,0},{4,7},{5,6},{6,5},{7,4},{8,11},{9,10},{10,... | collective-permute-start | bytes 614408 | tf_op jit(solution)/shard_map/ppermute | solution.py:414
  8.7 1.1 %collective-permute-start.1 = (bf16[272,256]{1,0:T(8,128)(2,1)}, bf16[272,256]{1,0:T(8,128)(2,1)S(1)}, u32[]{:S(2)}, u32[]{:S(2)}) collective-permute-start(bf16[272,256]{1,0:T(8,128)(2,1)} %get-tuple-element.38), channel_id=1, source_target_pairs={{0,5},{1,4},{2,7},{3,6},{4,1},{5,0},{6,3},{7,2},{8,13},{9,12},{10,... | collective-permute-start | bytes 417800 | tf_op jit(solution)/shard_map/ppermute | solution.py:417
  9.8 2.2 %collective-permute-done.refs_0_ = bf16[272,256]{1,0:T(8,128)(2,1)S(1)} collective-permute-done((bf16[272,256]{1,0:T(8,128)(2,1)}, bf16[272,256]{1,0:T(8,128)(2,1)S(1)}, u32[]{:S(2)}, u32[]{:S(2)}) %collective-permute-start) | collective-permute-done | bytes 139296 | tf_op jit(solution)/shard_map/ppermute | solution.py:415
  12.0 1.3 %collective-permute-start.2 = (bf16[272,256]{1,0:T(8,128)(2,1)}, bf16[272,256]{1,0:T(8,128)(2,1)S(1)}, u32[]{:S(2)}, u32[]{:S(2)}) collective-permute-start(bf16[272,256]{1,0:T(8,128)(2,1)} %get-tuple-element.39), channel_id=1, source_target_pairs={{0,1},{1,0},{2,3},{3,2},{4,8},{5,9},{6,10},{7,11},{8,4},{9,5},{10,... | collective-permute-start | bytes 417800 | tf_op jit(solution)/shard_map/ppermute | solution.py:416
  13.3 1.6 %collective-permute-start.3 = (bf16[272,256]{1,0:T(8,128)(2,1)}, bf16[272,256]{1,0:T(8,128)(2,1)S(1)}, u32[]{:S(2)}, u32[]{:S(2)}) collective-permute-start(bf16[272,256]{1,0:T(8,128)(2,1)} %get-tuple-element.40), channel_id=1, source_target_pairs={{0,1},{1,0},{2,3},{3,2},{4,9},{5,8},{6,11},{7,10},{8,5},{9,4},{10,... | collective-permute-start | bytes 417800 | tf_op jit(solution)/shard_map/ppermute | solution.py:418
  14.9 1.0 %copy-done.2 = bf16[672,256]{1,0:T(8,128)(2,1)S(1)} copy-done((bf16[672,256]{1,0:T(8,128)(2,1)S(1)}, bf16[672,256]{1,0:T(8,128)(2,1)}, u32[]{:S(2)}) %copy-start.2) | copy-done | bytes 344088
  15.9 1.5 %early.1 = (bf16[512,512]{1,0:T(8,128)(2,1)S(1)}, bf16[512,512]{1,0:T(8,128)(2,1)S(1)}, bf16[512,512]{1,0:T(8,128)(2,1)S(1)}, f32[2,256,256]{2,1,0:T(8,128)S(1)}, f32[3,256,256]{2,1,0:T(8,128)S(1)}) custom-call(bf16[512,1536]{1,0:T(8,128)(2,1)S(1)} %copy-done, bf16[672,256]{1,0:T(8,128)(2,1)S(1)} %copy-done.2, ...), custom_call_target="tpu_custom_call" | custom-call | flops 268435456 | bytes 4194304 | tf_op jit(solution)/shard_map/early/pallas_call | solution.py:422
  17.4 3.4 %collective-permute-done.3.refs_3_ = bf16[272,256]{1,0:T(8,128)(2,1)S(1)} collective-permute-done((bf16[272,256]{1,0:T(8,128)(2,1)}, bf16[272,256]{1,0:T(8,128)(2,1)S(1)}, u32[]{:S(2)}, u32[]{:S(2)}) %collective-permute-start.3) | collective-permute-done | bytes 139296 | tf_op jit(solution)/shard_map/ppermute | solution.py:418
  21.9 1.1 %collective-permute-start.9 = (bf16[256,256]{1,0:T(8,128)(2,1)S(1)}, bf16[256,256]{1,0:T(8,128)(2,1)S(1)}, u32[]{:S(2)}, u32[]{:S(2)}) collective-permute-start(bf16[256,256]{1,0:T(8,128)(2,1)S(1)} %get-tuple-element.53), channel_id=1, source_target_pairs={{0,1},{1,0},{2,3},{3,2},{4,8},{5,9},{6,10},{7,11},{8,4},{9,5},{10,... | collective-permute-start | bytes 393224 | tf_op jit(solution)/shard_map/ppermute | solution.py:455
  23.0 3.6 %collective-permute-done.5.refs_1_ = bf16[256,256]{1,0:T(8,128)(2,1)S(1)} collective-permute-done((bf16[256,256]{1,0:T(8,128)(2,1)S(1)}, bf16[256,256]{1,0:T(8,128)(2,1)S(1)}, u32[]{:S(2)}, u32[]{:S(2)}) %collective-permute-start.5) | collective-permute-done | bytes 131104 | tf_op jit(solution)/shard_map/ppermute | solution.py:452
  26.6 0.5 collective-permute-done.8.refs_3_
  27.1 0.5 merge.1
  27.6 0.8 %collective-permute-start.12 = (bf16[256,512]{1,0:T(8,128)(2,1)S(1)}, bf16[256,512]{1,0:T(8,128)(2,1)S(1)}, u32[]{:S(2)}, u32[]{:S(2)}) collective-permute-start(bf16[256,512]{1,0:T(8,128)(2,1)S(1)} %get-tuple-element.54.own_ref), channel_id=1, source_target_pairs={{0,1},{1,0},{2,3},{3,2},{4,5},{5,4},{6,7},{7,6},{8,9},{9,8},{10,11... | collective-permute-start | bytes 786440 | tf_op jit(solution)/shard_map/ppermute | solution.py:477
  28.7 1.3 %collective-permute-start.10 = (bf16[256,512]{1,0:T(8,128)(2,1)S(1)}, bf16[256,512]{1,0:T(8,128)(2,1)S(1)}, u32[]{:S(2)}, u32[]{:S(2)}) collective-permute-start(bf16[256,512]{1,0:T(8,128)(2,1)S(1)} %get-tuple-element.54.own_ref), channel_id=1, source_target_pairs={{0,2},{1,3},{2,0},{3,1},{4,6},{5,7},{6,4},{7,5},{8,10},{9,11},{10,... | collective-permute-start | bytes 786440 | tf_op jit(solution)/shard_map/ppermute | solution.py:478
  30.0 1.0 %collective-permute-start.11 = (bf16[256,512]{1,0:T(8,128)(2,1)S(1)}, bf16[256,512]{1,0:T(8,128)(2,1)S(1)}, u32[]{:S(2)}, u32[]{:S(2)}) collective-permute-start(bf16[256,512]{1,0:T(8,128)(2,1)S(1)} %get-tuple-element.54.own_ref), channel_id=1, source_target_pairs={{0,1},{1,0},{2,4},{3,5},{4,2},{5,3},{6,8},{7,9},{8,6},{9,7},{10,12... | collective-permute-start | bytes 786440 | tf_op jit(solution)/shard_map/ppermute | solution.py:479
  31.0 5.2 %near.1 = (bf16[16,128,256]{2,1,0:T(8,128)(2,1)S(1)}, f32[16,48,256]{2,1,0:T(8,128)S(1)}, f32[16,8,256]{2,1,0:T(8,128)S(1)}) custom-call(bf16[256,512]{1,0:T(8,128)(2,1)S(1)} %get-tuple-element.54.own_ref, bf16[256,512]{1,0:T(8,128)(2,1)S(1)} %collective-permute-done.12.side_ref, bf16[512,512]{1,0:T(8,128)(2,1)S(1)} %get-tuple-element.55.wq_ref, ...), custom_call_target="tpu_custom_call" | custom-call | flops 8589934592 | bytes 4194304 | tf_op jit(solution)/shard_map/near/pallas_call | solution.py:482
  36.2 6.1 %collective-permute-done.10.even_ref = bf16[256,512]{1,0:T(8,128)(2,1)S(1)} collective-permute-done((bf16[256,512]{1,0:T(8,128)(2,1)S(1)}, bf16[256,512]{1,0:T(8,128)(2,1)S(1)}, u32[]{:S(2)}, u32[]{:S(2)}) %collective-permute-start.10) | collective-permute-done | bytes 262176 | tf_op jit(solution)/shard_map/ppermute | solution.py:478
  42.3 0.8 %collective-permute-start.13 = (bf16[256,512]{1,0:T(8,128)(2,1)S(1)}, bf16[256,512]{1,0:T(8,128)(2,1)S(1)}, u32[]{:S(2)}, u32[]{:S(2)}) collective-permute-start(bf16[256,512]{1,0:T(8,128)(2,1)S(1)} %collective-permute-done.10.even_ref), channel_id=1, source_target_pairs={{0,1},{1,0},{2,3},{3,2},{4,5},{5,4},{6,7},{7,6},{8,9},{9,8},{10,11... | collective-permute-start | bytes 786440 | tf_op jit(solution)/shard_map/ppermute | solution.py:502
  43.1 0.7 %outer.1 = (bf16[4,512,128]{2,1,0:T(8,128)(2,1)S(1)}, bf16[16,48,512]{2,1,0:T(8,128)(2,1)S(1)}) custom-call(bf16[256,512]{1,0:T(8,128)(2,1)S(1)} %collective-permute-done.10.even_ref, bf16[256,512]{1,0:T(8,128)(2,1)S(1)} %collective-permute-done.11.odd_ref, bf16[512,512]{1,0:T(8,128)(2,1)S(1)} %get-tuple-element.56.wk_ref, ...), custom_call_target="tpu_custom_call" | custom-call | flops 536870912 | bytes 3145728 | tf_op jit(solution)/shard_map/outer/pallas_call | solution.py:504
  43.9 0.4 collective-permute-done.13.first_ref
  44.3 0.4 collective-permute-done.14.second_ref
  44.7 6.7 %far.1 = bf16[256,512]{1,0:T(8,128)(2,1)} custom-call(bf16[256,512]{1,0:T(8,128)(2,1)S(1)} %collective-permute-done.13.first_ref, bf16[256,512]{1,0:T(8,128)(2,1)S(1)} %collective-permute-done.14.second_ref, bf16[4,512,128]{2,1,0:T(8,128)(2,1)S(1)} %get-tuple-element.63.far_key_ref, bf16[16,48,512]{2,1,0:T(8,128)(2,1)S(1)} %get-tuple-element.64.far_value_ref, ...), custom_call_target="tpu_custom_call" | custom-call | flops 8589934592 | bytes 8388608 | tf_op jit(solution)/shard_map/far/pallas_call | solution.py:517
  (36 shorter events, 1.9 us)
Async XLA Ops:
  0.0 14.9 %copy-start = (bf16[512,1536]{1,0:T(8,128)(2,1)S(1)}, bf16[512,1536]{1,0:T(8,128)(2,1)}, u32[]{:S(2)}) copy-start(bf16[512,1536]{1,0:T(8,128)(2,1)} %w_ref.2) | copy-start | bytes 4718596
  5.8 7.5 %collective-permute-start.4 = (bf16[672,256]{1,0:T(8,128)(2,1)}, bf16[672,256]{1,0:T(8,128)(2,1)S(1)}, u32[]{:S(2)}, u32[]{:S(2)}) collective-permute-start(bf16[672,256]{1,0:T(8,128)(2,1)} %get-tuple-element.44), channel_id=1, source_target_pairs={{0,1},{1,0},{2,3},{3,2},{4,5},{5,4},{6,7},{7,6},{8,9},{9,8},{10,11... | collective-permute-start | bytes 1032200 | tf_op jit(solution)/shard_map/ppermute | solution.py:419
  6.5 5.5 %collective-permute-start = (bf16[272,256]{1,0:T(8,128)(2,1)}, bf16[272,256]{1,0:T(8,128)(2,1)S(1)}, u32[]{:S(2)}, u32[]{:S(2)}) collective-permute-start(bf16[272,256]{1,0:T(8,128)(2,1)} %get-tuple-element.37), channel_id=1, source_target_pairs={{0,4},{1,5},{2,6},{3,7},{4,0},{5,1},{6,2},{7,3},{8,12},{9,13},{10,... | collective-permute-start | bytes 417800 | tf_op jit(solution)/shard_map/ppermute | solution.py:415
  6.7 14.8 %collective-permute-start.6 = (bf16[400,256]{1,0:T(8,128)(2,1)}, bf16[400,256]{1,0:T(8,128)(2,1)S(1)}, u32[]{:S(2)}, u32[]{:S(2)}) collective-permute-start(bf16[400,256]{1,0:T(8,128)(2,1)} %get-tuple-element.48), channel_id=1, source_target_pairs={{0,2},{1,3},{2,0},{3,1},{4,6},{5,7},{6,4},{7,5},{8,10},{9,11},{10,... | collective-permute-start | bytes 614408 | tf_op jit(solution)/shard_map/ppermute | solution.py:414
  7.0 14.5 %collective-permute-start.7 = (bf16[400,256]{1,0:T(8,128)(2,1)}, bf16[400,256]{1,0:T(8,128)(2,1)S(1)}, u32[]{:S(2)}, u32[]{:S(2)}) collective-permute-start(bf16[400,256]{1,0:T(8,128)(2,1)} %get-tuple-element.49), channel_id=1, source_target_pairs={{0,3},{1,2},{2,1},{3,0},{4,7},{5,6},{6,5},{7,4},{8,11},{9,10},{10,... | collective-permute-start | bytes 614408 | tf_op jit(solution)/shard_map/ppermute | solution.py:414
  8.7 8.7 %collective-permute-start.1 = (bf16[272,256]{1,0:T(8,128)(2,1)}, bf16[272,256]{1,0:T(8,128)(2,1)S(1)}, u32[]{:S(2)}, u32[]{:S(2)}) collective-permute-start(bf16[272,256]{1,0:T(8,128)(2,1)} %get-tuple-element.38), channel_id=1, source_target_pairs={{0,5},{1,4},{2,7},{3,6},{4,1},{5,0},{6,3},{7,2},{8,13},{9,12},{10,... | collective-permute-start | bytes 417800 | tf_op jit(solution)/shard_map/ppermute | solution.py:417
  12.0 5.4 %collective-permute-start.2 = (bf16[272,256]{1,0:T(8,128)(2,1)}, bf16[272,256]{1,0:T(8,128)(2,1)S(1)}, u32[]{:S(2)}, u32[]{:S(2)}) collective-permute-start(bf16[272,256]{1,0:T(8,128)(2,1)} %get-tuple-element.39), channel_id=1, source_target_pairs={{0,1},{1,0},{2,3},{3,2},{4,8},{5,9},{6,10},{7,11},{8,4},{9,5},{10,... | collective-permute-start | bytes 417800 | tf_op jit(solution)/shard_map/ppermute | solution.py:416
  13.3 7.5 %collective-permute-start.3 = (bf16[272,256]{1,0:T(8,128)(2,1)}, bf16[272,256]{1,0:T(8,128)(2,1)S(1)}, u32[]{:S(2)}, u32[]{:S(2)}) collective-permute-start(bf16[272,256]{1,0:T(8,128)(2,1)} %get-tuple-element.40), channel_id=1, source_target_pairs={{0,1},{1,0},{2,3},{3,2},{4,9},{5,8},{6,11},{7,10},{8,5},{9,4},{10,... | collective-permute-start | bytes 417800 | tf_op jit(solution)/shard_map/ppermute | solution.py:418
  15.9 11.2 %copy-start.1 = (bf16[512,512]{1,0:T(8,128)(2,1)S(1)}, bf16[512,512]{1,0:T(8,128)(2,1)}, u32[]{:S(2)}) copy-start(bf16[512,512]{1,0:T(8,128)(2,1)} %refs_6_.1) | copy-start | bytes 1572868
  15.9 11.2 %copy-start.3 = (bf16[256,512]{1,0:T(8,128)(2,1)S(1)}, bf16[256,512]{1,0:T(8,128)(2,1)}, u32[]{:S(2)}) copy-start(bf16[256,512]{1,0:T(8,128)(2,1)} %refs_5_.1) | copy-start | bytes 786436
  15.9 11.2 %copy-start.4 = (f32[512]{0:T(512)S(1)}, f32[512]{0:T(512)}, u32[]{:S(2)}) copy-start(f32[512]{0:T(512)} %param.21) | copy-start | bytes 6148
  17.4 11.0 %copy-start.9 = (s32[16]{0:T(128)S(1)}, s32[16]{0:T(128)}, u32[]{:S(2)}) copy-start(s32[16]{0:T(128)} %window_ref.1) | copy-start | bytes 196
  21.2 5.4 %collective-permute-start.5 = (bf16[256,256]{1,0:T(8,128)(2,1)S(1)}, bf16[256,256]{1,0:T(8,128)(2,1)S(1)}, u32[]{:S(2)}, u32[]{:S(2)}) collective-permute-start(bf16[256,256]{1,0:T(8,128)(2,1)S(1)} %get-tuple-element.47), channel_id=1, source_target_pairs={{0,2},{1,3},{2,0},{3,1},{4,6},{5,7},{6,4},{7,5},{8,10},{9,11},{10,... | collective-permute-start | bytes 393224 | tf_op jit(solution)/shard_map/ppermute | solution.py:452
  21.8 5.2 %collective-permute-start.8 = (bf16[256,256]{1,0:T(8,128)(2,1)S(1)}, bf16[256,256]{1,0:T(8,128)(2,1)S(1)}, u32[]{:S(2)}, u32[]{:S(2)}) collective-permute-start(bf16[256,256]{1,0:T(8,128)(2,1)S(1)} %get-tuple-element.52), channel_id=1, source_target_pairs={{0,4},{1,5},{2,6},{3,7},{4,0},{5,1},{6,2},{7,3},{8,12},{9,13},{10,... | collective-permute-start | bytes 393224 | tf_op jit(solution)/shard_map/ppermute | solution.py:454
  21.9 5.2 %collective-permute-start.9 = (bf16[256,256]{1,0:T(8,128)(2,1)S(1)}, bf16[256,256]{1,0:T(8,128)(2,1)S(1)}, u32[]{:S(2)}, u32[]{:S(2)}) collective-permute-start(bf16[256,256]{1,0:T(8,128)(2,1)S(1)} %get-tuple-element.53), channel_id=1, source_target_pairs={{0,1},{1,0},{2,3},{3,2},{4,8},{5,9},{6,10},{7,11},{8,4},{9,5},{10,... | collective-permute-start | bytes 393224 | tf_op jit(solution)/shard_map/ppermute | solution.py:455
  27.6 3.4 %collective-permute-start.12 = (bf16[256,512]{1,0:T(8,128)(2,1)S(1)}, bf16[256,512]{1,0:T(8,128)(2,1)S(1)}, u32[]{:S(2)}, u32[]{:S(2)}) collective-permute-start(bf16[256,512]{1,0:T(8,128)(2,1)S(1)} %get-tuple-element.54.own_ref), channel_id=1, source_target_pairs={{0,1},{1,0},{2,3},{3,2},{4,5},{5,4},{6,7},{7,6},{8,9},{9,8},{10,11... | collective-permute-start | bytes 786440 | tf_op jit(solution)/shard_map/ppermute | solution.py:477
  28.7 13.6 %collective-permute-start.10 = (bf16[256,512]{1,0:T(8,128)(2,1)S(1)}, bf16[256,512]{1,0:T(8,128)(2,1)S(1)}, u32[]{:S(2)}, u32[]{:S(2)}) collective-permute-start(bf16[256,512]{1,0:T(8,128)(2,1)S(1)} %get-tuple-element.54.own_ref), channel_id=1, source_target_pairs={{0,2},{1,3},{2,0},{3,1},{4,6},{5,7},{6,4},{7,5},{8,10},{9,11},{10,... | collective-permute-start | bytes 786440 | tf_op jit(solution)/shard_map/ppermute | solution.py:478
  30.0 12.3 %collective-permute-start.11 = (bf16[256,512]{1,0:T(8,128)(2,1)S(1)}, bf16[256,512]{1,0:T(8,128)(2,1)S(1)}, u32[]{:S(2)}, u32[]{:S(2)}) collective-permute-start(bf16[256,512]{1,0:T(8,128)(2,1)S(1)} %get-tuple-element.54.own_ref), channel_id=1, source_target_pairs={{0,1},{1,0},{2,4},{3,5},{4,2},{5,3},{6,8},{7,9},{8,6},{9,7},{10,12... | collective-permute-start | bytes 786440 | tf_op jit(solution)/shard_map/ppermute | solution.py:479
  31.0 13.7 %copy-start.5 = (bf16[512,2048]{1,0:T(8,128)(2,1)S(1)}, bf16[512,2048]{1,0:T(8,128)(2,1)}, u32[]{:S(2)}) copy-start(bf16[512,2048]{1,0:T(8,128)(2,1)} %up_ref.1) | copy-start | bytes 6291460
  31.0 13.7 %copy-start.6 = (bf16[2048,512]{1,0:T(8,128)(2,1)S(1)}, bf16[2048,512]{1,0:T(8,128)(2,1)}, u32[]{:S(2)}) copy-start(bf16[2048,512]{1,0:T(8,128)(2,1)} %down_ref.1) | copy-start | bytes 6291460
  31.0 13.7 %copy-start.7 = (bf16[512,512]{1,0:T(8,128)(2,1)S(1)}, bf16[512,512]{1,0:T(8,128)(2,1)}, u32[]{:S(2)}) copy-start(bf16[512,512]{1,0:T(8,128)(2,1)} %w_out_ref.1) | copy-start | bytes 1572868
  31.0 13.7 %copy-start.8 = (f32[512]{0:T(512)S(1)}, f32[512]{0:T(512)}, u32[]{:S(2)}) copy-start(f32[512]{0:T(512)} %param.25) | copy-start | bytes 6148
  42.3 2.0 %collective-permute-start.13 = (bf16[256,512]{1,0:T(8,128)(2,1)S(1)}, bf16[256,512]{1,0:T(8,128)(2,1)S(1)}, u32[]{:S(2)}, u32[]{:S(2)}) collective-permute-start(bf16[256,512]{1,0:T(8,128)(2,1)S(1)} %collective-permute-done.10.even_ref), channel_id=1, source_target_pairs={{0,1},{1,0},{2,3},{3,2},{4,5},{5,4},{6,7},{7,6},{8,9},{9,8},{10,11... | collective-permute-start | bytes 786440 | tf_op jit(solution)/shard_map/ppermute | solution.py:502
  43.1 1.5 %collective-permute-start.14 = (bf16[256,512]{1,0:T(8,128)(2,1)S(1)}, bf16[256,512]{1,0:T(8,128)(2,1)S(1)}, u32[]{:S(2)}, u32[]{:S(2)}) collective-permute-start(bf16[256,512]{1,0:T(8,128)(2,1)S(1)} %collective-permute-done.11.odd_ref), channel_id=1, source_target_pairs={{0,1},{1,0},{2,3},{3,2},{4,5},{5,4},{6,7},{7,6},{8,9},{9,8},{10,11... | collective-permute-start | bytes 786440 | tf_op jit(solution)/shard_map/ppermute | solution.py:503
  (1 other events, 1.0 us)

commit v6 on v5

--- a/solution.py
+++ b/solution.py
@@ -35,6 +35,11 @@
 
 def dot_t(a, b):
     return lax.dot_general(a, b, (((1,), (1,)), ((), ())), preferred_element_type=jnp.float32)
+
+
+def silu(values):
+    half = 0.5 * values
+    return half + half * jnp.tanh(half)
 
 
 def layer_norm(values, gain):
@@ -99,7 +104,7 @@
     for k in range(GRID_PARTS):
         span = pl.ds(k * part, part)
         fetches[k + 1].wait()
-        message_ref[span] = jax.nn.silu(dot(grid_vmem[span], w_vmem[...])).astype(jnp.bfloat16)
+        message_ref[span] = silu(dot(grid_vmem[span], w_vmem[...])).astype(jnp.bfloat16)
     row = lax.broadcasted_iota(jnp.int32, (cap, rows), 1)
     picks = {
         key: jnp.where(row == by_slot[:, m : m + 1], 1.0, 0.0).astype(jnp.bfloat16) for m, key in enumerate(keys)
@@ -249,91 +254,86 @@
     lax.fori_loop(0, HEADS // GROUP, together, 0)
 
 
-def outer_kernel(even_ref, odd_ref, wk_ref, wv_ref, key_ref, value_ref):
+def gaps(device, start, rows, nodes):
+    total = lax.axis_size("band") * lax.axis_size("inner")
+    there = lax.axis_index("band") * lax.axis_size("inner") + lax.axis_index("inner") + device
+    lag = lax.broadcasted_iota(jnp.int32, (rows, nodes), 0) - lax.broadcasted_iota(jnp.int32, (rows, nodes), 1)
+    return jnp.where((there >= 0) & (there < total), jnp.abs(lag + (device * nodes + start)), 1 << 20)
+
+
+def extend(heads, keys, values, gap_ref, window_ref, query_ref, sums_ref, top_ref, scale):
+    scores = [dot(k, query_ref[h]) for h, k in zip(heads, keys)]
+    scores = [jnp.where(gap_ref[...] <= window_ref[h], x, -1e30) for h, x in zip(heads, scores)]
+    olds = [top_ref[h, 0:1, :] for h in heads]
+    tops = [jnp.maximum(old, jnp.max(x, axis=0, keepdims=True)) for old, x in zip(olds, scores)]
+    expos = [jnp.exp2((x - top) * scale).astype(jnp.bfloat16) for x, top in zip(scores, tops)]
+    for h, v, old, top, expo in zip(heads, values, olds, tops, expos):
+        yield h, sums_ref[h] * jnp.exp2((old - top) * scale) + dot(v, expo), top
+
+
+def outer_kernel(
+    even_ref, odd_ref, wk_ref, wv_ref, order_ref, window_ref, query_ref, sums_ref, top_ref,
+    sums_out, top_out,
+    key_ref, value_ref, gap_ref,
+):
     nodes, width = even_ref.shape
     head_dim = width // HEADS
+    per_group = LANES // head_dim
+    far = 2 - 4 * lax.rem(lax.axis_index("inner") // 2, 2)
+    scale = head_dim ** (-0.5) / math.log(2.0)
     value_ref[:, head_dim:, :] = jnp.ones_like(value_ref[:, head_dim:, :])
     project_keys(even_ref[...], wk_ref, wv_ref, key_ref, value_ref, 0)
     project_keys(odd_ref[...], wk_ref, wv_ref, key_ref, value_ref, nodes)
+    gap_ref[0:nodes] = gaps(far, 0, nodes, nodes)
+    gap_ref[nodes:] = gaps(-far, 0, nodes, nodes)
+
+    def together(i, carry):
+        heads = [order_ref[GROUP * i + k] for k in range(GROUP)]
+        widest = functools.reduce(jnp.maximum, [window_ref[h] for h in heads])
+
+        @pl.when(widest > nodes)
+        def _():
+            keys, values = [key_ref[h // per_group] for h in heads], [value_ref[h] for h in heads]
+            for h, sums, top in extend(
+                heads, keys, values, gap_ref, window_ref, query_ref, sums_ref, top_ref, scale
+            ):
+                sums_out[h] = sums
+                top_out[h] = jnp.broadcast_to(top, top_out.shape[1:])
+
+        @pl.when(widest <= nodes)
+        def _():
+            for h in heads:
+                sums_out[h] = sums_ref[h]
+                top_out[h] = top_ref[h]
+
+        return carry
+
+    lax.fori_loop(0, HEADS // GROUP, together, 0)
 
 
 def far_kernel(
-    first_ref, second_ref, far_key_ref, far_value_ref, wk_ref, wv_ref, order_ref, window_ref,
-    query_ref, sums_ref, top_ref, state_ref, w_out_ref, gain_ref, up_ref, down_ref,
+    first_ref, second_ref, wk_ref, wv_ref, window_ref, query_ref, sums_ref, top_ref,
+    state_ref, w_out_ref, gain_ref, up_ref, down_ref,
     out_ref,
     key_ref, value_ref, gap_ref, attended_ref,
 ):
     nodes, width = first_ref.shape
     head_dim = width // HEADS
     per_group = LANES // head_dim
-    total = lax.axis_size("band") * lax.axis_size("inner")
-    me = lax.axis_index("band") * lax.axis_size("inner") + lax.axis_index("inner")
-    odd = lax.rem(me, 2)
-    far = 2 - 4 * lax.rem(me // 2, 2)
-    side = 2 * odd - 1
-    first = (1 - odd) * (nodes - NEAR)
-    second = odd * NEAR
+    inner = lax.axis_index("inner")
+    odd = lax.rem(inner, 2)
     scale = head_dim ** (-0.5) / math.log(2.0)
-    absent = 1 << 20
-
     value_ref[:, head_dim:, :] = jnp.ones_like(value_ref[:, head_dim:, :])
-    by_even = odd == lax.rem(me // 2 + 1, 2)
-    beyond = jnp.where(by_even, first_ref[...], second_ref[...])
-    beyond = jnp.where(odd == 0, jnp.concatenate([beyond[NEAR:], beyond[:NEAR]], axis=0), beyond)
-    project_keys(beyond, wk_ref, wv_ref, key_ref, value_ref, 0)
-    lag = lax.broadcasted_iota(jnp.int32, (nodes, nodes), 0) - lax.broadcasted_iota(
-        jnp.int32, (nodes, nodes), 1
-    )
-
-    def gap(rows, device, offset):
-        inside = (me + device >= 0) & (me + device < total)
-        return jnp.where(inside, jnp.abs(rows + (device * nodes + offset)), absent)
-
-    gap_ref[0:NEAR] = gap(lag[0:NEAR], side, first)
-    gap_ref[NEAR:nodes] = gap(lag[0:NEAR], side, second)
-    gap_ref[nodes : 2 * nodes] = gap(lag, far, 0)
-    gap_ref[2 * nodes : 3 * nodes] = gap(lag, -far, 0)
-
-    def attend(heads, rows):
-        close = min(rows, nodes)
-        scores = [dot(key_ref[h // per_group, 0:close, :], query_ref[h]) for h in heads]
-        if rows > close:
-            scores = [
-                jnp.concatenate([x, dot(far_key_ref[h // per_group], query_ref[h])], axis=0)
-                for h, x in zip(heads, scores)
-            ]
-        scores = [
-            jnp.where(gap_ref[0:rows] <= window_ref[h], x, -1e30) for h, x in zip(heads, scores)
-        ]
-        olds = [top_ref[h, 0:1, :] for h in heads]
-        tops = [jnp.maximum(old, jnp.max(x, axis=0, keepdims=True)) for old, x in zip(olds, scores)]
-        expos = [jnp.exp2((x - top) * scale).astype(jnp.bfloat16) for x, top in zip(scores, tops)]
-        for h, old, top, expo in zip(heads, olds, tops, expos):
-            sums = sums_ref[h] * jnp.exp2((old - top) * scale)
-            sums += dot(value_ref[h, :, 0:close], expo[0:close])
-            if rows > close:
-                sums += dot(far_value_ref[h], expo[close:])
+    by_even = odd == lax.rem(inner // 2 + 1, 2)
+    project_keys(jnp.where(by_even, first_ref[...], second_ref[...]), wk_ref, wv_ref, key_ref, value_ref, 0)
+    gap_ref[...] = gaps(2 * odd - 1, 0, nodes, nodes)
+    for i in range(HEADS // GROUP):
+        heads = range(GROUP * i, GROUP * (i + 1))
+        keys, values = [key_ref[h // per_group] for h in heads], [value_ref[h] for h in heads]
+        for h, sums, _ in extend(
+            heads, keys, values, gap_ref, window_ref, query_ref, sums_ref, top_ref, scale
+        ):
             attended_ref[h] = (sums[0:head_dim] / sums[head_dim : head_dim + 1]).astype(jnp.bfloat16)
-
-    def together(i, carry):
-        heads = [order_ref[GROUP * i + k] for k in range(GROUP)]
-        widest = functools.reduce(jnp.maximum, [window_ref[h] for h in heads])
-
-        @pl.when(widest <= NEAR)
-        def _():
-            attend(heads, NEAR)
-
-        @pl.when((widest > NEAR) & (widest <= nodes))
-        def _():
-            attend(heads, nodes)
-
-        @pl.when(widest > nodes)
-        def _():
-            attend(heads, 3 * nodes)
-
-        return carry
-
-    lax.fori_loop(0, HEADS // GROUP, together, 0)
 
     attended = attended_ref[...].reshape(width, nodes)
     mixed = lax.dot_general(
@@ -341,8 +341,12 @@
     )
     mid = state_ref[...] + mixed
     normed = layer_norm(mid, gain_ref[...]).astype(jnp.bfloat16)
-    hidden = jax.nn.silu(dot(normed, up_ref[...])).astype(jnp.bfloat16)
-    out_ref[...] = (mid + dot(hidden, down_ref[...])).astype(jnp.bfloat16)
+    total = mid
+    chunk = math.gcd(up_ref.shape[1], 512)
+    for start in range(0, up_ref.shape[1], chunk):
+        hidden = silu(dot(normed, up_ref[:, start : start + chunk])).astype(jnp.bfloat16)
+        total = total + dot(hidden, down_ref[start : start + chunk, :])
+    out_ref[...] = total.astype(jnp.bfloat16)
 
 
 def cost(flops, size):
@@ -411,12 +415,16 @@
     def chip_trade(p, k=0):
         return [(g, g ^ (2 * p + k)) for g in range(devices)]
 
-    cross = [lax.ppermute(c, NODES, chip_trade(n // 2 + 1, n % 2)) for n, c in enumerate(cross)]
+    here_other = lax.ppermute(here_other, NODES, beside)
+    cross[0::2] = [lax.ppermute(c, NODES, chip_trade(p + 1)) for p, c in enumerate(cross[0::2])]
     even = lax.ppermute(even, NODES, bands_trade(0))
     odd = lax.ppermute(odd, NODES, bands_trade(1))
+    here_other, even_other, odd_other, *cross[1::2] = lax.optimization_barrier(
+        (here_other, even_other, odd_other, *cross[1::2])
+    )
+    cross[1::2] = [lax.ppermute(c, NODES, chip_trade(p + 1, 1)) for p, c in enumerate(cross[1::2])]
     even_other = lax.ppermute(even_other, NODES, bands_trade(0, 1))
     odd_other = lax.ppermute(odd_other, NODES, bands_trade(1, 1))
-    here_other = lax.ppermute(here_other, NODES, beside)
 
     w_qkv, window, here = lax.optimization_barrier((w_qkv, window, here))
     w_query, w_key, w_value, early_left, early_right = pl.pallas_call(
@@ -501,35 +509,40 @@
     even, odd, near, top = lax.optimization_barrier((even, odd, near, top))
     first = lax.ppermute(even, NODES, beside)
     second = lax.ppermute(odd, NODES, beside)
-    keys, values = pl.pallas_call(
+    near, top = pl.pallas_call(
         outer_kernel,
         out_shape=[
-            jax.ShapeDtypeStruct((width // LANES, 2 * nodes, LANES), bf16),
-            jax.ShapeDtypeStruct((HEADS, extra, 2 * nodes), bf16),
-        ],
-        in_specs=[VMEM] * 4,
+            jax.ShapeDtypeStruct((HEADS, extra, nodes), f32),
+            jax.ShapeDtypeStruct((HEADS, 8, nodes), f32),
+        ],
+        in_specs=[VMEM] * 4 + [SMEM] * 2 + [VMEM] * 3,
         out_specs=[VMEM] * 2,
-        compiler_params=params(16),
-        cost_estimate=cost(8 * nodes * width * width, 3 << 20),
+        scratch_shapes=[
+            pltpu.VMEM((width // LANES, 2 * nodes, LANES), bf16),
+            pltpu.VMEM((HEADS, extra, 2 * nodes), bf16),
+            pltpu.VMEM((2 * nodes, nodes), i32),
+        ],
+        compiler_params=params(24),
+        cost_estimate=cost(16 * nodes * width * width, 3 << 20),
         name="outer",
-    )(even, odd, w_key, w_value)
+    )(even, odd, w_key, w_value, order, window, query, near, top)
 
     return pl.pallas_call(
         far_kernel,
         out_shape=jax.ShapeDtypeStruct((nodes, width), bf16),
-        in_specs=[VMEM] * 6 + [SMEM] * 2 + [VMEM] * 8,
+        in_specs=[VMEM] * 4 + [SMEM] + [VMEM] * 8,
         out_specs=VMEM,
         scratch_shapes=[
             pltpu.VMEM((width // LANES, nodes, LANES), bf16),
             pltpu.VMEM((HEADS, extra, nodes), bf16),
-            pltpu.VMEM((3 * nodes, nodes), i32),
+            pltpu.VMEM((nodes, nodes), i32),
             pltpu.VMEM((HEADS, head_dim, nodes), bf16),
         ],
         compiler_params=params(40),
         cost_estimate=cost(8 << 30, 8 << 20),
         name="far",
     )(
-        first, second, keys, values, w_key, w_value, order, window,
+        first, second, w_key, w_value, window,
         query, near, top, state, w_out, gain_mlp.reshape(1, width), w_up, w_down,
     )
 

time: 52.4 us -> 51.1 us (0.975)
  the two profiles are of different devices: /device:TPU:15 before, /device:TPU:17 now
where the time goes in v6:
time: 51.1 us; the launch traced here: 50.9 us
  Pallas kernels  22.2 us (43%)
  waiting for transfers between devices  15.8 us (31%)
  starting transfers between devices  11.4 us (22%)
  local copies, waits for them, and re-layouts  1.02 us (2%)
    ppermute x1, waiting for transfers between devices, local(): even = lax.ppermute(normed, NODES, chips_trade(0))  7.28 us
    pallas_call x1, Pallas kernels, local(): pl.pallas_call(functools.partial(message_kernel, pairs), out_shape=outgoi...  5.9 us
    pallas_call x1, Pallas kernels, local(): pl.pallas_call(far_kernel, out_shape=jax.ShapeDtypeStruct((nodes, width),...  5.51 us
    pallas_call x1, Pallas kernels, local(): pl.pallas_call(near_kernel, out_shape=[jax.ShapeDtypeStruct((HEADS, LANES...  5.02 us
    pallas_call x1, Pallas kernels, local(): pl.pallas_call(outer_kernel, out_shape=[jax.ShapeDtypeStruct((HEADS, extr...  3.27 us
    ppermute x1, waiting for transfers between devices, local(): lax.ppermute(part, NODES, chip_trade(p + 1))  3.02 us
    ppermute x1, waiting for transfers between devices, local(): odd_other = lax.ppermute(odd_other, NODES, bands_trade(1, 1))  2.83 us
    ppermute x1, starting transfers between devices, local(): side = lax.ppermute(normed, NODES, beside)  1.58 us
  transfers between devices with their start and end apart: 15, of which 8 were waited for; matrix products, arithmetic and copies ran while one was open for 1% of the time, Pallas kernels for 20%

profile of v6, /device:TPU:17, one launch (start us, length us, event | category | flops | bytes accessed | tf_op | source)
XLA Modules:
  0.0 50.9 jit_solution(9113686029518406197)
XLA Ops:
  0.0 5.9 %messages.1 = (bf16[272,256]{1,0:T(8,128)(2,1)}, bf16[272,256]{1,0:T(8,128)(2,1)}, bf16[272,256]{1,0:T(8,128)(2,1)}, bf16[272,256]{1,0:T(8,128)(2,1)}, bf16[400,...) custom-call(bf16[1024,512]{1,0:T(8,128)(2,1)} %grid_ref.1, ...), custom_call_target="tpu_custom_call" | custom-call | flops 2147483648 | bytes 4194304 | tf_op jit(solution)/shard_map/messages/pallas_call | solution.py:388
  5.9 0.7 %collective-permute-start.1 = (bf16[672,256]{1,0:T(8,128)(2,1)}, bf16[672,256]{1,0:T(8,128)(2,1)S(1)}, u32[]{:S(2)}, u32[]{:S(2)}) collective-permute-start(bf16[672,256]{1,0:T(8,128)(2,1)} %get-tuple-element.42), channel_id=1, source_target_pairs={{0,1},{1,0},{2,3},{3,2},{4,5},{5,4},{6,7},{7,6},{8,9},{9,8},{10,11... | collective-permute-start | bytes 1032200 | tf_op jit(solution)/shard_map/ppermute | solution.py:418
  6.6 1.3 %collective-permute-start = (bf16[272,256]{1,0:T(8,128)(2,1)}, bf16[272,256]{1,0:T(8,128)(2,1)S(1)}, u32[]{:S(2)}, u32[]{:S(2)}) collective-permute-start(bf16[272,256]{1,0:T(8,128)(2,1)} %get-tuple-element.41), channel_id=1, source_target_pairs={{0,4},{1,5},{2,6},{3,7},{4,0},{5,1},{6,2},{7,3},{8,12},{9,13},{10,... | collective-permute-start | bytes 417800 | tf_op jit(solution)/shard_map/ppermute | solution.py:420
  8.0 1.2 %collective-permute-start.6 = (bf16[400,256]{1,0:T(8,128)(2,1)}, bf16[400,256]{1,0:T(8,128)(2,1)S(1)}, u32[]{:S(2)}, u32[]{:S(2)}) collective-permute-start(bf16[400,256]{1,0:T(8,128)(2,1)} %get-tuple-element.56), channel_id=1, source_target_pairs={{0,2},{1,3},{2,0},{3,1},{4,6},{5,7},{6,4},{7,5},{8,10},{9,11},{10,... | collective-permute-start | bytes 614408 | tf_op jit(solution)/shard_map/ppermute | solution.py:419
  9.2 0.8 %collective-permute-start.7 = (bf16[400,256]{1,0:T(8,128)(2,1)}, bf16[400,256]{1,0:T(8,128)(2,1)S(1)}, u32[]{:S(2)}, u32[]{:S(2)}) collective-permute-start(bf16[400,256]{1,0:T(8,128)(2,1)} %get-tuple-element.57), channel_id=1, source_target_pairs={{0,3},{1,2},{2,1},{3,0},{4,7},{5,6},{6,5},{7,4},{8,11},{9,10},{10,... | collective-permute-start | bytes 614408 | tf_op jit(solution)/shard_map/ppermute | solution.py:425
  9.9 1.4 %collective-permute-start.2 = (bf16[272,256]{1,0:T(8,128)(2,1)}, bf16[272,256]{1,0:T(8,128)(2,1)S(1)}, u32[]{:S(2)}, u32[]{:S(2)}) collective-permute-start(bf16[272,256]{1,0:T(8,128)(2,1)} %get-tuple-element.46), channel_id=1, source_target_pairs={{0,5},{1,4},{2,7},{3,6},{4,1},{5,0},{6,3},{7,2},{8,13},{9,12},{10,... | collective-permute-start | bytes 417800 | tf_op jit(solution)/shard_map/ppermute | solution.py:426
  11.3 0.8 %collective-permute-done.refs_0_ = bf16[272,256]{1,0:T(8,128)(2,1)S(1)} collective-permute-done((bf16[272,256]{1,0:T(8,128)(2,1)}, bf16[272,256]{1,0:T(8,128)(2,1)S(1)}, u32[]{:S(2)}, u32[]{:S(2)}) %collective-permute-start) | collective-permute-done | bytes 139296 | tf_op jit(solution)/shard_map/ppermute | solution.py:420
  12.1 0.9 %collective-permute-start.4 = (bf16[272,256]{1,0:T(8,128)(2,1)}, bf16[272,256]{1,0:T(8,128)(2,1)S(1)}, u32[]{:S(2)}, u32[]{:S(2)}) collective-permute-start(bf16[272,256]{1,0:T(8,128)(2,1)} %get-tuple-element.48), channel_id=1, source_target_pairs={{0,1},{1,0},{2,3},{3,2},{4,9},{5,8},{6,11},{7,10},{8,5},{9,4},{10,... | collective-permute-start | bytes 417800 | tf_op jit(solution)/shard_map/ppermute | solution.py:427
  13.0 1.0 %copy-done.2 = bf16[672,256]{1,0:T(8,128)(2,1)S(1)} copy-done((bf16[672,256]{1,0:T(8,128)(2,1)S(1)}, bf16[672,256]{1,0:T(8,128)(2,1)}, u32[]{:S(2)}) %copy-start.2) | copy-done | bytes 344088
  14.0 1.5 %early.1 = (bf16[512,512]{1,0:T(8,128)(2,1)S(1)}, bf16[512,512]{1,0:T(8,128)(2,1)S(1)}, bf16[512,512]{1,0:T(8,128)(2,1)S(1)}, f32[2,256,256]{2,1,0:T(8,128)S(1)}, f32[3,256,256]{2,1,0:T(8,128)S(1)}) custom-call(bf16[512,1536]{1,0:T(8,128)(2,1)S(1)} %copy-done, bf16[672,256]{1,0:T(8,128)(2,1)S(1)} %copy-done.2, ...), custom_call_target="tpu_custom_call" | custom-call | flops 268435456 | bytes 4194304 | tf_op jit(solution)/shard_map/early/pallas_call | solution.py:430
  15.6 0.4 collective-permute-done.2.refs_1_
  16.0 2.8 %collective-permute-done.4.refs_3_ = bf16[272,256]{1,0:T(8,128)(2,1)S(1)} collective-permute-done((bf16[272,256]{1,0:T(8,128)(2,1)}, bf16[272,256]{1,0:T(8,128)(2,1)S(1)}, u32[]{:S(2)}, u32[]{:S(2)}) %collective-permute-start.4) | collective-permute-done | bytes 139296 | tf_op jit(solution)/shard_map/ppermute | solution.py:427
  18.8 0.3 left.1
  19.1 1.3 %collective-permute-start.5 = (bf16[256,256]{1,0:T(8,128)(2,1)S(1)}, bf16[256,256]{1,0:T(8,128)(2,1)S(1)}, u32[]{:S(2)}, u32[]{:S(2)}) collective-permute-start(bf16[256,256]{1,0:T(8,128)(2,1)S(1)} %get-tuple-element.55), channel_id=1, source_target_pairs={{0,2},{1,3},{2,0},{3,1},{4,6},{5,7},{6,4},{7,5},{8,10},{9,11},{10,... | collective-permute-start | bytes 393224 | tf_op jit(solution)/shard_map/ppermute | solution.py:460
  20.9 3.0 %collective-permute-done.5.refs_1_ = bf16[256,256]{1,0:T(8,128)(2,1)S(1)} collective-permute-done((bf16[256,256]{1,0:T(8,128)(2,1)S(1)}, bf16[256,256]{1,0:T(8,128)(2,1)S(1)}, u32[]{:S(2)}, u32[]{:S(2)}) %collective-permute-start.5) | collective-permute-done | bytes 131104 | tf_op jit(solution)/shard_map/ppermute | solution.py:460
  23.9 1.3 %collective-permute-done.8.refs_3_ = bf16[256,256]{1,0:T(8,128)(2,1)S(1)} collective-permute-done((bf16[256,256]{1,0:T(8,128)(2,1)S(1)}, bf16[256,256]{1,0:T(8,128)(2,1)S(1)}, u32[]{:S(2)}, u32[]{:S(2)}) %collective-permute-start.8) | collective-permute-done | bytes 131104 | tf_op jit(solution)/shard_map/ppermute | solution.py:462
  25.3 0.5 merge.1
  25.8 1.6 %collective-permute-start.12 = (bf16[256,512]{1,0:T(8,128)(2,1)S(1)}, bf16[256,512]{1,0:T(8,128)(2,1)S(1)}, u32[]{:S(2)}, u32[]{:S(2)}) collective-permute-start(bf16[256,512]{1,0:T(8,128)(2,1)S(1)} %get-tuple-element.62.own_ref), channel_id=1, source_target_pairs={{0,1},{1,0},{2,3},{3,2},{4,5},{5,4},{6,7},{7,6},{8,9},{9,8},{10,11... | collective-permute-start | bytes 786440 | tf_op jit(solution)/shard_map/ppermute | solution.py:485
  27.9 0.9 %collective-permute-start.11 = (bf16[256,512]{1,0:T(8,128)(2,1)S(1)}, bf16[256,512]{1,0:T(8,128)(2,1)S(1)}, u32[]{:S(2)}, u32[]{:S(2)}) collective-permute-start(bf16[256,512]{1,0:T(8,128)(2,1)S(1)} %get-tuple-element.62.own_ref), channel_id=1, source_target_pairs={{0,1},{1,0},{2,4},{3,5},{4,2},{5,3},{6,8},{7,9},{8,6},{9,7},{10,12... | collective-permute-start | bytes 786440 | tf_op jit(solution)/shard_map/ppermute | solution.py:487
  28.9 5.0 %near.1 = (bf16[16,128,256]{2,1,0:T(8,128)(2,1)S(1)}, f32[16,48,256]{2,1,0:T(8,128)S(1)}, f32[16,8,256]{2,1,0:T(8,128)S(1)}) custom-call(bf16[256,512]{1,0:T(8,128)(2,1)S(1)} %get-tuple-element.62.own_ref, bf16[256,512]{1,0:T(8,128)(2,1)S(1)} %collective-permute-done.12.side_ref, bf16[512,512]{1,0:T(8,128)(2,1)S(1)} %get-tuple-element.63.wq_ref, ...), custom_call_target="tpu_custom_call" | custom-call | flops 8589934592 | bytes 4194304 | tf_op jit(solution)/shard_map/near/pallas_call | solution.py:490
  34.0 7.3 %collective-permute-done.10.even_ref = bf16[256,512]{1,0:T(8,128)(2,1)S(1)} collective-permute-done((bf16[256,512]{1,0:T(8,128)(2,1)S(1)}, bf16[256,512]{1,0:T(8,128)(2,1)S(1)}, u32[]{:S(2)}, u32[]{:S(2)}) %collective-permute-start.10) | collective-permute-done | bytes 262176 | tf_op jit(solution)/shard_map/ppermute | solution.py:486
  41.2 0.8 %collective-permute-start.13 = (bf16[256,512]{1,0:T(8,128)(2,1)S(1)}, bf16[256,512]{1,0:T(8,128)(2,1)S(1)}, u32[]{:S(2)}, u32[]{:S(2)}) collective-permute-start(bf16[256,512]{1,0:T(8,128)(2,1)S(1)} %collective-permute-done.10.even_ref), channel_id=1, source_target_pairs={{0,1},{1,0},{2,3},{3,2},{4,5},{5,4},{6,7},{7,6},{8,9},{9,8},{10,11... | collective-permute-start | bytes 786440 | tf_op jit(solution)/shard_map/ppermute | solution.py:510
  42.1 3.3 %outer.1 = (f32[16,48,256]{2,1,0:T(8,128)S(1)}, f32[16,8,256]{2,1,0:T(8,128)S(1)}) custom-call(bf16[256,512]{1,0:T(8,128)(2,1)S(1)} %collective-permute-done.10.even_ref, bf16[256,512]{1,0:T(8,128)(2,1)S(1)} %collective-permute-done.11.odd_ref, bf16[512,512]{1,0:T(8,128)(2,1)S(1)} %get-tuple-element.64.wk_ref, ...), custom_call_target="tpu_custom_call" | custom-call | flops 1073741824 | bytes 3145728 | tf_op jit(solution)/shard_map/outer/pallas_call | solution.py:512
  45.4 5.5 %far.1 = bf16[256,512]{1,0:T(8,128)(2,1)} custom-call(bf16[256,512]{1,0:T(8,128)(2,1)S(1)} %collective-permute-done.13.first_ref, bf16[256,512]{1,0:T(8,128)(2,1)S(1)} %collective-permute-done.14.second_ref, bf16[512,512]{1,0:T(8,128)(2,1)S(1)} %get-tuple-element.64.wk_ref, bf16[512,512]{1,0:T(8,128)(2,1)S(1)} %get-tuple-element.65.wv_ref, s32[16]{0:T(128)S(1)} %copy-done.9, ...), custom_call_target="tpu_custom_call" | custom-call | flops 8589934592 | bytes 8388608 | tf_op jit(solution)/shard_map/far/pallas_call | solution.py:530
  (36 shorter events, 1.2 us)
Async XLA Ops:
  0.0 13.0 %copy-start = (bf16[512,1536]{1,0:T(8,128)(2,1)S(1)}, bf16[512,1536]{1,0:T(8,128)(2,1)}, u32[]{:S(2)}) copy-start(bf16[512,1536]{1,0:T(8,128)(2,1)} %w_ref.2) | copy-start | bytes 4718596
  5.9 3.3 %collective-permute-start.1 = (bf16[672,256]{1,0:T(8,128)(2,1)}, bf16[672,256]{1,0:T(8,128)(2,1)S(1)}, u32[]{:S(2)}, u32[]{:S(2)}) collective-permute-start(bf16[672,256]{1,0:T(8,128)(2,1)} %get-tuple-element.42), channel_id=1, source_target_pairs={{0,1},{1,0},{2,3},{3,2},{4,5},{5,4},{6,7},{7,6},{8,9},{9,8},{10,11... | collective-permute-start | bytes 1032200 | tf_op jit(solution)/shard_map/ppermute | solution.py:418
  6.6 5.5 %collective-permute-start = (bf16[272,256]{1,0:T(8,128)(2,1)}, bf16[272,256]{1,0:T(8,128)(2,1)S(1)}, u32[]{:S(2)}, u32[]{:S(2)}) collective-permute-start(bf16[272,256]{1,0:T(8,128)(2,1)} %get-tuple-element.41), channel_id=1, source_target_pairs={{0,4},{1,5},{2,6},{3,7},{4,0},{5,1},{6,2},{7,3},{8,12},{9,13},{10,... | collective-permute-start | bytes 417800 | tf_op jit(solution)/shard_map/ppermute | solution.py:420
  8.0 12.5 %collective-permute-start.6 = (bf16[400,256]{1,0:T(8,128)(2,1)}, bf16[400,256]{1,0:T(8,128)(2,1)S(1)}, u32[]{:S(2)}, u32[]{:S(2)}) collective-permute-start(bf16[400,256]{1,0:T(8,128)(2,1)} %get-tuple-element.56), channel_id=1, source_target_pairs={{0,2},{1,3},{2,0},{3,1},{4,6},{5,7},{6,4},{7,5},{8,10},{9,11},{10,... | collective-permute-start | bytes 614408 | tf_op jit(solution)/shard_map/ppermute | solution.py:419
  9.2 11.2 %collective-permute-start.7 = (bf16[400,256]{1,0:T(8,128)(2,1)}, bf16[400,256]{1,0:T(8,128)(2,1)S(1)}, u32[]{:S(2)}, u32[]{:S(2)}) collective-permute-start(bf16[400,256]{1,0:T(8,128)(2,1)} %get-tuple-element.57), channel_id=1, source_target_pairs={{0,3},{1,2},{2,1},{3,0},{4,7},{5,6},{6,5},{7,4},{8,11},{9,10},{10,... | collective-permute-start | bytes 614408 | tf_op jit(solution)/shard_map/ppermute | solution.py:425
  9.9 5.6 %collective-permute-start.3 = (bf16[272,256]{1,0:T(8,128)(2,1)}, bf16[272,256]{1,0:T(8,128)(2,1)S(1)}, u32[]{:S(2)}, u32[]{:S(2)}) collective-permute-start(bf16[272,256]{1,0:T(8,128)(2,1)} %get-tuple-element.47), channel_id=1, source_target_pairs={{0,1},{1,0},{2,3},{3,2},{4,8},{5,9},{6,10},{7,11},{8,4},{9,5},{10,... | collective-permute-start | bytes 417800 | tf_op jit(solution)/shard_map/ppermute | solution.py:421
  9.9 6.1 %collective-permute-start.2 = (bf16[272,256]{1,0:T(8,128)(2,1)}, bf16[272,256]{1,0:T(8,128)(2,1)S(1)}, u32[]{:S(2)}, u32[]{:S(2)}) collective-permute-start(bf16[272,256]{1,0:T(8,128)(2,1)} %get-tuple-element.46), channel_id=1, source_target_pairs={{0,5},{1,4},{2,7},{3,6},{4,1},{5,0},{6,3},{7,2},{8,13},{9,12},{10,... | collective-permute-start | bytes 417800 | tf_op jit(solution)/shard_map/ppermute | solution.py:426
  12.1 6.7 %collective-permute-start.4 = (bf16[272,256]{1,0:T(8,128)(2,1)}, bf16[272,256]{1,0:T(8,128)(2,1)S(1)}, u32[]{:S(2)}, u32[]{:S(2)}) collective-permute-start(bf16[272,256]{1,0:T(8,128)(2,1)} %get-tuple-element.48), channel_id=1, source_target_pairs={{0,1},{1,0},{2,3},{3,2},{4,9},{5,8},{6,11},{7,10},{8,5},{9,4},{10,... | collective-permute-start | bytes 417800 | tf_op jit(solution)/shard_map/ppermute | solution.py:427
  14.0 11.3 %copy-start.1 = (bf16[512,512]{1,0:T(8,128)(2,1)S(1)}, bf16[512,512]{1,0:T(8,128)(2,1)}, u32[]{:S(2)}) copy-start(bf16[512,512]{1,0:T(8,128)(2,1)} %refs_6_.1) | copy-start | bytes 1572868
  14.0 11.3 %copy-start.3 = (bf16[256,512]{1,0:T(8,128)(2,1)S(1)}, bf16[256,512]{1,0:T(8,128)(2,1)}, u32[]{:S(2)}) copy-start(bf16[256,512]{1,0:T(8,128)(2,1)} %refs_5_.1) | copy-start | bytes 786436
  14.0 11.3 %copy-start.4 = (f32[512]{0:T(512)S(1)}, f32[512]{0:T(512)}, u32[]{:S(2)}) copy-start(f32[512]{0:T(512)} %param.21) | copy-start | bytes 6148
  15.5 11.9 %copy-start.9 = (s32[16]{0:T(128)S(1)}, s32[16]{0:T(128)}, u32[]{:S(2)}) copy-start(s32[16]{0:T(128)} %window_ref.2) | copy-start | bytes 196
  19.1 4.8 %collective-permute-start.5 = (bf16[256,256]{1,0:T(8,128)(2,1)S(1)}, bf16[256,256]{1,0:T(8,128)(2,1)S(1)}, u32[]{:S(2)}, u32[]{:S(2)}) collective-permute-start(bf16[256,256]{1,0:T(8,128)(2,1)S(1)} %get-tuple-element.55), channel_id=1, source_target_pairs={{0,2},{1,3},{2,0},{3,1},{4,6},{5,7},{6,4},{7,5},{8,10},{9,11},{10,... | collective-permute-start | bytes 393224 | tf_op jit(solution)/shard_map/ppermute | solution.py:460
  20.7 4.5 %collective-permute-start.8 = (bf16[256,256]{1,0:T(8,128)(2,1)S(1)}, bf16[256,256]{1,0:T(8,128)(2,1)S(1)}, u32[]{:S(2)}, u32[]{:S(2)}) collective-permute-start(bf16[256,256]{1,0:T(8,128)(2,1)S(1)} %get-tuple-element.60), channel_id=1, source_target_pairs={{0,4},{1,5},{2,6},{3,7},{4,0},{5,1},{6,2},{7,3},{8,12},{9,13},{10,... | collective-permute-start | bytes 393224 | tf_op jit(solution)/shard_map/ppermute | solution.py:462
  20.8 4.5 %collective-permute-start.9 = (bf16[256,256]{1,0:T(8,128)(2,1)S(1)}, bf16[256,256]{1,0:T(8,128)(2,1)S(1)}, u32[]{:S(2)}, u32[]{:S(2)}) collective-permute-start(bf16[256,256]{1,0:T(8,128)(2,1)S(1)} %get-tuple-element.61), channel_id=1, source_target_pairs={{0,1},{1,0},{2,3},{3,2},{4,8},{5,9},{6,10},{7,11},{8,4},{9,5},{10,... | collective-permute-start | bytes 393224 | tf_op jit(solution)/shard_map/ppermute | solution.py:463
  25.8 3.1 %collective-permute-start.12 = (bf16[256,512]{1,0:T(8,128)(2,1)S(1)}, bf16[256,512]{1,0:T(8,128)(2,1)S(1)}, u32[]{:S(2)}, u32[]{:S(2)}) collective-permute-start(bf16[256,512]{1,0:T(8,128)(2,1)S(1)} %get-tuple-element.62.own_ref), channel_id=1, source_target_pairs={{0,1},{1,0},{2,3},{3,2},{4,5},{5,4},{6,7},{7,6},{8,9},{9,8},{10,11... | collective-permute-start | bytes 786440 | tf_op jit(solution)/shard_map/ppermute | solution.py:485
  27.6 13.6 %collective-permute-start.10 = (bf16[256,512]{1,0:T(8,128)(2,1)S(1)}, bf16[256,512]{1,0:T(8,128)(2,1)S(1)}, u32[]{:S(2)}, u32[]{:S(2)}) collective-permute-start(bf16[256,512]{1,0:T(8,128)(2,1)S(1)} %get-tuple-element.62.own_ref), channel_id=1, source_target_pairs={{0,2},{1,3},{2,0},{3,1},{4,6},{5,7},{6,4},{7,5},{8,10},{9,11},{10,... | collective-permute-start | bytes 786440 | tf_op jit(solution)/shard_map/ppermute | solution.py:486
  27.9 13.3 %collective-permute-start.11 = (bf16[256,512]{1,0:T(8,128)(2,1)S(1)}, bf16[256,512]{1,0:T(8,128)(2,1)S(1)}, u32[]{:S(2)}, u32[]{:S(2)}) collective-permute-start(bf16[256,512]{1,0:T(8,128)(2,1)S(1)} %get-tuple-element.62.own_ref), channel_id=1, source_target_pairs={{0,1},{1,0},{2,4},{3,5},{4,2},{5,3},{6,8},{7,9},{8,6},{9,7},{10,12... | collective-permute-start | bytes 786440 | tf_op jit(solution)/shard_map/ppermute | solution.py:487
  28.9 16.5 %copy-start.6 = (bf16[2048,512]{1,0:T(8,128)(2,1)S(1)}, bf16[2048,512]{1,0:T(8,128)(2,1)}, u32[]{:S(2)}) copy-start(bf16[2048,512]{1,0:T(8,128)(2,1)} %down_ref.1) | copy-start | bytes 6291460
  33.9 11.4 %copy-start.5 = (bf16[512,2048]{1,0:T(8,128)(2,1)S(1)}, bf16[512,2048]{1,0:T(8,128)(2,1)}, u32[]{:S(2)}) copy-start(bf16[512,2048]{1,0:T(8,128)(2,1)} %up_ref.1) | copy-start | bytes 6291460
  33.9 11.4 %copy-start.7 = (bf16[512,512]{1,0:T(8,128)(2,1)S(1)}, bf16[512,512]{1,0:T(8,128)(2,1)}, u32[]{:S(2)}) copy-start(bf16[512,512]{1,0:T(8,128)(2,1)} %w_out_ref.1) | copy-start | bytes 1572868
  34.0 11.4 %copy-start.8 = (f32[512]{0:T(512)S(1)}, f32[512]{0:T(512)}, u32[]{:S(2)}) copy-start(f32[512]{0:T(512)} %param.25) | copy-start | bytes 6148
  41.2 4.1 %collective-permute-start.13 = (bf16[256,512]{1,0:T(8,128)(2,1)S(1)}, bf16[256,512]{1,0:T(8,128)(2,1)S(1)}, u32[]{:S(2)}, u32[]{:S(2)}) collective-permute-start(bf16[256,512]{1,0:T(8,128)(2,1)S(1)} %collective-permute-done.10.even_ref), channel_id=1, source_target_pairs={{0,1},{1,0},{2,3},{3,2},{4,5},{5,4},{6,7},{7,6},{8,9},{9,8},{10,11... | collective-permute-start | bytes 786440 | tf_op jit(solution)/shard_map/ppermute | solution.py:510
  42.1 3.3 %collective-permute-start.14 = (bf16[256,512]{1,0:T(8,128)(2,1)S(1)}, bf16[256,512]{1,0:T(8,128)(2,1)S(1)}, u32[]{:S(2)}, u32[]{:S(2)}) collective-permute-start(bf16[256,512]{1,0:T(8,128)(2,1)S(1)} %collective-permute-done.11.odd_ref), channel_id=1, source_target_pairs={{0,1},{1,0},{2,3},{3,2},{4,5},{5,4},{6,7},{7,6},{8,9},{9,8},{10,11... | collective-permute-start | bytes 786440 | tf_op jit(solution)/shard_map/ppermute | solution.py:511
  (1 other events, 1.0 us)

commit v7 on v6

--- a/solution.py
+++ b/solution.py
@@ -14,7 +14,7 @@
 NEAR = 128
 TILE = 16
 CAP = 128
-GRID_PARTS = 4
+GRID_PARTS = 2
 MOST = 56
 GROUP = 4
 
@@ -72,7 +72,7 @@
 def message_kernel(pair_count, grid_ref, w_ref, source_ref, target_ref, count_ref, *refs):
     count = 4 + 2 * pair_count
     out_refs, out_vmems = refs[:count], refs[count : 2 * count]
-    grid_vmem, w_vmem, message_ref, in_sems, out_sems = refs[2 * count :]
+    grid_vmem, w_vmem, message_ref, pick_ref, in_sems, out_sems = refs[2 * count :]
     rows = grid_ref.shape[0]
     cap = source_ref.shape[-1]
     half = w_ref.shape[1] // 2
@@ -85,7 +85,7 @@
         fetch.start()
     inner = lax.axis_index("inner")
     offsets = band_offsets()
-    keys = [(t, p, k) for t in range(3) for p in range(pair_count) for k in range(2)]
+    keys = [(t, p, k) for k in range(2) for t in range(3) for p in range(pair_count)]
     place = {(t, p, k): (offsets[t], inner ^ (2 * p + k)) for t, p, k in keys}
     by_slot = slot_columns(source_ref, [place[key] for key in keys])
     left, right = slice(0, half), slice(half, 2 * half)
@@ -100,25 +100,32 @@
             start += len(chosen) * cap
             out_vmem[start : start + TILE, :] = target_tile(target_ref, count_ref, [place[key] for key in chosen], half)
             start += TILE
+    row = lax.broadcasted_iota(jnp.int32, (cap, rows), 1)
+    for m in range(len(keys)):
+        pick_ref[m * cap : (m + 1) * cap, :] = jnp.where(row == by_slot[:, m : m + 1], 1.0, 0.0).astype(jnp.bfloat16)
     fetches[0].wait()
     for k in range(GRID_PARTS):
         span = pl.ds(k * part, part)
         fetches[k + 1].wait()
         message_ref[span] = silu(dot(grid_vmem[span], w_vmem[...])).astype(jnp.bfloat16)
-    row = lax.broadcasted_iota(jnp.int32, (cap, rows), 1)
-    picks = {
-        key: jnp.where(row == by_slot[:, m : m + 1], 1.0, 0.0).astype(jnp.bfloat16) for m, key in enumerate(keys)
-    }
     sends = []
-    for n in reversed(range(count)):
-        start = 0
-        for chosen, lanes in runs[n]:
-            taken = dot(jnp.concatenate([picks[key] for key in chosen], axis=0), message_ref[:, lanes])
-            out_vmems[n][start : start + len(chosen) * cap, :] = taken.astype(jnp.bfloat16)
-            start += len(chosen) * cap + TILE
-        send = pltpu.make_async_copy(out_vmems[n], out_refs[n], out_sems.at[n])
-        send.start()
-        sends.append(send)
+    per_core = len(keys) // 2
+    for k in range(2):
+        first = k * per_core
+        taken = dot(pick_ref[first * cap : (first + per_core) * cap, :], message_ref[...]).astype(jnp.bfloat16)
+        for n in range(count):
+            start = 0
+            if runs[n][0][0][0][2] != k:
+                continue
+            for chosen, lanes in runs[n]:
+                for key in chosen:
+                    m = keys.index(key) - first
+                    out_vmems[n][start : start + cap, :] = taken[m * cap : (m + 1) * cap, lanes]
+                    start += cap
+                start += TILE
+            send = pltpu.make_async_copy(out_vmems[n], out_refs[n], out_sems.at[n])
+            send.start()
+            sends.append(send)
     for send in sends:
         send.wait()
 
@@ -271,21 +278,32 @@
         yield h, sums_ref[h] * jnp.exp2((old - top) * scale) + dot(v, expo), top
 
 
-def outer_kernel(
-    even_ref, odd_ref, wk_ref, wv_ref, order_ref, window_ref, query_ref, sums_ref, top_ref,
-    sums_out, top_out,
-    key_ref, value_ref, gap_ref,
-):
-    nodes, width = even_ref.shape
-    head_dim = width // HEADS
+def next_node(odd, block, wk_ref, wv_ref, window_ref, query_ref, sums_ref, top_ref, key_ref, value_ref, gap_ref, store):
+    nodes = block.shape[0]
+    head_dim = wv_ref.shape[0] // HEADS
     per_group = LANES // head_dim
-    far = 2 - 4 * lax.rem(lax.axis_index("inner") // 2, 2)
     scale = head_dim ** (-0.5) / math.log(2.0)
     value_ref[:, head_dim:, :] = jnp.ones_like(value_ref[:, head_dim:, :])
-    project_keys(even_ref[...], wk_ref, wv_ref, key_ref, value_ref, 0)
-    project_keys(odd_ref[...], wk_ref, wv_ref, key_ref, value_ref, nodes)
-    gap_ref[0:nodes] = gaps(far, 0, nodes, nodes)
-    gap_ref[nodes:] = gaps(-far, 0, nodes, nodes)
+    project_keys(block, wk_ref, wv_ref, key_ref, value_ref, 0)
+    gap_ref[...] = gaps(2 * odd - 1, 0, nodes, nodes)
+    for i in range(HEADS // GROUP):
+        heads = range(GROUP * i, GROUP * (i + 1))
+        keys, values = [key_ref[h // per_group] for h in heads], [value_ref[h] for h in heads]
+        for h, sums, top in extend(
+            heads, keys, values, gap_ref, window_ref, query_ref, sums_ref, top_ref, scale
+        ):
+            store(h, sums, top)
+
+
+def next_but_one(ahead, block, wk_ref, wv_ref, order_ref, window_ref, query_ref, sums_ref, top_ref,
+                 sums_out, top_out, key_ref, value_ref, gap_ref):
+    nodes = block.shape[0]
+    head_dim = wv_ref.shape[0] // HEADS
+    per_group = LANES // head_dim
+    scale = head_dim ** (-0.5) / math.log(2.0)
+    value_ref[:, head_dim:, :] = jnp.ones_like(value_ref[:, head_dim:, :])
+    project_keys(block, wk_ref, wv_ref, key_ref, value_ref, 0)
+    gap_ref[...] = gaps(2 * ahead, 0, nodes, nodes)
 
     def together(i, carry):
         heads = [order_ref[GROUP * i + k] for k in range(GROUP)]
@@ -311,29 +329,65 @@
     lax.fori_loop(0, HEADS // GROUP, together, 0)
 
 
+def chip_side():
+    inner = lax.axis_index("inner")
+    ahead = 1 - 2 * lax.rem(inner // 2, 2)
+    return ahead, lax.rem(inner, 2) == (ahead + 1) // 2
+
+
+def mid_kernel(
+    beside_ref, block_ref, wk_ref, wv_ref, order_ref, window_ref, query_ref, sums_ref, top_ref,
+    sums_out, top_out,
+    key_ref, value_ref, gap_ref,
+):
+    ahead, close = chip_side()
+    scratch = (key_ref, value_ref, gap_ref)
+    next_but_one(ahead, block_ref[...], wk_ref, wv_ref, order_ref, window_ref, query_ref, sums_ref, top_ref,
+                 sums_out, top_out, *scratch)
+
+    def store(h, sums, top):
+        sums_out[h] = sums
+        top_out[h] = jnp.broadcast_to(top, top_out.shape[1:])
+
+    @pl.when(close)
+    def _():
+        odd = lax.rem(lax.axis_index("inner"), 2)
+        next_node(odd, beside_ref[...], wk_ref, wv_ref, window_ref, query_ref, sums_out, top_out, *scratch, store)
+
+
+def outer_kernel(
+    block_ref, wk_ref, wv_ref, order_ref, window_ref, query_ref, sums_ref, top_ref,
+    sums_out, top_out,
+    key_ref, value_ref, gap_ref,
+):
+    ahead, _ = chip_side()
+    next_but_one(-ahead, block_ref[...], wk_ref, wv_ref, order_ref, window_ref, query_ref, sums_ref, top_ref,
+                 sums_out, top_out, key_ref, value_ref, gap_ref)
+
+
 def far_kernel(
-    first_ref, second_ref, wk_ref, wv_ref, window_ref, query_ref, sums_ref, top_ref,
+    beside_ref, wk_ref, wv_ref, window_ref, query_ref, sums_ref, top_ref,
     state_ref, w_out_ref, gain_ref, up_ref, down_ref,
     out_ref,
     key_ref, value_ref, gap_ref, attended_ref,
 ):
-    nodes, width = first_ref.shape
+    nodes, width = beside_ref.shape
     head_dim = width // HEADS
-    per_group = LANES // head_dim
-    inner = lax.axis_index("inner")
-    odd = lax.rem(inner, 2)
-    scale = head_dim ** (-0.5) / math.log(2.0)
-    value_ref[:, head_dim:, :] = jnp.ones_like(value_ref[:, head_dim:, :])
-    by_even = odd == lax.rem(inner // 2 + 1, 2)
-    project_keys(jnp.where(by_even, first_ref[...], second_ref[...]), wk_ref, wv_ref, key_ref, value_ref, 0)
-    gap_ref[...] = gaps(2 * odd - 1, 0, nodes, nodes)
-    for i in range(HEADS // GROUP):
-        heads = range(GROUP * i, GROUP * (i + 1))
-        keys, values = [key_ref[h // per_group] for h in heads], [value_ref[h] for h in heads]
-        for h, sums, _ in extend(
-            heads, keys, values, gap_ref, window_ref, query_ref, sums_ref, top_ref, scale
-        ):
-            attended_ref[h] = (sums[0:head_dim] / sums[head_dim : head_dim + 1]).astype(jnp.bfloat16)
+    _, close = chip_side()
+
+    def store(h, sums, top):
+        attended_ref[h] = (sums[0:head_dim] / sums[head_dim : head_dim + 1]).astype(jnp.bfloat16)
+
+    @pl.when(jnp.logical_not(close))
+    def _():
+        odd = lax.rem(lax.axis_index("inner"), 2)
+        next_node(odd, beside_ref[...], wk_ref, wv_ref, window_ref, query_ref, sums_ref, top_ref,
+                  key_ref, value_ref, gap_ref, store)
+
+    @pl.when(close)
+    def _():
+        for h in range(HEADS):
+            store(h, sums_ref[h], None)
 
     attended = attended_ref[...].reshape(width, nodes)
     mixed = lax.dot_general(
@@ -395,6 +449,7 @@
             pltpu.VMEM(grid_rows.shape, bf16),
             pltpu.VMEM(w_message.shape, bf16),
             pltpu.VMEM((grid_dev, width), bf16),
+            pltpu.VMEM((3 * inners * cap, grid_dev), bf16),
             pltpu.SemaphoreType.DMA((GRID_PARTS + 1,)),
             pltpu.SemaphoreType.DMA((len(outgoing),)),
         ],
@@ -484,7 +539,6 @@
 
     side = lax.ppermute(normed, NODES, beside)
     even = lax.ppermute(normed, NODES, chips_trade(0))
-    odd = lax.ppermute(normed, NODES, chips_trade(1))
 
     extra = head_dim + 16
     query, near, top = pl.pallas_call(
@@ -506,43 +560,54 @@
         name="near",
     )(normed, side, w_query, w_key, w_value, order, window)
 
-    even, odd, near, top = lax.optimization_barrier((even, odd, near, top))
+    normed, even, near, top = lax.optimization_barrier((normed, even, near, top))
+    odd = lax.ppermute(normed, NODES, chips_trade(1))
     first = lax.ppermute(even, NODES, beside)
+    weights = (w_key, w_value, order, window)
+    sums_shape = [
+        jax.ShapeDtypeStruct((HEADS, extra, nodes), f32),
+        jax.ShapeDtypeStruct((HEADS, 8, nodes), f32),
+    ]
+    scratch = [
+        pltpu.VMEM((width // LANES, nodes, LANES), bf16),
+        pltpu.VMEM((HEADS, extra, nodes), bf16),
+        pltpu.VMEM((nodes, nodes), i32),
+    ]
+    near, top = pl.pallas_call(
+        mid_kernel,
+        out_shape=sums_shape,
+        in_specs=[VMEM] * 4 + [SMEM] * 2 + [VMEM] * 3,
+        out_specs=[VMEM] * 2,
+        scratch_shapes=scratch,
+        compiler_params=params(24),
+        cost_estimate=cost(16 * nodes * width * width, 3 << 20),
+        name="mid",
+    )(first, even, *weights, query, near, top)
+
+    odd, near, top = lax.optimization_barrier((odd, near, top))
     second = lax.ppermute(odd, NODES, beside)
     near, top = pl.pallas_call(
         outer_kernel,
-        out_shape=[
-            jax.ShapeDtypeStruct((HEADS, extra, nodes), f32),
-            jax.ShapeDtypeStruct((HEADS, 8, nodes), f32),
-        ],
-        in_specs=[VMEM] * 4 + [SMEM] * 2 + [VMEM] * 3,
+        out_shape=sums_shape,
+        in_specs=[VMEM] * 3 + [SMEM] * 2 + [VMEM] * 3,
         out_specs=[VMEM] * 2,
-        scratch_shapes=[
-            pltpu.VMEM((width // LANES, 2 * nodes, LANES), bf16),
-            pltpu.VMEM((HEADS, extra, 2 * nodes), bf16),
-            pltpu.VMEM((2 * nodes, nodes), i32),
-        ],
+        scratch_shapes=scratch,
         compiler_params=params(24),
-        cost_estimate=cost(16 * nodes * width * width, 3 << 20),
+        cost_estimate=cost(8 * nodes * width * width, 3 << 20),
         name="outer",
-    )(even, odd, w_key, w_value, order, window, query, near, top)
+    )(odd, *weights, query, near, top)
 
     return pl.pallas_call(
         far_kernel,
         out_shape=jax.ShapeDtypeStruct((nodes, width), bf16),
-        in_specs=[VMEM] * 4 + [SMEM] + [VMEM] * 8,
+        in_specs=[VMEM] * 3 + [SMEM] + [VMEM] * 8,
         out_specs=VMEM,
-        scratch_shapes=[
-            pltpu.VMEM((width // LANES, nodes, LANES), bf16),
-            pltpu.VMEM((HEADS, extra, nodes), bf16),
-            pltpu.VMEM((nodes, nodes), i32),
-            pltpu.VMEM((HEADS, head_dim, nodes), bf16),
-        ],
+        scratch_shapes=scratch + [pltpu.VMEM((HEADS, head_dim, nodes), bf16)],
         compiler_params=params(40),
         cost_estimate=cost(8 << 30, 8 << 20),
         name="far",
     )(
-        first, second, w_key, w_value, window,
+        second, w_key, w_value, window,
         query, near, top, state, w_out, gain_mlp.reshape(1, width), w_up, w_down,
     )
 

time: 51.1 us -> 53 us (1.037)
  the two profiles are of different devices: /device:TPU:17 before, /device:TPU:15 now
where the time goes in v7:
time: 53 us; the launch traced here: 52.3 us
  Pallas kernels  22.2 us (42%)
  starting transfers between devices  14.6 us (28%)
  waiting for transfers between devices  14 us (26%)
  local copies, waits for them, and re-layouts  1.02 us (2%)
    pallas_call x1, Pallas kernels, local(): pl.pallas_call(far_kernel, out_shape=jax.ShapeDtypeStruct((nodes, width),...  5.68 us
    pallas_call x1, Pallas kernels, local(): pl.pallas_call(functools.partial(message_kernel, pairs), out_shape=outgoi...  5.62 us
    pallas_call x1, Pallas kernels, local(): pl.pallas_call(near_kernel, out_shape=[jax.ShapeDtypeStruct((HEADS, LANES...  4.69 us
    ppermute x1, waiting for transfers between devices, local(): odd = lax.ppermute(normed, NODES, chips_trade(1))  4.63 us
    ppermute x1, waiting for transfers between devices, local(): lax.ppermute(part, NODES, chip_trade(p + 1))  2.48 us
    ppermute x1, starting transfers between devices, local(): odd = lax.ppermute(odd, NODES, bands_trade(1))  2.42 us
    ppermute x1, starting transfers between devices, local(): odd = lax.ppermute(normed, NODES, chips_trade(1))  2.24 us
    ppermute x1, waiting for transfers between devices, local(): even = lax.ppermute(normed, NODES, chips_trade(0))  2.16 us
  transfers between devices with their start and end apart: 15, of which 9 were waited for; matrix products, arithmetic and copies ran while one was open for 1% of the time, Pallas kernels for 20%

profile of v7, /device:TPU:15, one launch (start us, length us, event | category | flops | bytes accessed | tf_op | source)
XLA Modules:
  0.0 52.3 jit_solution(12631365858966048198)
XLA Ops:
  0.0 5.6 %messages.1 = (bf16[272,256]{1,0:T(8,128)(2,1)}, bf16[272,256]{1,0:T(8,128)(2,1)}, bf16[272,256]{1,0:T(8,128)(2,1)}, bf16[272,256]{1,0:T(8,128)(2,1)}, bf16[400,...) custom-call(bf16[1024,512]{1,0:T(8,128)(2,1)} %grid_ref.1, ...), custom_call_target="tpu_custom_call" | custom-call | flops 2147483648 | bytes 4194304 | tf_op jit(solution)/shard_map/messages/pallas_call | solution.py:442
  5.6 0.7 %collective-permute-start.1 = (bf16[672,256]{1,0:T(8,128)(2,1)}, bf16[672,256]{1,0:T(8,128)(2,1)S(1)}, u32[]{:S(2)}, u32[]{:S(2)}) collective-permute-start(bf16[672,256]{1,0:T(8,128)(2,1)} %get-tuple-element.47), channel_id=1, source_target_pairs={{0,1},{1,0},{2,3},{3,2},{4,5},{5,4},{6,7},{7,6},{8,9},{9,8},{10,11... | collective-permute-start | bytes 1032200 | tf_op jit(solution)/shard_map/ppermute | solution.py:473
  6.8 1.0 %collective-permute-done.1.other_ref = bf16[672,256]{1,0:T(8,128)(2,1)S(1)} collective-permute-done((bf16[672,256]{1,0:T(8,128)(2,1)}, bf16[672,256]{1,0:T(8,128)(2,1)S(1)}, u32[]{:S(2)}, u32[]{:S(2)}) %collective-permute-start.1) | collective-permute-done | bytes 344096 | tf_op jit(solution)/shard_map/ppermute | solution.py:473
  7.9 0.7 %collective-permute-start.7 = (bf16[400,256]{1,0:T(8,128)(2,1)}, bf16[400,256]{1,0:T(8,128)(2,1)S(1)}, u32[]{:S(2)}, u32[]{:S(2)}) collective-permute-start(bf16[400,256]{1,0:T(8,128)(2,1)} %get-tuple-element.62), channel_id=1, source_target_pairs={{0,3},{1,2},{2,1},{3,0},{4,7},{5,6},{6,5},{7,4},{8,11},{9,10},{10,... | collective-permute-start | bytes 614408 | tf_op jit(solution)/shard_map/ppermute | solution.py:480
  8.5 2.4 %collective-permute-start.3 = (bf16[272,256]{1,0:T(8,128)(2,1)}, bf16[272,256]{1,0:T(8,128)(2,1)S(1)}, u32[]{:S(2)}, u32[]{:S(2)}) collective-permute-start(bf16[272,256]{1,0:T(8,128)(2,1)} %get-tuple-element.52), channel_id=1, source_target_pairs={{0,1},{1,0},{2,3},{3,2},{4,8},{5,9},{6,10},{7,11},{8,4},{9,5},{10,... | collective-permute-start | bytes 417800 | tf_op jit(solution)/shard_map/ppermute | solution.py:476
  11.0 0.9 %collective-permute-done.refs_0_ = bf16[272,256]{1,0:T(8,128)(2,1)S(1)} collective-permute-done((bf16[272,256]{1,0:T(8,128)(2,1)}, bf16[272,256]{1,0:T(8,128)(2,1)S(1)}, u32[]{:S(2)}, u32[]{:S(2)}) %collective-permute-start) | collective-permute-done | bytes 139296 | tf_op jit(solution)/shard_map/ppermute | solution.py:475
  11.8 2.0 %collective-permute-start.4 = (bf16[272,256]{1,0:T(8,128)(2,1)}, bf16[272,256]{1,0:T(8,128)(2,1)S(1)}, u32[]{:S(2)}, u32[]{:S(2)}) collective-permute-start(bf16[272,256]{1,0:T(8,128)(2,1)} %get-tuple-element.53), channel_id=1, source_target_pairs={{0,1},{1,0},{2,3},{3,2},{4,9},{5,8},{6,11},{7,10},{8,5},{9,4},{10,... | collective-permute-start | bytes 417800 | tf_op jit(solution)/shard_map/ppermute | solution.py:482
  13.9 1.0 %copy-done.2 = bf16[672,256]{1,0:T(8,128)(2,1)S(1)} copy-done((bf16[672,256]{1,0:T(8,128)(2,1)S(1)}, bf16[672,256]{1,0:T(8,128)(2,1)}, u32[]{:S(2)}) %copy-start.2) | copy-done | bytes 344088
  14.9 1.5 %early.1 = (bf16[512,512]{1,0:T(8,128)(2,1)S(1)}, bf16[512,512]{1,0:T(8,128)(2,1)S(1)}, bf16[512,512]{1,0:T(8,128)(2,1)S(1)}, f32[2,256,256]{2,1,0:T(8,128)S(1)}, f32[3,256,256]{2,1,0:T(8,128)S(1)}) custom-call(bf16[512,1536]{1,0:T(8,128)(2,1)S(1)} %copy-done, bf16[672,256]{1,0:T(8,128)(2,1)S(1)} %copy-done.2, ...), custom_call_target="tpu_custom_call" | custom-call | flops 268435456 | bytes 4194304 | tf_op jit(solution)/shard_map/early/pallas_call | solution.py:485
  16.3 0.6 %collective-permute-done.2.refs_1_ = bf16[272,256]{1,0:T(8,128)(2,1)S(1)} collective-permute-done((bf16[272,256]{1,0:T(8,128)(2,1)}, bf16[272,256]{1,0:T(8,128)(2,1)S(1)}, u32[]{:S(2)}, u32[]{:S(2)}) %collective-permute-start.2) | collective-permute-done | bytes 139296 | tf_op jit(solution)/shard_map/ppermute | solution.py:481
  16.9 1.4 %collective-permute-done.4.refs_3_ = bf16[272,256]{1,0:T(8,128)(2,1)S(1)} collective-permute-done((bf16[272,256]{1,0:T(8,128)(2,1)}, bf16[272,256]{1,0:T(8,128)(2,1)S(1)}, u32[]{:S(2)}, u32[]{:S(2)}) %collective-permute-start.4) | collective-permute-done | bytes 139296 | tf_op jit(solution)/shard_map/ppermute | solution.py:482
  19.6 1.3 %collective-permute-start.9 = (bf16[256,256]{1,0:T(8,128)(2,1)S(1)}, bf16[256,256]{1,0:T(8,128)(2,1)S(1)}, u32[]{:S(2)}, u32[]{:S(2)}) collective-permute-start(bf16[256,256]{1,0:T(8,128)(2,1)S(1)} %get-tuple-element.66), channel_id=1, source_target_pairs={{0,1},{1,0},{2,3},{3,2},{4,8},{5,9},{6,10},{7,11},{8,4},{9,5},{10,... | collective-permute-start | bytes 393224 | tf_op jit(solution)/shard_map/ppermute | solution.py:518
  20.9 2.5 %collective-permute-done.5.refs_1_ = bf16[256,256]{1,0:T(8,128)(2,1)S(1)} collective-permute-done((bf16[256,256]{1,0:T(8,128)(2,1)S(1)}, bf16[256,256]{1,0:T(8,128)(2,1)S(1)}, u32[]{:S(2)}, u32[]{:S(2)}) %collective-permute-start.5) | collective-permute-done | bytes 131104 | tf_op jit(solution)/shard_map/ppermute | solution.py:515
  24.7 1.4 %collective-permute-start.11 = (bf16[256,512]{1,0:T(8,128)(2,1)S(1)}, bf16[256,512]{1,0:T(8,128)(2,1)S(1)}, u32[]{:S(2)}, u32[]{:S(2)}) collective-permute-start(bf16[256,512]{1,0:T(8,128)(2,1)S(1)} %get-tuple-element.74.own_ref), channel_id=1, source_target_pairs={{0,1},{1,0},{2,3},{3,2},{4,5},{5,4},{6,7},{7,6},{8,9},{9,8},{10,11... | collective-permute-start | bytes 786440 | tf_op jit(solution)/shard_map/ppermute | solution.py:540
  26.4 1.1 %collective-permute-start.10 = (bf16[256,512]{1,0:T(8,128)(2,1)S(1)}, bf16[256,512]{1,0:T(8,128)(2,1)S(1)}, u32[]{:S(2)}, u32[]{:S(2)}) collective-permute-start(bf16[256,512]{1,0:T(8,128)(2,1)S(1)} %get-tuple-element.74.own_ref), channel_id=1, source_target_pairs={{0,2},{1,3},{2,0},{3,1},{4,6},{5,7},{6,4},{7,5},{8,10},{9,11},{10,... | collective-permute-start | bytes 786440 | tf_op jit(solution)/shard_map/ppermute | solution.py:541
  27.5 4.7 %near.1 = (bf16[16,128,256]{2,1,0:T(8,128)(2,1)S(1)}, f32[16,48,256]{2,1,0:T(8,128)S(1)}, f32[16,8,256]{2,1,0:T(8,128)S(1)}) custom-call(bf16[256,512]{1,0:T(8,128)(2,1)S(1)} %get-tuple-element.74.own_ref, bf16[256,512]{1,0:T(8,128)(2,1)S(1)} %collective-permute-done.11.side_ref, bf16[512,512]{1,0:T(8,128)(2,1)S(1)} %get-tuple-element.68.wq_ref, ...), custom_call_target="tpu_custom_call" | custom-call | flops 8589934592 | bytes 4194304 | tf_op jit(solution)/shard_map/near/pallas_call | solution.py:544
  32.2 2.2 %collective-permute-done.10.block_ref = bf16[256,512]{1,0:T(8,128)(2,1)S(1)} collective-permute-done((bf16[256,512]{1,0:T(8,128)(2,1)S(1)}, bf16[256,512]{1,0:T(8,128)(2,1)S(1)}, u32[]{:S(2)}, u32[]{:S(2)}) %collective-permute-start.10) | collective-permute-done | bytes 262176 | tf_op jit(solution)/shard_map/ppermute | solution.py:541
  34.4 0.8 %collective-permute-start.13 = (bf16[256,512]{1,0:T(8,128)(2,1)S(1)}, bf16[256,512]{1,0:T(8,128)(2,1)S(1)}, u32[]{:S(2)}, u32[]{:S(2)}) collective-permute-start(bf16[256,512]{1,0:T(8,128)(2,1)S(1)} %collective-permute-done.10.block_ref), channel_id=1, source_target_pairs={{0,1},{1,0},{2,3},{3,2},{4,5},{5,4},{6,7},{7,6},{8,9},{9,8},{10,11... | collective-permute-start | bytes 786440 | tf_op jit(solution)/shard_map/ppermute | solution.py:565
  35.2 2.2 %collective-permute-start.12 = (bf16[256,512]{1,0:T(8,128)(2,1)S(1)}, bf16[256,512]{1,0:T(8,128)(2,1)S(1)}, u32[]{:S(2)}, u32[]{:S(2)}) collective-permute-start(bf16[256,512]{1,0:T(8,128)(2,1)S(1)} %get-tuple-element.74.own_ref), channel_id=1, source_target_pairs={{0,1},{1,0},{2,4},{3,5},{4,2},{5,3},{6,8},{7,9},{8,6},{9,7},{10,12... | collective-permute-start | bytes 786440 | tf_op jit(solution)/shard_map/ppermute | solution.py:564
  37.4 1.9 %mid.1 = (f32[16,48,256]{2,1,0:T(8,128)S(1)}, f32[16,8,256]{2,1,0:T(8,128)S(1)}) custom-call(bf16[256,512]{1,0:T(8,128)(2,1)S(1)} %collective-permute-done.13.beside_ref, bf16[256,512]{1,0:T(8,128)(2,1)S(1)} %collective-permute-done.10.block_ref, bf16[512,512]{1,0:T(8,128)(2,1)S(1)} %get-tuple-element.69.wk_ref, ...), custom_call_target="tpu_custom_call" | custom-call | flops 1073741824 | bytes 3145728 | tf_op jit(solution)/shard_map/mid/pallas_call | solution.py:576
  39.4 4.6 %collective-permute-done.12.block_ref = bf16[256,512]{1,0:T(8,128)(2,1)S(1)} collective-permute-done((bf16[256,512]{1,0:T(8,128)(2,1)S(1)}, bf16[256,512]{1,0:T(8,128)(2,1)S(1)}, u32[]{:S(2)}, u32[]{:S(2)}) %collective-permute-start.12) | collective-permute-done | bytes 262176 | tf_op jit(solution)/shard_map/ppermute | solution.py:564
  44.0 0.8 %collective-permute-start.14 = (bf16[256,512]{1,0:T(8,128)(2,1)S(1)}, bf16[256,512]{1,0:T(8,128)(2,1)S(1)}, u32[]{:S(2)}, u32[]{:S(2)}) collective-permute-start(bf16[256,512]{1,0:T(8,128)(2,1)S(1)} %collective-permute-done.12.block_ref), channel_id=1, source_target_pairs={{0,1},{1,0},{2,3},{3,2},{4,5},{5,4},{6,7},{7,6},{8,9},{9,8},{10,11... | collective-permute-start | bytes 786440 | tf_op jit(solution)/shard_map/ppermute | solution.py:588
  44.8 1.7 %outer.1 = (f32[16,48,256]{2,1,0:T(8,128)S(1)}, f32[16,8,256]{2,1,0:T(8,128)S(1)}) custom-call(bf16[256,512]{1,0:T(8,128)(2,1)S(1)} %collective-permute-done.12.block_ref, bf16[512,512]{1,0:T(8,128)(2,1)S(1)} %get-tuple-element.69.wk_ref, bf16[512,512]{1,0:T(8,128)(2,1)S(1)} %get-tuple-element.70.wv_ref, s32[16]{0:T(128)S(1)} %select_reduce_fusion.order_ref, ...), custom_call_target="tpu_custom_call" | custom-call | flops 536870912 | bytes 3145728 | tf_op jit(solution)/shard_map/outer/pallas_call | solution.py:589
  46.6 5.7 %far.1 = bf16[256,512]{1,0:T(8,128)(2,1)} custom-call(bf16[256,512]{1,0:T(8,128)(2,1)S(1)} %collective-permute-done.14.beside_ref, bf16[512,512]{1,0:T(8,128)(2,1)S(1)} %get-tuple-element.69.wk_ref, bf16[512,512]{1,0:T(8,128)(2,1)S(1)} %get-tuple-element.70.wv_ref, s32[16]{0:T(128)S(1)} %copy-done.5, bf16[16,128,256]{2,1,0:T(8,128)(2,1)S(1)} %get-tuple-element.76.query_ref, ...), custom_call_target="tpu_custom_call" | custom-call | flops 8589934592 | bytes 8388608 | tf_op jit(solution)/shard_map/far/pallas_call | solution.py:600
  (37 shorter events, 3.3 us)
Async XLA Ops:
  0.0 13.9 %copy-start = (bf16[512,1536]{1,0:T(8,128)(2,1)S(1)}, bf16[512,1536]{1,0:T(8,128)(2,1)}, u32[]{:S(2)}) copy-start(bf16[512,1536]{1,0:T(8,128)(2,1)} %w_ref.2) | copy-start | bytes 4718596
  5.6 2.2 %collective-permute-start.1 = (bf16[672,256]{1,0:T(8,128)(2,1)}, bf16[672,256]{1,0:T(8,128)(2,1)S(1)}, u32[]{:S(2)}, u32[]{:S(2)}) collective-permute-start(bf16[672,256]{1,0:T(8,128)(2,1)} %get-tuple-element.47), channel_id=1, source_target_pairs={{0,1},{1,0},{2,3},{3,2},{4,5},{5,4},{6,7},{7,6},{8,9},{9,8},{10,11... | collective-permute-start | bytes 1032200 | tf_op jit(solution)/shard_map/ppermute | solution.py:473
  6.4 5.5 %collective-permute-start = (bf16[272,256]{1,0:T(8,128)(2,1)}, bf16[272,256]{1,0:T(8,128)(2,1)S(1)}, u32[]{:S(2)}, u32[]{:S(2)}) collective-permute-start(bf16[272,256]{1,0:T(8,128)(2,1)} %get-tuple-element.46), channel_id=1, source_target_pairs={{0,4},{1,5},{2,6},{3,7},{4,0},{5,1},{6,2},{7,3},{8,12},{9,13},{10,... | collective-permute-start | bytes 417800 | tf_op jit(solution)/shard_map/ppermute | solution.py:475
  6.6 12.4 %collective-permute-start.6 = (bf16[400,256]{1,0:T(8,128)(2,1)}, bf16[400,256]{1,0:T(8,128)(2,1)S(1)}, u32[]{:S(2)}, u32[]{:S(2)}) collective-permute-start(bf16[400,256]{1,0:T(8,128)(2,1)} %get-tuple-element.61), channel_id=1, source_target_pairs={{0,2},{1,3},{2,0},{3,1},{4,6},{5,7},{6,4},{7,5},{8,10},{9,11},{10,... | collective-permute-start | bytes 614408 | tf_op jit(solution)/shard_map/ppermute | solution.py:474
  7.9 11.1 %collective-permute-start.7 = (bf16[400,256]{1,0:T(8,128)(2,1)}, bf16[400,256]{1,0:T(8,128)(2,1)S(1)}, u32[]{:S(2)}, u32[]{:S(2)}) collective-permute-start(bf16[400,256]{1,0:T(8,128)(2,1)} %get-tuple-element.62), channel_id=1, source_target_pairs={{0,3},{1,2},{2,1},{3,0},{4,7},{5,6},{6,5},{7,4},{8,11},{9,10},{10,... | collective-permute-start | bytes 614408 | tf_op jit(solution)/shard_map/ppermute | solution.py:480
  8.5 7.8 %collective-permute-start.3 = (bf16[272,256]{1,0:T(8,128)(2,1)}, bf16[272,256]{1,0:T(8,128)(2,1)S(1)}, u32[]{:S(2)}, u32[]{:S(2)}) collective-permute-start(bf16[272,256]{1,0:T(8,128)(2,1)} %get-tuple-element.52), channel_id=1, source_target_pairs={{0,1},{1,0},{2,3},{3,2},{4,8},{5,9},{6,10},{7,11},{8,4},{9,5},{10,... | collective-permute-start | bytes 417800 | tf_op jit(solution)/shard_map/ppermute | solution.py:476
  11.0 6.0 %collective-permute-start.2 = (bf16[272,256]{1,0:T(8,128)(2,1)}, bf16[272,256]{1,0:T(8,128)(2,1)S(1)}, u32[]{:S(2)}, u32[]{:S(2)}) collective-permute-start(bf16[272,256]{1,0:T(8,128)(2,1)} %get-tuple-element.51), channel_id=1, source_target_pairs={{0,5},{1,4},{2,7},{3,6},{4,1},{5,0},{6,3},{7,2},{8,13},{9,12},{10,... | collective-permute-start | bytes 417800 | tf_op jit(solution)/shard_map/ppermute | solution.py:481
  11.8 6.5 %collective-permute-start.4 = (bf16[272,256]{1,0:T(8,128)(2,1)}, bf16[272,256]{1,0:T(8,128)(2,1)S(1)}, u32[]{:S(2)}, u32[]{:S(2)}) collective-permute-start(bf16[272,256]{1,0:T(8,128)(2,1)} %get-tuple-element.53), channel_id=1, source_target_pairs={{0,1},{1,0},{2,3},{3,2},{4,9},{5,8},{6,11},{7,10},{8,5},{9,4},{10,... | collective-permute-start | bytes 417800 | tf_op jit(solution)/shard_map/ppermute | solution.py:482
  14.8 9.3 %copy-start.1 = (bf16[512,512]{1,0:T(8,128)(2,1)S(1)}, bf16[512,512]{1,0:T(8,128)(2,1)}, u32[]{:S(2)}) copy-start(bf16[512,512]{1,0:T(8,128)(2,1)} %refs_6_.1) | copy-start | bytes 1572868
  14.8 9.3 %copy-start.3 = (bf16[256,512]{1,0:T(8,128)(2,1)S(1)}, bf16[256,512]{1,0:T(8,128)(2,1)}, u32[]{:S(2)}) copy-start(bf16[256,512]{1,0:T(8,128)(2,1)} %refs_5_.1) | copy-start | bytes 786436
  14.8 9.3 %copy-start.4 = (f32[512]{0:T(512)S(1)}, f32[512]{0:T(512)}, u32[]{:S(2)}) copy-start(f32[512]{0:T(512)} %param.21) | copy-start | bytes 6148
  16.3 9.8 %copy-start.5 = (s32[16]{0:T(128)S(1)}, s32[16]{0:T(128)}, u32[]{:S(2)}) copy-start(s32[16]{0:T(128)} %window_ref.3) | copy-start | bytes 196
  18.6 4.7 %collective-permute-start.5 = (bf16[256,256]{1,0:T(8,128)(2,1)S(1)}, bf16[256,256]{1,0:T(8,128)(2,1)S(1)}, u32[]{:S(2)}, u32[]{:S(2)}) collective-permute-start(bf16[256,256]{1,0:T(8,128)(2,1)S(1)} %get-tuple-element.60), channel_id=1, source_target_pairs={{0,2},{1,3},{2,0},{3,1},{4,6},{5,7},{6,4},{7,5},{8,10},{9,11},{10,... | collective-permute-start | bytes 393224 | tf_op jit(solution)/shard_map/ppermute | solution.py:515
  19.3 4.4 %collective-permute-start.8 = (bf16[256,256]{1,0:T(8,128)(2,1)S(1)}, bf16[256,256]{1,0:T(8,128)(2,1)S(1)}, u32[]{:S(2)}, u32[]{:S(2)}) collective-permute-start(bf16[256,256]{1,0:T(8,128)(2,1)S(1)} %get-tuple-element.65), channel_id=1, source_target_pairs={{0,4},{1,5},{2,6},{3,7},{4,0},{5,1},{6,2},{7,3},{8,12},{9,13},{10,... | collective-permute-start | bytes 393224 | tf_op jit(solution)/shard_map/ppermute | solution.py:517
  19.6 4.6 %collective-permute-start.9 = (bf16[256,256]{1,0:T(8,128)(2,1)S(1)}, bf16[256,256]{1,0:T(8,128)(2,1)S(1)}, u32[]{:S(2)}, u32[]{:S(2)}) collective-permute-start(bf16[256,256]{1,0:T(8,128)(2,1)S(1)} %get-tuple-element.66), channel_id=1, source_target_pairs={{0,1},{1,0},{2,3},{3,2},{4,8},{5,9},{6,10},{7,11},{8,4},{9,5},{10,... | collective-permute-start | bytes 393224 | tf_op jit(solution)/shard_map/ppermute | solution.py:518
  24.7 2.8 %collective-permute-start.11 = (bf16[256,512]{1,0:T(8,128)(2,1)S(1)}, bf16[256,512]{1,0:T(8,128)(2,1)S(1)}, u32[]{:S(2)}, u32[]{:S(2)}) collective-permute-start(bf16[256,512]{1,0:T(8,128)(2,1)S(1)} %get-tuple-element.74.own_ref), channel_id=1, source_target_pairs={{0,1},{1,0},{2,3},{3,2},{4,5},{5,4},{6,7},{7,6},{8,9},{9,8},{10,11... | collective-permute-start | bytes 786440 | tf_op jit(solution)/shard_map/ppermute | solution.py:540
  26.4 8.0 %collective-permute-start.10 = (bf16[256,512]{1,0:T(8,128)(2,1)S(1)}, bf16[256,512]{1,0:T(8,128)(2,1)S(1)}, u32[]{:S(2)}, u32[]{:S(2)}) collective-permute-start(bf16[256,512]{1,0:T(8,128)(2,1)S(1)} %get-tuple-element.74.own_ref), channel_id=1, source_target_pairs={{0,2},{1,3},{2,0},{3,1},{4,6},{5,7},{6,4},{7,5},{8,10},{9,11},{10,... | collective-permute-start | bytes 786440 | tf_op jit(solution)/shard_map/ppermute | solution.py:541
  34.4 3.0 %collective-permute-start.13 = (bf16[256,512]{1,0:T(8,128)(2,1)S(1)}, bf16[256,512]{1,0:T(8,128)(2,1)S(1)}, u32[]{:S(2)}, u32[]{:S(2)}) collective-permute-start(bf16[256,512]{1,0:T(8,128)(2,1)S(1)} %collective-permute-done.10.block_ref), channel_id=1, source_target_pairs={{0,1},{1,0},{2,3},{3,2},{4,5},{5,4},{6,7},{7,6},{8,9},{9,8},{10,11... | collective-permute-start | bytes 786440 | tf_op jit(solution)/shard_map/ppermute | solution.py:565
  35.2 8.8 %collective-permute-start.12 = (bf16[256,512]{1,0:T(8,128)(2,1)S(1)}, bf16[256,512]{1,0:T(8,128)(2,1)S(1)}, u32[]{:S(2)}, u32[]{:S(2)}) collective-permute-start(bf16[256,512]{1,0:T(8,128)(2,1)S(1)} %get-tuple-element.74.own_ref), channel_id=1, source_target_pairs={{0,1},{1,0},{2,4},{3,5},{4,2},{5,3},{6,8},{7,9},{8,6},{9,7},{10,12... | collective-permute-start | bytes 786440 | tf_op jit(solution)/shard_map/ppermute | solution.py:564
  37.4 9.1 %copy-start.7 = (bf16[2048,512]{1,0:T(8,128)(2,1)S(1)}, bf16[2048,512]{1,0:T(8,128)(2,1)}, u32[]{:S(2)}) copy-start(bf16[2048,512]{1,0:T(8,128)(2,1)} %down_ref.1) | copy-start | bytes 6291460
  39.3 7.2 %copy-start.6 = (bf16[512,2048]{1,0:T(8,128)(2,1)S(1)}, bf16[512,2048]{1,0:T(8,128)(2,1)}, u32[]{:S(2)}) copy-start(bf16[512,2048]{1,0:T(8,128)(2,1)} %up_ref.1) | copy-start | bytes 6291460
  39.4 7.2 %copy-start.8 = (bf16[512,512]{1,0:T(8,128)(2,1)S(1)}, bf16[512,512]{1,0:T(8,128)(2,1)}, u32[]{:S(2)}) copy-start(bf16[512,512]{1,0:T(8,128)(2,1)} %w_out_ref.1) | copy-start | bytes 1572868
  39.4 7.2 %copy-start.9 = (f32[512]{0:T(512)S(1)}, f32[512]{0:T(512)}, u32[]{:S(2)}) copy-start(f32[512]{0:T(512)} %param.25) | copy-start | bytes 6148
  44.0 2.5 %collective-permute-start.14 = (bf16[256,512]{1,0:T(8,128)(2,1)S(1)}, bf16[256,512]{1,0:T(8,128)(2,1)S(1)}, u32[]{:S(2)}, u32[]{:S(2)}) collective-permute-start(bf16[256,512]{1,0:T(8,128)(2,1)S(1)} %collective-permute-done.12.block_ref), channel_id=1, source_target_pairs={{0,1},{1,0},{2,3},{3,2},{4,5},{5,4},{6,7},{7,6},{8,9},{9,8},{10,11... | collective-permute-start | bytes 786440 | tf_op jit(solution)/shard_map/ppermute | solution.py:588
  (1 other events, 1.0 us)

commit v8 on v6

--- a/solution.py
+++ b/solution.py
@@ -14,7 +14,7 @@
 NEAR = 128
 TILE = 16
 CAP = 128
-GRID_PARTS = 4
+GRID_PARTS = 2
 MOST = 56
 GROUP = 4
 
@@ -72,7 +72,7 @@
 def message_kernel(pair_count, grid_ref, w_ref, source_ref, target_ref, count_ref, *refs):
     count = 4 + 2 * pair_count
     out_refs, out_vmems = refs[:count], refs[count : 2 * count]
-    grid_vmem, w_vmem, message_ref, in_sems, out_sems = refs[2 * count :]
+    grid_vmem, w_vmem, message_ref, pick_ref, in_sems, out_sems = refs[2 * count :]
     rows = grid_ref.shape[0]
     cap = source_ref.shape[-1]
     half = w_ref.shape[1] // 2
@@ -85,7 +85,7 @@
         fetch.start()
     inner = lax.axis_index("inner")
     offsets = band_offsets()
-    keys = [(t, p, k) for t in range(3) for p in range(pair_count) for k in range(2)]
+    keys = [(t, p, k) for k in range(2) for t in range(3) for p in range(pair_count)]
     place = {(t, p, k): (offsets[t], inner ^ (2 * p + k)) for t, p, k in keys}
     by_slot = slot_columns(source_ref, [place[key] for key in keys])
     left, right = slice(0, half), slice(half, 2 * half)
@@ -100,25 +100,32 @@
             start += len(chosen) * cap
             out_vmem[start : start + TILE, :] = target_tile(target_ref, count_ref, [place[key] for key in chosen], half)
             start += TILE
+    row = lax.broadcasted_iota(jnp.int32, (cap, rows), 1)
+    for m in range(len(keys)):
+        pick_ref[m * cap : (m + 1) * cap, :] = jnp.where(row == by_slot[:, m : m + 1], 1.0, 0.0).astype(jnp.bfloat16)
     fetches[0].wait()
     for k in range(GRID_PARTS):
         span = pl.ds(k * part, part)
         fetches[k + 1].wait()
         message_ref[span] = silu(dot(grid_vmem[span], w_vmem[...])).astype(jnp.bfloat16)
-    row = lax.broadcasted_iota(jnp.int32, (cap, rows), 1)
-    picks = {
-        key: jnp.where(row == by_slot[:, m : m + 1], 1.0, 0.0).astype(jnp.bfloat16) for m, key in enumerate(keys)
-    }
     sends = []
-    for n in reversed(range(count)):
-        start = 0
-        for chosen, lanes in runs[n]:
-            taken = dot(jnp.concatenate([picks[key] for key in chosen], axis=0), message_ref[:, lanes])
-            out_vmems[n][start : start + len(chosen) * cap, :] = taken.astype(jnp.bfloat16)
-            start += len(chosen) * cap + TILE
-        send = pltpu.make_async_copy(out_vmems[n], out_refs[n], out_sems.at[n])
-        send.start()
-        sends.append(send)
+    per_core = len(keys) // 2
+    for k in range(2):
+        first = k * per_core
+        taken = dot(pick_ref[first * cap : (first + per_core) * cap, :], message_ref[...]).astype(jnp.bfloat16)
+        for n in range(count):
+            start = 0
+            if runs[n][0][0][0][2] != k:
+                continue
+            for chosen, lanes in runs[n]:
+                for key in chosen:
+                    m = keys.index(key) - first
+                    out_vmems[n][start : start + cap, :] = taken[m * cap : (m + 1) * cap, lanes]
+                    start += cap
+                start += TILE
+            send = pltpu.make_async_copy(out_vmems[n], out_refs[n], out_sems.at[n])
+            send.start()
+            sends.append(send)
     for send in sends:
         send.wait()
 
@@ -137,7 +144,7 @@
         yield n, dot(jnp.concatenate(hits, axis=1), jnp.concatenate(rows, axis=0))
 
 
-def early_kernel(pair_count, w_ref, own_ref, other_ref, query_ref, key_ref, value_ref, left_ref, right_ref):
+def early_kernel(pair_count, w_ref, own_ref, other_ref, order_ref, query_ref, key_ref, value_ref, left_ref, right_ref):
     width = w_ref.shape[0]
     head_dim = width // HEADS
     span = 3 * LANES
@@ -336,17 +343,18 @@
             attended_ref[h] = (sums[0:head_dim] / sums[head_dim : head_dim + 1]).astype(jnp.bfloat16)
 
     attended = attended_ref[...].reshape(width, nodes)
-    mixed = lax.dot_general(
-        attended, w_out_ref[...], (((0,), (0,)), ((), ())), preferred_element_type=jnp.float32
-    )
-    mid = state_ref[...] + mixed
-    normed = layer_norm(mid, gain_ref[...]).astype(jnp.bfloat16)
-    total = mid
     chunk = math.gcd(up_ref.shape[1], 512)
-    for start in range(0, up_ref.shape[1], chunk):
-        hidden = silu(dot(normed, up_ref[:, start : start + chunk])).astype(jnp.bfloat16)
-        total = total + dot(hidden, down_ref[start : start + chunk, :])
-    out_ref[...] = total.astype(jnp.bfloat16)
+    for first in range(0, nodes, NEAR):
+        rows = slice(first, first + NEAR)
+        mixed = lax.dot_general(
+            attended[:, rows], w_out_ref[...], (((0,), (0,)), ((), ())), preferred_element_type=jnp.float32
+        )
+        total = state_ref[rows] + mixed
+        normed = layer_norm(total, gain_ref[...]).astype(jnp.bfloat16)
+        for start in range(0, up_ref.shape[1], chunk):
+            hidden = silu(dot(normed, up_ref[:, start : start + chunk])).astype(jnp.bfloat16)
+            total = total + dot(hidden, down_ref[start : start + chunk, :])
+        out_ref[rows] = total.astype(jnp.bfloat16)
 
 
 def cost(flops, size):
@@ -395,6 +403,7 @@
             pltpu.VMEM(grid_rows.shape, bf16),
             pltpu.VMEM(w_message.shape, bf16),
             pltpu.VMEM((grid_dev, width), bf16),
+            pltpu.VMEM((3 * inners * cap, grid_dev), bf16),
             pltpu.SemaphoreType.DMA((GRID_PARTS + 1,)),
             pltpu.SemaphoreType.DMA((len(outgoing),)),
         ],
@@ -427,23 +436,22 @@
     odd_other = lax.ppermute(odd_other, NODES, bands_trade(1, 1))
 
     w_qkv, window, here = lax.optimization_barrier((w_qkv, window, here))
+    head = jnp.arange(HEADS, dtype=i32)
+    ahead = (window[None, :] > window[:, None]) | (
+        (window[None, :] == window[:, None]) & (head[None, :] < head[:, None])
+    )
+    rank = jnp.sum(ahead.astype(i32), axis=1)
+    order = jnp.sum(jnp.where(rank[None, :] == head[:, None], head[None, :], 0), axis=1).astype(i32)
     w_query, w_key, w_value, early_left, early_right = pl.pallas_call(
         functools.partial(early_kernel, pairs),
         out_shape=[jax.ShapeDtypeStruct((width, width), bf16)] * 3
         + [jax.ShapeDtypeStruct((n, nodes, half), f32) for n in (pairs, 3)],
-        in_specs=[VMEM] * 3,
+        in_specs=[VMEM] * 3 + [SMEM],
         out_specs=[VMEM] * 5,
         compiler_params=params(24),
         cost_estimate=cost(1 << 28, 4 << 20),
         name="early",
-    )(w_qkv, here, here_other)
-    head = jnp.arange(HEADS, dtype=i32)
-    ahead = (window[None, :] > window[:, None]) | (
-        (window[None, :] == window[:, None]) & (head[None, :] < head[:, None])
-    )
-    rank = jnp.sum(ahead.astype(i32), axis=1)
-    order = jnp.sum(jnp.where(rank[None, :] == head[:, None], head[None, :], 0), axis=1).astype(i32)
-
+    )(w_qkv, here, here_other, order)
     def sums(arrays, early, kept, name):
         count = early.shape[0]
         return pl.pallas_call(

time: 51.1 us -> 51.2 us (level)
  the two profiles are of different devices: /device:TPU:17 before, /device:TPU:15 now
where the time goes in v8:
time: 51.2 us; the launch traced here: 50.3 us
  Pallas kernels  23.4 us (46%)
  starting transfers between devices  14.3 us (28%)
  waiting for transfers between devices  11 us (21%)
  local copies, waits for them, and re-layouts  1.01 us (2%)
    pallas_call x1, Pallas kernels, local(): pl.pallas_call(far_kernel, out_shape=jax.ShapeDtypeStruct((nodes, width),...  6.45 us
    ppermute x1, waiting for transfers between devices, local(): even = lax.ppermute(normed, NODES, chips_trade(0))  5.94 us
    pallas_call x1, Pallas kernels, local(): pl.pallas_call(functools.partial(message_kernel, pairs), out_shape=outgoi...  5.61 us
    pallas_call x1, Pallas kernels, local(): pl.pallas_call(near_kernel, out_shape=[jax.ShapeDtypeStruct((HEADS, LANES...  5.03 us
    pallas_call x1, Pallas kernels, local(): pl.pallas_call(outer_kernel, out_shape=[jax.ShapeDtypeStruct((HEADS, extr...  3.28 us
    ppermute x1, waiting for transfers between devices, local(): lax.ppermute(part, NODES, chip_trade(p + 1))  2.51 us
    ppermute x1, starting transfers between devices, local(): odd = lax.ppermute(odd, NODES, bands_trade(1))  2.42 us
    ppermute x1, starting transfers between devices, local(): odd_other = lax.ppermute(odd_other, NODES, bands_trade(1, 1))  2.03 us
  transfers between devices with their start and end apart: 15, of which 6 were waited for; matrix products, arithmetic and copies ran while one was open for 1% of the time, Pallas kernels for 22%

profile of v8, /device:TPU:15, one launch (start us, length us, event | category | flops | bytes accessed | tf_op | source)
XLA Modules:
  0.0 50.3 jit_solution(11805189740418099023)
XLA Ops:
  0.0 5.6 %messages.1 = (bf16[272,256]{1,0:T(8,128)(2,1)}, bf16[272,256]{1,0:T(8,128)(2,1)}, bf16[272,256]{1,0:T(8,128)(2,1)}, bf16[272,256]{1,0:T(8,128)(2,1)}, bf16[400,...) custom-call(bf16[1024,512]{1,0:T(8,128)(2,1)} %grid_ref.1, ...), custom_call_target="tpu_custom_call" | custom-call | flops 2147483648 | bytes 4194304 | tf_op jit(solution)/shard_map/messages/pallas_call | solution.py:396
  5.6 0.7 %collective-permute-start.1 = (bf16[672,256]{1,0:T(8,128)(2,1)}, bf16[672,256]{1,0:T(8,128)(2,1)S(1)}, u32[]{:S(2)}, u32[]{:S(2)}) collective-permute-start(bf16[672,256]{1,0:T(8,128)(2,1)} %get-tuple-element.42), channel_id=1, source_target_pairs={{0,1},{1,0},{2,3},{3,2},{4,5},{5,4},{6,7},{7,6},{8,9},{9,8},{10,11... | collective-permute-start | bytes 1032200 | tf_op jit(solution)/shard_map/ppermute | solution.py:427
  6.8 2.4 %collective-permute-start.3 = (bf16[272,256]{1,0:T(8,128)(2,1)}, bf16[272,256]{1,0:T(8,128)(2,1)S(1)}, u32[]{:S(2)}, u32[]{:S(2)}) collective-permute-start(bf16[272,256]{1,0:T(8,128)(2,1)} %get-tuple-element.47), channel_id=1, source_target_pairs={{0,1},{1,0},{2,3},{3,2},{4,8},{5,9},{6,10},{7,11},{8,4},{9,5},{10,... | collective-permute-start | bytes 417800 | tf_op jit(solution)/shard_map/ppermute | solution.py:430
  9.2 2.0 %collective-permute-start.7 = (bf16[400,256]{1,0:T(8,128)(2,1)}, bf16[400,256]{1,0:T(8,128)(2,1)S(1)}, u32[]{:S(2)}, u32[]{:S(2)}) collective-permute-start(bf16[400,256]{1,0:T(8,128)(2,1)} %get-tuple-element.58), channel_id=1, source_target_pairs={{0,3},{1,2},{2,1},{3,0},{4,7},{5,6},{6,5},{7,4},{8,11},{9,10},{10,... | collective-permute-start | bytes 614408 | tf_op jit(solution)/shard_map/ppermute | solution.py:434
  11.2 0.6 %collective-permute-done.refs_0_ = bf16[272,256]{1,0:T(8,128)(2,1)S(1)} collective-permute-done((bf16[272,256]{1,0:T(8,128)(2,1)}, bf16[272,256]{1,0:T(8,128)(2,1)S(1)}, u32[]{:S(2)}, u32[]{:S(2)}) %collective-permute-start) | collective-permute-done | bytes 139296 | tf_op jit(solution)/shard_map/ppermute | solution.py:429
  11.8 2.0 %collective-permute-start.4 = (bf16[272,256]{1,0:T(8,128)(2,1)}, bf16[272,256]{1,0:T(8,128)(2,1)S(1)}, u32[]{:S(2)}, u32[]{:S(2)}) collective-permute-start(bf16[272,256]{1,0:T(8,128)(2,1)} %get-tuple-element.48), channel_id=1, source_target_pairs={{0,1},{1,0},{2,3},{3,2},{4,9},{5,8},{6,11},{7,10},{8,5},{9,4},{10,... | collective-permute-start | bytes 417800 | tf_op jit(solution)/shard_map/ppermute | solution.py:436
  14.2 1.0 %copy-done.2 = bf16[672,256]{1,0:T(8,128)(2,1)S(1)} copy-done((bf16[672,256]{1,0:T(8,128)(2,1)S(1)}, bf16[672,256]{1,0:T(8,128)(2,1)}, u32[]{:S(2)}) %copy-start.2) | copy-done | bytes 344088
  15.2 2.0 %early.1 = (bf16[512,512]{1,0:T(8,128)(2,1)S(1)}, bf16[512,512]{1,0:T(8,128)(2,1)S(1)}, bf16[512,512]{1,0:T(8,128)(2,1)S(1)}, f32[2,256,256]{2,1,0:T(8,128)S(1)}, f32[3,256,256]{2,1,0:T(8,128)S(1)}) custom-call(bf16[512,1536]{1,0:T(8,128)(2,1)S(1)} %copy-done, bf16[672,256]{1,0:T(8,128)(2,1)S(1)} %copy-done.2, ...), custom_call_target="tpu_custom_call" | custom-call | flops 268435456 | bytes 4194304 | tf_op jit(solution)/shard_map/early/pallas_call | solution.py:445
  17.2 1.2 %collective-permute-done.4.refs_3_ = bf16[272,256]{1,0:T(8,128)(2,1)S(1)} collective-permute-done((bf16[272,256]{1,0:T(8,128)(2,1)}, bf16[272,256]{1,0:T(8,128)(2,1)S(1)}, u32[]{:S(2)}, u32[]{:S(2)}) %collective-permute-start.4) | collective-permute-done | bytes 139296 | tf_op jit(solution)/shard_map/ppermute | solution.py:436
  18.4 0.3 left.1
  18.7 0.3 collective-permute-start.5
  19.3 0.3 collective-permute-start.8
  19.6 1.3 %collective-permute-start.9 = (bf16[256,256]{1,0:T(8,128)(2,1)S(1)}, bf16[256,256]{1,0:T(8,128)(2,1)S(1)}, u32[]{:S(2)}, u32[]{:S(2)}) collective-permute-start(bf16[256,256]{1,0:T(8,128)(2,1)S(1)} %get-tuple-element.62), channel_id=1, source_target_pairs={{0,1},{1,0},{2,3},{3,2},{4,8},{5,9},{6,10},{7,11},{8,4},{9,5},{10,... | collective-permute-start | bytes 393224 | tf_op jit(solution)/shard_map/ppermute | solution.py:471
  20.9 2.5 %collective-permute-done.5.refs_1_ = bf16[256,256]{1,0:T(8,128)(2,1)S(1)} collective-permute-done((bf16[256,256]{1,0:T(8,128)(2,1)S(1)}, bf16[256,256]{1,0:T(8,128)(2,1)S(1)}, u32[]{:S(2)}, u32[]{:S(2)}) %collective-permute-start.5) | collective-permute-done | bytes 131104 | tf_op jit(solution)/shard_map/ppermute | solution.py:468
  23.7 0.5 %collective-permute-done.9.refs_4_ = bf16[256,256]{1,0:T(8,128)(2,1)S(1)} collective-permute-done((bf16[256,256]{1,0:T(8,128)(2,1)S(1)}, bf16[256,256]{1,0:T(8,128)(2,1)S(1)}, u32[]{:S(2)}, u32[]{:S(2)}) %collective-permute-start.9) | collective-permute-done | bytes 131104 | tf_op jit(solution)/shard_map/ppermute | solution.py:471
  24.2 0.5 merge.1
  24.7 1.4 %collective-permute-start.12 = (bf16[256,512]{1,0:T(8,128)(2,1)S(1)}, bf16[256,512]{1,0:T(8,128)(2,1)S(1)}, u32[]{:S(2)}, u32[]{:S(2)}) collective-permute-start(bf16[256,512]{1,0:T(8,128)(2,1)S(1)} %get-tuple-element.63.own_ref), channel_id=1, source_target_pairs={{0,1},{1,0},{2,3},{3,2},{4,5},{5,4},{6,7},{7,6},{8,9},{9,8},{10,11... | collective-permute-start | bytes 786440 | tf_op jit(solution)/shard_map/ppermute | solution.py:493
  26.1 1.0 %collective-permute-start.10 = (bf16[256,512]{1,0:T(8,128)(2,1)S(1)}, bf16[256,512]{1,0:T(8,128)(2,1)S(1)}, u32[]{:S(2)}, u32[]{:S(2)}) collective-permute-start(bf16[256,512]{1,0:T(8,128)(2,1)S(1)} %get-tuple-element.63.own_ref), channel_id=1, source_target_pairs={{0,2},{1,3},{2,0},{3,1},{4,6},{5,7},{6,4},{7,5},{8,10},{9,11},{10,... | collective-permute-start | bytes 786440 | tf_op jit(solution)/shard_map/ppermute | solution.py:494
  27.1 1.5 %collective-permute-start.11 = (bf16[256,512]{1,0:T(8,128)(2,1)S(1)}, bf16[256,512]{1,0:T(8,128)(2,1)S(1)}, u32[]{:S(2)}, u32[]{:S(2)}) collective-permute-start(bf16[256,512]{1,0:T(8,128)(2,1)S(1)} %get-tuple-element.63.own_ref), channel_id=1, source_target_pairs={{0,1},{1,0},{2,4},{3,5},{4,2},{5,3},{6,8},{7,9},{8,6},{9,7},{10,12... | collective-permute-start | bytes 786440 | tf_op jit(solution)/shard_map/ppermute | solution.py:495
  28.6 5.0 %near.1 = (bf16[16,128,256]{2,1,0:T(8,128)(2,1)S(1)}, f32[16,48,256]{2,1,0:T(8,128)S(1)}, f32[16,8,256]{2,1,0:T(8,128)S(1)}) custom-call(bf16[256,512]{1,0:T(8,128)(2,1)S(1)} %get-tuple-element.63.own_ref, bf16[256,512]{1,0:T(8,128)(2,1)S(1)} %collective-permute-done.12.side_ref, bf16[512,512]{1,0:T(8,128)(2,1)S(1)} %get-tuple-element.64.wq_ref, ...), custom_call_target="tpu_custom_call" | custom-call | flops 8589934592 | bytes 4194304 | tf_op jit(solution)/shard_map/near/pallas_call | solution.py:498
  33.7 5.9 %collective-permute-done.10.even_ref = bf16[256,512]{1,0:T(8,128)(2,1)S(1)} collective-permute-done((bf16[256,512]{1,0:T(8,128)(2,1)S(1)}, bf16[256,512]{1,0:T(8,128)(2,1)S(1)}, u32[]{:S(2)}, u32[]{:S(2)}) %collective-permute-start.10) | collective-permute-done | bytes 262176 | tf_op jit(solution)/shard_map/ppermute | solution.py:494
  39.6 0.9 %collective-permute-start.13 = (bf16[256,512]{1,0:T(8,128)(2,1)S(1)}, bf16[256,512]{1,0:T(8,128)(2,1)S(1)}, u32[]{:S(2)}, u32[]{:S(2)}) collective-permute-start(bf16[256,512]{1,0:T(8,128)(2,1)S(1)} %collective-permute-done.10.even_ref), channel_id=1, source_target_pairs={{0,1},{1,0},{2,3},{3,2},{4,5},{5,4},{6,7},{7,6},{8,9},{9,8},{10,11... | collective-permute-start | bytes 786440 | tf_op jit(solution)/shard_map/ppermute | solution.py:518
  40.5 3.3 %outer.1 = (f32[16,48,256]{2,1,0:T(8,128)S(1)}, f32[16,8,256]{2,1,0:T(8,128)S(1)}) custom-call(bf16[256,512]{1,0:T(8,128)(2,1)S(1)} %collective-permute-done.10.even_ref, bf16[256,512]{1,0:T(8,128)(2,1)S(1)} %collective-permute-done.11.odd_ref, bf16[512,512]{1,0:T(8,128)(2,1)S(1)} %get-tuple-element.65.wk_ref, ...), custom_call_target="tpu_custom_call" | custom-call | flops 1073741824 | bytes 3145728 | tf_op jit(solution)/shard_map/outer/pallas_call | solution.py:520
  43.8 6.5 %far.1 = bf16[256,512]{1,0:T(8,128)(2,1)} custom-call(bf16[256,512]{1,0:T(8,128)(2,1)S(1)} %collective-permute-done.13.first_ref, bf16[256,512]{1,0:T(8,128)(2,1)S(1)} %collective-permute-done.14.second_ref, bf16[512,512]{1,0:T(8,128)(2,1)S(1)} %get-tuple-element.65.wk_ref, bf16[512,512]{1,0:T(8,128)(2,1)S(1)} %get-tuple-element.66.wv_ref, s32[16]{0:T(128)S(1)} %copy-done.9, ...), custom_call_target="tpu_custom_call" | custom-call | flops 8589934592 | bytes 8388608 | tf_op jit(solution)/shard_map/far/pallas_call | solution.py:538
  (36 shorter events, 1.4 us)
Async XLA Ops:
  0.0 13.9 %copy-start.9 = (s32[16]{0:T(128)S(1)}, s32[16]{0:T(128)}, u32[]{:S(2)}) copy-start(s32[16]{0:T(128)} %window_ref.2) | copy-start | bytes 196
  0.0 14.2 %copy-start = (bf16[512,1536]{1,0:T(8,128)(2,1)S(1)}, bf16[512,1536]{1,0:T(8,128)(2,1)}, u32[]{:S(2)}) copy-start(bf16[512,1536]{1,0:T(8,128)(2,1)} %w_ref.2) | copy-start | bytes 4718596
  5.6 3.6 %collective-permute-start.1 = (bf16[672,256]{1,0:T(8,128)(2,1)}, bf16[672,256]{1,0:T(8,128)(2,1)S(1)}, u32[]{:S(2)}, u32[]{:S(2)}) collective-permute-start(bf16[672,256]{1,0:T(8,128)(2,1)} %get-tuple-element.42), channel_id=1, source_target_pairs={{0,1},{1,0},{2,3},{3,2},{4,5},{5,4},{6,7},{7,6},{8,9},{9,8},{10,11... | collective-permute-start | bytes 1032200 | tf_op jit(solution)/shard_map/ppermute | solution.py:427
  6.4 5.5 %collective-permute-start = (bf16[272,256]{1,0:T(8,128)(2,1)}, bf16[272,256]{1,0:T(8,128)(2,1)S(1)}, u32[]{:S(2)}, u32[]{:S(2)}) collective-permute-start(bf16[272,256]{1,0:T(8,128)(2,1)} %get-tuple-element.41), channel_id=1, source_target_pairs={{0,4},{1,5},{2,6},{3,7},{4,0},{5,1},{6,2},{7,3},{8,12},{9,13},{10,... | collective-permute-start | bytes 417800 | tf_op jit(solution)/shard_map/ppermute | solution.py:429
  6.6 12.4 %collective-permute-start.6 = (bf16[400,256]{1,0:T(8,128)(2,1)}, bf16[400,256]{1,0:T(8,128)(2,1)S(1)}, u32[]{:S(2)}, u32[]{:S(2)}) collective-permute-start(bf16[400,256]{1,0:T(8,128)(2,1)} %get-tuple-element.57), channel_id=1, source_target_pairs={{0,2},{1,3},{2,0},{3,1},{4,6},{5,7},{6,4},{7,5},{8,10},{9,11},{10,... | collective-permute-start | bytes 614408 | tf_op jit(solution)/shard_map/ppermute | solution.py:428
  6.8 10.4 %collective-permute-start.3 = (bf16[272,256]{1,0:T(8,128)(2,1)}, bf16[272,256]{1,0:T(8,128)(2,1)S(1)}, u32[]{:S(2)}, u32[]{:S(2)}) collective-permute-start(bf16[272,256]{1,0:T(8,128)(2,1)} %get-tuple-element.47), channel_id=1, source_target_pairs={{0,1},{1,0},{2,3},{3,2},{4,8},{5,9},{6,10},{7,11},{8,4},{9,5},{10,... | collective-permute-start | bytes 417800 | tf_op jit(solution)/shard_map/ppermute | solution.py:430
  9.2 9.7 %collective-permute-start.7 = (bf16[400,256]{1,0:T(8,128)(2,1)}, bf16[400,256]{1,0:T(8,128)(2,1)S(1)}, u32[]{:S(2)}, u32[]{:S(2)}) collective-permute-start(bf16[400,256]{1,0:T(8,128)(2,1)} %get-tuple-element.58), channel_id=1, source_target_pairs={{0,3},{1,2},{2,1},{3,0},{4,7},{5,6},{6,5},{7,4},{8,11},{9,10},{10,... | collective-permute-start | bytes 614408 | tf_op jit(solution)/shard_map/ppermute | solution.py:434
  11.2 5.9 %collective-permute-start.2 = (bf16[272,256]{1,0:T(8,128)(2,1)}, bf16[272,256]{1,0:T(8,128)(2,1)S(1)}, u32[]{:S(2)}, u32[]{:S(2)}) collective-permute-start(bf16[272,256]{1,0:T(8,128)(2,1)} %get-tuple-element.46), channel_id=1, source_target_pairs={{0,5},{1,4},{2,7},{3,6},{4,1},{5,0},{6,3},{7,2},{8,13},{9,12},{10,... | collective-permute-start | bytes 417800 | tf_op jit(solution)/shard_map/ppermute | solution.py:435
  11.8 6.5 %collective-permute-start.4 = (bf16[272,256]{1,0:T(8,128)(2,1)}, bf16[272,256]{1,0:T(8,128)(2,1)S(1)}, u32[]{:S(2)}, u32[]{:S(2)}) collective-permute-start(bf16[272,256]{1,0:T(8,128)(2,1)} %get-tuple-element.48), channel_id=1, source_target_pairs={{0,1},{1,0},{2,3},{3,2},{4,9},{5,8},{6,11},{7,10},{8,5},{9,4},{10,... | collective-permute-start | bytes 417800 | tf_op jit(solution)/shard_map/ppermute | solution.py:436
  15.2 9.0 %copy-start.1 = (bf16[512,512]{1,0:T(8,128)(2,1)S(1)}, bf16[512,512]{1,0:T(8,128)(2,1)}, u32[]{:S(2)}) copy-start(bf16[512,512]{1,0:T(8,128)(2,1)} %refs_6_.1) | copy-start | bytes 1572868
  15.2 9.1 %copy-start.3 = (bf16[256,512]{1,0:T(8,128)(2,1)S(1)}, bf16[256,512]{1,0:T(8,128)(2,1)}, u32[]{:S(2)}) copy-start(bf16[256,512]{1,0:T(8,128)(2,1)} %refs_5_.1) | copy-start | bytes 786436
  15.2 9.1 %copy-start.4 = (f32[512]{0:T(512)S(1)}, f32[512]{0:T(512)}, u32[]{:S(2)}) copy-start(f32[512]{0:T(512)} %param.21) | copy-start | bytes 6148
  18.7 4.7 %collective-permute-start.5 = (bf16[256,256]{1,0:T(8,128)(2,1)S(1)}, bf16[256,256]{1,0:T(8,128)(2,1)S(1)}, u32[]{:S(2)}, u32[]{:S(2)}) collective-permute-start(bf16[256,256]{1,0:T(8,128)(2,1)S(1)} %get-tuple-element.56), channel_id=1, source_target_pairs={{0,2},{1,3},{2,0},{3,1},{4,6},{5,7},{6,4},{7,5},{8,10},{9,11},{10,... | collective-permute-start | bytes 393224 | tf_op jit(solution)/shard_map/ppermute | solution.py:468
  19.3 4.4 %collective-permute-start.8 = (bf16[256,256]{1,0:T(8,128)(2,1)S(1)}, bf16[256,256]{1,0:T(8,128)(2,1)S(1)}, u32[]{:S(2)}, u32[]{:S(2)}) collective-permute-start(bf16[256,256]{1,0:T(8,128)(2,1)S(1)} %get-tuple-element.61), channel_id=1, source_target_pairs={{0,4},{1,5},{2,6},{3,7},{4,0},{5,1},{6,2},{7,3},{8,12},{9,13},{10,... | collective-permute-start | bytes 393224 | tf_op jit(solution)/shard_map/ppermute | solution.py:470
  19.6 4.6 %collective-permute-start.9 = (bf16[256,256]{1,0:T(8,128)(2,1)S(1)}, bf16[256,256]{1,0:T(8,128)(2,1)S(1)}, u32[]{:S(2)}, u32[]{:S(2)}) collective-permute-start(bf16[256,256]{1,0:T(8,128)(2,1)S(1)} %get-tuple-element.62), channel_id=1, source_target_pairs={{0,1},{1,0},{2,3},{3,2},{4,8},{5,9},{6,10},{7,11},{8,4},{9,5},{10,... | collective-permute-start | bytes 393224 | tf_op jit(solution)/shard_map/ppermute | solution.py:471
  24.7 3.9 %collective-permute-start.12 = (bf16[256,512]{1,0:T(8,128)(2,1)S(1)}, bf16[256,512]{1,0:T(8,128)(2,1)S(1)}, u32[]{:S(2)}, u32[]{:S(2)}) collective-permute-start(bf16[256,512]{1,0:T(8,128)(2,1)S(1)} %get-tuple-element.63.own_ref), channel_id=1, source_target_pairs={{0,1},{1,0},{2,3},{3,2},{4,5},{5,4},{6,7},{7,6},{8,9},{9,8},{10,11... | collective-permute-start | bytes 786440 | tf_op jit(solution)/shard_map/ppermute | solution.py:493
  26.1 13.5 %collective-permute-start.10 = (bf16[256,512]{1,0:T(8,128)(2,1)S(1)}, bf16[256,512]{1,0:T(8,128)(2,1)S(1)}, u32[]{:S(2)}, u32[]{:S(2)}) collective-permute-start(bf16[256,512]{1,0:T(8,128)(2,1)S(1)} %get-tuple-element.63.own_ref), channel_id=1, source_target_pairs={{0,2},{1,3},{2,0},{3,1},{4,6},{5,7},{6,4},{7,5},{8,10},{9,11},{10,... | collective-permute-start | bytes 786440 | tf_op jit(solution)/shard_map/ppermute | solution.py:494
  27.1 12.5 %collective-permute-start.11 = (bf16[256,512]{1,0:T(8,128)(2,1)S(1)}, bf16[256,512]{1,0:T(8,128)(2,1)S(1)}, u32[]{:S(2)}, u32[]{:S(2)}) collective-permute-start(bf16[256,512]{1,0:T(8,128)(2,1)S(1)} %get-tuple-element.63.own_ref), channel_id=1, source_target_pairs={{0,1},{1,0},{2,4},{3,5},{4,2},{5,3},{6,8},{7,9},{8,6},{9,7},{10,12... | collective-permute-start | bytes 786440 | tf_op jit(solution)/shard_map/ppermute | solution.py:495
  28.6 15.2 %copy-start.6 = (bf16[2048,512]{1,0:T(8,128)(2,1)S(1)}, bf16[2048,512]{1,0:T(8,128)(2,1)}, u32[]{:S(2)}) copy-start(bf16[2048,512]{1,0:T(8,128)(2,1)} %down_ref.1) | copy-start | bytes 6291460
  33.6 10.2 %copy-start.5 = (bf16[512,2048]{1,0:T(8,128)(2,1)S(1)}, bf16[512,2048]{1,0:T(8,128)(2,1)}, u32[]{:S(2)}) copy-start(bf16[512,2048]{1,0:T(8,128)(2,1)} %up_ref.1) | copy-start | bytes 6291460
  33.6 10.2 %copy-start.7 = (bf16[512,512]{1,0:T(8,128)(2,1)S(1)}, bf16[512,512]{1,0:T(8,128)(2,1)}, u32[]{:S(2)}) copy-start(bf16[512,512]{1,0:T(8,128)(2,1)} %w_out_ref.1) | copy-start | bytes 1572868
  33.7 10.2 %copy-start.8 = (f32[512]{0:T(512)S(1)}, f32[512]{0:T(512)}, u32[]{:S(2)}) copy-start(f32[512]{0:T(512)} %param.25) | copy-start | bytes 6148
  39.6 4.1 %collective-permute-start.13 = (bf16[256,512]{1,0:T(8,128)(2,1)S(1)}, bf16[256,512]{1,0:T(8,128)(2,1)S(1)}, u32[]{:S(2)}, u32[]{:S(2)}) collective-permute-start(bf16[256,512]{1,0:T(8,128)(2,1)S(1)} %collective-permute-done.10.even_ref), channel_id=1, source_target_pairs={{0,1},{1,0},{2,3},{3,2},{4,5},{5,4},{6,7},{7,6},{8,9},{9,8},{10,11... | collective-permute-start | bytes 786440 | tf_op jit(solution)/shard_map/ppermute | solution.py:518
  40.5 3.3 %collective-permute-start.14 = (bf16[256,512]{1,0:T(8,128)(2,1)S(1)}, bf16[256,512]{1,0:T(8,128)(2,1)S(1)}, u32[]{:S(2)}, u32[]{:S(2)}) collective-permute-start(bf16[256,512]{1,0:T(8,128)(2,1)S(1)} %collective-permute-done.11.odd_ref), channel_id=1, source_target_pairs={{0,1},{1,0},{2,3},{3,2},{4,5},{5,4},{6,7},{7,6},{8,9},{9,8},{10,11... | collective-permute-start | bytes 786440 | tf_op jit(solution)/shard_map/ppermute | solution.py:519
  (1 other events, 1.0 us)

commit v9 on v8

--- a/solution.py
+++ b/solution.py
@@ -343,18 +343,16 @@
             attended_ref[h] = (sums[0:head_dim] / sums[head_dim : head_dim + 1]).astype(jnp.bfloat16)
 
     attended = attended_ref[...].reshape(width, nodes)
+    mixed = lax.dot_general(
+        attended, w_out_ref[...], (((0,), (0,)), ((), ())), preferred_element_type=jnp.float32
+    )
+    total = state_ref[...] + mixed
+    normed = layer_norm(total, gain_ref[...]).astype(jnp.bfloat16)
     chunk = math.gcd(up_ref.shape[1], 512)
-    for first in range(0, nodes, NEAR):
-        rows = slice(first, first + NEAR)
-        mixed = lax.dot_general(
-            attended[:, rows], w_out_ref[...], (((0,), (0,)), ((), ())), preferred_element_type=jnp.float32
-        )
-        total = state_ref[rows] + mixed
-        normed = layer_norm(total, gain_ref[...]).astype(jnp.bfloat16)
-        for start in range(0, up_ref.shape[1], chunk):
-            hidden = silu(dot(normed, up_ref[:, start : start + chunk])).astype(jnp.bfloat16)
-            total = total + dot(hidden, down_ref[start : start + chunk, :])
-        out_ref[rows] = total.astype(jnp.bfloat16)
+    for start in range(0, up_ref.shape[1], chunk):
+        hidden = silu(dot(normed, up_ref[:, start : start + chunk])).astype(jnp.bfloat16)
+        total = total + dot(hidden, down_ref[start : start + chunk, :])
+    out_ref[...] = total.astype(jnp.bfloat16)
 
 
 def cost(flops, size):

time: 51.2 us -> 49.8 us (0.973)
  Pallas kernels: 23.4 us -> 22.5 us
    pallas_call x1, Pallas kernels: 6.45 us -> 5.51 us  [local(): pl.pallas_call(far_kernel, out_shape=jax.ShapeDtypeStruct((nodes, width),...]
where the time goes in v9:
time: 49.8 us; the launch traced here: 49.3 us
  Pallas kernels  22.5 us (45%)
  starting transfers between devices  14.3 us (29%)
  waiting for transfers between devices  11 us (22%)
  local copies, waits for them, and re-layouts  1.01 us (2%)
    ppermute x1, waiting for transfers between devices, local(): even = lax.ppermute(normed, NODES, chips_trade(0))  5.95 us
    pallas_call x1, Pallas kernels, local(): pl.pallas_call(functools.partial(message_kernel, pairs), out_shape=outgoi...  5.61 us
    pallas_call x1, Pallas kernels, local(): pl.pallas_call(far_kernel, out_shape=jax.ShapeDtypeStruct((nodes, width),...  5.51 us
    pallas_call x1, Pallas kernels, local(): pl.pallas_call(near_kernel, out_shape=[jax.ShapeDtypeStruct((HEADS, LANES...  5.02 us
    pallas_call x1, Pallas kernels, local(): pl.pallas_call(outer_kernel, out_shape=[jax.ShapeDtypeStruct((HEADS, extr...  3.27 us
    ppermute x1, waiting for transfers between devices, local(): lax.ppermute(part, NODES, chip_trade(p + 1))  2.51 us
    ppermute x1, starting transfers between devices, local(): odd = lax.ppermute(odd, NODES, bands_trade(1))  2.42 us
    ppermute x1, starting transfers between devices, local(): odd_other = lax.ppermute(odd_other, NODES, bands_trade(1, 1))  2.03 us
  transfers between devices with their start and end apart: 15, of which 6 were waited for; matrix products, arithmetic and copies ran while one was open for 1% of the time, Pallas kernels for 22%

profile of v9, /device:TPU:15, one launch (start us, length us, event | category | flops | bytes accessed | tf_op | source)
XLA Modules:
  0.0 49.3 jit_solution(12449103764484769751)
XLA Ops:
  0.0 5.6 %messages.1 = (bf16[272,256]{1,0:T(8,128)(2,1)}, bf16[272,256]{1,0:T(8,128)(2,1)}, bf16[272,256]{1,0:T(8,128)(2,1)}, bf16[272,256]{1,0:T(8,128)(2,1)}, bf16[400,...) custom-call(bf16[1024,512]{1,0:T(8,128)(2,1)} %grid_ref.1, ...), custom_call_target="tpu_custom_call" | custom-call | flops 2147483648 | bytes 4194304 | tf_op jit(solution)/shard_map/messages/pallas_call | solution.py:394
  5.6 0.7 %collective-permute-start.1 = (bf16[672,256]{1,0:T(8,128)(2,1)}, bf16[672,256]{1,0:T(8,128)(2,1)S(1)}, u32[]{:S(2)}, u32[]{:S(2)}) collective-permute-start(bf16[672,256]{1,0:T(8,128)(2,1)} %get-tuple-element.42), channel_id=1, source_target_pairs={{0,1},{1,0},{2,3},{3,2},{4,5},{5,4},{6,7},{7,6},{8,9},{9,8},{10,11... | collective-permute-start | bytes 1032200 | tf_op jit(solution)/shard_map/ppermute | solution.py:425
  6.8 2.4 %collective-permute-start.3 = (bf16[272,256]{1,0:T(8,128)(2,1)}, bf16[272,256]{1,0:T(8,128)(2,1)S(1)}, u32[]{:S(2)}, u32[]{:S(2)}) collective-permute-start(bf16[272,256]{1,0:T(8,128)(2,1)} %get-tuple-element.47), channel_id=1, source_target_pairs={{0,1},{1,0},{2,3},{3,2},{4,8},{5,9},{6,10},{7,11},{8,4},{9,5},{10,... | collective-permute-start | bytes 417800 | tf_op jit(solution)/shard_map/ppermute | solution.py:428
  9.2 2.0 %collective-permute-start.7 = (bf16[400,256]{1,0:T(8,128)(2,1)}, bf16[400,256]{1,0:T(8,128)(2,1)S(1)}, u32[]{:S(2)}, u32[]{:S(2)}) collective-permute-start(bf16[400,256]{1,0:T(8,128)(2,1)} %get-tuple-element.58), channel_id=1, source_target_pairs={{0,3},{1,2},{2,1},{3,0},{4,7},{5,6},{6,5},{7,4},{8,11},{9,10},{10,... | collective-permute-start | bytes 614408 | tf_op jit(solution)/shard_map/ppermute | solution.py:432
  11.2 0.6 %collective-permute-done.refs_0_ = bf16[272,256]{1,0:T(8,128)(2,1)S(1)} collective-permute-done((bf16[272,256]{1,0:T(8,128)(2,1)}, bf16[272,256]{1,0:T(8,128)(2,1)S(1)}, u32[]{:S(2)}, u32[]{:S(2)}) %collective-permute-start) | collective-permute-done | bytes 139296 | tf_op jit(solution)/shard_map/ppermute | solution.py:427
  11.8 2.0 %collective-permute-start.4 = (bf16[272,256]{1,0:T(8,128)(2,1)}, bf16[272,256]{1,0:T(8,128)(2,1)S(1)}, u32[]{:S(2)}, u32[]{:S(2)}) collective-permute-start(bf16[272,256]{1,0:T(8,128)(2,1)} %get-tuple-element.48), channel_id=1, source_target_pairs={{0,1},{1,0},{2,3},{3,2},{4,9},{5,8},{6,11},{7,10},{8,5},{9,4},{10,... | collective-permute-start | bytes 417800 | tf_op jit(solution)/shard_map/ppermute | solution.py:434
  14.2 1.0 %copy-done.2 = bf16[672,256]{1,0:T(8,128)(2,1)S(1)} copy-done((bf16[672,256]{1,0:T(8,128)(2,1)S(1)}, bf16[672,256]{1,0:T(8,128)(2,1)}, u32[]{:S(2)}) %copy-start.2) | copy-done | bytes 344088
  15.2 2.0 %early.1 = (bf16[512,512]{1,0:T(8,128)(2,1)S(1)}, bf16[512,512]{1,0:T(8,128)(2,1)S(1)}, bf16[512,512]{1,0:T(8,128)(2,1)S(1)}, f32[2,256,256]{2,1,0:T(8,128)S(1)}, f32[3,256,256]{2,1,0:T(8,128)S(1)}) custom-call(bf16[512,1536]{1,0:T(8,128)(2,1)S(1)} %copy-done, bf16[672,256]{1,0:T(8,128)(2,1)S(1)} %copy-done.2, ...), custom_call_target="tpu_custom_call" | custom-call | flops 268435456 | bytes 4194304 | tf_op jit(solution)/shard_map/early/pallas_call | solution.py:443
  17.2 1.2 %collective-permute-done.4.refs_3_ = bf16[272,256]{1,0:T(8,128)(2,1)S(1)} collective-permute-done((bf16[272,256]{1,0:T(8,128)(2,1)}, bf16[272,256]{1,0:T(8,128)(2,1)S(1)}, u32[]{:S(2)}, u32[]{:S(2)}) %collective-permute-start.4) | collective-permute-done | bytes 139296 | tf_op jit(solution)/shard_map/ppermute | solution.py:434
  18.4 0.3 left.1
  18.7 0.3 collective-permute-start.5
  19.3 0.3 collective-permute-start.8
  19.6 1.3 %collective-permute-start.9 = (bf16[256,256]{1,0:T(8,128)(2,1)S(1)}, bf16[256,256]{1,0:T(8,128)(2,1)S(1)}, u32[]{:S(2)}, u32[]{:S(2)}) collective-permute-start(bf16[256,256]{1,0:T(8,128)(2,1)S(1)} %get-tuple-element.62), channel_id=1, source_target_pairs={{0,1},{1,0},{2,3},{3,2},{4,8},{5,9},{6,10},{7,11},{8,4},{9,5},{10,... | collective-permute-start | bytes 393224 | tf_op jit(solution)/shard_map/ppermute | solution.py:469
  20.9 2.5 %collective-permute-done.5.refs_1_ = bf16[256,256]{1,0:T(8,128)(2,1)S(1)} collective-permute-done((bf16[256,256]{1,0:T(8,128)(2,1)S(1)}, bf16[256,256]{1,0:T(8,128)(2,1)S(1)}, u32[]{:S(2)}, u32[]{:S(2)}) %collective-permute-start.5) | collective-permute-done | bytes 131104 | tf_op jit(solution)/shard_map/ppermute | solution.py:466
  23.7 0.5 %collective-permute-done.9.refs_4_ = bf16[256,256]{1,0:T(8,128)(2,1)S(1)} collective-permute-done((bf16[256,256]{1,0:T(8,128)(2,1)S(1)}, bf16[256,256]{1,0:T(8,128)(2,1)S(1)}, u32[]{:S(2)}, u32[]{:S(2)}) %collective-permute-start.9) | collective-permute-done | bytes 131104 | tf_op jit(solution)/shard_map/ppermute | solution.py:469
  24.2 0.5 %merge.1 = (f32[256,512]{1,0:T(8,128)S(1)}, bf16[256,512]{1,0:T(8,128)(2,1)S(1)}) custom-call(f32[256,256]{1,0:T(8,128)S(1)} %get-tuple-element.55.refs_0_, bf16[256,256]{1,0:T(8,128)(2,1)S(1)} %collective-permute-done.5.refs_1_, f32[256,256]{1,0:T(8,128)S(1)} %get-tuple-element.60.refs_2_, bf16[256,256]{1,0:T(8,128)(2,1)S(1)} %collective-permute-done.8.refs_3_, ...), custom_call_target="tpu_custom_call" | custom-call | flops 134217728 | bytes 2097152 | tf_op jit(solution)/shard_map/merge/pallas_call | solution.py:471
  24.7 1.4 %collective-permute-start.12 = (bf16[256,512]{1,0:T(8,128)(2,1)S(1)}, bf16[256,512]{1,0:T(8,128)(2,1)S(1)}, u32[]{:S(2)}, u32[]{:S(2)}) collective-permute-start(bf16[256,512]{1,0:T(8,128)(2,1)S(1)} %get-tuple-element.63.own_ref), channel_id=1, source_target_pairs={{0,1},{1,0},{2,3},{3,2},{4,5},{5,4},{6,7},{7,6},{8,9},{9,8},{10,11... | collective-permute-start | bytes 786440 | tf_op jit(solution)/shard_map/ppermute | solution.py:491
  26.1 1.0 %collective-permute-start.10 = (bf16[256,512]{1,0:T(8,128)(2,1)S(1)}, bf16[256,512]{1,0:T(8,128)(2,1)S(1)}, u32[]{:S(2)}, u32[]{:S(2)}) collective-permute-start(bf16[256,512]{1,0:T(8,128)(2,1)S(1)} %get-tuple-element.63.own_ref), channel_id=1, source_target_pairs={{0,2},{1,3},{2,0},{3,1},{4,6},{5,7},{6,4},{7,5},{8,10},{9,11},{10,... | collective-permute-start | bytes 786440 | tf_op jit(solution)/shard_map/ppermute | solution.py:492
  27.1 1.5 %collective-permute-start.11 = (bf16[256,512]{1,0:T(8,128)(2,1)S(1)}, bf16[256,512]{1,0:T(8,128)(2,1)S(1)}, u32[]{:S(2)}, u32[]{:S(2)}) collective-permute-start(bf16[256,512]{1,0:T(8,128)(2,1)S(1)} %get-tuple-element.63.own_ref), channel_id=1, source_target_pairs={{0,1},{1,0},{2,4},{3,5},{4,2},{5,3},{6,8},{7,9},{8,6},{9,7},{10,12... | collective-permute-start | bytes 786440 | tf_op jit(solution)/shard_map/ppermute | solution.py:493
  28.6 5.0 %near.1 = (bf16[16,128,256]{2,1,0:T(8,128)(2,1)S(1)}, f32[16,48,256]{2,1,0:T(8,128)S(1)}, f32[16,8,256]{2,1,0:T(8,128)S(1)}) custom-call(bf16[256,512]{1,0:T(8,128)(2,1)S(1)} %get-tuple-element.63.own_ref, bf16[256,512]{1,0:T(8,128)(2,1)S(1)} %collective-permute-done.12.side_ref, bf16[512,512]{1,0:T(8,128)(2,1)S(1)} %get-tuple-element.64.wq_ref, ...), custom_call_target="tpu_custom_call" | custom-call | flops 8589934592 | bytes 4194304 | tf_op jit(solution)/shard_map/near/pallas_call | solution.py:496
  33.7 6.0 %collective-permute-done.10.even_ref = bf16[256,512]{1,0:T(8,128)(2,1)S(1)} collective-permute-done((bf16[256,512]{1,0:T(8,128)(2,1)S(1)}, bf16[256,512]{1,0:T(8,128)(2,1)S(1)}, u32[]{:S(2)}, u32[]{:S(2)}) %collective-permute-start.10) | collective-permute-done | bytes 262176 | tf_op jit(solution)/shard_map/ppermute | solution.py:492
  39.6 0.9 %collective-permute-start.13 = (bf16[256,512]{1,0:T(8,128)(2,1)S(1)}, bf16[256,512]{1,0:T(8,128)(2,1)S(1)}, u32[]{:S(2)}, u32[]{:S(2)}) collective-permute-start(bf16[256,512]{1,0:T(8,128)(2,1)S(1)} %collective-permute-done.10.even_ref), channel_id=1, source_target_pairs={{0,1},{1,0},{2,3},{3,2},{4,5},{5,4},{6,7},{7,6},{8,9},{9,8},{10,11... | collective-permute-start | bytes 786440 | tf_op jit(solution)/shard_map/ppermute | solution.py:516
  40.5 3.3 %outer.1 = (f32[16,48,256]{2,1,0:T(8,128)S(1)}, f32[16,8,256]{2,1,0:T(8,128)S(1)}) custom-call(bf16[256,512]{1,0:T(8,128)(2,1)S(1)} %collective-permute-done.10.even_ref, bf16[256,512]{1,0:T(8,128)(2,1)S(1)} %collective-permute-done.11.odd_ref, bf16[512,512]{1,0:T(8,128)(2,1)S(1)} %get-tuple-element.65.wk_ref, ...), custom_call_target="tpu_custom_call" | custom-call | flops 1073741824 | bytes 3145728 | tf_op jit(solution)/shard_map/outer/pallas_call | solution.py:518
  43.8 5.5 %far.1 = bf16[256,512]{1,0:T(8,128)(2,1)} custom-call(bf16[256,512]{1,0:T(8,128)(2,1)S(1)} %collective-permute-done.13.first_ref, bf16[256,512]{1,0:T(8,128)(2,1)S(1)} %collective-permute-done.14.second_ref, bf16[512,512]{1,0:T(8,128)(2,1)S(1)} %get-tuple-element.65.wk_ref, bf16[512,512]{1,0:T(8,128)(2,1)S(1)} %get-tuple-element.66.wv_ref, s32[16]{0:T(128)S(1)} %copy-done.9, ...), custom_call_target="tpu_custom_call" | custom-call | flops 8589934592 | bytes 8388608 | tf_op jit(solution)/shard_map/far/pallas_call | solution.py:536
  (36 shorter events, 1.4 us)
Async XLA Ops:
  0.0 13.9 %copy-start.9 = (s32[16]{0:T(128)S(1)}, s32[16]{0:T(128)}, u32[]{:S(2)}) copy-start(s32[16]{0:T(128)} %window_ref.2) | copy-start | bytes 196
  0.0 14.2 %copy-start = (bf16[512,1536]{1,0:T(8,128)(2,1)S(1)}, bf16[512,1536]{1,0:T(8,128)(2,1)}, u32[]{:S(2)}) copy-start(bf16[512,1536]{1,0:T(8,128)(2,1)} %w_ref.2) | copy-start | bytes 4718596
  5.6 3.6 %collective-permute-start.1 = (bf16[672,256]{1,0:T(8,128)(2,1)}, bf16[672,256]{1,0:T(8,128)(2,1)S(1)}, u32[]{:S(2)}, u32[]{:S(2)}) collective-permute-start(bf16[672,256]{1,0:T(8,128)(2,1)} %get-tuple-element.42), channel_id=1, source_target_pairs={{0,1},{1,0},{2,3},{3,2},{4,5},{5,4},{6,7},{7,6},{8,9},{9,8},{10,11... | collective-permute-start | bytes 1032200 | tf_op jit(solution)/shard_map/ppermute | solution.py:425
  6.4 5.5 %collective-permute-start = (bf16[272,256]{1,0:T(8,128)(2,1)}, bf16[272,256]{1,0:T(8,128)(2,1)S(1)}, u32[]{:S(2)}, u32[]{:S(2)}) collective-permute-start(bf16[272,256]{1,0:T(8,128)(2,1)} %get-tuple-element.41), channel_id=1, source_target_pairs={{0,4},{1,5},{2,6},{3,7},{4,0},{5,1},{6,2},{7,3},{8,12},{9,13},{10,... | collective-permute-start | bytes 417800 | tf_op jit(solution)/shard_map/ppermute | solution.py:427
  6.6 12.4 %collective-permute-start.6 = (bf16[400,256]{1,0:T(8,128)(2,1)}, bf16[400,256]{1,0:T(8,128)(2,1)S(1)}, u32[]{:S(2)}, u32[]{:S(2)}) collective-permute-start(bf16[400,256]{1,0:T(8,128)(2,1)} %get-tuple-element.57), channel_id=1, source_target_pairs={{0,2},{1,3},{2,0},{3,1},{4,6},{5,7},{6,4},{7,5},{8,10},{9,11},{10,... | collective-permute-start | bytes 614408 | tf_op jit(solution)/shard_map/ppermute | solution.py:426
  6.8 10.4 %collective-permute-start.3 = (bf16[272,256]{1,0:T(8,128)(2,1)}, bf16[272,256]{1,0:T(8,128)(2,1)S(1)}, u32[]{:S(2)}, u32[]{:S(2)}) collective-permute-start(bf16[272,256]{1,0:T(8,128)(2,1)} %get-tuple-element.47), channel_id=1, source_target_pairs={{0,1},{1,0},{2,3},{3,2},{4,8},{5,9},{6,10},{7,11},{8,4},{9,5},{10,... | collective-permute-start | bytes 417800 | tf_op jit(solution)/shard_map/ppermute | solution.py:428
  9.2 9.7 %collective-permute-start.7 = (bf16[400,256]{1,0:T(8,128)(2,1)}, bf16[400,256]{1,0:T(8,128)(2,1)S(1)}, u32[]{:S(2)}, u32[]{:S(2)}) collective-permute-start(bf16[400,256]{1,0:T(8,128)(2,1)} %get-tuple-element.58), channel_id=1, source_target_pairs={{0,3},{1,2},{2,1},{3,0},{4,7},{5,6},{6,5},{7,4},{8,11},{9,10},{10,... | collective-permute-start | bytes 614408 | tf_op jit(solution)/shard_map/ppermute | solution.py:432
  11.2 5.9 %collective-permute-start.2 = (bf16[272,256]{1,0:T(8,128)(2,1)}, bf16[272,256]{1,0:T(8,128)(2,1)S(1)}, u32[]{:S(2)}, u32[]{:S(2)}) collective-permute-start(bf16[272,256]{1,0:T(8,128)(2,1)} %get-tuple-element.46), channel_id=1, source_target_pairs={{0,5},{1,4},{2,7},{3,6},{4,1},{5,0},{6,3},{7,2},{8,13},{9,12},{10,... | collective-permute-start | bytes 417800 | tf_op jit(solution)/shard_map/ppermute | solution.py:433
  11.8 6.5 %collective-permute-start.4 = (bf16[272,256]{1,0:T(8,128)(2,1)}, bf16[272,256]{1,0:T(8,128)(2,1)S(1)}, u32[]{:S(2)}, u32[]{:S(2)}) collective-permute-start(bf16[272,256]{1,0:T(8,128)(2,1)} %get-tuple-element.48), channel_id=1, source_target_pairs={{0,1},{1,0},{2,3},{3,2},{4,9},{5,8},{6,11},{7,10},{8,5},{9,4},{10,... | collective-permute-start | bytes 417800 | tf_op jit(solution)/shard_map/ppermute | solution.py:434
  15.2 9.0 %copy-start.1 = (bf16[512,512]{1,0:T(8,128)(2,1)S(1)}, bf16[512,512]{1,0:T(8,128)(2,1)}, u32[]{:S(2)}) copy-start(bf16[512,512]{1,0:T(8,128)(2,1)} %refs_6_.1) | copy-start | bytes 1572868
  15.2 9.1 %copy-start.3 = (bf16[256,512]{1,0:T(8,128)(2,1)S(1)}, bf16[256,512]{1,0:T(8,128)(2,1)}, u32[]{:S(2)}) copy-start(bf16[256,512]{1,0:T(8,128)(2,1)} %refs_5_.1) | copy-start | bytes 786436
  15.2 9.1 %copy-start.4 = (f32[512]{0:T(512)S(1)}, f32[512]{0:T(512)}, u32[]{:S(2)}) copy-start(f32[512]{0:T(512)} %param.21) | copy-start | bytes 6148
  18.7 4.7 %collective-permute-start.5 = (bf16[256,256]{1,0:T(8,128)(2,1)S(1)}, bf16[256,256]{1,0:T(8,128)(2,1)S(1)}, u32[]{:S(2)}, u32[]{:S(2)}) collective-permute-start(bf16[256,256]{1,0:T(8,128)(2,1)S(1)} %get-tuple-element.56), channel_id=1, source_target_pairs={{0,2},{1,3},{2,0},{3,1},{4,6},{5,7},{6,4},{7,5},{8,10},{9,11},{10,... | collective-permute-start | bytes 393224 | tf_op jit(solution)/shard_map/ppermute | solution.py:466
  19.3 4.4 %collective-permute-start.8 = (bf16[256,256]{1,0:T(8,128)(2,1)S(1)}, bf16[256,256]{1,0:T(8,128)(2,1)S(1)}, u32[]{:S(2)}, u32[]{:S(2)}) collective-permute-start(bf16[256,256]{1,0:T(8,128)(2,1)S(1)} %get-tuple-element.61), channel_id=1, source_target_pairs={{0,4},{1,5},{2,6},{3,7},{4,0},{5,1},{6,2},{7,3},{8,12},{9,13},{10,... | collective-permute-start | bytes 393224 | tf_op jit(solution)/shard_map/ppermute | solution.py:468
  19.6 4.6 %collective-permute-start.9 = (bf16[256,256]{1,0:T(8,128)(2,1)S(1)}, bf16[256,256]{1,0:T(8,128)(2,1)S(1)}, u32[]{:S(2)}, u32[]{:S(2)}) collective-permute-start(bf16[256,256]{1,0:T(8,128)(2,1)S(1)} %get-tuple-element.62), channel_id=1, source_target_pairs={{0,1},{1,0},{2,3},{3,2},{4,8},{5,9},{6,10},{7,11},{8,4},{9,5},{10,... | collective-permute-start | bytes 393224 | tf_op jit(solution)/shard_map/ppermute | solution.py:469
  24.7 3.9 %collective-permute-start.12 = (bf16[256,512]{1,0:T(8,128)(2,1)S(1)}, bf16[256,512]{1,0:T(8,128)(2,1)S(1)}, u32[]{:S(2)}, u32[]{:S(2)}) collective-permute-start(bf16[256,512]{1,0:T(8,128)(2,1)S(1)} %get-tuple-element.63.own_ref), channel_id=1, source_target_pairs={{0,1},{1,0},{2,3},{3,2},{4,5},{5,4},{6,7},{7,6},{8,9},{9,8},{10,11... | collective-permute-start | bytes 786440 | tf_op jit(solution)/shard_map/ppermute | solution.py:491
  26.1 13.5 %collective-permute-start.10 = (bf16[256,512]{1,0:T(8,128)(2,1)S(1)}, bf16[256,512]{1,0:T(8,128)(2,1)S(1)}, u32[]{:S(2)}, u32[]{:S(2)}) collective-permute-start(bf16[256,512]{1,0:T(8,128)(2,1)S(1)} %get-tuple-element.63.own_ref), channel_id=1, source_target_pairs={{0,2},{1,3},{2,0},{3,1},{4,6},{5,7},{6,4},{7,5},{8,10},{9,11},{10,... | collective-permute-start | bytes 786440 | tf_op jit(solution)/shard_map/ppermute | solution.py:492
  27.1 12.5 %collective-permute-start.11 = (bf16[256,512]{1,0:T(8,128)(2,1)S(1)}, bf16[256,512]{1,0:T(8,128)(2,1)S(1)}, u32[]{:S(2)}, u32[]{:S(2)}) collective-permute-start(bf16[256,512]{1,0:T(8,128)(2,1)S(1)} %get-tuple-element.63.own_ref), channel_id=1, source_target_pairs={{0,1},{1,0},{2,4},{3,5},{4,2},{5,3},{6,8},{7,9},{8,6},{9,7},{10,12... | collective-permute-start | bytes 786440 | tf_op jit(solution)/shard_map/ppermute | solution.py:493
  28.6 15.2 %copy-start.6 = (bf16[2048,512]{1,0:T(8,128)(2,1)S(1)}, bf16[2048,512]{1,0:T(8,128)(2,1)}, u32[]{:S(2)}) copy-start(bf16[2048,512]{1,0:T(8,128)(2,1)} %down_ref.1) | copy-start | bytes 6291460
  33.6 10.2 %copy-start.5 = (bf16[512,2048]{1,0:T(8,128)(2,1)S(1)}, bf16[512,2048]{1,0:T(8,128)(2,1)}, u32[]{:S(2)}) copy-start(bf16[512,2048]{1,0:T(8,128)(2,1)} %up_ref.1) | copy-start | bytes 6291460
  33.6 10.2 %copy-start.7 = (bf16[512,512]{1,0:T(8,128)(2,1)S(1)}, bf16[512,512]{1,0:T(8,128)(2,1)}, u32[]{:S(2)}) copy-start(bf16[512,512]{1,0:T(8,128)(2,1)} %w_out_ref.1) | copy-start | bytes 1572868
  33.6 10.2 %copy-start.8 = (f32[512]{0:T(512)S(1)}, f32[512]{0:T(512)}, u32[]{:S(2)}) copy-start(f32[512]{0:T(512)} %param.25) | copy-start | bytes 6148
  39.6 4.1 %collective-permute-start.13 = (bf16[256,512]{1,0:T(8,128)(2,1)S(1)}, bf16[256,512]{1,0:T(8,128)(2,1)S(1)}, u32[]{:S(2)}, u32[]{:S(2)}) collective-permute-start(bf16[256,512]{1,0:T(8,128)(2,1)S(1)} %collective-permute-done.10.even_ref), channel_id=1, source_target_pairs={{0,1},{1,0},{2,3},{3,2},{4,5},{5,4},{6,7},{7,6},{8,9},{9,8},{10,11... | collective-permute-start | bytes 786440 | tf_op jit(solution)/shard_map/ppermute | solution.py:516
  40.5 3.3 %collective-permute-start.14 = (bf16[256,512]{1,0:T(8,128)(2,1)S(1)}, bf16[256,512]{1,0:T(8,128)(2,1)S(1)}, u32[]{:S(2)}, u32[]{:S(2)}) collective-permute-start(bf16[256,512]{1,0:T(8,128)(2,1)S(1)} %collective-permute-done.11.odd_ref), channel_id=1, source_target_pairs={{0,1},{1,0},{2,3},{3,2},{4,5},{5,4},{6,7},{7,6},{8,9},{9,8},{10,11... | collective-permute-start | bytes 786440 | tf_op jit(solution)/shard_map/ppermute | solution.py:517
  (1 other events, 1.0 us)

commit v10 on v9

--- a/solution.py
+++ b/solution.py
@@ -14,7 +14,8 @@
 NEAR = 128
 TILE = 16
 CAP = 128
-GRID_PARTS = 2
+GRID_PARTS = 8
+CHUNKS = 2
 MOST = 56
 GROUP = 4
 
@@ -76,11 +77,12 @@
     rows = grid_ref.shape[0]
     cap = source_ref.shape[-1]
     half = w_ref.shape[1] // 2
-    part = rows // GRID_PARTS
-    fetches = [pltpu.make_async_copy(w_ref, w_vmem, in_sems.at[GRID_PARTS])]
-    for k in range(GRID_PARTS):
-        span = pl.ds(k * part, part)
-        fetches.append(pltpu.make_async_copy(grid_ref.at[span], grid_vmem.at[span], in_sems.at[k]))
+    fetches = []
+    for source, target in ((w_ref, w_vmem), (grid_ref, grid_vmem)):
+        part = source.shape[0] // GRID_PARTS
+        for n in range(GRID_PARTS):
+            span = pl.ds(n * part, part)
+            fetches.append(pltpu.make_async_copy(source.at[span], target.at[span], in_sems.at[len(fetches)]))
     for fetch in fetches:
         fetch.start()
     inner = lax.axis_index("inner")
@@ -103,10 +105,12 @@
     row = lax.broadcasted_iota(jnp.int32, (cap, rows), 1)
     for m in range(len(keys)):
         pick_ref[m * cap : (m + 1) * cap, :] = jnp.where(row == by_slot[:, m : m + 1], 1.0, 0.0).astype(jnp.bfloat16)
-    fetches[0].wait()
-    for k in range(GRID_PARTS):
-        span = pl.ds(k * part, part)
-        fetches[k + 1].wait()
+    for fetch in fetches[:GRID_PARTS]:
+        fetch.wait()
+    for n in range(CHUNKS):
+        for fetch in fetches[GRID_PARTS * (CHUNKS + n) // CHUNKS : GRID_PARTS * (CHUNKS + n + 1) // CHUNKS]:
+            fetch.wait()
+        span = pl.ds(n * (rows // CHUNKS), rows // CHUNKS)
         message_ref[span] = silu(dot(grid_vmem[span], w_vmem[...])).astype(jnp.bfloat16)
     sends = []
     per_core = len(keys) // 2
@@ -289,38 +293,56 @@
     far = 2 - 4 * lax.rem(lax.axis_index("inner") // 2, 2)
     scale = head_dim ** (-0.5) / math.log(2.0)
     value_ref[:, head_dim:, :] = jnp.ones_like(value_ref[:, head_dim:, :])
-    project_keys(even_ref[...], wk_ref, wv_ref, key_ref, value_ref, 0)
-    project_keys(odd_ref[...], wk_ref, wv_ref, key_ref, value_ref, nodes)
+    project_keys(jnp.concatenate([even_ref[...], odd_ref[...]], axis=0), wk_ref, wv_ref, key_ref, value_ref, 0)
     gap_ref[0:nodes] = gaps(far, 0, nodes, nodes)
     gap_ref[nodes:] = gaps(-far, 0, nodes, nodes)
 
-    def together(i, carry):
-        heads = [order_ref[GROUP * i + k] for k in range(GROUP)]
-        widest = functools.reduce(jnp.maximum, [window_ref[h] for h in heads])
-
-        @pl.when(widest > nodes)
-        def _():
-            keys, values = [key_ref[h // per_group] for h in heads], [value_ref[h] for h in heads]
-            for h, sums, top in extend(
-                heads, keys, values, gap_ref, window_ref, query_ref, sums_ref, top_ref, scale
-            ):
-                sums_out[h] = sums
-                top_out[h] = jnp.broadcast_to(top, top_out.shape[1:])
-
-        @pl.when(widest <= nodes)
-        def _():
-            for h in heads:
-                sums_out[h] = sums_ref[h]
-                top_out[h] = top_ref[h]
-
-        return carry
-
-    lax.fori_loop(0, HEADS // GROUP, together, 0)
+    def wide(n):
+        return window_ref[order_ref[n]] > nodes
+
+    def reach(first, last):
+        heads = [order_ref[n] for n in range(first, last)]
+        keys, values = [key_ref[h // per_group] for h in heads], [value_ref[h] for h in heads]
+        for h, sums, top in extend(
+            heads, keys, values, gap_ref, window_ref, query_ref, sums_ref, top_ref, scale
+        ):
+            sums_out[h] = sums
+            top_out[h] = jnp.broadcast_to(top, top_out.shape[1:])
+
+    def leave(first, last):
+        for n in range(first, last):
+            h = order_ref[n]
+            sums_out[h] = sums_ref[h]
+            top_out[h] = top_ref[h]
+
+    @pl.when(wide(GROUP))
+    def _():
+        reach(0, 2 * GROUP)
+
+    @pl.when(jnp.logical_not(wide(GROUP)))
+    def _():
+        reach(0, GROUP)
+        leave(GROUP, 2 * GROUP)
+
+    for first in range(2 * GROUP, HEADS, GROUP):
+        pl.when(wide(first))(functools.partial(reach, first, first + GROUP))
+        pl.when(jnp.logical_not(wide(first)))(functools.partial(leave, first, first + GROUP))
+
+
+def turn_kernel(up_ref, down_ref, w_out_ref, gain_ref, state_ref, up_t, down_t, w_out_t, gain_t, state_t):
+    side = 2 * LANES
+    one = lax.broadcasted_iota(jnp.int32, (side, side), 0) == lax.broadcasted_iota(jnp.int32, (side, side), 1)
+    unit = jnp.where(one, 1.0, 0.0).astype(jnp.bfloat16)
+    for ref, turned in ((up_ref, up_t), (down_ref, down_t), (w_out_ref, w_out_t)):
+        for start in range(0, ref.shape[1], side):
+            turned[start : start + side, :] = dot_t(unit, ref[:, start : start + side]).astype(jnp.bfloat16)
+    gain_t[...] = jnp.transpose(jnp.broadcast_to(gain_ref[...], (LANES, gain_ref.shape[1])))
+    state_t[...] = jnp.transpose(state_ref[...])
 
 
 def far_kernel(
     first_ref, second_ref, wk_ref, wv_ref, window_ref, query_ref, sums_ref, top_ref,
-    state_ref, w_out_ref, gain_ref, up_ref, down_ref,
+    up_t, down_t, w_out_t, gain_t, state_t,
     out_ref,
     key_ref, value_ref, gap_ref, attended_ref,
 ):
@@ -342,17 +364,16 @@
         ):
             attended_ref[h] = (sums[0:head_dim] / sums[head_dim : head_dim + 1]).astype(jnp.bfloat16)
 
-    attended = attended_ref[...].reshape(width, nodes)
-    mixed = lax.dot_general(
-        attended, w_out_ref[...], (((0,), (0,)), ((), ())), preferred_element_type=jnp.float32
-    )
-    total = state_ref[...] + mixed
-    normed = layer_norm(total, gain_ref[...]).astype(jnp.bfloat16)
-    chunk = math.gcd(up_ref.shape[1], 512)
-    for start in range(0, up_ref.shape[1], chunk):
-        hidden = silu(dot(normed, up_ref[:, start : start + chunk])).astype(jnp.bfloat16)
-        total = total + dot(hidden, down_ref[start : start + chunk, :])
-    out_ref[...] = total.astype(jnp.bfloat16)
+    total = state_t[...] + dot(w_out_t[...], attended_ref[...].reshape(width, nodes))
+    center = total - jnp.mean(total, axis=0, keepdims=True)
+    spread = jnp.mean(center * center, axis=0, keepdims=True)
+    gain = jnp.concatenate([gain_t[...]] * (nodes // LANES), axis=1)
+    normed = (center * lax.rsqrt(spread + norm_eps) * gain).astype(jnp.bfloat16)
+    chunk = math.gcd(up_t.shape[0], 512)
+    for start in range(0, up_t.shape[0], chunk):
+        hidden = silu(dot(up_t[start : start + chunk, :], normed)).astype(jnp.bfloat16)
+        total = total + dot(down_t[:, start : start + chunk], hidden)
+    out_ref[...] = jnp.transpose(total).astype(jnp.bfloat16)
 
 
 def cost(flops, size):
@@ -402,7 +423,7 @@
             pltpu.VMEM(w_message.shape, bf16),
             pltpu.VMEM((grid_dev, width), bf16),
             pltpu.VMEM((3 * inners * cap, grid_dev), bf16),
-            pltpu.SemaphoreType.DMA((GRID_PARTS + 1,)),
+            pltpu.SemaphoreType.DMA((2 * GRID_PARTS,)),
             pltpu.SemaphoreType.DMA((len(outgoing),)),
         ],
         compiler_params=params(MOST),
@@ -512,7 +533,18 @@
         name="near",
     )(normed, side, w_query, w_key, w_value, order, window)
 
-    even, odd, near, top = lax.optimization_barrier((even, odd, near, top))
+    w_up, w_down, w_out, state, near, top = lax.optimization_barrier((w_up, w_down, w_out, state, near, top))
+    turned = pl.pallas_call(
+        turn_kernel,
+        out_shape=[jax.ShapeDtypeStruct(w.shape[::-1], bf16) for w in (w_up, w_down, w_out)]
+        + [jax.ShapeDtypeStruct((width, LANES), f32), jax.ShapeDtypeStruct((width, nodes), f32)],
+        in_specs=[VMEM] * 5,
+        out_specs=[VMEM] * 5,
+        compiler_params=params(24),
+        cost_estimate=cost(4 << 30, 10 << 20),
+        name="turn",
+    )(w_up, w_down, w_out, gain_mlp.reshape(1, width), state)
+    even, odd, near, top, *turned = lax.optimization_barrier((even, odd, near, top, *turned))
     first = lax.ppermute(even, NODES, beside)
     second = lax.ppermute(odd, NODES, beside)
     near, top = pl.pallas_call(
@@ -549,7 +581,7 @@
         name="far",
     )(
         first, second, w_key, w_value, window,
-        query, near, top, state, w_out, gain_mlp.reshape(1, width), w_up, w_down,
+        query, near, top, *turned,
     )
 
 

time: 49.8 us -> 52.3 us (1.050)
  waiting for transfers between devices: 11 us -> 16 us
  starting transfers between devices: 14.3 us -> 10.9 us
  Pallas kernels: 22.5 us -> 23.2 us
    ppermute x1, waiting for transfers between devices: 0.29 us -> 3.92 us  [local(): from_even = lax.ppermute(to_even, NODES, bands_trade(0))]
    ppermute x1, waiting for transfers between devices: 0.01 us -> 3.35 us  [local(): lax.ppermute(c, NODES, chip_trade(p + 1, 1))]
    ppermute x1, waiting for transfers between devices: 2.51 us -> 0.65 us  [local(): lax.ppermute(part, NODES, chip_trade(p + 1))]
    pallas_call x0 -> x1, Pallas kernels: none -> 1.43 us  [local(): pl.pallas_call(turn_kernel, out_shape=[jax.ShapeDtypeStruct(w.shape[::-1]...]
    ppermute x1, starting transfers between devices: 1.04 us -> 0.01 us  [local(): even = lax.ppermute(normed, NODES, chips_trade(0))]
    ppermute x1, starting transfers between devices: 2 us -> 0.98 us  [local(): lax.ppermute(c, NODES, chip_trade(p + 1, 1))]
    ppermute x1, waiting for transfers between devices: 1.16 us -> 0.25 us  [local(): odd_other = lax.ppermute(odd_other, NODES, bands_trade(1, 1))]
    ppermute x1, waiting for transfers between devices: 0.01 us -> 0.77 us  [local(): odd = lax.ppermute(normed, NODES, chips_trade(1))]
  transfers between devices with their start and end apart: 15 -> 15, of which waited for: 6 -> 7; matrix products, arithmetic and copies ran while one was open for 1% -> 1% of each run, Pallas kernels for 22% -> 22%
where the time goes in v10:
time: 52.3 us; the launch traced here: 51.5 us
  Pallas kernels  23.2 us (44%)
  waiting for transfers between devices  16 us (31%)
  starting transfers between devices  10.9 us (21%)
  local copies, waits for them, and re-layouts  1.01 us (2%)
    ppermute x1, waiting for transfers between devices, local(): even = lax.ppermute(normed, NODES, chips_trade(0))  5.95 us
    pallas_call x1, Pallas kernels, local(): pl.pallas_call(functools.partial(message_kernel, pairs), out_shape=outgoi...  5.82 us
    pallas_call x1, Pallas kernels, local(): pl.pallas_call(far_kernel, out_shape=jax.ShapeDtypeStruct((nodes, width),...  5.45 us
    pallas_call x1, Pallas kernels, local(): pl.pallas_call(near_kernel, out_shape=[jax.ShapeDtypeStruct((HEADS, LANES...  4.84 us
    ppermute x1, waiting for transfers between devices, local(): from_even = lax.ppermute(to_even, NODES, bands_trade(0))  3.92 us
    ppermute x1, waiting for transfers between devices, local(): lax.ppermute(c, NODES, chip_trade(p + 1, 1))  3.35 us
    pallas_call x1, Pallas kernels, local(): pl.pallas_call(outer_kernel, out_shape=[jax.ShapeDtypeStruct((HEADS, extr...  2.52 us
    ppermute x1, starting transfers between devices, local(): odd = lax.ppermute(odd, NODES, bands_trade(1))  2.42 us
  transfers between devices with their start and end apart: 15, of which 7 were waited for; matrix products, arithmetic and copies ran while one was open for 1% of the time, Pallas kernels for 22%

profile of v10, /device:TPU:15, one launch (start us, length us, event | category | flops | bytes accessed | tf_op | source)
XLA Modules:
  0.0 51.5 jit_solution(7255446030357765094)
XLA Ops:
  0.0 5.8 %messages.1 = (bf16[272,256]{1,0:T(8,128)(2,1)}, bf16[272,256]{1,0:T(8,128)(2,1)}, bf16[272,256]{1,0:T(8,128)(2,1)}, bf16[272,256]{1,0:T(8,128)(2,1)}, bf16[400,...) custom-call(bf16[1024,512]{1,0:T(8,128)(2,1)} %grid_ref.1, ...), custom_call_target="tpu_custom_call" | custom-call | flops 2147483648 | bytes 4194304 | tf_op jit(solution)/shard_map/messages/pallas_call | solution.py:415
  5.8 0.7 %collective-permute-start.1 = (bf16[672,256]{1,0:T(8,128)(2,1)}, bf16[672,256]{1,0:T(8,128)(2,1)S(1)}, u32[]{:S(2)}, u32[]{:S(2)}) collective-permute-start(bf16[672,256]{1,0:T(8,128)(2,1)} %get-tuple-element.58), channel_id=1, source_target_pairs={{0,1},{1,0},{2,3},{3,2},{4,5},{5,4},{6,7},{7,6},{8,9},{9,8},{10,11... | collective-permute-start | bytes 1032200 | tf_op jit(solution)/shard_map/ppermute | solution.py:446
  6.8 2.4 %collective-permute-start.3 = (bf16[272,256]{1,0:T(8,128)(2,1)}, bf16[272,256]{1,0:T(8,128)(2,1)S(1)}, u32[]{:S(2)}, u32[]{:S(2)}) collective-permute-start(bf16[272,256]{1,0:T(8,128)(2,1)} %get-tuple-element.63), channel_id=1, source_target_pairs={{0,1},{1,0},{2,3},{3,2},{4,8},{5,9},{6,10},{7,11},{8,4},{9,5},{10,... | collective-permute-start | bytes 417800 | tf_op jit(solution)/shard_map/ppermute | solution.py:449
  9.4 1.5 %collective-permute-start.4 = (bf16[272,256]{1,0:T(8,128)(2,1)}, bf16[272,256]{1,0:T(8,128)(2,1)S(1)}, u32[]{:S(2)}, u32[]{:S(2)}) collective-permute-start(bf16[272,256]{1,0:T(8,128)(2,1)} %get-tuple-element.64), channel_id=1, source_target_pairs={{0,1},{1,0},{2,3},{3,2},{4,9},{5,8},{6,11},{7,10},{8,5},{9,4},{10,... | collective-permute-start | bytes 417800 | tf_op jit(solution)/shard_map/ppermute | solution.py:455
  11.0 1.1 %collective-permute-done.refs_0_ = bf16[272,256]{1,0:T(8,128)(2,1)S(1)} collective-permute-done((bf16[272,256]{1,0:T(8,128)(2,1)}, bf16[272,256]{1,0:T(8,128)(2,1)S(1)}, u32[]{:S(2)}, u32[]{:S(2)}) %collective-permute-start) | collective-permute-done | bytes 139296 | tf_op jit(solution)/shard_map/ppermute | solution.py:448
  12.0 1.0 %collective-permute-start.7 = (bf16[400,256]{1,0:T(8,128)(2,1)}, bf16[400,256]{1,0:T(8,128)(2,1)S(1)}, u32[]{:S(2)}, u32[]{:S(2)}) collective-permute-start(bf16[400,256]{1,0:T(8,128)(2,1)} %get-tuple-element.74), channel_id=1, source_target_pairs={{0,3},{1,2},{2,1},{3,0},{4,7},{5,6},{6,5},{7,4},{8,11},{9,10},{10,... | collective-permute-start | bytes 614408 | tf_op jit(solution)/shard_map/ppermute | solution.py:453
  13.3 1.0 %copy-done.2 = bf16[672,256]{1,0:T(8,128)(2,1)S(1)} copy-done((bf16[672,256]{1,0:T(8,128)(2,1)S(1)}, bf16[672,256]{1,0:T(8,128)(2,1)}, u32[]{:S(2)}) %copy-start.2) | copy-done | bytes 344088
  14.3 2.0 %early.1 = (bf16[512,512]{1,0:T(8,128)(2,1)S(1)}, bf16[512,512]{1,0:T(8,128)(2,1)S(1)}, bf16[512,512]{1,0:T(8,128)(2,1)S(1)}, f32[2,256,256]{2,1,0:T(8,128)S(1)}, f32[3,256,256]{2,1,0:T(8,128)S(1)}) custom-call(bf16[512,1536]{1,0:T(8,128)(2,1)S(1)} %copy-done, bf16[672,256]{1,0:T(8,128)(2,1)S(1)} %copy-done.2, ...), custom_call_target="tpu_custom_call" | custom-call | flops 268435456 | bytes 4194304 | tf_op jit(solution)/shard_map/early/pallas_call | solution.py:464
  16.6 0.3 left.1
  16.9 1.0 %collective-permute-start.5 = (bf16[256,256]{1,0:T(8,128)(2,1)S(1)}, bf16[256,256]{1,0:T(8,128)(2,1)S(1)}, u32[]{:S(2)}, u32[]{:S(2)}) collective-permute-start(bf16[256,256]{1,0:T(8,128)(2,1)S(1)} %get-tuple-element.72), channel_id=1, source_target_pairs={{0,2},{1,3},{2,0},{3,1},{4,6},{5,7},{6,4},{7,5},{8,10},{9,11},{10,... | collective-permute-start | bytes 393224 | tf_op jit(solution)/shard_map/ppermute | solution.py:487
  18.0 3.3 %collective-permute-done.7.refs_1_ = bf16[400,256]{1,0:T(8,128)(2,1)S(1)} collective-permute-done((bf16[400,256]{1,0:T(8,128)(2,1)}, bf16[400,256]{1,0:T(8,128)(2,1)S(1)}, u32[]{:S(2)}, u32[]{:S(2)}) %collective-permute-start.7) | collective-permute-done | bytes 204832 | tf_op jit(solution)/shard_map/ppermute | solution.py:453
  21.7 0.6 %collective-permute-start.9 = (bf16[256,256]{1,0:T(8,128)(2,1)S(1)}, bf16[256,256]{1,0:T(8,128)(2,1)S(1)}, u32[]{:S(2)}, u32[]{:S(2)}) collective-permute-start(bf16[256,256]{1,0:T(8,128)(2,1)S(1)} %get-tuple-element.78), channel_id=1, source_target_pairs={{0,1},{1,0},{2,3},{3,2},{4,8},{5,9},{6,10},{7,11},{8,4},{9,5},{10,... | collective-permute-start | bytes 393224 | tf_op jit(solution)/shard_map/ppermute | solution.py:490
  22.3 0.7 %collective-permute-done.5.refs_1_ = bf16[256,256]{1,0:T(8,128)(2,1)S(1)} collective-permute-done((bf16[256,256]{1,0:T(8,128)(2,1)S(1)}, bf16[256,256]{1,0:T(8,128)(2,1)S(1)}, u32[]{:S(2)}, u32[]{:S(2)}) %collective-permute-start.5) | collective-permute-done | bytes 131104 | tf_op jit(solution)/shard_map/ppermute | solution.py:487
  23.0 3.9 %collective-permute-done.8.refs_3_ = bf16[256,256]{1,0:T(8,128)(2,1)S(1)} collective-permute-done((bf16[256,256]{1,0:T(8,128)(2,1)S(1)}, bf16[256,256]{1,0:T(8,128)(2,1)S(1)}, u32[]{:S(2)}, u32[]{:S(2)}) %collective-permute-start.8) | collective-permute-done | bytes 131104 | tf_op jit(solution)/shard_map/ppermute | solution.py:489
  26.9 0.5 merge.1
  27.4 0.8 %collective-permute-start.12 = (bf16[256,512]{1,0:T(8,128)(2,1)S(1)}, bf16[256,512]{1,0:T(8,128)(2,1)S(1)}, u32[]{:S(2)}, u32[]{:S(2)}) collective-permute-start(bf16[256,512]{1,0:T(8,128)(2,1)S(1)} %get-tuple-element.79.own_ref), channel_id=1, source_target_pairs={{0,1},{1,0},{2,3},{3,2},{4,5},{5,4},{6,7},{7,6},{8,9},{9,8},{10,11... | collective-permute-start | bytes 786440 | tf_op jit(solution)/shard_map/ppermute | solution.py:512
  28.2 1.7 %collective-permute-start.11 = (bf16[256,512]{1,0:T(8,128)(2,1)S(1)}, bf16[256,512]{1,0:T(8,128)(2,1)S(1)}, u32[]{:S(2)}, u32[]{:S(2)}) collective-permute-start(bf16[256,512]{1,0:T(8,128)(2,1)S(1)} %get-tuple-element.79.own_ref), channel_id=1, source_target_pairs={{0,1},{1,0},{2,4},{3,5},{4,2},{5,3},{6,8},{7,9},{8,6},{9,7},{10,12... | collective-permute-start | bytes 786440 | tf_op jit(solution)/shard_map/ppermute | solution.py:514
  30.0 4.8 %near.1 = (bf16[16,128,256]{2,1,0:T(8,128)(2,1)S(1)}, f32[16,48,256]{2,1,0:T(8,128)S(1)}, f32[16,8,256]{2,1,0:T(8,128)S(1)}) custom-call(bf16[256,512]{1,0:T(8,128)(2,1)S(1)} %get-tuple-element.79.own_ref, bf16[256,512]{1,0:T(8,128)(2,1)S(1)} %collective-permute-done.12.side_ref, bf16[512,512]{1,0:T(8,128)(2,1)S(1)} %get-tuple-element.81.wq_ref, ...), custom_call_target="tpu_custom_call" | custom-call | flops 8589934592 | bytes 4194304 | tf_op jit(solution)/shard_map/near/pallas_call | solution.py:517
  34.9 1.4 %turn.1 = (bf16[2048,512]{1,0:T(8,128)(2,1)S(1)}, bf16[512,2048]{1,0:T(8,128)(2,1)S(1)}, bf16[512,512]{1,0:T(8,128)(2,1)S(1)}, f32[512,128]{1,0:T(8,128)S(1)}, f32[512,256]{1,0:T(8,128)S(1)}) custom-call(bf16[512,2048]{1,0:T(8,128)(2,1)S(1)} %copy-done.5, bf16[2048,512]{1,0:T(8,128)(2,1)S(1)} %copy-done.6, bf16[512,512]{1,0:T(8,128)(2,1)S(1)} %copy-done.7, ...), custom_call_target="tpu_custom_call" | custom-call | flops 4294967296 | bytes 10485760 | tf_op jit(solution)/shard_map/turn/pallas_call | solution.py:537
  36.3 0.8 %collective-permute-done.11.odd_ref = bf16[256,512]{1,0:T(8,128)(2,1)S(1)} collective-permute-done((bf16[256,512]{1,0:T(8,128)(2,1)S(1)}, bf16[256,512]{1,0:T(8,128)(2,1)S(1)}, u32[]{:S(2)}, u32[]{:S(2)}) %collective-permute-start.11) | collective-permute-done | bytes 262176 | tf_op jit(solution)/shard_map/ppermute | solution.py:514
  37.1 6.0 %collective-permute-done.10.even_ref = bf16[256,512]{1,0:T(8,128)(2,1)S(1)} collective-permute-done((bf16[256,512]{1,0:T(8,128)(2,1)S(1)}, bf16[256,512]{1,0:T(8,128)(2,1)S(1)}, u32[]{:S(2)}, u32[]{:S(2)}) %collective-permute-start.10) | collective-permute-done | bytes 262176 | tf_op jit(solution)/shard_map/ppermute | solution.py:513
  43.0 0.5 collective-permute-start.13
  43.5 2.5 %outer.1 = (f32[16,48,256]{2,1,0:T(8,128)S(1)}, f32[16,8,256]{2,1,0:T(8,128)S(1)}) custom-call(bf16[256,512]{1,0:T(8,128)(2,1)S(1)} %collective-permute-done.10.even_ref, bf16[256,512]{1,0:T(8,128)(2,1)S(1)} %collective-permute-done.11.odd_ref, bf16[512,512]{1,0:T(8,128)(2,1)S(1)} %get-tuple-element.82.wk_ref, ...), custom_call_target="tpu_custom_call" | custom-call | flops 1073741824 | bytes 3145728 | tf_op jit(solution)/shard_map/outer/pallas_call | solution.py:550
  46.1 5.5 %far.1 = bf16[256,512]{1,0:T(8,128)(2,1)} custom-call(bf16[256,512]{1,0:T(8,128)(2,1)S(1)} %collective-permute-done.13.first_ref, bf16[256,512]{1,0:T(8,128)(2,1)S(1)} %collective-permute-done.14.second_ref, bf16[512,512]{1,0:T(8,128)(2,1)S(1)} %get-tuple-element.82.wk_ref, bf16[512,512]{1,0:T(8,128)(2,1)S(1)} %get-tuple-element.83.wv_ref, s32[16]{0:T(128)S(1)} %copy-done.9, ...), custom_call_target="tpu_custom_call" | custom-call | flops 8589934592 | bytes 8388608 | tf_op jit(solution)/shard_map/far/pallas_call | solution.py:568
  (37 shorter events, 1.4 us)
Async XLA Ops:
  0.0 13.0 %copy-start.9 = (s32[16]{0:T(128)S(1)}, s32[16]{0:T(128)}, u32[]{:S(2)}) copy-start(s32[16]{0:T(128)} %window_ref.2) | copy-start | bytes 196
  0.0 13.3 %copy-start = (bf16[512,1536]{1,0:T(8,128)(2,1)S(1)}, bf16[512,1536]{1,0:T(8,128)(2,1)}, u32[]{:S(2)}) copy-start(bf16[512,1536]{1,0:T(8,128)(2,1)} %w_ref.2) | copy-start | bytes 4718596
  5.8 3.6 %collective-permute-start.1 = (bf16[672,256]{1,0:T(8,128)(2,1)}, bf16[672,256]{1,0:T(8,128)(2,1)S(1)}, u32[]{:S(2)}, u32[]{:S(2)}) collective-permute-start(bf16[672,256]{1,0:T(8,128)(2,1)} %get-tuple-element.58), channel_id=1, source_target_pairs={{0,1},{1,0},{2,3},{3,2},{4,5},{5,4},{6,7},{7,6},{8,9},{9,8},{10,11... | collective-permute-start | bytes 1032200 | tf_op jit(solution)/shard_map/ppermute | solution.py:446
  6.6 5.5 %collective-permute-start = (bf16[272,256]{1,0:T(8,128)(2,1)}, bf16[272,256]{1,0:T(8,128)(2,1)S(1)}, u32[]{:S(2)}, u32[]{:S(2)}) collective-permute-start(bf16[272,256]{1,0:T(8,128)(2,1)} %get-tuple-element.57), channel_id=1, source_target_pairs={{0,4},{1,5},{2,6},{3,7},{4,0},{5,1},{6,2},{7,3},{8,12},{9,13},{10,... | collective-permute-start | bytes 417800 | tf_op jit(solution)/shard_map/ppermute | solution.py:448
  6.8 9.6 %collective-permute-start.3 = (bf16[272,256]{1,0:T(8,128)(2,1)}, bf16[272,256]{1,0:T(8,128)(2,1)S(1)}, u32[]{:S(2)}, u32[]{:S(2)}) collective-permute-start(bf16[272,256]{1,0:T(8,128)(2,1)} %get-tuple-element.63), channel_id=1, source_target_pairs={{0,1},{1,0},{2,3},{3,2},{4,8},{5,9},{6,10},{7,11},{8,4},{9,5},{10,... | collective-permute-start | bytes 417800 | tf_op jit(solution)/shard_map/ppermute | solution.py:449
  9.2 8.8 %collective-permute-start.6 = (bf16[400,256]{1,0:T(8,128)(2,1)}, bf16[400,256]{1,0:T(8,128)(2,1)S(1)}, u32[]{:S(2)}, u32[]{:S(2)}) collective-permute-start(bf16[400,256]{1,0:T(8,128)(2,1)} %get-tuple-element.73), channel_id=1, source_target_pairs={{0,2},{1,3},{2,0},{3,1},{4,6},{5,7},{6,4},{7,5},{8,10},{9,11},{10,... | collective-permute-start | bytes 614408 | tf_op jit(solution)/shard_map/ppermute | solution.py:447
  9.4 6.9 %collective-permute-start.2 = (bf16[272,256]{1,0:T(8,128)(2,1)}, bf16[272,256]{1,0:T(8,128)(2,1)S(1)}, u32[]{:S(2)}, u32[]{:S(2)}) collective-permute-start(bf16[272,256]{1,0:T(8,128)(2,1)} %get-tuple-element.62), channel_id=1, source_target_pairs={{0,5},{1,4},{2,7},{3,6},{4,1},{5,0},{6,3},{7,2},{8,13},{9,12},{10,... | collective-permute-start | bytes 417800 | tf_op jit(solution)/shard_map/ppermute | solution.py:454
  9.4 7.2 %collective-permute-start.4 = (bf16[272,256]{1,0:T(8,128)(2,1)}, bf16[272,256]{1,0:T(8,128)(2,1)S(1)}, u32[]{:S(2)}, u32[]{:S(2)}) collective-permute-start(bf16[272,256]{1,0:T(8,128)(2,1)} %get-tuple-element.64), channel_id=1, source_target_pairs={{0,1},{1,0},{2,3},{3,2},{4,9},{5,8},{6,11},{7,10},{8,5},{9,4},{10,... | collective-permute-start | bytes 417800 | tf_op jit(solution)/shard_map/ppermute | solution.py:455
  12.0 9.3 %collective-permute-start.7 = (bf16[400,256]{1,0:T(8,128)(2,1)}, bf16[400,256]{1,0:T(8,128)(2,1)S(1)}, u32[]{:S(2)}, u32[]{:S(2)}) collective-permute-start(bf16[400,256]{1,0:T(8,128)(2,1)} %get-tuple-element.74), channel_id=1, source_target_pairs={{0,3},{1,2},{2,1},{3,0},{4,7},{5,6},{6,5},{7,4},{8,11},{9,10},{10,... | collective-permute-start | bytes 614408 | tf_op jit(solution)/shard_map/ppermute | solution.py:453
  14.3 12.6 %copy-start.1 = (bf16[512,512]{1,0:T(8,128)(2,1)S(1)}, bf16[512,512]{1,0:T(8,128)(2,1)}, u32[]{:S(2)}) copy-start(bf16[512,512]{1,0:T(8,128)(2,1)} %refs_6_.1) | copy-start | bytes 1572868
  14.3 12.6 %copy-start.3 = (bf16[256,512]{1,0:T(8,128)(2,1)S(1)}, bf16[256,512]{1,0:T(8,128)(2,1)}, u32[]{:S(2)}) copy-start(bf16[256,512]{1,0:T(8,128)(2,1)} %refs_5_.1) | copy-start | bytes 786436
  14.3 12.6 %copy-start.4 = (f32[512]{0:T(512)S(1)}, f32[512]{0:T(512)}, u32[]{:S(2)}) copy-start(f32[512]{0:T(512)} %param.21) | copy-start | bytes 6148
  16.9 6.0 %collective-permute-start.5 = (bf16[256,256]{1,0:T(8,128)(2,1)S(1)}, bf16[256,256]{1,0:T(8,128)(2,1)S(1)}, u32[]{:S(2)}, u32[]{:S(2)}) collective-permute-start(bf16[256,256]{1,0:T(8,128)(2,1)S(1)} %get-tuple-element.72), channel_id=1, source_target_pairs={{0,2},{1,3},{2,0},{3,1},{4,6},{5,7},{6,4},{7,5},{8,10},{9,11},{10,... | collective-permute-start | bytes 393224 | tf_op jit(solution)/shard_map/ppermute | solution.py:487
  21.6 5.3 %collective-permute-start.8 = (bf16[256,256]{1,0:T(8,128)(2,1)S(1)}, bf16[256,256]{1,0:T(8,128)(2,1)S(1)}, u32[]{:S(2)}, u32[]{:S(2)}) collective-permute-start(bf16[256,256]{1,0:T(8,128)(2,1)S(1)} %get-tuple-element.77), channel_id=1, source_target_pairs={{0,4},{1,5},{2,6},{3,7},{4,0},{5,1},{6,2},{7,3},{8,12},{9,13},{10,... | collective-permute-start | bytes 393224 | tf_op jit(solution)/shard_map/ppermute | solution.py:489
  21.7 5.2 %collective-permute-start.9 = (bf16[256,256]{1,0:T(8,128)(2,1)S(1)}, bf16[256,256]{1,0:T(8,128)(2,1)S(1)}, u32[]{:S(2)}, u32[]{:S(2)}) collective-permute-start(bf16[256,256]{1,0:T(8,128)(2,1)S(1)} %get-tuple-element.78), channel_id=1, source_target_pairs={{0,1},{1,0},{2,3},{3,2},{4,8},{5,9},{6,10},{7,11},{8,4},{9,5},{10,... | collective-permute-start | bytes 393224 | tf_op jit(solution)/shard_map/ppermute | solution.py:490
  27.4 2.5 %collective-permute-start.12 = (bf16[256,512]{1,0:T(8,128)(2,1)S(1)}, bf16[256,512]{1,0:T(8,128)(2,1)S(1)}, u32[]{:S(2)}, u32[]{:S(2)}) collective-permute-start(bf16[256,512]{1,0:T(8,128)(2,1)S(1)} %get-tuple-element.79.own_ref), channel_id=1, source_target_pairs={{0,1},{1,0},{2,3},{3,2},{4,5},{5,4},{6,7},{7,6},{8,9},{9,8},{10,11... | collective-permute-start | bytes 786440 | tf_op jit(solution)/shard_map/ppermute | solution.py:512
  28.2 8.8 %collective-permute-start.11 = (bf16[256,512]{1,0:T(8,128)(2,1)S(1)}, bf16[256,512]{1,0:T(8,128)(2,1)S(1)}, u32[]{:S(2)}, u32[]{:S(2)}) collective-permute-start(bf16[256,512]{1,0:T(8,128)(2,1)S(1)} %get-tuple-element.79.own_ref), channel_id=1, source_target_pairs={{0,1},{1,0},{2,4},{3,5},{4,2},{5,3},{6,8},{7,9},{8,6},{9,7},{10,12... | collective-permute-start | bytes 786440 | tf_op jit(solution)/shard_map/ppermute | solution.py:514
  29.9 13.1 %collective-permute-start.10 = (bf16[256,512]{1,0:T(8,128)(2,1)S(1)}, bf16[256,512]{1,0:T(8,128)(2,1)S(1)}, u32[]{:S(2)}, u32[]{:S(2)}) collective-permute-start(bf16[256,512]{1,0:T(8,128)(2,1)S(1)} %get-tuple-element.79.own_ref), channel_id=1, source_target_pairs={{0,2},{1,3},{2,0},{3,1},{4,6},{5,7},{6,4},{7,5},{8,10},{9,11},{10,... | collective-permute-start | bytes 786440 | tf_op jit(solution)/shard_map/ppermute | solution.py:513
  29.9 4.9 %copy-start.5 = (bf16[512,2048]{1,0:T(8,128)(2,1)S(1)}, bf16[512,2048]{1,0:T(8,128)(2,1)}, u32[]{:S(2)}) copy-start(bf16[512,2048]{1,0:T(8,128)(2,1)} %up_ref) | copy-start | bytes 6291460
  29.9 4.9 %copy-start.6 = (bf16[2048,512]{1,0:T(8,128)(2,1)S(1)}, bf16[2048,512]{1,0:T(8,128)(2,1)}, u32[]{:S(2)}) copy-start(bf16[2048,512]{1,0:T(8,128)(2,1)} %down_ref) | copy-start | bytes 6291460
  29.9 4.9 %copy-start.7 = (bf16[512,512]{1,0:T(8,128)(2,1)S(1)}, bf16[512,512]{1,0:T(8,128)(2,1)}, u32[]{:S(2)}) copy-start(bf16[512,512]{1,0:T(8,128)(2,1)} %w_out_ref) | copy-start | bytes 1572868
  30.0 4.9 %copy-start.8 = (f32[512]{0:T(512)S(1)}, f32[512]{0:T(512)}, u32[]{:S(2)}) copy-start(f32[512]{0:T(512)} %param.25) | copy-start | bytes 6148
  43.0 3.0 %collective-permute-start.13 = (bf16[256,512]{1,0:T(8,128)(2,1)S(1)}, bf16[256,512]{1,0:T(8,128)(2,1)S(1)}, u32[]{:S(2)}, u32[]{:S(2)}) collective-permute-start(bf16[256,512]{1,0:T(8,128)(2,1)S(1)} %collective-permute-done.10.even_ref), channel_id=1, source_target_pairs={{0,1},{1,0},{2,3},{3,2},{4,5},{5,4},{6,7},{7,6},{8,9},{9,8},{10,11... | collective-permute-start | bytes 786440 | tf_op jit(solution)/shard_map/ppermute | solution.py:548
  43.5 2.6 %collective-permute-start.14 = (bf16[256,512]{1,0:T(8,128)(2,1)S(1)}, bf16[256,512]{1,0:T(8,128)(2,1)S(1)}, u32[]{:S(2)}, u32[]{:S(2)}) collective-permute-start(bf16[256,512]{1,0:T(8,128)(2,1)S(1)} %collective-permute-done.11.odd_ref), channel_id=1, source_target_pairs={{0,1},{1,0},{2,3},{3,2},{4,5},{5,4},{6,7},{7,6},{8,9},{9,8},{10,11... | collective-permute-start | bytes 786440 | tf_op jit(solution)/shard_map/ppermute | solution.py:549
  (1 other events, 1.0 us)

commit v11 on v9

--- a/solution.py
+++ b/solution.py
@@ -69,10 +69,10 @@
     return jnp.concatenate([tile] * (lanes // cap), axis=1)
 
 
-def message_kernel(pair_count, grid_ref, w_ref, source_ref, target_ref, count_ref, *refs):
+def message_kernel(pair_count, grid_ref, w_ref, source_in, target_in, count_in, *refs):
     count = 4 + 2 * pair_count
     out_refs, out_vmems = refs[:count], refs[count : 2 * count]
-    grid_vmem, w_vmem, message_ref, pick_ref, in_sems, out_sems = refs[2 * count :]
+    source_ref, target_ref, count_ref, grid_vmem, w_vmem, message_ref, pick_ref, in_sems, edge_sems, out_sems = refs[2 * count :]
     rows = grid_ref.shape[0]
     cap = source_ref.shape[-1]
     half = w_ref.shape[1] // 2
@@ -81,8 +81,12 @@
     for k in range(GRID_PARTS):
         span = pl.ds(k * part, part)
         fetches.append(pltpu.make_async_copy(grid_ref.at[span], grid_vmem.at[span], in_sems.at[k]))
-    for fetch in fetches:
+    edges = ((source_in, source_ref), (target_in, target_ref), (count_in, count_ref))
+    edge_fetches = [pltpu.make_async_copy(a, b, edge_sems.at[n]) for n, (a, b) in enumerate(edges)]
+    for fetch in edge_fetches + fetches:
         fetch.start()
+    for fetch in edge_fetches:
+        fetch.wait()
     inner = lax.axis_index("inner")
     offsets = band_offsets()
     keys = [(t, p, k) for k in range(2) for t in range(3) for p in range(pair_count)]
@@ -144,7 +148,7 @@
         yield n, dot(jnp.concatenate(hits, axis=1), jnp.concatenate(rows, axis=0))
 
 
-def early_kernel(pair_count, w_ref, own_ref, other_ref, order_ref, query_ref, key_ref, value_ref, left_ref, right_ref):
+def early_kernel(pair_count, w_ref, own_ref, other_ref, plan_ref, query_ref, key_ref, value_ref, left_ref, right_ref):
     width = w_ref.shape[0]
     head_dim = width // HEADS
     span = 3 * LANES
@@ -201,7 +205,7 @@
 
 
 def near_kernel(
-    own_ref, side_ref, wq_ref, wk_ref, wv_ref, order_ref, window_ref,
+    own_ref, side_ref, wq_ref, wk_ref, wv_ref, plan_ref,
     query_ref, sums_ref, top_ref,
     key_ref, value_ref, gap_ref,
 ):
@@ -233,28 +237,30 @@
     gap_ref[nodes : nodes + NEAR] = jnp.abs(lag[0:NEAR] + (side * nodes + first))
     gap_ref[nodes + NEAR : 2 * nodes] = jnp.abs(lag[0:NEAR] + (side * nodes + second))
 
-    def attend(heads, rows):
+    def attend(heads, windows, rows):
         scores = [dot(key_ref[h // per_group, 0:rows, :], query_ref[h]) for h in heads]
         scores = [
-            jnp.where(gap_ref[0:rows] <= window_ref[h], x, -1e30) for h, x in zip(heads, scores)
+            jnp.where(gap_ref[0:rows] <= w, x, -1e30) for w, x in zip(windows, scores)
         ]
         tops = [jnp.max(x, axis=0, keepdims=True) for x in scores]
         expos = [jnp.exp2((x - top) * scale).astype(jnp.bfloat16) for x, top in zip(scores, tops)]
-        for h, top, expo in zip(heads, tops, expos):
+        for h, w, top, expo in zip(heads, windows, tops, expos):
             sums_ref[h] = dot(value_ref[h, :, 0:rows], expo)
-            top_ref[h] = jnp.broadcast_to(top, top_ref.shape[1:])
+            top_ref[h, 0:1] = top
+            top_ref[h, 1:2] = jnp.full((1, nodes), w.astype(jnp.float32))
 
     def together(i, carry):
-        heads = [order_ref[GROUP * i + k] for k in range(GROUP)]
-        widest = functools.reduce(jnp.maximum, [window_ref[h] for h in heads])
+        heads = [plan_ref[0, GROUP * i + k] for k in range(GROUP)]
+        windows = [plan_ref[1, GROUP * i + k] for k in range(GROUP)]
+        widest = windows[0]
 
         @pl.when(widest <= NEAR)
         def _():
-            attend(heads, nodes + NEAR)
+            attend(heads, windows, nodes + NEAR)
 
         @pl.when(widest > NEAR)
         def _():
-            attend(heads, 2 * nodes)
+            attend(heads, windows, 2 * nodes)
 
         return carry
 
@@ -265,12 +271,13 @@
     total = lax.axis_size("band") * lax.axis_size("inner")
     there = lax.axis_index("band") * lax.axis_size("inner") + lax.axis_index("inner") + device
     lag = lax.broadcasted_iota(jnp.int32, (rows, nodes), 0) - lax.broadcasted_iota(jnp.int32, (rows, nodes), 1)
-    return jnp.where((there >= 0) & (there < total), jnp.abs(lag + (device * nodes + start)), 1 << 20)
-
-
-def extend(heads, keys, values, gap_ref, window_ref, query_ref, sums_ref, top_ref, scale):
+    gap = jnp.where((there >= 0) & (there < total), jnp.abs(lag + (device * nodes + start)), 1 << 20)
+    return gap.astype(jnp.float32)
+
+
+def extend(heads, keys, values, gap_ref, query_ref, sums_ref, top_ref, scale):
     scores = [dot(k, query_ref[h]) for h, k in zip(heads, keys)]
-    scores = [jnp.where(gap_ref[...] <= window_ref[h], x, -1e30) for h, x in zip(heads, scores)]
+    scores = [jnp.where(gap_ref[...] <= top_ref[h, 1:2, :], x, -1e30) for h, x in zip(heads, scores)]
     olds = [top_ref[h, 0:1, :] for h in heads]
     tops = [jnp.maximum(old, jnp.max(x, axis=0, keepdims=True)) for old, x in zip(olds, scores)]
     expos = [jnp.exp2((x - top) * scale).astype(jnp.bfloat16) for x, top in zip(scores, tops)]
@@ -279,7 +286,7 @@
 
 
 def outer_kernel(
-    even_ref, odd_ref, wk_ref, wv_ref, order_ref, window_ref, query_ref, sums_ref, top_ref,
+    even_ref, odd_ref, wk_ref, wv_ref, plan_ref, query_ref, sums_ref, top_ref,
     sums_out, top_out,
     key_ref, value_ref, gap_ref,
 ):
@@ -289,37 +296,45 @@
     far = 2 - 4 * lax.rem(lax.axis_index("inner") // 2, 2)
     scale = head_dim ** (-0.5) / math.log(2.0)
     value_ref[:, head_dim:, :] = jnp.ones_like(value_ref[:, head_dim:, :])
-    project_keys(even_ref[...], wk_ref, wv_ref, key_ref, value_ref, 0)
-    project_keys(odd_ref[...], wk_ref, wv_ref, key_ref, value_ref, nodes)
+    project_keys(jnp.concatenate([even_ref[...], odd_ref[...]], axis=0), wk_ref, wv_ref, key_ref, value_ref, 0)
     gap_ref[0:nodes] = gaps(far, 0, nodes, nodes)
     gap_ref[nodes:] = gaps(-far, 0, nodes, nodes)
 
-    def together(i, carry):
-        heads = [order_ref[GROUP * i + k] for k in range(GROUP)]
-        widest = functools.reduce(jnp.maximum, [window_ref[h] for h in heads])
-
-        @pl.when(widest > nodes)
-        def _():
-            keys, values = [key_ref[h // per_group] for h in heads], [value_ref[h] for h in heads]
-            for h, sums, top in extend(
-                heads, keys, values, gap_ref, window_ref, query_ref, sums_ref, top_ref, scale
-            ):
-                sums_out[h] = sums
-                top_out[h] = jnp.broadcast_to(top, top_out.shape[1:])
-
-        @pl.when(widest <= nodes)
-        def _():
-            for h in heads:
-                sums_out[h] = sums_ref[h]
-                top_out[h] = top_ref[h]
-
-        return carry
-
-    lax.fori_loop(0, HEADS // GROUP, together, 0)
+    def wide(n):
+        return plan_ref[1, n] > nodes
+
+    def reach(first, last):
+        heads = [plan_ref[0, n] for n in range(first, last)]
+        keys, values = [key_ref[h // per_group] for h in heads], [value_ref[h] for h in heads]
+        for h, sums, top in extend(
+            heads, keys, values, gap_ref, query_ref, sums_ref, top_ref, scale
+        ):
+            sums_out[h] = sums
+            top_out[h, 0:1] = top
+            top_out[h, 1:2] = top_ref[h, 1:2]
+
+    def leave(first, last):
+        for n in range(first, last):
+            h = plan_ref[0, n]
+            sums_out[h] = sums_ref[h]
+            top_out[h, 0:2] = top_ref[h, 0:2]
+
+    @pl.when(wide(GROUP))
+    def _():
+        reach(0, 2 * GROUP)
+
+    @pl.when(jnp.logical_not(wide(GROUP)))
+    def _():
+        reach(0, GROUP)
+        leave(GROUP, 2 * GROUP)
+
+    for first in range(2 * GROUP, HEADS, GROUP):
+        pl.when(wide(first))(functools.partial(reach, first, first + GROUP))
+        pl.when(jnp.logical_not(wide(first)))(functools.partial(leave, first, first + GROUP))
 
 
 def far_kernel(
-    first_ref, second_ref, wk_ref, wv_ref, window_ref, query_ref, sums_ref, top_ref,
+    first_ref, second_ref, wk_ref, wv_ref, query_ref, sums_ref, top_ref,
     state_ref, w_out_ref, gain_ref, up_ref, down_ref,
     out_ref,
     key_ref, value_ref, gap_ref, attended_ref,
@@ -338,7 +353,7 @@
         heads = range(GROUP * i, GROUP * (i + 1))
         keys, values = [key_ref[h // per_group] for h in heads], [value_ref[h] for h in heads]
         for h, sums, _ in extend(
-            heads, keys, values, gap_ref, window_ref, query_ref, sums_ref, top_ref, scale
+            heads, keys, values, gap_ref, query_ref, sums_ref, top_ref, scale
         ):
             attended_ref[h] = (sums[0:head_dim] / sums[head_dim : head_dim + 1]).astype(jnp.bfloat16)
 
@@ -394,15 +409,19 @@
     even, even_other, odd, odd_other, *cross, here, here_other = pl.pallas_call(
         functools.partial(message_kernel, pairs),
         out_shape=outgoing,
-        in_specs=[ANY] * 2 + [VMEM] * 2 + [SMEM],
+        in_specs=[ANY] * 5,
         out_specs=[ANY] * len(outgoing),
         scratch_shapes=[pltpu.VMEM(a.shape, bf16) for a in outgoing]
         + [
+            pltpu.VMEM(edges[0].shape, i32),
+            pltpu.VMEM(edges[1].shape, i32),
+            pltpu.SMEM(edges[2].shape, i32),
             pltpu.VMEM(grid_rows.shape, bf16),
             pltpu.VMEM(w_message.shape, bf16),
             pltpu.VMEM((grid_dev, width), bf16),
             pltpu.VMEM((3 * inners * cap, grid_dev), bf16),
             pltpu.SemaphoreType.DMA((GRID_PARTS + 1,)),
+            pltpu.SemaphoreType.DMA((3,)),
             pltpu.SemaphoreType.DMA((len(outgoing),)),
         ],
         compiler_params=params(MOST),
@@ -439,17 +458,18 @@
         (window[None, :] == window[:, None]) & (head[None, :] < head[:, None])
     )
     rank = jnp.sum(ahead.astype(i32), axis=1)
-    order = jnp.sum(jnp.where(rank[None, :] == head[:, None], head[None, :], 0), axis=1).astype(i32)
+    sorted_to = rank[None, :] == head[:, None]
+    plan = jnp.sum(jnp.where(sorted_to[None], jnp.stack([head, window])[:, None, :], 0), axis=2).astype(i32)
     w_query, w_key, w_value, early_left, early_right = pl.pallas_call(
         functools.partial(early_kernel, pairs),
         out_shape=[jax.ShapeDtypeStruct((width, width), bf16)] * 3
         + [jax.ShapeDtypeStruct((n, nodes, half), f32) for n in (pairs, 3)],
-        in_specs=[VMEM] * 3 + [SMEM],
+        in_specs=[VMEM] * 3 + [ANY],
         out_specs=[VMEM] * 5,
         compiler_params=params(24),
         cost_estimate=cost(1 << 28, 4 << 20),
         name="early",
-    )(w_qkv, here, here_other, order)
+    )(w_qkv, here, here_other, plan)
     def sums(arrays, early, kept, name):
         count = early.shape[0]
         return pl.pallas_call(
@@ -490,6 +510,7 @@
 
     side = lax.ppermute(normed, NODES, beside)
     even = lax.ppermute(normed, NODES, chips_trade(0))
+    side, normed = lax.optimization_barrier((side, normed))
     odd = lax.ppermute(normed, NODES, chips_trade(1))
 
     extra = head_dim + 16
@@ -500,7 +521,7 @@
             jax.ShapeDtypeStruct((HEADS, extra, nodes), f32),
             jax.ShapeDtypeStruct((HEADS, 8, nodes), f32),
         ],
-        in_specs=[VMEM] * 5 + [SMEM] * 2,
+        in_specs=[VMEM] * 5 + [SMEM],
         out_specs=[VMEM] * 3,
         scratch_shapes=[
             pltpu.VMEM((width // LANES, 2 * nodes, LANES), bf16),
@@ -510,7 +531,7 @@
         compiler_params=params(32),
         cost_estimate=cost(8 << 30, 4 << 20),
         name="near",
-    )(normed, side, w_query, w_key, w_value, order, window)
+    )(normed, side, w_query, w_key, w_value, plan)
 
     even, odd, near, top = lax.optimization_barrier((even, odd, near, top))
     first = lax.ppermute(even, NODES, beside)
@@ -521,34 +542,34 @@
             jax.ShapeDtypeStruct((HEADS, extra, nodes), f32),
             jax.ShapeDtypeStruct((HEADS, 8, nodes), f32),
         ],
-        in_specs=[VMEM] * 4 + [SMEM] * 2 + [VMEM] * 3,
+        in_specs=[VMEM] * 4 + [SMEM] + [VMEM] * 3,
         out_specs=[VMEM] * 2,
         scratch_shapes=[
             pltpu.VMEM((width // LANES, 2 * nodes, LANES), bf16),
             pltpu.VMEM((HEADS, extra, 2 * nodes), bf16),
-            pltpu.VMEM((2 * nodes, nodes), i32),
+            pltpu.VMEM((2 * nodes, nodes), f32),
         ],
         compiler_params=params(24),
         cost_estimate=cost(16 * nodes * width * width, 3 << 20),
         name="outer",
-    )(even, odd, w_key, w_value, order, window, query, near, top)
+    )(even, odd, w_key, w_value, plan, query, near, top)
 
     return pl.pallas_call(
         far_kernel,
         out_shape=jax.ShapeDtypeStruct((nodes, width), bf16),
-        in_specs=[VMEM] * 4 + [SMEM] + [VMEM] * 8,
+        in_specs=[VMEM] * 12,
         out_specs=VMEM,
         scratch_shapes=[
             pltpu.VMEM((width // LANES, nodes, LANES), bf16),
             pltpu.VMEM((HEADS, extra, nodes), bf16),
-            pltpu.VMEM((nodes, nodes), i32),
+            pltpu.VMEM((nodes, nodes), f32),
             pltpu.VMEM((HEADS, head_dim, nodes), bf16),
         ],
         compiler_params=params(40),
         cost_estimate=cost(8 << 30, 8 << 20),
         name="far",
     )(
-        first, second, w_key, w_value, window,
+        first, second, w_key, w_value,
         query, near, top, state, w_out, gain_mlp.reshape(1, width), w_up, w_down,
     )
 

time: 49.8 us -> 49.3 us (0.990); the launches traced: 49.3 us -> 49.4 us
  waiting for transfers between devices: 11 us -> 14.1 us
  starting transfers between devices: 14.3 us -> 12.7 us
  Pallas kernels: 22.5 us -> 21 us
    ppermute x1, waiting for transfers between devices: 0.29 us -> 1.8 us  [local(): from_even = lax.ppermute(to_even, NODES, bands_trade(0))]
    ppermute x1, starting transfers between devices: 1.29 us -> 0.49 us  [local(): from_odd = lax.ppermute(to_odd, NODES, bands_trade(1))]
    ppermute x1, starting transfers between devices: 0.31 us -> 1.11 us  [local(): lax.ppermute(part, NODES, chip_trade(p + 1))]
    ppermute x1, waiting for transfers between devices: 0.01 us -> 0.74 us  [local(): side = lax.ppermute(normed, NODES, beside)]
    ppermute x1, waiting for transfers between devices: 5.95 us -> 6.58 us  [local(): even = lax.ppermute(normed, NODES, chips_trade(0))]
    ppermute x1, starting transfers between devices: 1.04 us -> 0.42 us  [local(): even = lax.ppermute(normed, NODES, chips_trade(0))]
    ppermute x1, starting transfers between devices: 1.45 us -> 0.86 us  [local(): odd = lax.ppermute(normed, NODES, chips_trade(1))]
    pallas_call x1, Pallas kernels: 5.51 us -> 4.95 us  [local(): pl.pallas_call(far_kernel, out_shape=jax.ShapeDtypeStruct((nodes, width),...]
  transfers between devices with their start and end apart: 15 -> 15, of which waited for: 6 -> 8; matrix products, arithmetic and copies ran while one was open for 1% -> 1% of each run, Pallas kernels for 22% -> 20%
where the time goes in v11:
time: 49.3 us; the launch traced here: 49.4 us
  Pallas kernels  21 us (43%)
  waiting for transfers between devices  14.1 us (29%)
  starting transfers between devices  12.7 us (26%)
  local copies, waits for them, and re-layouts  1.02 us (2%)
    ppermute x1, waiting for transfers between devices, local(): even = lax.ppermute(normed, NODES, chips_trade(0))  6.58 us
    pallas_call x1, Pallas kernels, local(): pl.pallas_call(functools.partial(message_kernel, pairs), out_shape=outgoi...  5.45 us
    pallas_call x1, Pallas kernels, local(): pl.pallas_call(far_kernel, out_shape=jax.ShapeDtypeStruct((nodes, width),...  4.95 us
    pallas_call x1, Pallas kernels, local(): pl.pallas_call(near_kernel, out_shape=[jax.ShapeDtypeStruct((HEADS, LANES...  4.85 us
    pallas_call x1, Pallas kernels, local(): pl.pallas_call(outer_kernel, out_shape=[jax.ShapeDtypeStruct((HEADS, extr...  3.2 us
    ppermute x1, waiting for transfers between devices, local(): lax.ppermute(part, NODES, chip_trade(p + 1))  2.77 us
    ppermute x1, starting transfers between devices, local(): odd = lax.ppermute(odd, NODES, bands_trade(1))  2.43 us
    ppermute x1, starting transfers between devices, local(): odd_other = lax.ppermute(odd_other, NODES, bands_trade(1, 1))  2.36 us
  transfers between devices with their start and end apart: 15, of which 8 were waited for; matrix products, arithmetic and copies ran while one was open for 1% of the time, Pallas kernels for 20%

profile of v11, /device:TPU:15, one launch (start us, length us, event | category | flops | bytes accessed | tf_op | source)
XLA Modules:
  0.0 49.4 jit_solution(7954996094107180611)
XLA Ops:
  0.0 5.5 %messages.1 = (bf16[272,256]{1,0:T(8,128)(2,1)}, bf16[272,256]{1,0:T(8,128)(2,1)}, bf16[272,256]{1,0:T(8,128)(2,1)}, bf16[272,256]{1,0:T(8,128)(2,1)}, bf16[400,...) custom-call(bf16[1024,512]{1,0:T(8,128)(2,1)} %grid_ref.1, ...), custom_call_target="tpu_custom_call" | custom-call | flops 2147483648 | bytes 4194304 | tf_op jit(solution)/shard_map/messages/pallas_call | solution.py:409
  5.5 0.7 %collective-permute-start.1 = (bf16[672,256]{1,0:T(8,128)(2,1)}, bf16[672,256]{1,0:T(8,128)(2,1)S(1)}, u32[]{:S(2)}, u32[]{:S(2)}) collective-permute-start(bf16[672,256]{1,0:T(8,128)(2,1)} %get-tuple-element.44), channel_id=1, source_target_pairs={{0,1},{1,0},{2,3},{3,2},{4,5},{5,4},{6,7},{7,6},{8,9},{9,8},{10,11... | collective-permute-start | bytes 1032200 | tf_op jit(solution)/shard_map/ppermute | solution.py:444
  6.6 2.4 %collective-permute-start.3 = (bf16[272,256]{1,0:T(8,128)(2,1)}, bf16[272,256]{1,0:T(8,128)(2,1)S(1)}, u32[]{:S(2)}, u32[]{:S(2)}) collective-permute-start(bf16[272,256]{1,0:T(8,128)(2,1)} %get-tuple-element.49), channel_id=1, source_target_pairs={{0,1},{1,0},{2,3},{3,2},{4,8},{5,9},{6,10},{7,11},{8,4},{9,5},{10,... | collective-permute-start | bytes 417800 | tf_op jit(solution)/shard_map/ppermute | solution.py:447
  9.3 2.1 %collective-permute-start.7 = (bf16[400,256]{1,0:T(8,128)(2,1)}, bf16[400,256]{1,0:T(8,128)(2,1)S(1)}, u32[]{:S(2)}, u32[]{:S(2)}) collective-permute-start(bf16[400,256]{1,0:T(8,128)(2,1)} %get-tuple-element.60), channel_id=1, source_target_pairs={{0,3},{1,2},{2,1},{3,0},{4,7},{5,6},{6,5},{7,4},{8,11},{9,10},{10,... | collective-permute-start | bytes 614408 | tf_op jit(solution)/shard_map/ppermute | solution.py:451
  11.6 2.4 %collective-permute-start.4 = (bf16[272,256]{1,0:T(8,128)(2,1)}, bf16[272,256]{1,0:T(8,128)(2,1)S(1)}, u32[]{:S(2)}, u32[]{:S(2)}) collective-permute-start(bf16[272,256]{1,0:T(8,128)(2,1)} %get-tuple-element.50), channel_id=1, source_target_pairs={{0,1},{1,0},{2,3},{3,2},{4,9},{5,8},{6,11},{7,10},{8,5},{9,4},{10,... | collective-permute-start | bytes 417800 | tf_op jit(solution)/shard_map/ppermute | solution.py:453
  14.1 1.0 %copy-done.2 = bf16[672,256]{1,0:T(8,128)(2,1)S(1)} copy-done((bf16[672,256]{1,0:T(8,128)(2,1)S(1)}, bf16[672,256]{1,0:T(8,128)(2,1)}, u32[]{:S(2)}) %copy-start.2) | copy-done | bytes 344088
  15.1 1.5 %early.1 = (bf16[512,512]{1,0:T(8,128)(2,1)S(1)}, bf16[512,512]{1,0:T(8,128)(2,1)S(1)}, bf16[512,512]{1,0:T(8,128)(2,1)S(1)}, f32[2,256,256]{2,1,0:T(8,128)S(1)}, f32[3,256,256]{2,1,0:T(8,128)S(1)}) custom-call(bf16[512,1536]{1,0:T(8,128)(2,1)S(1)} %copy-done, bf16[672,256]{1,0:T(8,128)(2,1)S(1)} %copy-done.2, ...), custom_call_target="tpu_custom_call" | custom-call | flops 268435456 | bytes 4194304 | tf_op jit(solution)/shard_map/early/pallas_call | solution.py:463
  16.7 1.7 %collective-permute-done.4.refs_3_ = bf16[272,256]{1,0:T(8,128)(2,1)S(1)} collective-permute-done((bf16[272,256]{1,0:T(8,128)(2,1)}, bf16[272,256]{1,0:T(8,128)(2,1)S(1)}, u32[]{:S(2)}, u32[]{:S(2)}) %collective-permute-start.4) | collective-permute-done | bytes 139296 | tf_op jit(solution)/shard_map/ppermute | solution.py:453
  18.4 0.3 left.1
  18.7 1.1 %collective-permute-start.5 = (bf16[256,256]{1,0:T(8,128)(2,1)S(1)}, bf16[256,256]{1,0:T(8,128)(2,1)S(1)}, u32[]{:S(2)}, u32[]{:S(2)}) collective-permute-start(bf16[256,256]{1,0:T(8,128)(2,1)S(1)} %get-tuple-element.58), channel_id=1, source_target_pairs={{0,2},{1,3},{2,0},{3,1},{4,6},{5,7},{6,4},{7,5},{8,10},{9,11},{10,... | collective-permute-start | bytes 393224 | tf_op jit(solution)/shard_map/ppermute | solution.py:486
  19.9 0.3 right.1
  20.2 0.5 collective-permute-start.9
  20.7 2.8 %collective-permute-done.5.refs_1_ = bf16[256,256]{1,0:T(8,128)(2,1)S(1)} collective-permute-done((bf16[256,256]{1,0:T(8,128)(2,1)S(1)}, bf16[256,256]{1,0:T(8,128)(2,1)S(1)}, u32[]{:S(2)}, u32[]{:S(2)}) %collective-permute-start.5) | collective-permute-done | bytes 131104 | tf_op jit(solution)/shard_map/ppermute | solution.py:486
  23.5 1.8 %collective-permute-done.8.refs_3_ = bf16[256,256]{1,0:T(8,128)(2,1)S(1)} collective-permute-done((bf16[256,256]{1,0:T(8,128)(2,1)S(1)}, bf16[256,256]{1,0:T(8,128)(2,1)S(1)}, u32[]{:S(2)}, u32[]{:S(2)}) %collective-permute-start.8) | collective-permute-done | bytes 131104 | tf_op jit(solution)/shard_map/ppermute | solution.py:488
  25.4 0.5 %merge.1 = (f32[256,512]{1,0:T(8,128)S(1)}, bf16[256,512]{1,0:T(8,128)(2,1)S(1)}) custom-call(f32[256,256]{1,0:T(8,128)S(1)} %get-tuple-element.57.refs_0_, bf16[256,256]{1,0:T(8,128)(2,1)S(1)} %collective-permute-done.5.refs_1_, f32[256,256]{1,0:T(8,128)S(1)} %get-tuple-element.62.refs_2_, bf16[256,256]{1,0:T(8,128)(2,1)S(1)} %collective-permute-done.8.refs_3_, ...), custom_call_target="tpu_custom_call" | custom-call | flops 134217728 | bytes 2097152 | tf_op jit(solution)/shard_map/merge/pallas_call | solution.py:491
  25.9 0.9 %collective-permute-start.11 = (bf16[256,512]{1,0:T(8,128)(2,1)S(1)}, bf16[256,512]{1,0:T(8,128)(2,1)S(1)}, u32[]{:S(2)}, u32[]{:S(2)}) collective-permute-start(bf16[256,512]{1,0:T(8,128)(2,1)S(1)} %get-tuple-element.66.own_ref), channel_id=1, source_target_pairs={{0,1},{1,0},{2,3},{3,2},{4,5},{5,4},{6,7},{7,6},{8,9},{9,8},{10,11... | collective-permute-start | bytes 786440 | tf_op jit(solution)/shard_map/ppermute | solution.py:511
  26.8 0.4 collective-permute-start.10
  27.2 0.7 %collective-permute-done.11.side_ref = bf16[256,512]{1,0:T(8,128)(2,1)S(1)} collective-permute-done((bf16[256,512]{1,0:T(8,128)(2,1)S(1)}, bf16[256,512]{1,0:T(8,128)(2,1)S(1)}, u32[]{:S(2)}, u32[]{:S(2)}) %collective-permute-start.11) | collective-permute-done | bytes 262176 | tf_op jit(solution)/shard_map/ppermute | solution.py:511
  28.0 0.9 %collective-permute-start.12 = (bf16[256,512]{1,0:T(8,128)(2,1)S(1)}, bf16[256,512]{1,0:T(8,128)(2,1)S(1)}, u32[]{:S(2)}, u32[]{:S(2)}) collective-permute-start(bf16[256,512]{1,0:T(8,128)(2,1)S(1)} %get-tuple-element.66.own_ref), channel_id=1, source_target_pairs={{0,1},{1,0},{2,4},{3,5},{4,2},{5,3},{6,8},{7,9},{8,6},{9,7},{10,12... | collective-permute-start | bytes 786440 | tf_op jit(solution)/shard_map/ppermute | solution.py:514
  28.8 4.9 %near.1 = (bf16[16,128,256]{2,1,0:T(8,128)(2,1)S(1)}, f32[16,48,256]{2,1,0:T(8,128)S(1)}, f32[16,8,256]{2,1,0:T(8,128)S(1)}) custom-call(bf16[256,512]{1,0:T(8,128)(2,1)S(1)} %get-tuple-element.66.own_ref, bf16[256,512]{1,0:T(8,128)(2,1)S(1)} %collective-permute-done.11.side_ref, bf16[512,512]{1,0:T(8,128)(2,1)S(1)} %get-tuple-element.68.wq_ref, ...), custom_call_target="tpu_custom_call" | custom-call | flops 8589934592 | bytes 4194304 | tf_op jit(solution)/shard_map/near/pallas_call | solution.py:517
  33.7 6.6 %collective-permute-done.10.even_ref = bf16[256,512]{1,0:T(8,128)(2,1)S(1)} collective-permute-done((bf16[256,512]{1,0:T(8,128)(2,1)S(1)}, bf16[256,512]{1,0:T(8,128)(2,1)S(1)}, u32[]{:S(2)}, u32[]{:S(2)}) %collective-permute-start.10) | collective-permute-done | bytes 262176 | tf_op jit(solution)/shard_map/ppermute | solution.py:512
  40.3 0.9 %collective-permute-start.13 = (bf16[256,512]{1,0:T(8,128)(2,1)S(1)}, bf16[256,512]{1,0:T(8,128)(2,1)S(1)}, u32[]{:S(2)}, u32[]{:S(2)}) collective-permute-start(bf16[256,512]{1,0:T(8,128)(2,1)S(1)} %collective-permute-done.10.even_ref), channel_id=1, source_target_pairs={{0,1},{1,0},{2,3},{3,2},{4,5},{5,4},{6,7},{7,6},{8,9},{9,8},{10,11... | collective-permute-start | bytes 786440 | tf_op jit(solution)/shard_map/ppermute | solution.py:537
  41.2 3.2 %outer.1 = (f32[16,48,256]{2,1,0:T(8,128)S(1)}, f32[16,8,256]{2,1,0:T(8,128)S(1)}) custom-call(bf16[256,512]{1,0:T(8,128)(2,1)S(1)} %collective-permute-done.10.even_ref, bf16[256,512]{1,0:T(8,128)(2,1)S(1)} %collective-permute-done.12.odd_ref, bf16[512,512]{1,0:T(8,128)(2,1)S(1)} %get-tuple-element.69.wk_ref, ...), custom_call_target="tpu_custom_call" | custom-call | flops 1073741824 | bytes 3145728 | tf_op jit(solution)/shard_map/outer/pallas_call | solution.py:539
  44.4 5.0 %far.1 = bf16[256,512]{1,0:T(8,128)(2,1)} custom-call(bf16[256,512]{1,0:T(8,128)(2,1)S(1)} %collective-permute-done.13.first_ref, bf16[256,512]{1,0:T(8,128)(2,1)S(1)} %collective-permute-done.14.second_ref, bf16[512,512]{1,0:T(8,128)(2,1)S(1)} %get-tuple-element.69.wk_ref, bf16[512,512]{1,0:T(8,128)(2,1)S(1)} %get-tuple-element.70.wv_ref, ...), custom_call_target="tpu_custom_call" | custom-call | flops 8589934592 | bytes 8388608 | tf_op jit(solution)/shard_map/far/pallas_call | solution.py:557
  (39 shorter events, 1.4 us)
Async XLA Ops:
  0.0 9.1 %copy-start.9 = (s32[16]{0:T(128)S(1)}, s32[16]{0:T(128)}, u32[]{:S(2)}) copy-start(s32[16]{0:T(128)} %param.23) | copy-start | bytes 196
  0.0 14.1 %copy-start = (bf16[512,1536]{1,0:T(8,128)(2,1)S(1)}, bf16[512,1536]{1,0:T(8,128)(2,1)}, u32[]{:S(2)}) copy-start(bf16[512,1536]{1,0:T(8,128)(2,1)} %w_ref.2) | copy-start | bytes 4718596
  5.5 3.8 %collective-permute-start.1 = (bf16[672,256]{1,0:T(8,128)(2,1)}, bf16[672,256]{1,0:T(8,128)(2,1)S(1)}, u32[]{:S(2)}, u32[]{:S(2)}) collective-permute-start(bf16[672,256]{1,0:T(8,128)(2,1)} %get-tuple-element.44), channel_id=1, source_target_pairs={{0,1},{1,0},{2,3},{3,2},{4,5},{5,4},{6,7},{7,6},{8,9},{9,8},{10,11... | collective-permute-start | bytes 1032200 | tf_op jit(solution)/shard_map/ppermute | solution.py:444
  6.2 13.7 %collective-permute-start.6 = (bf16[400,256]{1,0:T(8,128)(2,1)}, bf16[400,256]{1,0:T(8,128)(2,1)S(1)}, u32[]{:S(2)}, u32[]{:S(2)}) collective-permute-start(bf16[400,256]{1,0:T(8,128)(2,1)} %get-tuple-element.59), channel_id=1, source_target_pairs={{0,2},{1,3},{2,0},{3,1},{4,6},{5,7},{6,4},{7,5},{8,10},{9,11},{10,... | collective-permute-start | bytes 614408 | tf_op jit(solution)/shard_map/ppermute | solution.py:445
  6.5 5.1 %collective-permute-start = (bf16[272,256]{1,0:T(8,128)(2,1)}, bf16[272,256]{1,0:T(8,128)(2,1)S(1)}, u32[]{:S(2)}, u32[]{:S(2)}) collective-permute-start(bf16[272,256]{1,0:T(8,128)(2,1)} %get-tuple-element.43), channel_id=1, source_target_pairs={{0,4},{1,5},{2,6},{3,7},{4,0},{5,1},{6,2},{7,3},{8,12},{9,13},{10,... | collective-permute-start | bytes 417800 | tf_op jit(solution)/shard_map/ppermute | solution.py:446
  6.6 9.9 %collective-permute-start.3 = (bf16[272,256]{1,0:T(8,128)(2,1)}, bf16[272,256]{1,0:T(8,128)(2,1)S(1)}, u32[]{:S(2)}, u32[]{:S(2)}) collective-permute-start(bf16[272,256]{1,0:T(8,128)(2,1)} %get-tuple-element.49), channel_id=1, source_target_pairs={{0,1},{1,0},{2,3},{3,2},{4,8},{5,9},{6,10},{7,11},{8,4},{9,5},{10,... | collective-permute-start | bytes 417800 | tf_op jit(solution)/shard_map/ppermute | solution.py:447
  9.3 10.6 %collective-permute-start.7 = (bf16[400,256]{1,0:T(8,128)(2,1)}, bf16[400,256]{1,0:T(8,128)(2,1)S(1)}, u32[]{:S(2)}, u32[]{:S(2)}) collective-permute-start(bf16[400,256]{1,0:T(8,128)(2,1)} %get-tuple-element.60), channel_id=1, source_target_pairs={{0,3},{1,2},{2,1},{3,0},{4,7},{5,6},{6,5},{7,4},{8,11},{9,10},{10,... | collective-permute-start | bytes 614408 | tf_op jit(solution)/shard_map/ppermute | solution.py:451
  11.3 5.4 %collective-permute-start.2 = (bf16[272,256]{1,0:T(8,128)(2,1)}, bf16[272,256]{1,0:T(8,128)(2,1)S(1)}, u32[]{:S(2)}, u32[]{:S(2)}) collective-permute-start(bf16[272,256]{1,0:T(8,128)(2,1)} %get-tuple-element.48), channel_id=1, source_target_pairs={{0,5},{1,4},{2,7},{3,6},{4,1},{5,0},{6,3},{7,2},{8,13},{9,12},{10,... | collective-permute-start | bytes 417800 | tf_op jit(solution)/shard_map/ppermute | solution.py:452
  11.6 6.8 %collective-permute-start.4 = (bf16[272,256]{1,0:T(8,128)(2,1)}, bf16[272,256]{1,0:T(8,128)(2,1)S(1)}, u32[]{:S(2)}, u32[]{:S(2)}) collective-permute-start(bf16[272,256]{1,0:T(8,128)(2,1)} %get-tuple-element.50), channel_id=1, source_target_pairs={{0,1},{1,0},{2,3},{3,2},{4,9},{5,8},{6,11},{7,10},{8,5},{9,4},{10,... | collective-permute-start | bytes 417800 | tf_op jit(solution)/shard_map/ppermute | solution.py:453
  15.1 10.3 %copy-start.1 = (bf16[512,512]{1,0:T(8,128)(2,1)S(1)}, bf16[512,512]{1,0:T(8,128)(2,1)}, u32[]{:S(2)}) copy-start(bf16[512,512]{1,0:T(8,128)(2,1)} %refs_6_.1) | copy-start | bytes 1572868
  15.1 10.3 %copy-start.3 = (bf16[256,512]{1,0:T(8,128)(2,1)S(1)}, bf16[256,512]{1,0:T(8,128)(2,1)}, u32[]{:S(2)}) copy-start(bf16[256,512]{1,0:T(8,128)(2,1)} %refs_5_.1) | copy-start | bytes 786436
  15.1 10.3 %copy-start.4 = (f32[512]{0:T(512)S(1)}, f32[512]{0:T(512)}, u32[]{:S(2)}) copy-start(f32[512]{0:T(512)} %param.21) | copy-start | bytes 6148
  18.7 4.7 %collective-permute-start.5 = (bf16[256,256]{1,0:T(8,128)(2,1)S(1)}, bf16[256,256]{1,0:T(8,128)(2,1)S(1)}, u32[]{:S(2)}, u32[]{:S(2)}) collective-permute-start(bf16[256,256]{1,0:T(8,128)(2,1)S(1)} %get-tuple-element.58), channel_id=1, source_target_pairs={{0,2},{1,3},{2,0},{3,1},{4,6},{5,7},{6,4},{7,5},{8,10},{9,11},{10,... | collective-permute-start | bytes 393224 | tf_op jit(solution)/shard_map/ppermute | solution.py:486
  20.2 5.1 %collective-permute-start.8 = (bf16[256,256]{1,0:T(8,128)(2,1)S(1)}, bf16[256,256]{1,0:T(8,128)(2,1)S(1)}, u32[]{:S(2)}, u32[]{:S(2)}) collective-permute-start(bf16[256,256]{1,0:T(8,128)(2,1)S(1)} %get-tuple-element.63), channel_id=1, source_target_pairs={{0,4},{1,5},{2,6},{3,7},{4,0},{5,1},{6,2},{7,3},{8,12},{9,13},{10,... | collective-permute-start | bytes 393224 | tf_op jit(solution)/shard_map/ppermute | solution.py:488
  20.2 5.1 %collective-permute-start.9 = (bf16[256,256]{1,0:T(8,128)(2,1)S(1)}, bf16[256,256]{1,0:T(8,128)(2,1)S(1)}, u32[]{:S(2)}, u32[]{:S(2)}) collective-permute-start(bf16[256,256]{1,0:T(8,128)(2,1)S(1)} %get-tuple-element.64), channel_id=1, source_target_pairs={{0,1},{1,0},{2,3},{3,2},{4,8},{5,9},{6,10},{7,11},{8,4},{9,5},{10,... | collective-permute-start | bytes 393224 | tf_op jit(solution)/shard_map/ppermute | solution.py:489
  25.9 2.1 %collective-permute-start.11 = (bf16[256,512]{1,0:T(8,128)(2,1)S(1)}, bf16[256,512]{1,0:T(8,128)(2,1)S(1)}, u32[]{:S(2)}, u32[]{:S(2)}) collective-permute-start(bf16[256,512]{1,0:T(8,128)(2,1)S(1)} %get-tuple-element.66.own_ref), channel_id=1, source_target_pairs={{0,1},{1,0},{2,3},{3,2},{4,5},{5,4},{6,7},{7,6},{8,9},{9,8},{10,11... | collective-permute-start | bytes 786440 | tf_op jit(solution)/shard_map/ppermute | solution.py:511
  26.8 13.5 %collective-permute-start.10 = (bf16[256,512]{1,0:T(8,128)(2,1)S(1)}, bf16[256,512]{1,0:T(8,128)(2,1)S(1)}, u32[]{:S(2)}, u32[]{:S(2)}) collective-permute-start(bf16[256,512]{1,0:T(8,128)(2,1)S(1)} %get-tuple-element.66.own_ref), channel_id=1, source_target_pairs={{0,2},{1,3},{2,0},{3,1},{4,6},{5,7},{6,4},{7,5},{8,10},{9,11},{10,... | collective-permute-start | bytes 786440 | tf_op jit(solution)/shard_map/ppermute | solution.py:512
  28.0 12.3 %collective-permute-start.12 = (bf16[256,512]{1,0:T(8,128)(2,1)S(1)}, bf16[256,512]{1,0:T(8,128)(2,1)S(1)}, u32[]{:S(2)}, u32[]{:S(2)}) collective-permute-start(bf16[256,512]{1,0:T(8,128)(2,1)S(1)} %get-tuple-element.66.own_ref), channel_id=1, source_target_pairs={{0,1},{1,0},{2,4},{3,5},{4,2},{5,3},{6,8},{7,9},{8,6},{9,7},{10,12... | collective-permute-start | bytes 786440 | tf_op jit(solution)/shard_map/ppermute | solution.py:514
  28.8 15.6 %copy-start.6 = (bf16[2048,512]{1,0:T(8,128)(2,1)S(1)}, bf16[2048,512]{1,0:T(8,128)(2,1)}, u32[]{:S(2)}) copy-start(bf16[2048,512]{1,0:T(8,128)(2,1)} %down_ref.1) | copy-start | bytes 6291460
  33.7 10.7 %copy-start.5 = (bf16[512,2048]{1,0:T(8,128)(2,1)S(1)}, bf16[512,2048]{1,0:T(8,128)(2,1)}, u32[]{:S(2)}) copy-start(bf16[512,2048]{1,0:T(8,128)(2,1)} %up_ref.1) | copy-start | bytes 6291460
  33.7 10.7 %copy-start.7 = (bf16[512,512]{1,0:T(8,128)(2,1)S(1)}, bf16[512,512]{1,0:T(8,128)(2,1)}, u32[]{:S(2)}) copy-start(bf16[512,512]{1,0:T(8,128)(2,1)} %w_out_ref.1) | copy-start | bytes 1572868
  33.7 10.7 %copy-start.8 = (f32[512]{0:T(512)S(1)}, f32[512]{0:T(512)}, u32[]{:S(2)}) copy-start(f32[512]{0:T(512)} %param.25) | copy-start | bytes 6148
  40.3 4.1 %collective-permute-start.13 = (bf16[256,512]{1,0:T(8,128)(2,1)S(1)}, bf16[256,512]{1,0:T(8,128)(2,1)S(1)}, u32[]{:S(2)}, u32[]{:S(2)}) collective-permute-start(bf16[256,512]{1,0:T(8,128)(2,1)S(1)} %collective-permute-done.10.even_ref), channel_id=1, source_target_pairs={{0,1},{1,0},{2,3},{3,2},{4,5},{5,4},{6,7},{7,6},{8,9},{9,8},{10,11... | collective-permute-start | bytes 786440 | tf_op jit(solution)/shard_map/ppermute | solution.py:537
  41.2 3.2 %collective-permute-start.14 = (bf16[256,512]{1,0:T(8,128)(2,1)S(1)}, bf16[256,512]{1,0:T(8,128)(2,1)S(1)}, u32[]{:S(2)}, u32[]{:S(2)}) collective-permute-start(bf16[256,512]{1,0:T(8,128)(2,1)S(1)} %collective-permute-done.12.odd_ref), channel_id=1, source_target_pairs={{0,1},{1,0},{2,3},{3,2},{4,5},{5,4},{6,7},{7,6},{8,9},{9,8},{10,11... | collective-permute-start | bytes 786440 | tf_op jit(solution)/shard_map/ppermute | solution.py:538
  (1 other events, 1.0 us)

commit v12 on v11

--- a/solution.py
+++ b/solution.py
@@ -117,7 +117,7 @@
     for k in range(2):
         first = k * per_core
         taken = dot(pick_ref[first * cap : (first + per_core) * cap, :], message_ref[...]).astype(jnp.bfloat16)
-        for n in range(count):
+        for n in reversed(range(count)):
             start = 0
             if runs[n][0][0][0][2] != k:
                 continue
@@ -286,10 +286,12 @@
 
 
 def outer_kernel(
-    even_ref, odd_ref, wk_ref, wv_ref, plan_ref, query_ref, sums_ref, top_ref,
+    even_ref, odd_ref, wk_ref, wv_ref, plan_in, query_ref, sums_ref, top_ref,
     sums_out, top_out,
-    key_ref, value_ref, gap_ref,
+    key_ref, value_ref, gap_ref, plan_ref, sem,
 ):
+    fetch = pltpu.make_async_copy(plan_in, plan_ref, sem)
+    fetch.start()
     nodes, width = even_ref.shape
     head_dim = width // HEADS
     per_group = LANES // head_dim
@@ -299,6 +301,8 @@
     project_keys(jnp.concatenate([even_ref[...], odd_ref[...]], axis=0), wk_ref, wv_ref, key_ref, value_ref, 0)
     gap_ref[0:nodes] = gaps(far, 0, nodes, nodes)
     gap_ref[nodes:] = gaps(-far, 0, nodes, nodes)
+
+    fetch.wait()
 
     def wide(n):
         return plan_ref[1, n] > nodes
@@ -542,12 +546,14 @@
             jax.ShapeDtypeStruct((HEADS, extra, nodes), f32),
             jax.ShapeDtypeStruct((HEADS, 8, nodes), f32),
         ],
-        in_specs=[VMEM] * 4 + [SMEM] + [VMEM] * 3,
+        in_specs=[VMEM] * 4 + [ANY] + [VMEM] * 3,
         out_specs=[VMEM] * 2,
         scratch_shapes=[
             pltpu.VMEM((width // LANES, 2 * nodes, LANES), bf16),
             pltpu.VMEM((HEADS, extra, 2 * nodes), bf16),
             pltpu.VMEM((2 * nodes, nodes), f32),
+            pltpu.SMEM((2, HEADS), i32),
+            pltpu.SemaphoreType.DMA(()),
         ],
         compiler_params=params(24),
         cost_estimate=cost(16 * nodes * width * width, 3 << 20),

time: 49.3 us -> 48.9 us (level)
  Pallas kernels: 21 us -> 20.1 us
    pallas_call x1, Pallas kernels: 3.2 us -> 2.38 us  [local(): pl.pallas_call(outer_kernel, out_shape=[jax.ShapeDtypeStruct((HEADS, extr...]
  transfers between devices with their start and end apart: 15 -> 15, of which waited for: 8 -> 8; matrix products, arithmetic and copies ran while one was open for 1% -> 1% of each run, Pallas kernels for 20% -> 19%
where the time goes in v12:
time: 48.9 us; the launch traced here: 48.6 us
  Pallas kernels  20.1 us (41%)
  waiting for transfers between devices  14.3 us (29%)
  starting transfers between devices  12.7 us (26%)
  local copies, waits for them, and re-layouts  1.02 us (2%)
    ppermute x1, waiting for transfers between devices, local(): even = lax.ppermute(normed, NODES, chips_trade(0))  6.74 us
    pallas_call x1, Pallas kernels, local(): pl.pallas_call(functools.partial(message_kernel, pairs), out_shape=outgoi...  5.53 us
    pallas_call x1, Pallas kernels, local(): pl.pallas_call(far_kernel, out_shape=jax.ShapeDtypeStruct((nodes, width),...  4.95 us
    pallas_call x1, Pallas kernels, local(): pl.pallas_call(near_kernel, out_shape=[jax.ShapeDtypeStruct((HEADS, LANES...  4.69 us
    ppermute x1, waiting for transfers between devices, local(): lax.ppermute(part, NODES, chip_trade(p + 1))  2.78 us
    ppermute x1, starting transfers between devices, local(): odd = lax.ppermute(odd, NODES, bands_trade(1))  2.43 us
    pallas_call x1, Pallas kernels, local(): pl.pallas_call(outer_kernel, out_shape=[jax.ShapeDtypeStruct((HEADS, extr...  2.38 us
    ppermute x1, starting transfers between devices, local(): odd_other = lax.ppermute(odd_other, NODES, bands_trade(1, 1))  2.36 us
  transfers between devices with their start and end apart: 15, of which 8 were waited for; matrix products, arithmetic and copies ran while one was open for 1% of the time, Pallas kernels for 19%

profile of v12, /device:TPU:15, one launch (start us, length us, event | category | flops | bytes accessed | tf_op | source)
XLA Modules:
  0.0 48.6 jit_solution(7227755735218180648)
XLA Ops:
  0.0 5.5 %messages.1 = (bf16[272,256]{1,0:T(8,128)(2,1)}, bf16[272,256]{1,0:T(8,128)(2,1)}, bf16[272,256]{1,0:T(8,128)(2,1)}, bf16[272,256]{1,0:T(8,128)(2,1)}, bf16[400,...) custom-call(bf16[1024,512]{1,0:T(8,128)(2,1)} %grid_ref.1, ...), custom_call_target="tpu_custom_call" | custom-call | flops 2147483648 | bytes 4194304 | tf_op jit(solution)/shard_map/messages/pallas_call | solution.py:413
  5.5 0.7 %collective-permute-start.1 = (bf16[672,256]{1,0:T(8,128)(2,1)}, bf16[672,256]{1,0:T(8,128)(2,1)S(1)}, u32[]{:S(2)}, u32[]{:S(2)}) collective-permute-start(bf16[672,256]{1,0:T(8,128)(2,1)} %get-tuple-element.44), channel_id=1, source_target_pairs={{0,1},{1,0},{2,3},{3,2},{4,5},{5,4},{6,7},{7,6},{8,9},{9,8},{10,11... | collective-permute-start | bytes 1032200 | tf_op jit(solution)/shard_map/ppermute | solution.py:448
  6.7 2.4 %collective-permute-start.3 = (bf16[272,256]{1,0:T(8,128)(2,1)}, bf16[272,256]{1,0:T(8,128)(2,1)S(1)}, u32[]{:S(2)}, u32[]{:S(2)}) collective-permute-start(bf16[272,256]{1,0:T(8,128)(2,1)} %get-tuple-element.49), channel_id=1, source_target_pairs={{0,1},{1,0},{2,3},{3,2},{4,8},{5,9},{6,10},{7,11},{8,4},{9,5},{10,... | collective-permute-start | bytes 417800 | tf_op jit(solution)/shard_map/ppermute | solution.py:451
  9.4 2.1 %collective-permute-start.7 = (bf16[400,256]{1,0:T(8,128)(2,1)}, bf16[400,256]{1,0:T(8,128)(2,1)S(1)}, u32[]{:S(2)}, u32[]{:S(2)}) collective-permute-start(bf16[400,256]{1,0:T(8,128)(2,1)} %get-tuple-element.60), channel_id=1, source_target_pairs={{0,3},{1,2},{2,1},{3,0},{4,7},{5,6},{6,5},{7,4},{8,11},{9,10},{10,... | collective-permute-start | bytes 614408 | tf_op jit(solution)/shard_map/ppermute | solution.py:455
  11.7 2.4 %collective-permute-start.4 = (bf16[272,256]{1,0:T(8,128)(2,1)}, bf16[272,256]{1,0:T(8,128)(2,1)S(1)}, u32[]{:S(2)}, u32[]{:S(2)}) collective-permute-start(bf16[272,256]{1,0:T(8,128)(2,1)} %get-tuple-element.50), channel_id=1, source_target_pairs={{0,1},{1,0},{2,3},{3,2},{4,9},{5,8},{6,11},{7,10},{8,5},{9,4},{10,... | collective-permute-start | bytes 417800 | tf_op jit(solution)/shard_map/ppermute | solution.py:457
  14.2 1.0 %copy-done.2 = bf16[672,256]{1,0:T(8,128)(2,1)S(1)} copy-done((bf16[672,256]{1,0:T(8,128)(2,1)S(1)}, bf16[672,256]{1,0:T(8,128)(2,1)}, u32[]{:S(2)}) %copy-start.2) | copy-done | bytes 344088
  15.2 1.5 %early.1 = (bf16[512,512]{1,0:T(8,128)(2,1)S(1)}, bf16[512,512]{1,0:T(8,128)(2,1)S(1)}, bf16[512,512]{1,0:T(8,128)(2,1)S(1)}, f32[2,256,256]{2,1,0:T(8,128)S(1)}, f32[3,256,256]{2,1,0:T(8,128)S(1)}) custom-call(bf16[512,1536]{1,0:T(8,128)(2,1)S(1)} %copy-done, bf16[672,256]{1,0:T(8,128)(2,1)S(1)} %copy-done.2, ...), custom_call_target="tpu_custom_call" | custom-call | flops 268435456 | bytes 4194304 | tf_op jit(solution)/shard_map/early/pallas_call | solution.py:467
  16.8 1.7 %collective-permute-done.4.refs_3_ = bf16[272,256]{1,0:T(8,128)(2,1)S(1)} collective-permute-done((bf16[272,256]{1,0:T(8,128)(2,1)}, bf16[272,256]{1,0:T(8,128)(2,1)S(1)}, u32[]{:S(2)}, u32[]{:S(2)}) %collective-permute-start.4) | collective-permute-done | bytes 139296 | tf_op jit(solution)/shard_map/ppermute | solution.py:457
  18.5 0.3 left.1
  18.8 1.1 %collective-permute-start.5 = (bf16[256,256]{1,0:T(8,128)(2,1)S(1)}, bf16[256,256]{1,0:T(8,128)(2,1)S(1)}, u32[]{:S(2)}, u32[]{:S(2)}) collective-permute-start(bf16[256,256]{1,0:T(8,128)(2,1)S(1)} %get-tuple-element.58), channel_id=1, source_target_pairs={{0,2},{1,3},{2,0},{3,1},{4,6},{5,7},{6,4},{7,5},{8,10},{9,11},{10,... | collective-permute-start | bytes 393224 | tf_op jit(solution)/shard_map/ppermute | solution.py:490
  19.9 0.3 right.1
  20.3 0.5 collective-permute-start.9
  20.8 2.8 %collective-permute-done.5.refs_1_ = bf16[256,256]{1,0:T(8,128)(2,1)S(1)} collective-permute-done((bf16[256,256]{1,0:T(8,128)(2,1)S(1)}, bf16[256,256]{1,0:T(8,128)(2,1)S(1)}, u32[]{:S(2)}, u32[]{:S(2)}) %collective-permute-start.5) | collective-permute-done | bytes 131104 | tf_op jit(solution)/shard_map/ppermute | solution.py:490
  23.6 1.8 %collective-permute-done.8.refs_3_ = bf16[256,256]{1,0:T(8,128)(2,1)S(1)} collective-permute-done((bf16[256,256]{1,0:T(8,128)(2,1)S(1)}, bf16[256,256]{1,0:T(8,128)(2,1)S(1)}, u32[]{:S(2)}, u32[]{:S(2)}) %collective-permute-start.8) | collective-permute-done | bytes 131104 | tf_op jit(solution)/shard_map/ppermute | solution.py:492
  25.5 0.5 %merge.1 = (f32[256,512]{1,0:T(8,128)S(1)}, bf16[256,512]{1,0:T(8,128)(2,1)S(1)}) custom-call(f32[256,256]{1,0:T(8,128)S(1)} %get-tuple-element.57.refs_0_, bf16[256,256]{1,0:T(8,128)(2,1)S(1)} %collective-permute-done.5.refs_1_, f32[256,256]{1,0:T(8,128)S(1)} %get-tuple-element.62.refs_2_, bf16[256,256]{1,0:T(8,128)(2,1)S(1)} %collective-permute-done.8.refs_3_, ...), custom_call_target="tpu_custom_call" | custom-call | flops 134217728 | bytes 2097152 | tf_op jit(solution)/shard_map/merge/pallas_call | solution.py:495
  26.0 0.9 %collective-permute-start.11 = (bf16[256,512]{1,0:T(8,128)(2,1)S(1)}, bf16[256,512]{1,0:T(8,128)(2,1)S(1)}, u32[]{:S(2)}, u32[]{:S(2)}) collective-permute-start(bf16[256,512]{1,0:T(8,128)(2,1)S(1)} %get-tuple-element.66.own_ref), channel_id=1, source_target_pairs={{0,1},{1,0},{2,3},{3,2},{4,5},{5,4},{6,7},{7,6},{8,9},{9,8},{10,11... | collective-permute-start | bytes 786440 | tf_op jit(solution)/shard_map/ppermute | solution.py:515
  26.9 0.4 collective-permute-start.10
  27.3 0.7 %collective-permute-done.11.side_ref = bf16[256,512]{1,0:T(8,128)(2,1)S(1)} collective-permute-done((bf16[256,512]{1,0:T(8,128)(2,1)S(1)}, bf16[256,512]{1,0:T(8,128)(2,1)S(1)}, u32[]{:S(2)}, u32[]{:S(2)}) %collective-permute-start.11) | collective-permute-done | bytes 262176 | tf_op jit(solution)/shard_map/ppermute | solution.py:515
  28.0 0.9 %collective-permute-start.12 = (bf16[256,512]{1,0:T(8,128)(2,1)S(1)}, bf16[256,512]{1,0:T(8,128)(2,1)S(1)}, u32[]{:S(2)}, u32[]{:S(2)}) collective-permute-start(bf16[256,512]{1,0:T(8,128)(2,1)S(1)} %get-tuple-element.66.own_ref), channel_id=1, source_target_pairs={{0,1},{1,0},{2,4},{3,5},{4,2},{5,3},{6,8},{7,9},{8,6},{9,7},{10,12... | collective-permute-start | bytes 786440 | tf_op jit(solution)/shard_map/ppermute | solution.py:518
  28.9 4.7 %near.1 = (bf16[16,128,256]{2,1,0:T(8,128)(2,1)S(1)}, f32[16,48,256]{2,1,0:T(8,128)S(1)}, f32[16,8,256]{2,1,0:T(8,128)S(1)}) custom-call(bf16[256,512]{1,0:T(8,128)(2,1)S(1)} %get-tuple-element.66.own_ref, bf16[256,512]{1,0:T(8,128)(2,1)S(1)} %collective-permute-done.11.side_ref, bf16[512,512]{1,0:T(8,128)(2,1)S(1)} %get-tuple-element.68.wq_ref, ...), custom_call_target="tpu_custom_call" | custom-call | flops 8589934592 | bytes 4194304 | tf_op jit(solution)/shard_map/near/pallas_call | solution.py:521
  33.6 6.7 %collective-permute-done.10.even_ref = bf16[256,512]{1,0:T(8,128)(2,1)S(1)} collective-permute-done((bf16[256,512]{1,0:T(8,128)(2,1)S(1)}, bf16[256,512]{1,0:T(8,128)(2,1)S(1)}, u32[]{:S(2)}, u32[]{:S(2)}) %collective-permute-start.10) | collective-permute-done | bytes 262176 | tf_op jit(solution)/shard_map/ppermute | solution.py:516
  40.4 0.9 %collective-permute-start.13 = (bf16[256,512]{1,0:T(8,128)(2,1)S(1)}, bf16[256,512]{1,0:T(8,128)(2,1)S(1)}, u32[]{:S(2)}, u32[]{:S(2)}) collective-permute-start(bf16[256,512]{1,0:T(8,128)(2,1)S(1)} %collective-permute-done.10.even_ref), channel_id=1, source_target_pairs={{0,1},{1,0},{2,3},{3,2},{4,5},{5,4},{6,7},{7,6},{8,9},{9,8},{10,11... | collective-permute-start | bytes 786440 | tf_op jit(solution)/shard_map/ppermute | solution.py:541
  41.2 2.4 %outer.1 = (f32[16,48,256]{2,1,0:T(8,128)S(1)}, f32[16,8,256]{2,1,0:T(8,128)S(1)}) custom-call(bf16[256,512]{1,0:T(8,128)(2,1)S(1)} %collective-permute-done.10.even_ref, bf16[256,512]{1,0:T(8,128)(2,1)S(1)} %collective-permute-done.12.odd_ref, bf16[512,512]{1,0:T(8,128)(2,1)S(1)} %get-tuple-element.69.wk_ref, ...), custom_call_target="tpu_custom_call" | custom-call | flops 1073741824 | bytes 3145728 | tf_op jit(solution)/shard_map/outer/pallas_call | solution.py:543
  43.7 4.9 %far.1 = bf16[256,512]{1,0:T(8,128)(2,1)} custom-call(bf16[256,512]{1,0:T(8,128)(2,1)S(1)} %collective-permute-done.13.first_ref, bf16[256,512]{1,0:T(8,128)(2,1)S(1)} %collective-permute-done.14.second_ref, bf16[512,512]{1,0:T(8,128)(2,1)S(1)} %get-tuple-element.69.wk_ref, bf16[512,512]{1,0:T(8,128)(2,1)S(1)} %get-tuple-element.70.wv_ref, ...), custom_call_target="tpu_custom_call" | custom-call | flops 8589934592 | bytes 8388608 | tf_op jit(solution)/shard_map/far/pallas_call | solution.py:563
  (39 shorter events, 1.4 us)
Async XLA Ops:
  0.0 9.2 %copy-start.9 = (s32[16]{0:T(128)S(1)}, s32[16]{0:T(128)}, u32[]{:S(2)}) copy-start(s32[16]{0:T(128)} %param.23) | copy-start | bytes 196
  0.0 14.2 %copy-start = (bf16[512,1536]{1,0:T(8,128)(2,1)S(1)}, bf16[512,1536]{1,0:T(8,128)(2,1)}, u32[]{:S(2)}) copy-start(bf16[512,1536]{1,0:T(8,128)(2,1)} %w_ref.2) | copy-start | bytes 4718596
  5.5 3.8 %collective-permute-start.1 = (bf16[672,256]{1,0:T(8,128)(2,1)}, bf16[672,256]{1,0:T(8,128)(2,1)S(1)}, u32[]{:S(2)}, u32[]{:S(2)}) collective-permute-start(bf16[672,256]{1,0:T(8,128)(2,1)} %get-tuple-element.44), channel_id=1, source_target_pairs={{0,1},{1,0},{2,3},{3,2},{4,5},{5,4},{6,7},{7,6},{8,9},{9,8},{10,11... | collective-permute-start | bytes 1032200 | tf_op jit(solution)/shard_map/ppermute | solution.py:448
  6.3 13.7 %collective-permute-start.6 = (bf16[400,256]{1,0:T(8,128)(2,1)}, bf16[400,256]{1,0:T(8,128)(2,1)S(1)}, u32[]{:S(2)}, u32[]{:S(2)}) collective-permute-start(bf16[400,256]{1,0:T(8,128)(2,1)} %get-tuple-element.59), channel_id=1, source_target_pairs={{0,2},{1,3},{2,0},{3,1},{4,6},{5,7},{6,4},{7,5},{8,10},{9,11},{10,... | collective-permute-start | bytes 614408 | tf_op jit(solution)/shard_map/ppermute | solution.py:449
  6.6 5.1 %collective-permute-start = (bf16[272,256]{1,0:T(8,128)(2,1)}, bf16[272,256]{1,0:T(8,128)(2,1)S(1)}, u32[]{:S(2)}, u32[]{:S(2)}) collective-permute-start(bf16[272,256]{1,0:T(8,128)(2,1)} %get-tuple-element.43), channel_id=1, source_target_pairs={{0,4},{1,5},{2,6},{3,7},{4,0},{5,1},{6,2},{7,3},{8,12},{9,13},{10,... | collective-permute-start | bytes 417800 | tf_op jit(solution)/shard_map/ppermute | solution.py:450
  6.7 9.9 %collective-permute-start.3 = (bf16[272,256]{1,0:T(8,128)(2,1)}, bf16[272,256]{1,0:T(8,128)(2,1)S(1)}, u32[]{:S(2)}, u32[]{:S(2)}) collective-permute-start(bf16[272,256]{1,0:T(8,128)(2,1)} %get-tuple-element.49), channel_id=1, source_target_pairs={{0,1},{1,0},{2,3},{3,2},{4,8},{5,9},{6,10},{7,11},{8,4},{9,5},{10,... | collective-permute-start | bytes 417800 | tf_op jit(solution)/shard_map/ppermute | solution.py:451
  9.4 10.6 %collective-permute-start.7 = (bf16[400,256]{1,0:T(8,128)(2,1)}, bf16[400,256]{1,0:T(8,128)(2,1)S(1)}, u32[]{:S(2)}, u32[]{:S(2)}) collective-permute-start(bf16[400,256]{1,0:T(8,128)(2,1)} %get-tuple-element.60), channel_id=1, source_target_pairs={{0,3},{1,2},{2,1},{3,0},{4,7},{5,6},{6,5},{7,4},{8,11},{9,10},{10,... | collective-permute-start | bytes 614408 | tf_op jit(solution)/shard_map/ppermute | solution.py:455
  11.4 5.4 %collective-permute-start.2 = (bf16[272,256]{1,0:T(8,128)(2,1)}, bf16[272,256]{1,0:T(8,128)(2,1)S(1)}, u32[]{:S(2)}, u32[]{:S(2)}) collective-permute-start(bf16[272,256]{1,0:T(8,128)(2,1)} %get-tuple-element.48), channel_id=1, source_target_pairs={{0,5},{1,4},{2,7},{3,6},{4,1},{5,0},{6,3},{7,2},{8,13},{9,12},{10,... | collective-permute-start | bytes 417800 | tf_op jit(solution)/shard_map/ppermute | solution.py:456
  11.7 6.8 %collective-permute-start.4 = (bf16[272,256]{1,0:T(8,128)(2,1)}, bf16[272,256]{1,0:T(8,128)(2,1)S(1)}, u32[]{:S(2)}, u32[]{:S(2)}) collective-permute-start(bf16[272,256]{1,0:T(8,128)(2,1)} %get-tuple-element.50), channel_id=1, source_target_pairs={{0,1},{1,0},{2,3},{3,2},{4,9},{5,8},{6,11},{7,10},{8,5},{9,4},{10,... | collective-permute-start | bytes 417800 | tf_op jit(solution)/shard_map/ppermute | solution.py:457
  15.2 10.3 %copy-start.1 = (bf16[512,512]{1,0:T(8,128)(2,1)S(1)}, bf16[512,512]{1,0:T(8,128)(2,1)}, u32[]{:S(2)}) copy-start(bf16[512,512]{1,0:T(8,128)(2,1)} %refs_6_.1) | copy-start | bytes 1572868
  15.2 10.3 %copy-start.3 = (bf16[256,512]{1,0:T(8,128)(2,1)S(1)}, bf16[256,512]{1,0:T(8,128)(2,1)}, u32[]{:S(2)}) copy-start(bf16[256,512]{1,0:T(8,128)(2,1)} %refs_5_.1) | copy-start | bytes 786436
  15.2 10.3 %copy-start.4 = (f32[512]{0:T(512)S(1)}, f32[512]{0:T(512)}, u32[]{:S(2)}) copy-start(f32[512]{0:T(512)} %param.21) | copy-start | bytes 6148
  18.8 4.7 %collective-permute-start.5 = (bf16[256,256]{1,0:T(8,128)(2,1)S(1)}, bf16[256,256]{1,0:T(8,128)(2,1)S(1)}, u32[]{:S(2)}, u32[]{:S(2)}) collective-permute-start(bf16[256,256]{1,0:T(8,128)(2,1)S(1)} %get-tuple-element.58), channel_id=1, source_target_pairs={{0,2},{1,3},{2,0},{3,1},{4,6},{5,7},{6,4},{7,5},{8,10},{9,11},{10,... | collective-permute-start | bytes 393224 | tf_op jit(solution)/shard_map/ppermute | solution.py:490
  20.2 5.1 %collective-permute-start.8 = (bf16[256,256]{1,0:T(8,128)(2,1)S(1)}, bf16[256,256]{1,0:T(8,128)(2,1)S(1)}, u32[]{:S(2)}, u32[]{:S(2)}) collective-permute-start(bf16[256,256]{1,0:T(8,128)(2,1)S(1)} %get-tuple-element.63), channel_id=1, source_target_pairs={{0,4},{1,5},{2,6},{3,7},{4,0},{5,1},{6,2},{7,3},{8,12},{9,13},{10,... | collective-permute-start | bytes 393224 | tf_op jit(solution)/shard_map/ppermute | solution.py:492
  20.3 5.1 %collective-permute-start.9 = (bf16[256,256]{1,0:T(8,128)(2,1)S(1)}, bf16[256,256]{1,0:T(8,128)(2,1)S(1)}, u32[]{:S(2)}, u32[]{:S(2)}) collective-permute-start(bf16[256,256]{1,0:T(8,128)(2,1)S(1)} %get-tuple-element.64), channel_id=1, source_target_pairs={{0,1},{1,0},{2,3},{3,2},{4,8},{5,9},{6,10},{7,11},{8,4},{9,5},{10,... | collective-permute-start | bytes 393224 | tf_op jit(solution)/shard_map/ppermute | solution.py:493
  26.0 2.1 %collective-permute-start.11 = (bf16[256,512]{1,0:T(8,128)(2,1)S(1)}, bf16[256,512]{1,0:T(8,128)(2,1)S(1)}, u32[]{:S(2)}, u32[]{:S(2)}) collective-permute-start(bf16[256,512]{1,0:T(8,128)(2,1)S(1)} %get-tuple-element.66.own_ref), channel_id=1, source_target_pairs={{0,1},{1,0},{2,3},{3,2},{4,5},{5,4},{6,7},{7,6},{8,9},{9,8},{10,11... | collective-permute-start | bytes 786440 | tf_op jit(solution)/shard_map/ppermute | solution.py:515
  26.9 13.5 %collective-permute-start.10 = (bf16[256,512]{1,0:T(8,128)(2,1)S(1)}, bf16[256,512]{1,0:T(8,128)(2,1)S(1)}, u32[]{:S(2)}, u32[]{:S(2)}) collective-permute-start(bf16[256,512]{1,0:T(8,128)(2,1)S(1)} %get-tuple-element.66.own_ref), channel_id=1, source_target_pairs={{0,2},{1,3},{2,0},{3,1},{4,6},{5,7},{6,4},{7,5},{8,10},{9,11},{10,... | collective-permute-start | bytes 786440 | tf_op jit(solution)/shard_map/ppermute | solution.py:516
  28.0 12.3 %collective-permute-start.12 = (bf16[256,512]{1,0:T(8,128)(2,1)S(1)}, bf16[256,512]{1,0:T(8,128)(2,1)S(1)}, u32[]{:S(2)}, u32[]{:S(2)}) collective-permute-start(bf16[256,512]{1,0:T(8,128)(2,1)S(1)} %get-tuple-element.66.own_ref), channel_id=1, source_target_pairs={{0,1},{1,0},{2,4},{3,5},{4,2},{5,3},{6,8},{7,9},{8,6},{9,7},{10,12... | collective-permute-start | bytes 786440 | tf_op jit(solution)/shard_map/ppermute | solution.py:518
  28.9 14.8 %copy-start.6 = (bf16[2048,512]{1,0:T(8,128)(2,1)S(1)}, bf16[2048,512]{1,0:T(8,128)(2,1)}, u32[]{:S(2)}) copy-start(bf16[2048,512]{1,0:T(8,128)(2,1)} %down_ref.1) | copy-start | bytes 6291460
  33.6 10.1 %copy-start.5 = (bf16[512,2048]{1,0:T(8,128)(2,1)S(1)}, bf16[512,2048]{1,0:T(8,128)(2,1)}, u32[]{:S(2)}) copy-start(bf16[512,2048]{1,0:T(8,128)(2,1)} %up_ref.1) | copy-start | bytes 6291460
  33.6 10.1 %copy-start.7 = (bf16[512,512]{1,0:T(8,128)(2,1)S(1)}, bf16[512,512]{1,0:T(8,128)(2,1)}, u32[]{:S(2)}) copy-start(bf16[512,512]{1,0:T(8,128)(2,1)} %w_out_ref.1) | copy-start | bytes 1572868
  33.6 10.1 %copy-start.8 = (f32[512]{0:T(512)S(1)}, f32[512]{0:T(512)}, u32[]{:S(2)}) copy-start(f32[512]{0:T(512)} %param.25) | copy-start | bytes 6148
  40.4 3.2 %collective-permute-start.13 = (bf16[256,512]{1,0:T(8,128)(2,1)S(1)}, bf16[256,512]{1,0:T(8,128)(2,1)S(1)}, u32[]{:S(2)}, u32[]{:S(2)}) collective-permute-start(bf16[256,512]{1,0:T(8,128)(2,1)S(1)} %collective-permute-done.10.even_ref), channel_id=1, source_target_pairs={{0,1},{1,0},{2,3},{3,2},{4,5},{5,4},{6,7},{7,6},{8,9},{9,8},{10,11... | collective-permute-start | bytes 786440 | tf_op jit(solution)/shard_map/ppermute | solution.py:541
  41.2 2.4 %collective-permute-start.14 = (bf16[256,512]{1,0:T(8,128)(2,1)S(1)}, bf16[256,512]{1,0:T(8,128)(2,1)S(1)}, u32[]{:S(2)}, u32[]{:S(2)}) collective-permute-start(bf16[256,512]{1,0:T(8,128)(2,1)S(1)} %collective-permute-done.12.odd_ref), channel_id=1, source_target_pairs={{0,1},{1,0},{2,3},{3,2},{4,5},{5,4},{6,7},{7,6},{8,9},{9,8},{10,11... | collective-permute-start | bytes 786440 | tf_op jit(solution)/shard_map/ppermute | solution.py:542
  (1 other events, 1.0 us)

commit v13 on v12

--- a/solution.py
+++ b/solution.py
@@ -286,22 +286,20 @@
 
 
 def outer_kernel(
-    even_ref, odd_ref, wk_ref, wv_ref, plan_in, query_ref, sums_ref, top_ref,
+    by_pair, block_ref, wk_ref, wv_ref, plan_in, query_ref, sums_ref, top_ref,
     sums_out, top_out,
     key_ref, value_ref, gap_ref, plan_ref, sem,
 ):
     fetch = pltpu.make_async_copy(plan_in, plan_ref, sem)
     fetch.start()
-    nodes, width = even_ref.shape
+    nodes, width = block_ref.shape
     head_dim = width // HEADS
     per_group = LANES // head_dim
     far = 2 - 4 * lax.rem(lax.axis_index("inner") // 2, 2)
     scale = head_dim ** (-0.5) / math.log(2.0)
     value_ref[:, head_dim:, :] = jnp.ones_like(value_ref[:, head_dim:, :])
-    project_keys(jnp.concatenate([even_ref[...], odd_ref[...]], axis=0), wk_ref, wv_ref, key_ref, value_ref, 0)
-    gap_ref[0:nodes] = gaps(far, 0, nodes, nodes)
-    gap_ref[nodes:] = gaps(-far, 0, nodes, nodes)
-
+    project_keys(block_ref[...], wk_ref, wv_ref, key_ref, value_ref, 0)
+    gap_ref[...] = gaps(far if by_pair else -far, 0, nodes, nodes)
     fetch.wait()
 
     def wide(n):
@@ -537,28 +535,33 @@
         name="near",
     )(normed, side, w_query, w_key, w_value, plan)
 
-    even, odd, near, top = lax.optimization_barrier((even, odd, near, top))
+    def outer(by_pair, block, near, top):
+        return pl.pallas_call(
+            functools.partial(outer_kernel, by_pair),
+            out_shape=[
+                jax.ShapeDtypeStruct((HEADS, extra, nodes), f32),
+                jax.ShapeDtypeStruct((HEADS, 8, nodes), f32),
+            ],
+            in_specs=[VMEM] * 3 + [ANY] + [VMEM] * 3,
+            out_specs=[VMEM] * 2,
+            scratch_shapes=[
+                pltpu.VMEM((width // LANES, nodes, LANES), bf16),
+                pltpu.VMEM((HEADS, extra, nodes), bf16),
+                pltpu.VMEM((nodes, nodes), f32),
+                pltpu.SMEM((2, HEADS), i32),
+                pltpu.SemaphoreType.DMA(()),
+            ],
+            compiler_params=params(24),
+            cost_estimate=cost(8 * nodes * width * width, 3 << 20),
+            name="pair" if by_pair else "other",
+        )(block, w_key, w_value, plan, query, near, top)
+
+    odd, near, top = lax.optimization_barrier((odd, near, top))
+    second = lax.ppermute(odd, NODES, beside)
+    near, top = outer(False, odd, near, top)
+    even, near, top = lax.optimization_barrier((even, near, top))
     first = lax.ppermute(even, NODES, beside)
-    second = lax.ppermute(odd, NODES, beside)
-    near, top = pl.pallas_call(
-        outer_kernel,
-        out_shape=[
-            jax.ShapeDtypeStruct((HEADS, extra, nodes), f32),
-            jax.ShapeDtypeStruct((HEADS, 8, nodes), f32),
-        ],
-        in_specs=[VMEM] * 4 + [ANY] + [VMEM] * 3,
-        out_specs=[VMEM] * 2,
-        scratch_shapes=[
-            pltpu.VMEM((width // LANES, 2 * nodes, LANES), bf16),
-            pltpu.VMEM((HEADS, extra, 2 * nodes), bf16),
-            pltpu.VMEM((2 * nodes, nodes), f32),
-            pltpu.SMEM((2, HEADS), i32),
-            pltpu.SemaphoreType.DMA(()),
-        ],
-        compiler_params=params(24),
-        cost_estimate=cost(16 * nodes * width * width, 3 << 20),
-        name="outer",
-    )(even, odd, w_key, w_value, plan, query, near, top)
+    near, top = outer(True, even, near, top)
 
     return pl.pallas_call(
         far_kernel,

time: 48.9 us -> 48.5 us (level)
  waiting for transfers between devices: 14.3 us -> 12.5 us
  Pallas kernels: 20.1 us -> 21.2 us
    ppermute x1, waiting for transfers between devices: 6.74 us -> 2.24 us  [local(): even = lax.ppermute(normed, NODES, chips_trade(0))]
    ppermute x1, waiting for transfers between devices: 0.01 us -> 2.75 us  [local(): odd = lax.ppermute(normed, NODES, chips_trade(1))]
    pallas_call x1 -> x2, Pallas kernels: 2.38 us -> 3.36 us  [outer(): pl.pallas_call(functools.partial(outer_kernel, by_pair), out_shape=[jax.S...]
  transfers between devices with their start and end apart: 15 -> 15, of which waited for: 8 -> 9; matrix products, arithmetic and copies ran while one was open for 1% -> 1% of each run, Pallas kernels for 19% -> 21%
where the time goes in v13:
time: 48.5 us; the launch traced here: 48 us
  Pallas kernels  21.2 us (44%)
  starting transfers between devices  12.8 us (26%)
  waiting for transfers between devices  12.5 us (26%)
  local copies, waits for them, and re-layouts  1.02 us (2%)
    pallas_call x1, Pallas kernels, local(): pl.pallas_call(functools.partial(message_kernel, pairs), out_shape=outgoi...  5.53 us
    pallas_call x1, Pallas kernels, local(): pl.pallas_call(far_kernel, out_shape=jax.ShapeDtypeStruct((nodes, width),...  4.94 us
    pallas_call x1, Pallas kernels, local(): pl.pallas_call(near_kernel, out_shape=[jax.ShapeDtypeStruct((HEADS, LANES...  4.85 us
    pallas_call x2, Pallas kernels, outer(): pl.pallas_call(functools.partial(outer_kernel, by_pair), out_shape=[jax.S...  3.36 us
    ppermute x1, waiting for transfers between devices, local(): lax.ppermute(part, NODES, chip_trade(p + 1))  2.77 us
    ppermute x1, waiting for transfers between devices, local(): odd = lax.ppermute(normed, NODES, chips_trade(1))  2.75 us
    ppermute x1, starting transfers between devices, local(): odd = lax.ppermute(odd, NODES, bands_trade(1))  2.43 us
    ppermute x1, starting transfers between devices, local(): odd_other = lax.ppermute(odd_other, NODES, bands_trade(1, 1))  2.36 us
  transfers between devices with their start and end apart: 15, of which 9 were waited for; matrix products, arithmetic and copies ran while one was open for 1% of the time, Pallas kernels for 21%

profile of v13, /device:TPU:15, one launch (start us, length us, event | category | flops | bytes accessed | tf_op | source)
XLA Modules:
  0.0 48.0 jit_solution(5707852824784191134)
XLA Ops:
  0.0 5.5 %messages.1 = (bf16[272,256]{1,0:T(8,128)(2,1)}, bf16[272,256]{1,0:T(8,128)(2,1)}, bf16[272,256]{1,0:T(8,128)(2,1)}, bf16[272,256]{1,0:T(8,128)(2,1)}, bf16[400,...) custom-call(bf16[1024,512]{1,0:T(8,128)(2,1)} %grid_ref.1, ...), custom_call_target="tpu_custom_call" | custom-call | flops 2147483648 | bytes 4194304 | tf_op jit(solution)/shard_map/messages/pallas_call | solution.py:411
  5.5 0.7 %collective-permute-start.1 = (bf16[672,256]{1,0:T(8,128)(2,1)}, bf16[672,256]{1,0:T(8,128)(2,1)S(1)}, u32[]{:S(2)}, u32[]{:S(2)}) collective-permute-start(bf16[672,256]{1,0:T(8,128)(2,1)} %get-tuple-element.48), channel_id=1, source_target_pairs={{0,1},{1,0},{2,3},{3,2},{4,5},{5,4},{6,7},{7,6},{8,9},{9,8},{10,11... | collective-permute-start | bytes 1032200 | tf_op jit(solution)/shard_map/ppermute | solution.py:446
  6.7 2.4 %collective-permute-start.3 = (bf16[272,256]{1,0:T(8,128)(2,1)}, bf16[272,256]{1,0:T(8,128)(2,1)S(1)}, u32[]{:S(2)}, u32[]{:S(2)}) collective-permute-start(bf16[272,256]{1,0:T(8,128)(2,1)} %get-tuple-element.53), channel_id=1, source_target_pairs={{0,1},{1,0},{2,3},{3,2},{4,8},{5,9},{6,10},{7,11},{8,4},{9,5},{10,... | collective-permute-start | bytes 417800 | tf_op jit(solution)/shard_map/ppermute | solution.py:449
  9.4 2.1 %collective-permute-start.7 = (bf16[400,256]{1,0:T(8,128)(2,1)}, bf16[400,256]{1,0:T(8,128)(2,1)S(1)}, u32[]{:S(2)}, u32[]{:S(2)}) collective-permute-start(bf16[400,256]{1,0:T(8,128)(2,1)} %get-tuple-element.64), channel_id=1, source_target_pairs={{0,3},{1,2},{2,1},{3,0},{4,7},{5,6},{6,5},{7,4},{8,11},{9,10},{10,... | collective-permute-start | bytes 614408 | tf_op jit(solution)/shard_map/ppermute | solution.py:453
  11.7 2.4 %collective-permute-start.4 = (bf16[272,256]{1,0:T(8,128)(2,1)}, bf16[272,256]{1,0:T(8,128)(2,1)S(1)}, u32[]{:S(2)}, u32[]{:S(2)}) collective-permute-start(bf16[272,256]{1,0:T(8,128)(2,1)} %get-tuple-element.54), channel_id=1, source_target_pairs={{0,1},{1,0},{2,3},{3,2},{4,9},{5,8},{6,11},{7,10},{8,5},{9,4},{10,... | collective-permute-start | bytes 417800 | tf_op jit(solution)/shard_map/ppermute | solution.py:455
  14.2 1.0 %copy-done.2 = bf16[672,256]{1,0:T(8,128)(2,1)S(1)} copy-done((bf16[672,256]{1,0:T(8,128)(2,1)S(1)}, bf16[672,256]{1,0:T(8,128)(2,1)}, u32[]{:S(2)}) %copy-start.2) | copy-done | bytes 344088
  15.2 1.5 %early.1 = (bf16[512,512]{1,0:T(8,128)(2,1)S(1)}, bf16[512,512]{1,0:T(8,128)(2,1)S(1)}, bf16[512,512]{1,0:T(8,128)(2,1)S(1)}, f32[2,256,256]{2,1,0:T(8,128)S(1)}, f32[3,256,256]{2,1,0:T(8,128)S(1)}) custom-call(bf16[512,1536]{1,0:T(8,128)(2,1)S(1)} %copy-done, bf16[672,256]{1,0:T(8,128)(2,1)S(1)} %copy-done.2, ...), custom_call_target="tpu_custom_call" | custom-call | flops 268435456 | bytes 4194304 | tf_op jit(solution)/shard_map/early/pallas_call | solution.py:465
  16.8 1.7 %collective-permute-done.4.refs_3_ = bf16[272,256]{1,0:T(8,128)(2,1)S(1)} collective-permute-done((bf16[272,256]{1,0:T(8,128)(2,1)}, bf16[272,256]{1,0:T(8,128)(2,1)S(1)}, u32[]{:S(2)}, u32[]{:S(2)}) %collective-permute-start.4) | collective-permute-done | bytes 139296 | tf_op jit(solution)/shard_map/ppermute | solution.py:455
  18.8 1.1 %collective-permute-start.5 = (bf16[256,256]{1,0:T(8,128)(2,1)S(1)}, bf16[256,256]{1,0:T(8,128)(2,1)S(1)}, u32[]{:S(2)}, u32[]{:S(2)}) collective-permute-start(bf16[256,256]{1,0:T(8,128)(2,1)S(1)} %get-tuple-element.62), channel_id=1, source_target_pairs={{0,2},{1,3},{2,0},{3,1},{4,6},{5,7},{6,4},{7,5},{8,10},{9,11},{10,... | collective-permute-start | bytes 393224 | tf_op jit(solution)/shard_map/ppermute | solution.py:488
  20.3 0.5 %collective-permute-start.9 = (bf16[256,256]{1,0:T(8,128)(2,1)S(1)}, bf16[256,256]{1,0:T(8,128)(2,1)S(1)}, u32[]{:S(2)}, u32[]{:S(2)}) collective-permute-start(bf16[256,256]{1,0:T(8,128)(2,1)S(1)} %get-tuple-element.68), channel_id=1, source_target_pairs={{0,1},{1,0},{2,3},{3,2},{4,8},{5,9},{6,10},{7,11},{8,4},{9,5},{10,... | collective-permute-start | bytes 393224 | tf_op jit(solution)/shard_map/ppermute | solution.py:491
  20.8 2.8 %collective-permute-done.5.refs_1_ = bf16[256,256]{1,0:T(8,128)(2,1)S(1)} collective-permute-done((bf16[256,256]{1,0:T(8,128)(2,1)S(1)}, bf16[256,256]{1,0:T(8,128)(2,1)S(1)}, u32[]{:S(2)}, u32[]{:S(2)}) %collective-permute-start.5) | collective-permute-done | bytes 131104 | tf_op jit(solution)/shard_map/ppermute | solution.py:488
  23.6 1.8 %collective-permute-done.8.refs_3_ = bf16[256,256]{1,0:T(8,128)(2,1)S(1)} collective-permute-done((bf16[256,256]{1,0:T(8,128)(2,1)S(1)}, bf16[256,256]{1,0:T(8,128)(2,1)S(1)}, u32[]{:S(2)}, u32[]{:S(2)}) %collective-permute-start.8) | collective-permute-done | bytes 131104 | tf_op jit(solution)/shard_map/ppermute | solution.py:490
  25.5 0.5 %merge.1 = (f32[256,512]{1,0:T(8,128)S(1)}, bf16[256,512]{1,0:T(8,128)(2,1)S(1)}) custom-call(f32[256,256]{1,0:T(8,128)S(1)} %get-tuple-element.61.refs_0_, bf16[256,256]{1,0:T(8,128)(2,1)S(1)} %collective-permute-done.5.refs_1_, f32[256,256]{1,0:T(8,128)S(1)} %get-tuple-element.66.refs_2_, bf16[256,256]{1,0:T(8,128)(2,1)S(1)} %collective-permute-done.8.refs_3_, ...), custom_call_target="tpu_custom_call" | custom-call | flops 134217728 | bytes 2097152 | tf_op jit(solution)/shard_map/merge/pallas_call | solution.py:493
  25.9 0.9 %collective-permute-start.11 = (bf16[256,512]{1,0:T(8,128)(2,1)S(1)}, bf16[256,512]{1,0:T(8,128)(2,1)S(1)}, u32[]{:S(2)}, u32[]{:S(2)}) collective-permute-start(bf16[256,512]{1,0:T(8,128)(2,1)S(1)} %get-tuple-element.70.own_ref), channel_id=1, source_target_pairs={{0,1},{1,0},{2,3},{3,2},{4,5},{5,4},{6,7},{7,6},{8,9},{9,8},{10,11... | collective-permute-start | bytes 786440 | tf_op jit(solution)/shard_map/ppermute | solution.py:513
  26.9 0.4 collective-permute-start.10
  27.3 0.7 %collective-permute-done.11.side_ref = bf16[256,512]{1,0:T(8,128)(2,1)S(1)} collective-permute-done((bf16[256,512]{1,0:T(8,128)(2,1)S(1)}, bf16[256,512]{1,0:T(8,128)(2,1)S(1)}, u32[]{:S(2)}, u32[]{:S(2)}) %collective-permute-start.11) | collective-permute-done | bytes 262176 | tf_op jit(solution)/shard_map/ppermute | solution.py:513
  28.0 0.9 %collective-permute-start.12 = (bf16[256,512]{1,0:T(8,128)(2,1)S(1)}, bf16[256,512]{1,0:T(8,128)(2,1)S(1)}, u32[]{:S(2)}, u32[]{:S(2)}) collective-permute-start(bf16[256,512]{1,0:T(8,128)(2,1)S(1)} %get-tuple-element.70.own_ref), channel_id=1, source_target_pairs={{0,1},{1,0},{2,4},{3,5},{4,2},{5,3},{6,8},{7,9},{8,6},{9,7},{10,12... | collective-permute-start | bytes 786440 | tf_op jit(solution)/shard_map/ppermute | solution.py:516
  28.9 4.8 %near.1 = (bf16[16,128,256]{2,1,0:T(8,128)(2,1)S(1)}, f32[16,48,256]{2,1,0:T(8,128)S(1)}, f32[16,8,256]{2,1,0:T(8,128)S(1)}) custom-call(bf16[256,512]{1,0:T(8,128)(2,1)S(1)} %get-tuple-element.70.own_ref, bf16[256,512]{1,0:T(8,128)(2,1)S(1)} %collective-permute-done.11.side_ref, bf16[512,512]{1,0:T(8,128)(2,1)S(1)} %get-tuple-element.72.wq_ref, ...), custom_call_target="tpu_custom_call" | custom-call | flops 8589934592 | bytes 4194304 | tf_op jit(solution)/shard_map/near/pallas_call | solution.py:519
  33.7 2.8 %collective-permute-done.12.block_ref = bf16[256,512]{1,0:T(8,128)(2,1)S(1)} collective-permute-done((bf16[256,512]{1,0:T(8,128)(2,1)S(1)}, bf16[256,512]{1,0:T(8,128)(2,1)S(1)}, u32[]{:S(2)}, u32[]{:S(2)}) %collective-permute-start.12) | collective-permute-done | bytes 262176 | tf_op jit(solution)/shard_map/ppermute | solution.py:516
  36.5 1.6 %other.1 = (f32[16,48,256]{2,1,0:T(8,128)S(1)}, f32[16,8,256]{2,1,0:T(8,128)S(1)}) custom-call(bf16[256,512]{1,0:T(8,128)(2,1)S(1)} %collective-permute-done.12.block_ref, bf16[512,512]{1,0:T(8,128)(2,1)S(1)} %get-tuple-element.73.wk_ref, bf16[512,512]{1,0:T(8,128)(2,1)S(1)} %get-tuple-element.74.wv_ref, s32[2,16]{1,0:T(2,128)S(1)} %select_reduce_fusion.plan_ref.plan_in, ...), custom_call_target="tpu_custom_call" | custom-call | flops 536870912 | bytes 3145728 | tf_op jit(solution)/shard_map/other/pallas_call | solution.py:539
  38.1 2.2 %collective-permute-done.10.block_ref = bf16[256,512]{1,0:T(8,128)(2,1)S(1)} collective-permute-done((bf16[256,512]{1,0:T(8,128)(2,1)S(1)}, bf16[256,512]{1,0:T(8,128)(2,1)S(1)}, u32[]{:S(2)}, u32[]{:S(2)}) %collective-permute-start.10) | collective-permute-done | bytes 262176 | tf_op jit(solution)/shard_map/ppermute | solution.py:514
  40.4 0.8 %collective-permute-start.13 = (bf16[256,512]{1,0:T(8,128)(2,1)S(1)}, bf16[256,512]{1,0:T(8,128)(2,1)S(1)}, u32[]{:S(2)}, u32[]{:S(2)}) collective-permute-start(bf16[256,512]{1,0:T(8,128)(2,1)S(1)} %collective-permute-done.10.block_ref), channel_id=1, source_target_pairs={{0,1},{1,0},{2,3},{3,2},{4,5},{5,4},{6,7},{7,6},{8,9},{9,8},{10,11... | collective-permute-start | bytes 786440 | tf_op jit(solution)/shard_map/ppermute | solution.py:563
  41.2 1.8 %pair.1 = (f32[16,48,256]{2,1,0:T(8,128)S(1)}, f32[16,8,256]{2,1,0:T(8,128)S(1)}) custom-call(bf16[256,512]{1,0:T(8,128)(2,1)S(1)} %collective-permute-done.10.block_ref, bf16[512,512]{1,0:T(8,128)(2,1)S(1)} %get-tuple-element.73.wk_ref, bf16[512,512]{1,0:T(8,128)(2,1)S(1)} %get-tuple-element.74.wv_ref, s32[2,16]{1,0:T(2,128)S(1)} %select_reduce_fusion.plan_ref.plan_in, ...), custom_call_target="tpu_custom_call" | custom-call | flops 536870912 | bytes 3145728 | tf_op jit(solution)/shard_map/pair/pallas_call | solution.py:539
  43.1 4.9 %far.1 = bf16[256,512]{1,0:T(8,128)(2,1)} custom-call(bf16[256,512]{1,0:T(8,128)(2,1)S(1)} %collective-permute-done.13.first_ref, bf16[256,512]{1,0:T(8,128)(2,1)S(1)} %collective-permute-done.14.second_ref, bf16[512,512]{1,0:T(8,128)(2,1)S(1)} %get-tuple-element.73.wk_ref, bf16[512,512]{1,0:T(8,128)(2,1)S(1)} %get-tuple-element.74.wv_ref, ...), custom_call_target="tpu_custom_call" | custom-call | flops 8589934592 | bytes 8388608 | tf_op jit(solution)/shard_map/far/pallas_call | solution.py:566
  (40 shorter events, 2.0 us)
Async XLA Ops:
  0.0 9.2 %copy-start.9 = (s32[16]{0:T(128)S(1)}, s32[16]{0:T(128)}, u32[]{:S(2)}) copy-start(s32[16]{0:T(128)} %param.23) | copy-start | bytes 196
  0.0 14.2 %copy-start = (bf16[512,1536]{1,0:T(8,128)(2,1)S(1)}, bf16[512,1536]{1,0:T(8,128)(2,1)}, u32[]{:S(2)}) copy-start(bf16[512,1536]{1,0:T(8,128)(2,1)} %w_ref.2) | copy-start | bytes 4718596
  5.5 3.8 %collective-permute-start.1 = (bf16[672,256]{1,0:T(8,128)(2,1)}, bf16[672,256]{1,0:T(8,128)(2,1)S(1)}, u32[]{:S(2)}, u32[]{:S(2)}) collective-permute-start(bf16[672,256]{1,0:T(8,128)(2,1)} %get-tuple-element.48), channel_id=1, source_target_pairs={{0,1},{1,0},{2,3},{3,2},{4,5},{5,4},{6,7},{7,6},{8,9},{9,8},{10,11... | collective-permute-start | bytes 1032200 | tf_op jit(solution)/shard_map/ppermute | solution.py:446
  6.3 13.7 %collective-permute-start.6 = (bf16[400,256]{1,0:T(8,128)(2,1)}, bf16[400,256]{1,0:T(8,128)(2,1)S(1)}, u32[]{:S(2)}, u32[]{:S(2)}) collective-permute-start(bf16[400,256]{1,0:T(8,128)(2,1)} %get-tuple-element.63), channel_id=1, source_target_pairs={{0,2},{1,3},{2,0},{3,1},{4,6},{5,7},{6,4},{7,5},{8,10},{9,11},{10,... | collective-permute-start | bytes 614408 | tf_op jit(solution)/shard_map/ppermute | solution.py:447
  6.6 5.1 %collective-permute-start = (bf16[272,256]{1,0:T(8,128)(2,1)}, bf16[272,256]{1,0:T(8,128)(2,1)S(1)}, u32[]{:S(2)}, u32[]{:S(2)}) collective-permute-start(bf16[272,256]{1,0:T(8,128)(2,1)} %get-tuple-element.47), channel_id=1, source_target_pairs={{0,4},{1,5},{2,6},{3,7},{4,0},{5,1},{6,2},{7,3},{8,12},{9,13},{10,... | collective-permute-start | bytes 417800 | tf_op jit(solution)/shard_map/ppermute | solution.py:448
  6.7 9.9 %collective-permute-start.3 = (bf16[272,256]{1,0:T(8,128)(2,1)}, bf16[272,256]{1,0:T(8,128)(2,1)S(1)}, u32[]{:S(2)}, u32[]{:S(2)}) collective-permute-start(bf16[272,256]{1,0:T(8,128)(2,1)} %get-tuple-element.53), channel_id=1, source_target_pairs={{0,1},{1,0},{2,3},{3,2},{4,8},{5,9},{6,10},{7,11},{8,4},{9,5},{10,... | collective-permute-start | bytes 417800 | tf_op jit(solution)/shard_map/ppermute | solution.py:449
  9.4 10.6 %collective-permute-start.7 = (bf16[400,256]{1,0:T(8,128)(2,1)}, bf16[400,256]{1,0:T(8,128)(2,1)S(1)}, u32[]{:S(2)}, u32[]{:S(2)}) collective-permute-start(bf16[400,256]{1,0:T(8,128)(2,1)} %get-tuple-element.64), channel_id=1, source_target_pairs={{0,3},{1,2},{2,1},{3,0},{4,7},{5,6},{6,5},{7,4},{8,11},{9,10},{10,... | collective-permute-start | bytes 614408 | tf_op jit(solution)/shard_map/ppermute | solution.py:453
  11.4 5.4 %collective-permute-start.2 = (bf16[272,256]{1,0:T(8,128)(2,1)}, bf16[272,256]{1,0:T(8,128)(2,1)S(1)}, u32[]{:S(2)}, u32[]{:S(2)}) collective-permute-start(bf16[272,256]{1,0:T(8,128)(2,1)} %get-tuple-element.52), channel_id=1, source_target_pairs={{0,5},{1,4},{2,7},{3,6},{4,1},{5,0},{6,3},{7,2},{8,13},{9,12},{10,... | collective-permute-start | bytes 417800 | tf_op jit(solution)/shard_map/ppermute | solution.py:454
  11.7 6.8 %collective-permute-start.4 = (bf16[272,256]{1,0:T(8,128)(2,1)}, bf16[272,256]{1,0:T(8,128)(2,1)S(1)}, u32[]{:S(2)}, u32[]{:S(2)}) collective-permute-start(bf16[272,256]{1,0:T(8,128)(2,1)} %get-tuple-element.54), channel_id=1, source_target_pairs={{0,1},{1,0},{2,3},{3,2},{4,9},{5,8},{6,11},{7,10},{8,5},{9,4},{10,... | collective-permute-start | bytes 417800 | tf_op jit(solution)/shard_map/ppermute | solution.py:455
  15.2 10.3 %copy-start.1 = (bf16[512,512]{1,0:T(8,128)(2,1)S(1)}, bf16[512,512]{1,0:T(8,128)(2,1)}, u32[]{:S(2)}) copy-start(bf16[512,512]{1,0:T(8,128)(2,1)} %refs_6_.1) | copy-start | bytes 1572868
  15.2 10.3 %copy-start.3 = (bf16[256,512]{1,0:T(8,128)(2,1)S(1)}, bf16[256,512]{1,0:T(8,128)(2,1)}, u32[]{:S(2)}) copy-start(bf16[256,512]{1,0:T(8,128)(2,1)} %refs_5_.1) | copy-start | bytes 786436
  15.2 10.3 %copy-start.4 = (f32[512]{0:T(512)S(1)}, f32[512]{0:T(512)}, u32[]{:S(2)}) copy-start(f32[512]{0:T(512)} %param.21) | copy-start | bytes 6148
  18.8 4.7 %collective-permute-start.5 = (bf16[256,256]{1,0:T(8,128)(2,1)S(1)}, bf16[256,256]{1,0:T(8,128)(2,1)S(1)}, u32[]{:S(2)}, u32[]{:S(2)}) collective-permute-start(bf16[256,256]{1,0:T(8,128)(2,1)S(1)} %get-tuple-element.62), channel_id=1, source_target_pairs={{0,2},{1,3},{2,0},{3,1},{4,6},{5,7},{6,4},{7,5},{8,10},{9,11},{10,... | collective-permute-start | bytes 393224 | tf_op jit(solution)/shard_map/ppermute | solution.py:488
  20.2 5.1 %collective-permute-start.8 = (bf16[256,256]{1,0:T(8,128)(2,1)S(1)}, bf16[256,256]{1,0:T(8,128)(2,1)S(1)}, u32[]{:S(2)}, u32[]{:S(2)}) collective-permute-start(bf16[256,256]{1,0:T(8,128)(2,1)S(1)} %get-tuple-element.67), channel_id=1, source_target_pairs={{0,4},{1,5},{2,6},{3,7},{4,0},{5,1},{6,2},{7,3},{8,12},{9,13},{10,... | collective-permute-start | bytes 393224 | tf_op jit(solution)/shard_map/ppermute | solution.py:490
  20.3 5.1 %collective-permute-start.9 = (bf16[256,256]{1,0:T(8,128)(2,1)S(1)}, bf16[256,256]{1,0:T(8,128)(2,1)S(1)}, u32[]{:S(2)}, u32[]{:S(2)}) collective-permute-start(bf16[256,256]{1,0:T(8,128)(2,1)S(1)} %get-tuple-element.68), channel_id=1, source_target_pairs={{0,1},{1,0},{2,3},{3,2},{4,8},{5,9},{6,10},{7,11},{8,4},{9,5},{10,... | collective-permute-start | bytes 393224 | tf_op jit(solution)/shard_map/ppermute | solution.py:491
  25.9 2.1 %collective-permute-start.11 = (bf16[256,512]{1,0:T(8,128)(2,1)S(1)}, bf16[256,512]{1,0:T(8,128)(2,1)S(1)}, u32[]{:S(2)}, u32[]{:S(2)}) collective-permute-start(bf16[256,512]{1,0:T(8,128)(2,1)S(1)} %get-tuple-element.70.own_ref), channel_id=1, source_target_pairs={{0,1},{1,0},{2,3},{3,2},{4,5},{5,4},{6,7},{7,6},{8,9},{9,8},{10,11... | collective-permute-start | bytes 786440 | tf_op jit(solution)/shard_map/ppermute | solution.py:513
  26.9 13.5 %collective-permute-start.10 = (bf16[256,512]{1,0:T(8,128)(2,1)S(1)}, bf16[256,512]{1,0:T(8,128)(2,1)S(1)}, u32[]{:S(2)}, u32[]{:S(2)}) collective-permute-start(bf16[256,512]{1,0:T(8,128)(2,1)S(1)} %get-tuple-element.70.own_ref), channel_id=1, source_target_pairs={{0,2},{1,3},{2,0},{3,1},{4,6},{5,7},{6,4},{7,5},{8,10},{9,11},{10,... | collective-permute-start | bytes 786440 | tf_op jit(solution)/shard_map/ppermute | solution.py:514
  28.0 8.5 %collective-permute-start.12 = (bf16[256,512]{1,0:T(8,128)(2,1)S(1)}, bf16[256,512]{1,0:T(8,128)(2,1)S(1)}, u32[]{:S(2)}, u32[]{:S(2)}) collective-permute-start(bf16[256,512]{1,0:T(8,128)(2,1)S(1)} %get-tuple-element.70.own_ref), channel_id=1, source_target_pairs={{0,1},{1,0},{2,4},{3,5},{4,2},{5,3},{6,8},{7,9},{8,6},{9,7},{10,12... | collective-permute-start | bytes 786440 | tf_op jit(solution)/shard_map/ppermute | solution.py:516
  36.5 6.5 %copy-start.6 = (bf16[2048,512]{1,0:T(8,128)(2,1)S(1)}, bf16[2048,512]{1,0:T(8,128)(2,1)}, u32[]{:S(2)}) copy-start(bf16[2048,512]{1,0:T(8,128)(2,1)} %down_ref.1) | copy-start | bytes 6291460
  38.1 4.9 %copy-start.5 = (bf16[512,2048]{1,0:T(8,128)(2,1)S(1)}, bf16[512,2048]{1,0:T(8,128)(2,1)}, u32[]{:S(2)}) copy-start(bf16[512,2048]{1,0:T(8,128)(2,1)} %up_ref.1) | copy-start | bytes 6291460
  38.1 4.9 %copy-start.7 = (bf16[512,512]{1,0:T(8,128)(2,1)S(1)}, bf16[512,512]{1,0:T(8,128)(2,1)}, u32[]{:S(2)}) copy-start(bf16[512,512]{1,0:T(8,128)(2,1)} %w_out_ref.1) | copy-start | bytes 1572868
  38.1 4.9 %copy-start.8 = (f32[512]{0:T(512)S(1)}, f32[512]{0:T(512)}, u32[]{:S(2)}) copy-start(f32[512]{0:T(512)} %param.25) | copy-start | bytes 6148
  40.4 2.6 %collective-permute-start.13 = (bf16[256,512]{1,0:T(8,128)(2,1)S(1)}, bf16[256,512]{1,0:T(8,128)(2,1)S(1)}, u32[]{:S(2)}, u32[]{:S(2)}) collective-permute-start(bf16[256,512]{1,0:T(8,128)(2,1)S(1)} %collective-permute-done.10.block_ref), channel_id=1, source_target_pairs={{0,1},{1,0},{2,3},{3,2},{4,5},{5,4},{6,7},{7,6},{8,9},{9,8},{10,11... | collective-permute-start | bytes 786440 | tf_op jit(solution)/shard_map/ppermute | solution.py:563
  41.2 1.8 %collective-permute-start.14 = (bf16[256,512]{1,0:T(8,128)(2,1)S(1)}, bf16[256,512]{1,0:T(8,128)(2,1)S(1)}, u32[]{:S(2)}, u32[]{:S(2)}) collective-permute-start(bf16[256,512]{1,0:T(8,128)(2,1)S(1)} %collective-permute-done.12.block_ref), channel_id=1, source_target_pairs={{0,1},{1,0},{2,3},{3,2},{4,5},{5,4},{6,7},{7,6},{8,9},{9,8},{10,11... | collective-permute-start | bytes 786440 | tf_op jit(solution)/shard_map/ppermute | solution.py:560
  (1 other events, 1.0 us)

commit v14 on v13

--- a/solution.py
+++ b/solution.py
@@ -484,7 +484,7 @@
             name=name,
         )(*arrays, early)
 
-    left, *parts = sums([even, even_other, odd, odd_other], early_left, 0, "left")
+    left, *parts = sums([even, odd_other, odd, even_other], early_left, 0, "left")
     parts = [lax.ppermute(part, NODES, chip_trade(p + 1)) for p, part in enumerate(parts)]
     to_even, to_odd, right = sums(cross, early_right, 2, "right")
     from_even = lax.ppermute(to_even, NODES, bands_trade(0))

time: 48.5 us -> 49.4 us (1.019)
  starting transfers between devices: 12.8 us -> 15.7 us
  waiting for transfers between devices: 12.5 us -> 9.95 us
    ppermute x1, waiting for transfers between devices: 2.77 us -> 0.05 us  [local(): lax.ppermute(part, NODES, chip_trade(p + 1))]
    ppermute x1, starting transfers between devices: 2.36 us -> 0.01 us  [local(): odd_other = lax.ppermute(odd_other, NODES, bands_trade(1, 1))]
    ppermute x1, starting transfers between devices: 0.01 us -> 1.23 us  [local(): even_other = lax.ppermute(even_other, NODES, bands_trade(0, 1))]
    ppermute x1, waiting for transfers between devices: 0.08 us -> 1.3 us  [local(): from_odd = lax.ppermute(to_odd, NODES, bands_trade(1))]
    ppermute x1, starting transfers between devices: 0.49 us -> 1.66 us  [local(): from_odd = lax.ppermute(to_odd, NODES, bands_trade(1))]
    ppermute x1, starting transfers between devices: 0.92 us -> 2.01 us  [local(): side = lax.ppermute(normed, NODES, beside)]
    ppermute x1, waiting for transfers between devices: 2.75 us -> 1.67 us  [local(): odd = lax.ppermute(normed, NODES, chips_trade(1))]
    ppermute x1, starting transfers between devices: 0.07 us -> 1 us  [local(): from_even = lax.ppermute(to_even, NODES, bands_trade(0))]
  transfers between devices with their start and end apart: 15 -> 15, of which waited for: 9 -> 8; matrix products, arithmetic and copies ran while one was open for 1% -> 1% of each run, Pallas kernels for 21% -> 21%
where the time goes in v14:
time: 49.4 us; the launch traced here: 48.6 us
  Pallas kernels  21.4 us (43%)
  starting transfers between devices  15.7 us (32%)
  waiting for transfers between devices  9.95 us (20%)
  local copies, waits for them, and re-layouts  1.02 us (2%)
    pallas_call x1, Pallas kernels, local(): pl.pallas_call(functools.partial(message_kernel, pairs), out_shape=outgoi...  5.53 us
    pallas_call x1, Pallas kernels, local(): pl.pallas_call(near_kernel, out_shape=[jax.ShapeDtypeStruct((HEADS, LANES...  5.01 us
    pallas_call x1, Pallas kernels, local(): pl.pallas_call(far_kernel, out_shape=jax.ShapeDtypeStruct((nodes, width),...  4.94 us
    pallas_call x2, Pallas kernels, outer(): pl.pallas_call(functools.partial(outer_kernel, by_pair), out_shape=[jax.S...  3.36 us
    ppermute x1, starting transfers between devices, local(): odd = lax.ppermute(odd, NODES, bands_trade(1))  2.43 us
    ppermute x1, waiting for transfers between devices, local(): even = lax.ppermute(normed, NODES, chips_trade(0))  2.24 us
    ppermute x1, starting transfers between devices, local(): lax.ppermute(c, NODES, chip_trade(p + 1, 1))  2.06 us
    ppermute x1, starting transfers between devices, local(): side = lax.ppermute(normed, NODES, beside)  2.01 us
  transfers between devices with their start and end apart: 15, of which 8 were waited for; matrix products, arithmetic and copies ran while one was open for 1% of the time, Pallas kernels for 21%

profile of v14, /device:TPU:15, one launch (start us, length us, event | category | flops | bytes accessed | tf_op | source)
XLA Modules:
  0.0 48.6 jit_solution(17468911501924112200)
XLA Ops:
  0.0 5.5 %messages.1 = (bf16[272,256]{1,0:T(8,128)(2,1)}, bf16[272,256]{1,0:T(8,128)(2,1)}, bf16[272,256]{1,0:T(8,128)(2,1)}, bf16[272,256]{1,0:T(8,128)(2,1)}, bf16[400,...) custom-call(bf16[1024,512]{1,0:T(8,128)(2,1)} %grid_ref.1, ...), custom_call_target="tpu_custom_call" | custom-call | flops 2147483648 | bytes 4194304 | tf_op jit(solution)/shard_map/messages/pallas_call | solution.py:411
  5.5 0.7 %collective-permute-start.1 = (bf16[672,256]{1,0:T(8,128)(2,1)}, bf16[672,256]{1,0:T(8,128)(2,1)S(1)}, u32[]{:S(2)}, u32[]{:S(2)}) collective-permute-start(bf16[672,256]{1,0:T(8,128)(2,1)} %get-tuple-element.48), channel_id=1, source_target_pairs={{0,1},{1,0},{2,3},{3,2},{4,5},{5,4},{6,7},{7,6},{8,9},{9,8},{10,11... | collective-permute-start | bytes 1032200 | tf_op jit(solution)/shard_map/ppermute | solution.py:446
  6.7 2.4 %collective-permute-start.3 = (bf16[272,256]{1,0:T(8,128)(2,1)}, bf16[272,256]{1,0:T(8,128)(2,1)S(1)}, u32[]{:S(2)}, u32[]{:S(2)}) collective-permute-start(bf16[272,256]{1,0:T(8,128)(2,1)} %get-tuple-element.53), channel_id=1, source_target_pairs={{0,1},{1,0},{2,3},{3,2},{4,8},{5,9},{6,10},{7,11},{8,4},{9,5},{10,... | collective-permute-start | bytes 417800 | tf_op jit(solution)/shard_map/ppermute | solution.py:449
  9.4 2.1 %collective-permute-start.7 = (bf16[400,256]{1,0:T(8,128)(2,1)}, bf16[400,256]{1,0:T(8,128)(2,1)S(1)}, u32[]{:S(2)}, u32[]{:S(2)}) collective-permute-start(bf16[400,256]{1,0:T(8,128)(2,1)} %get-tuple-element.64), channel_id=1, source_target_pairs={{0,3},{1,2},{2,1},{3,0},{4,7},{5,6},{6,5},{7,4},{8,11},{9,10},{10,... | collective-permute-start | bytes 614408 | tf_op jit(solution)/shard_map/ppermute | solution.py:453
  11.7 1.2 %collective-permute-start.4 = (bf16[272,256]{1,0:T(8,128)(2,1)}, bf16[272,256]{1,0:T(8,128)(2,1)S(1)}, u32[]{:S(2)}, u32[]{:S(2)}) collective-permute-start(bf16[272,256]{1,0:T(8,128)(2,1)} %get-tuple-element.54), channel_id=1, source_target_pairs={{0,5},{1,4},{2,7},{3,6},{4,1},{5,0},{6,3},{7,2},{8,13},{9,12},{10,... | collective-permute-start | bytes 417800 | tf_op jit(solution)/shard_map/ppermute | solution.py:454
  13.1 1.0 %copy-done.2 = bf16[672,256]{1,0:T(8,128)(2,1)S(1)} copy-done((bf16[672,256]{1,0:T(8,128)(2,1)S(1)}, bf16[672,256]{1,0:T(8,128)(2,1)}, u32[]{:S(2)}) %copy-start.2) | copy-done | bytes 344088
  14.0 1.5 %early.1 = (bf16[512,512]{1,0:T(8,128)(2,1)S(1)}, bf16[512,512]{1,0:T(8,128)(2,1)S(1)}, bf16[512,512]{1,0:T(8,128)(2,1)S(1)}, f32[2,256,256]{2,1,0:T(8,128)S(1)}, f32[3,256,256]{2,1,0:T(8,128)S(1)}) custom-call(bf16[512,1536]{1,0:T(8,128)(2,1)S(1)} %copy-done, bf16[672,256]{1,0:T(8,128)(2,1)S(1)} %copy-done.2, ...), custom_call_target="tpu_custom_call" | custom-call | flops 268435456 | bytes 4194304 | tf_op jit(solution)/shard_map/early/pallas_call | solution.py:465
  15.5 1.3 %collective-permute-done.2.refs_1_ = bf16[272,256]{1,0:T(8,128)(2,1)S(1)} collective-permute-done((bf16[272,256]{1,0:T(8,128)(2,1)}, bf16[272,256]{1,0:T(8,128)(2,1)S(1)}, u32[]{:S(2)}, u32[]{:S(2)}) %collective-permute-start.2) | collective-permute-done | bytes 139296 | tf_op jit(solution)/shard_map/ppermute | solution.py:455
  16.8 0.9 %collective-permute-done.4.refs_3_ = bf16[272,256]{1,0:T(8,128)(2,1)S(1)} collective-permute-done((bf16[272,256]{1,0:T(8,128)(2,1)}, bf16[272,256]{1,0:T(8,128)(2,1)S(1)}, u32[]{:S(2)}, u32[]{:S(2)}) %collective-permute-start.4) | collective-permute-done | bytes 139296 | tf_op jit(solution)/shard_map/ppermute | solution.py:454
  18.1 1.3 %collective-permute-start.5 = (bf16[256,256]{1,0:T(8,128)(2,1)S(1)}, bf16[256,256]{1,0:T(8,128)(2,1)S(1)}, u32[]{:S(2)}, u32[]{:S(2)}) collective-permute-start(bf16[256,256]{1,0:T(8,128)(2,1)S(1)} %get-tuple-element.62), channel_id=1, source_target_pairs={{0,2},{1,3},{2,0},{3,1},{4,6},{5,7},{6,4},{7,5},{8,10},{9,11},{10,... | collective-permute-start | bytes 393224 | tf_op jit(solution)/shard_map/ppermute | solution.py:488
  19.6 1.0 %collective-permute-start.8 = (bf16[256,256]{1,0:T(8,128)(2,1)S(1)}, bf16[256,256]{1,0:T(8,128)(2,1)S(1)}, u32[]{:S(2)}, u32[]{:S(2)}) collective-permute-start(bf16[256,256]{1,0:T(8,128)(2,1)S(1)} %get-tuple-element.67), channel_id=1, source_target_pairs={{0,4},{1,5},{2,6},{3,7},{4,0},{5,1},{6,2},{7,3},{8,12},{9,13},{10,... | collective-permute-start | bytes 393224 | tf_op jit(solution)/shard_map/ppermute | solution.py:490
  20.6 1.7 %collective-permute-start.9 = (bf16[256,256]{1,0:T(8,128)(2,1)S(1)}, bf16[256,256]{1,0:T(8,128)(2,1)S(1)}, u32[]{:S(2)}, u32[]{:S(2)}) collective-permute-start(bf16[256,256]{1,0:T(8,128)(2,1)S(1)} %get-tuple-element.68), channel_id=1, source_target_pairs={{0,1},{1,0},{2,3},{3,2},{4,8},{5,9},{6,10},{7,11},{8,4},{9,5},{10,... | collective-permute-start | bytes 393224 | tf_op jit(solution)/shard_map/ppermute | solution.py:491
  22.3 1.3 %collective-permute-done.8.refs_3_ = bf16[256,256]{1,0:T(8,128)(2,1)S(1)} collective-permute-done((bf16[256,256]{1,0:T(8,128)(2,1)S(1)}, bf16[256,256]{1,0:T(8,128)(2,1)S(1)}, u32[]{:S(2)}, u32[]{:S(2)}) %collective-permute-start.8) | collective-permute-done | bytes 131104 | tf_op jit(solution)/shard_map/ppermute | solution.py:490
  23.6 1.3 %collective-permute-done.9.refs_4_ = bf16[256,256]{1,0:T(8,128)(2,1)S(1)} collective-permute-done((bf16[256,256]{1,0:T(8,128)(2,1)S(1)}, bf16[256,256]{1,0:T(8,128)(2,1)S(1)}, u32[]{:S(2)}, u32[]{:S(2)}) %collective-permute-start.9) | collective-permute-done | bytes 131104 | tf_op jit(solution)/shard_map/ppermute | solution.py:491
  25.4 2.0 %collective-permute-start.11 = (bf16[256,512]{1,0:T(8,128)(2,1)S(1)}, bf16[256,512]{1,0:T(8,128)(2,1)S(1)}, u32[]{:S(2)}, u32[]{:S(2)}) collective-permute-start(bf16[256,512]{1,0:T(8,128)(2,1)S(1)} %get-tuple-element.70.own_ref), channel_id=1, source_target_pairs={{0,1},{1,0},{2,3},{3,2},{4,5},{5,4},{6,7},{7,6},{8,9},{9,8},{10,11... | collective-permute-start | bytes 786440 | tf_op jit(solution)/shard_map/ppermute | solution.py:513
  27.7 0.9 %collective-permute-done.11.side_ref = bf16[256,512]{1,0:T(8,128)(2,1)S(1)} collective-permute-done((bf16[256,512]{1,0:T(8,128)(2,1)S(1)}, bf16[256,512]{1,0:T(8,128)(2,1)S(1)}, u32[]{:S(2)}, u32[]{:S(2)}) %collective-permute-start.11) | collective-permute-done | bytes 262176 | tf_op jit(solution)/shard_map/ppermute | solution.py:513
  28.6 1.8 %collective-permute-start.12 = (bf16[256,512]{1,0:T(8,128)(2,1)S(1)}, bf16[256,512]{1,0:T(8,128)(2,1)S(1)}, u32[]{:S(2)}, u32[]{:S(2)}) collective-permute-start(bf16[256,512]{1,0:T(8,128)(2,1)S(1)} %get-tuple-element.70.own_ref), channel_id=1, source_target_pairs={{0,1},{1,0},{2,4},{3,5},{4,2},{5,3},{6,8},{7,9},{8,6},{9,7},{10,12... | collective-permute-start | bytes 786440 | tf_op jit(solution)/shard_map/ppermute | solution.py:516
  30.4 5.0 %near.1 = (bf16[16,128,256]{2,1,0:T(8,128)(2,1)S(1)}, f32[16,48,256]{2,1,0:T(8,128)S(1)}, f32[16,8,256]{2,1,0:T(8,128)S(1)}) custom-call(bf16[256,512]{1,0:T(8,128)(2,1)S(1)} %get-tuple-element.70.own_ref, bf16[256,512]{1,0:T(8,128)(2,1)S(1)} %collective-permute-done.11.side_ref, bf16[512,512]{1,0:T(8,128)(2,1)S(1)} %get-tuple-element.72.wq_ref, ...), custom_call_target="tpu_custom_call" | custom-call | flops 8589934592 | bytes 4194304 | tf_op jit(solution)/shard_map/near/pallas_call | solution.py:519
  35.4 1.7 %collective-permute-done.12.block_ref = bf16[256,512]{1,0:T(8,128)(2,1)S(1)} collective-permute-done((bf16[256,512]{1,0:T(8,128)(2,1)S(1)}, bf16[256,512]{1,0:T(8,128)(2,1)S(1)}, u32[]{:S(2)}, u32[]{:S(2)}) %collective-permute-start.12) | collective-permute-done | bytes 262176 | tf_op jit(solution)/shard_map/ppermute | solution.py:516
  37.1 1.6 %other.1 = (f32[16,48,256]{2,1,0:T(8,128)S(1)}, f32[16,8,256]{2,1,0:T(8,128)S(1)}) custom-call(bf16[256,512]{1,0:T(8,128)(2,1)S(1)} %collective-permute-done.12.block_ref, bf16[512,512]{1,0:T(8,128)(2,1)S(1)} %get-tuple-element.73.wk_ref, bf16[512,512]{1,0:T(8,128)(2,1)S(1)} %get-tuple-element.74.wv_ref, s32[2,16]{1,0:T(2,128)S(1)} %select_reduce_fusion.plan_ref.plan_in, ...), custom_call_target="tpu_custom_call" | custom-call | flops 536870912 | bytes 3145728 | tf_op jit(solution)/shard_map/other/pallas_call | solution.py:539
  38.7 2.2 %collective-permute-done.10.block_ref = bf16[256,512]{1,0:T(8,128)(2,1)S(1)} collective-permute-done((bf16[256,512]{1,0:T(8,128)(2,1)S(1)}, bf16[256,512]{1,0:T(8,128)(2,1)S(1)}, u32[]{:S(2)}, u32[]{:S(2)}) %collective-permute-start.10) | collective-permute-done | bytes 262176 | tf_op jit(solution)/shard_map/ppermute | solution.py:514
  41.0 0.8 %collective-permute-start.13 = (bf16[256,512]{1,0:T(8,128)(2,1)S(1)}, bf16[256,512]{1,0:T(8,128)(2,1)S(1)}, u32[]{:S(2)}, u32[]{:S(2)}) collective-permute-start(bf16[256,512]{1,0:T(8,128)(2,1)S(1)} %collective-permute-done.10.block_ref), channel_id=1, source_target_pairs={{0,1},{1,0},{2,3},{3,2},{4,5},{5,4},{6,7},{7,6},{8,9},{9,8},{10,11... | collective-permute-start | bytes 786440 | tf_op jit(solution)/shard_map/ppermute | solution.py:563
  41.8 1.8 %pair.1 = (f32[16,48,256]{2,1,0:T(8,128)S(1)}, f32[16,8,256]{2,1,0:T(8,128)S(1)}) custom-call(bf16[256,512]{1,0:T(8,128)(2,1)S(1)} %collective-permute-done.10.block_ref, bf16[512,512]{1,0:T(8,128)(2,1)S(1)} %get-tuple-element.73.wk_ref, bf16[512,512]{1,0:T(8,128)(2,1)S(1)} %get-tuple-element.74.wv_ref, s32[2,16]{1,0:T(2,128)S(1)} %select_reduce_fusion.plan_ref.plan_in, ...), custom_call_target="tpu_custom_call" | custom-call | flops 536870912 | bytes 3145728 | tf_op jit(solution)/shard_map/pair/pallas_call | solution.py:539
  43.6 4.9 %far.1 = bf16[256,512]{1,0:T(8,128)(2,1)} custom-call(bf16[256,512]{1,0:T(8,128)(2,1)S(1)} %collective-permute-done.13.first_ref, bf16[256,512]{1,0:T(8,128)(2,1)S(1)} %collective-permute-done.14.second_ref, bf16[512,512]{1,0:T(8,128)(2,1)S(1)} %get-tuple-element.73.wk_ref, bf16[512,512]{1,0:T(8,128)(2,1)S(1)} %get-tuple-element.74.wv_ref, ...), custom_call_target="tpu_custom_call" | custom-call | flops 8589934592 | bytes 8388608 | tf_op jit(solution)/shard_map/far/pallas_call | solution.py:566
  (40 shorter events, 2.5 us)
Async XLA Ops:
  0.0 9.2 %copy-start.9 = (s32[16]{0:T(128)S(1)}, s32[16]{0:T(128)}, u32[]{:S(2)}) copy-start(s32[16]{0:T(128)} %param.23) | copy-start | bytes 196
  0.0 13.0 %copy-start = (bf16[512,1536]{1,0:T(8,128)(2,1)S(1)}, bf16[512,1536]{1,0:T(8,128)(2,1)}, u32[]{:S(2)}) copy-start(bf16[512,1536]{1,0:T(8,128)(2,1)} %w_ref.2) | copy-start | bytes 4718596
  5.5 3.8 %collective-permute-start.1 = (bf16[672,256]{1,0:T(8,128)(2,1)}, bf16[672,256]{1,0:T(8,128)(2,1)S(1)}, u32[]{:S(2)}, u32[]{:S(2)}) collective-permute-start(bf16[672,256]{1,0:T(8,128)(2,1)} %get-tuple-element.48), channel_id=1, source_target_pairs={{0,1},{1,0},{2,3},{3,2},{4,5},{5,4},{6,7},{7,6},{8,9},{9,8},{10,11... | collective-permute-start | bytes 1032200 | tf_op jit(solution)/shard_map/ppermute | solution.py:446
  6.3 13.1 %collective-permute-start.6 = (bf16[400,256]{1,0:T(8,128)(2,1)}, bf16[400,256]{1,0:T(8,128)(2,1)S(1)}, u32[]{:S(2)}, u32[]{:S(2)}) collective-permute-start(bf16[400,256]{1,0:T(8,128)(2,1)} %get-tuple-element.63), channel_id=1, source_target_pairs={{0,2},{1,3},{2,0},{3,1},{4,6},{5,7},{6,4},{7,5},{8,10},{9,11},{10,... | collective-permute-start | bytes 614408 | tf_op jit(solution)/shard_map/ppermute | solution.py:447
  6.6 5.1 %collective-permute-start = (bf16[272,256]{1,0:T(8,128)(2,1)}, bf16[272,256]{1,0:T(8,128)(2,1)S(1)}, u32[]{:S(2)}, u32[]{:S(2)}) collective-permute-start(bf16[272,256]{1,0:T(8,128)(2,1)} %get-tuple-element.47), channel_id=1, source_target_pairs={{0,4},{1,5},{2,6},{3,7},{4,0},{5,1},{6,2},{7,3},{8,12},{9,13},{10,... | collective-permute-start | bytes 417800 | tf_op jit(solution)/shard_map/ppermute | solution.py:448
  6.7 8.8 %collective-permute-start.3 = (bf16[272,256]{1,0:T(8,128)(2,1)}, bf16[272,256]{1,0:T(8,128)(2,1)S(1)}, u32[]{:S(2)}, u32[]{:S(2)}) collective-permute-start(bf16[272,256]{1,0:T(8,128)(2,1)} %get-tuple-element.53), channel_id=1, source_target_pairs={{0,1},{1,0},{2,3},{3,2},{4,8},{5,9},{6,10},{7,11},{8,4},{9,5},{10,... | collective-permute-start | bytes 417800 | tf_op jit(solution)/shard_map/ppermute | solution.py:449
  9.4 10.0 %collective-permute-start.7 = (bf16[400,256]{1,0:T(8,128)(2,1)}, bf16[400,256]{1,0:T(8,128)(2,1)S(1)}, u32[]{:S(2)}, u32[]{:S(2)}) collective-permute-start(bf16[400,256]{1,0:T(8,128)(2,1)} %get-tuple-element.64), channel_id=1, source_target_pairs={{0,3},{1,2},{2,1},{3,0},{4,7},{5,6},{6,5},{7,4},{8,11},{9,10},{10,... | collective-permute-start | bytes 614408 | tf_op jit(solution)/shard_map/ppermute | solution.py:453
  11.4 5.4 %collective-permute-start.2 = (bf16[272,256]{1,0:T(8,128)(2,1)}, bf16[272,256]{1,0:T(8,128)(2,1)S(1)}, u32[]{:S(2)}, u32[]{:S(2)}) collective-permute-start(bf16[272,256]{1,0:T(8,128)(2,1)} %get-tuple-element.52), channel_id=1, source_target_pairs={{0,1},{1,0},{2,3},{3,2},{4,9},{5,8},{6,11},{7,10},{8,5},{9,4},{10,... | collective-permute-start | bytes 417800 | tf_op jit(solution)/shard_map/ppermute | solution.py:455
  11.7 6.1 %collective-permute-start.4 = (bf16[272,256]{1,0:T(8,128)(2,1)}, bf16[272,256]{1,0:T(8,128)(2,1)S(1)}, u32[]{:S(2)}, u32[]{:S(2)}) collective-permute-start(bf16[272,256]{1,0:T(8,128)(2,1)} %get-tuple-element.54), channel_id=1, source_target_pairs={{0,5},{1,4},{2,7},{3,6},{4,1},{5,0},{6,3},{7,2},{8,13},{9,12},{10,... | collective-permute-start | bytes 417800 | tf_op jit(solution)/shard_map/ppermute | solution.py:454
  14.0 10.9 %copy-start.1 = (bf16[512,512]{1,0:T(8,128)(2,1)S(1)}, bf16[512,512]{1,0:T(8,128)(2,1)}, u32[]{:S(2)}) copy-start(bf16[512,512]{1,0:T(8,128)(2,1)} %refs_6_.1) | copy-start | bytes 1572868
  14.0 10.9 %copy-start.3 = (bf16[256,512]{1,0:T(8,128)(2,1)S(1)}, bf16[256,512]{1,0:T(8,128)(2,1)}, u32[]{:S(2)}) copy-start(bf16[256,512]{1,0:T(8,128)(2,1)} %refs_5_.1) | copy-start | bytes 786436
  14.0 10.9 %copy-start.4 = (f32[512]{0:T(512)S(1)}, f32[512]{0:T(512)}, u32[]{:S(2)}) copy-start(f32[512]{0:T(512)} %param.21) | copy-start | bytes 6148
  18.1 4.3 %collective-permute-start.5 = (bf16[256,256]{1,0:T(8,128)(2,1)S(1)}, bf16[256,256]{1,0:T(8,128)(2,1)S(1)}, u32[]{:S(2)}, u32[]{:S(2)}) collective-permute-start(bf16[256,256]{1,0:T(8,128)(2,1)S(1)} %get-tuple-element.62), channel_id=1, source_target_pairs={{0,2},{1,3},{2,0},{3,1},{4,6},{5,7},{6,4},{7,5},{8,10},{9,11},{10,... | collective-permute-start | bytes 393224 | tf_op jit(solution)/shard_map/ppermute | solution.py:488
  19.6 4.0 %collective-permute-start.8 = (bf16[256,256]{1,0:T(8,128)(2,1)S(1)}, bf16[256,256]{1,0:T(8,128)(2,1)S(1)}, u32[]{:S(2)}, u32[]{:S(2)}) collective-permute-start(bf16[256,256]{1,0:T(8,128)(2,1)S(1)} %get-tuple-element.67), channel_id=1, source_target_pairs={{0,4},{1,5},{2,6},{3,7},{4,0},{5,1},{6,2},{7,3},{8,12},{9,13},{10,... | collective-permute-start | bytes 393224 | tf_op jit(solution)/shard_map/ppermute | solution.py:490
  20.6 4.3 %collective-permute-start.9 = (bf16[256,256]{1,0:T(8,128)(2,1)S(1)}, bf16[256,256]{1,0:T(8,128)(2,1)S(1)}, u32[]{:S(2)}, u32[]{:S(2)}) collective-permute-start(bf16[256,256]{1,0:T(8,128)(2,1)S(1)} %get-tuple-element.68), channel_id=1, source_target_pairs={{0,1},{1,0},{2,3},{3,2},{4,8},{5,9},{6,10},{7,11},{8,4},{9,5},{10,... | collective-permute-start | bytes 393224 | tf_op jit(solution)/shard_map/ppermute | solution.py:491
  25.4 3.2 %collective-permute-start.11 = (bf16[256,512]{1,0:T(8,128)(2,1)S(1)}, bf16[256,512]{1,0:T(8,128)(2,1)S(1)}, u32[]{:S(2)}, u32[]{:S(2)}) collective-permute-start(bf16[256,512]{1,0:T(8,128)(2,1)S(1)} %get-tuple-element.70.own_ref), channel_id=1, source_target_pairs={{0,1},{1,0},{2,3},{3,2},{4,5},{5,4},{6,7},{7,6},{8,9},{9,8},{10,11... | collective-permute-start | bytes 786440 | tf_op jit(solution)/shard_map/ppermute | solution.py:513
  27.4 13.5 %collective-permute-start.10 = (bf16[256,512]{1,0:T(8,128)(2,1)S(1)}, bf16[256,512]{1,0:T(8,128)(2,1)S(1)}, u32[]{:S(2)}, u32[]{:S(2)}) collective-permute-start(bf16[256,512]{1,0:T(8,128)(2,1)S(1)} %get-tuple-element.70.own_ref), channel_id=1, source_target_pairs={{0,2},{1,3},{2,0},{3,1},{4,6},{5,7},{6,4},{7,5},{8,10},{9,11},{10,... | collective-permute-start | bytes 786440 | tf_op jit(solution)/shard_map/ppermute | solution.py:514
  28.6 8.5 %collective-permute-start.12 = (bf16[256,512]{1,0:T(8,128)(2,1)S(1)}, bf16[256,512]{1,0:T(8,128)(2,1)S(1)}, u32[]{:S(2)}, u32[]{:S(2)}) collective-permute-start(bf16[256,512]{1,0:T(8,128)(2,1)S(1)} %get-tuple-element.70.own_ref), channel_id=1, source_target_pairs={{0,1},{1,0},{2,4},{3,5},{4,2},{5,3},{6,8},{7,9},{8,6},{9,7},{10,12... | collective-permute-start | bytes 786440 | tf_op jit(solution)/shard_map/ppermute | solution.py:516
  37.1 6.5 %copy-start.6 = (bf16[2048,512]{1,0:T(8,128)(2,1)S(1)}, bf16[2048,512]{1,0:T(8,128)(2,1)}, u32[]{:S(2)}) copy-start(bf16[2048,512]{1,0:T(8,128)(2,1)} %down_ref.1) | copy-start | bytes 6291460
  38.7 4.9 %copy-start.5 = (bf16[512,2048]{1,0:T(8,128)(2,1)S(1)}, bf16[512,2048]{1,0:T(8,128)(2,1)}, u32[]{:S(2)}) copy-start(bf16[512,2048]{1,0:T(8,128)(2,1)} %up_ref.1) | copy-start | bytes 6291460
  38.7 4.9 %copy-start.7 = (bf16[512,512]{1,0:T(8,128)(2,1)S(1)}, bf16[512,512]{1,0:T(8,128)(2,1)}, u32[]{:S(2)}) copy-start(bf16[512,512]{1,0:T(8,128)(2,1)} %w_out_ref.1) | copy-start | bytes 1572868
  38.7 4.9 %copy-start.8 = (f32[512]{0:T(512)S(1)}, f32[512]{0:T(512)}, u32[]{:S(2)}) copy-start(f32[512]{0:T(512)} %param.25) | copy-start | bytes 6148
  41.0 2.6 %collective-permute-start.13 = (bf16[256,512]{1,0:T(8,128)(2,1)S(1)}, bf16[256,512]{1,0:T(8,128)(2,1)S(1)}, u32[]{:S(2)}, u32[]{:S(2)}) collective-permute-start(bf16[256,512]{1,0:T(8,128)(2,1)S(1)} %collective-permute-done.10.block_ref), channel_id=1, source_target_pairs={{0,1},{1,0},{2,3},{3,2},{4,5},{5,4},{6,7},{7,6},{8,9},{9,8},{10,11... | collective-permute-start | bytes 786440 | tf_op jit(solution)/shard_map/ppermute | solution.py:563
  41.8 1.8 %collective-permute-start.14 = (bf16[256,512]{1,0:T(8,128)(2,1)S(1)}, bf16[256,512]{1,0:T(8,128)(2,1)S(1)}, u32[]{:S(2)}, u32[]{:S(2)}) collective-permute-start(bf16[256,512]{1,0:T(8,128)(2,1)S(1)} %collective-permute-done.12.block_ref), channel_id=1, source_target_pairs={{0,1},{1,0},{2,3},{3,2},{4,5},{5,4},{6,7},{7,6},{8,9},{9,8},{10,11... | collective-permute-start | bytes 786440 | tf_op jit(solution)/shard_map/ppermute | solution.py:560
  (1 other events, 1.0 us)

commit v15 on v13

--- a/solution.py
+++ b/solution.py
@@ -351,8 +351,8 @@
     by_even = odd == lax.rem(inner // 2 + 1, 2)
     project_keys(jnp.where(by_even, first_ref[...], second_ref[...]), wk_ref, wv_ref, key_ref, value_ref, 0)
     gap_ref[...] = gaps(2 * odd - 1, 0, nodes, nodes)
-    for i in range(HEADS // GROUP):
-        heads = range(GROUP * i, GROUP * (i + 1))
+    for i in range(HEADS // (2 * GROUP)):
+        heads = range(2 * GROUP * i, 2 * GROUP * (i + 1))
         keys, values = [key_ref[h // per_group] for h in heads], [value_ref[h] for h in heads]
         for h, sums, _ in extend(
             heads, keys, values, gap_ref, query_ref, sums_ref, top_ref, scale
@@ -365,7 +365,7 @@
     )
     total = state_ref[...] + mixed
     normed = layer_norm(total, gain_ref[...]).astype(jnp.bfloat16)
-    chunk = math.gcd(up_ref.shape[1], 512)
+    chunk = math.gcd(up_ref.shape[1], 1024)
     for start in range(0, up_ref.shape[1], chunk):
         hidden = silu(dot(normed, up_ref[:, start : start + chunk])).astype(jnp.bfloat16)
         total = total + dot(hidden, down_ref[start : start + chunk, :])

time: 48.5 us -> 48 us (0.990)
    pallas_call x2, Pallas kernels: 3.36 us -> 4.12 us  [outer(): pl.pallas_call(functools.partial(outer_kernel, by_pair), out_shape=[jax.S...]
    pallas_call x1, Pallas kernels: 4.94 us -> 4.42 us  [local(): pl.pallas_call(far_kernel, out_shape=jax.ShapeDtypeStruct((nodes, width),...]
  transfers between devices with their start and end apart: 15 -> 15, of which waited for: 9 -> 9; matrix products, arithmetic and copies ran while one was open for 1% -> 1% of each run, Pallas kernels for 21% -> 23%
where the time goes in v15:
time: 48 us; the launch traced here: 47.9 us
  Pallas kernels  21.5 us (45%)
  starting transfers between devices  12.8 us (27%)
  waiting for transfers between devices  12.1 us (25%)
  local copies, waits for them, and re-layouts  1.02 us (2%)
    pallas_call x1, Pallas kernels, local(): pl.pallas_call(functools.partial(message_kernel, pairs), out_shape=outgoi...  5.53 us
    pallas_call x1, Pallas kernels, local(): pl.pallas_call(near_kernel, out_shape=[jax.ShapeDtypeStruct((HEADS, LANES...  4.85 us
    pallas_call x1, Pallas kernels, local(): pl.pallas_call(far_kernel, out_shape=jax.ShapeDtypeStruct((nodes, width),...  4.42 us
    pallas_call x2, Pallas kernels, outer(): pl.pallas_call(functools.partial(outer_kernel, by_pair), out_shape=[jax.S...  4.12 us
    ppermute x1, waiting for transfers between devices, local(): lax.ppermute(part, NODES, chip_trade(p + 1))  2.77 us
    ppermute x1, waiting for transfers between devices, local(): odd = lax.ppermute(normed, NODES, chips_trade(1))  2.75 us
    ppermute x1, starting transfers between devices, local(): odd = lax.ppermute(odd, NODES, bands_trade(1))  2.43 us
    ppermute x1, starting transfers between devices, local(): odd_other = lax.ppermute(odd_other, NODES, bands_trade(1, 1))  2.36 us
  transfers between devices with their start and end apart: 15, of which 9 were waited for; matrix products, arithmetic and copies ran while one was open for 1% of the time, Pallas kernels for 23%

profile of v15, /device:TPU:15, one launch (start us, length us, event | category | flops | bytes accessed | tf_op | source)
XLA Modules:
  0.0 47.9 jit_solution(9557330596370619889)
XLA Ops:
  0.0 5.5 %messages.1 = (bf16[272,256]{1,0:T(8,128)(2,1)}, bf16[272,256]{1,0:T(8,128)(2,1)}, bf16[272,256]{1,0:T(8,128)(2,1)}, bf16[272,256]{1,0:T(8,128)(2,1)}, bf16[400,...) custom-call(bf16[1024,512]{1,0:T(8,128)(2,1)} %grid_ref.1, ...), custom_call_target="tpu_custom_call" | custom-call | flops 2147483648 | bytes 4194304 | tf_op jit(solution)/shard_map/messages/pallas_call | solution.py:411
  5.5 0.7 %collective-permute-start.1 = (bf16[672,256]{1,0:T(8,128)(2,1)}, bf16[672,256]{1,0:T(8,128)(2,1)S(1)}, u32[]{:S(2)}, u32[]{:S(2)}) collective-permute-start(bf16[672,256]{1,0:T(8,128)(2,1)} %get-tuple-element.48), channel_id=1, source_target_pairs={{0,1},{1,0},{2,3},{3,2},{4,5},{5,4},{6,7},{7,6},{8,9},{9,8},{10,11... | collective-permute-start | bytes 1032200 | tf_op jit(solution)/shard_map/ppermute | solution.py:446
  6.7 2.4 %collective-permute-start.3 = (bf16[272,256]{1,0:T(8,128)(2,1)}, bf16[272,256]{1,0:T(8,128)(2,1)S(1)}, u32[]{:S(2)}, u32[]{:S(2)}) collective-permute-start(bf16[272,256]{1,0:T(8,128)(2,1)} %get-tuple-element.53), channel_id=1, source_target_pairs={{0,1},{1,0},{2,3},{3,2},{4,8},{5,9},{6,10},{7,11},{8,4},{9,5},{10,... | collective-permute-start | bytes 417800 | tf_op jit(solution)/shard_map/ppermute | solution.py:449
  9.4 2.1 %collective-permute-start.7 = (bf16[400,256]{1,0:T(8,128)(2,1)}, bf16[400,256]{1,0:T(8,128)(2,1)S(1)}, u32[]{:S(2)}, u32[]{:S(2)}) collective-permute-start(bf16[400,256]{1,0:T(8,128)(2,1)} %get-tuple-element.64), channel_id=1, source_target_pairs={{0,3},{1,2},{2,1},{3,0},{4,7},{5,6},{6,5},{7,4},{8,11},{9,10},{10,... | collective-permute-start | bytes 614408 | tf_op jit(solution)/shard_map/ppermute | solution.py:453
  11.7 2.4 %collective-permute-start.4 = (bf16[272,256]{1,0:T(8,128)(2,1)}, bf16[272,256]{1,0:T(8,128)(2,1)S(1)}, u32[]{:S(2)}, u32[]{:S(2)}) collective-permute-start(bf16[272,256]{1,0:T(8,128)(2,1)} %get-tuple-element.54), channel_id=1, source_target_pairs={{0,1},{1,0},{2,3},{3,2},{4,9},{5,8},{6,11},{7,10},{8,5},{9,4},{10,... | collective-permute-start | bytes 417800 | tf_op jit(solution)/shard_map/ppermute | solution.py:455
  14.2 1.0 %copy-done.2 = bf16[672,256]{1,0:T(8,128)(2,1)S(1)} copy-done((bf16[672,256]{1,0:T(8,128)(2,1)S(1)}, bf16[672,256]{1,0:T(8,128)(2,1)}, u32[]{:S(2)}) %copy-start.2) | copy-done | bytes 344088
  15.2 1.5 %early.1 = (bf16[512,512]{1,0:T(8,128)(2,1)S(1)}, bf16[512,512]{1,0:T(8,128)(2,1)S(1)}, bf16[512,512]{1,0:T(8,128)(2,1)S(1)}, f32[2,256,256]{2,1,0:T(8,128)S(1)}, f32[3,256,256]{2,1,0:T(8,128)S(1)}) custom-call(bf16[512,1536]{1,0:T(8,128)(2,1)S(1)} %copy-done, bf16[672,256]{1,0:T(8,128)(2,1)S(1)} %copy-done.2, ...), custom_call_target="tpu_custom_call" | custom-call | flops 268435456 | bytes 4194304 | tf_op jit(solution)/shard_map/early/pallas_call | solution.py:465
  16.8 1.7 %collective-permute-done.4.refs_3_ = bf16[272,256]{1,0:T(8,128)(2,1)S(1)} collective-permute-done((bf16[272,256]{1,0:T(8,128)(2,1)}, bf16[272,256]{1,0:T(8,128)(2,1)S(1)}, u32[]{:S(2)}, u32[]{:S(2)}) %collective-permute-start.4) | collective-permute-done | bytes 139296 | tf_op jit(solution)/shard_map/ppermute | solution.py:455
  18.8 1.1 %collective-permute-start.5 = (bf16[256,256]{1,0:T(8,128)(2,1)S(1)}, bf16[256,256]{1,0:T(8,128)(2,1)S(1)}, u32[]{:S(2)}, u32[]{:S(2)}) collective-permute-start(bf16[256,256]{1,0:T(8,128)(2,1)S(1)} %get-tuple-element.62), channel_id=1, source_target_pairs={{0,2},{1,3},{2,0},{3,1},{4,6},{5,7},{6,4},{7,5},{8,10},{9,11},{10,... | collective-permute-start | bytes 393224 | tf_op jit(solution)/shard_map/ppermute | solution.py:488
  20.3 0.5 %collective-permute-start.9 = (bf16[256,256]{1,0:T(8,128)(2,1)S(1)}, bf16[256,256]{1,0:T(8,128)(2,1)S(1)}, u32[]{:S(2)}, u32[]{:S(2)}) collective-permute-start(bf16[256,256]{1,0:T(8,128)(2,1)S(1)} %get-tuple-element.68), channel_id=1, source_target_pairs={{0,1},{1,0},{2,3},{3,2},{4,8},{5,9},{6,10},{7,11},{8,4},{9,5},{10,... | collective-permute-start | bytes 393224 | tf_op jit(solution)/shard_map/ppermute | solution.py:491
  20.8 2.8 %collective-permute-done.5.refs_1_ = bf16[256,256]{1,0:T(8,128)(2,1)S(1)} collective-permute-done((bf16[256,256]{1,0:T(8,128)(2,1)S(1)}, bf16[256,256]{1,0:T(8,128)(2,1)S(1)}, u32[]{:S(2)}, u32[]{:S(2)}) %collective-permute-start.5) | collective-permute-done | bytes 131104 | tf_op jit(solution)/shard_map/ppermute | solution.py:488
  23.6 1.8 %collective-permute-done.8.refs_3_ = bf16[256,256]{1,0:T(8,128)(2,1)S(1)} collective-permute-done((bf16[256,256]{1,0:T(8,128)(2,1)S(1)}, bf16[256,256]{1,0:T(8,128)(2,1)S(1)}, u32[]{:S(2)}, u32[]{:S(2)}) %collective-permute-start.8) | collective-permute-done | bytes 131104 | tf_op jit(solution)/shard_map/ppermute | solution.py:490
  25.5 0.5 %merge.1 = (f32[256,512]{1,0:T(8,128)S(1)}, bf16[256,512]{1,0:T(8,128)(2,1)S(1)}) custom-call(f32[256,256]{1,0:T(8,128)S(1)} %get-tuple-element.61.refs_0_, bf16[256,256]{1,0:T(8,128)(2,1)S(1)} %collective-permute-done.5.refs_1_, f32[256,256]{1,0:T(8,128)S(1)} %get-tuple-element.66.refs_2_, bf16[256,256]{1,0:T(8,128)(2,1)S(1)} %collective-permute-done.8.refs_3_, ...), custom_call_target="tpu_custom_call" | custom-call | flops 134217728 | bytes 2097152 | tf_op jit(solution)/shard_map/merge/pallas_call | solution.py:493
  25.9 0.9 %collective-permute-start.11 = (bf16[256,512]{1,0:T(8,128)(2,1)S(1)}, bf16[256,512]{1,0:T(8,128)(2,1)S(1)}, u32[]{:S(2)}, u32[]{:S(2)}) collective-permute-start(bf16[256,512]{1,0:T(8,128)(2,1)S(1)} %get-tuple-element.70.own_ref), channel_id=1, source_target_pairs={{0,1},{1,0},{2,3},{3,2},{4,5},{5,4},{6,7},{7,6},{8,9},{9,8},{10,11... | collective-permute-start | bytes 786440 | tf_op jit(solution)/shard_map/ppermute | solution.py:513
  26.9 0.4 collective-permute-start.10
  27.3 0.7 %collective-permute-done.11.side_ref = bf16[256,512]{1,0:T(8,128)(2,1)S(1)} collective-permute-done((bf16[256,512]{1,0:T(8,128)(2,1)S(1)}, bf16[256,512]{1,0:T(8,128)(2,1)S(1)}, u32[]{:S(2)}, u32[]{:S(2)}) %collective-permute-start.11) | collective-permute-done | bytes 262176 | tf_op jit(solution)/shard_map/ppermute | solution.py:513
  28.0 0.9 %collective-permute-start.12 = (bf16[256,512]{1,0:T(8,128)(2,1)S(1)}, bf16[256,512]{1,0:T(8,128)(2,1)S(1)}, u32[]{:S(2)}, u32[]{:S(2)}) collective-permute-start(bf16[256,512]{1,0:T(8,128)(2,1)S(1)} %get-tuple-element.70.own_ref), channel_id=1, source_target_pairs={{0,1},{1,0},{2,4},{3,5},{4,2},{5,3},{6,8},{7,9},{8,6},{9,7},{10,12... | collective-permute-start | bytes 786440 | tf_op jit(solution)/shard_map/ppermute | solution.py:516
  28.9 4.8 %near.1 = (bf16[16,128,256]{2,1,0:T(8,128)(2,1)S(1)}, f32[16,48,256]{2,1,0:T(8,128)S(1)}, f32[16,8,256]{2,1,0:T(8,128)S(1)}) custom-call(bf16[256,512]{1,0:T(8,128)(2,1)S(1)} %get-tuple-element.70.own_ref, bf16[256,512]{1,0:T(8,128)(2,1)S(1)} %collective-permute-done.11.side_ref, bf16[512,512]{1,0:T(8,128)(2,1)S(1)} %get-tuple-element.72.wq_ref, ...), custom_call_target="tpu_custom_call" | custom-call | flops 8589934592 | bytes 4194304 | tf_op jit(solution)/shard_map/near/pallas_call | solution.py:519
  33.7 2.8 %collective-permute-done.12.block_ref = bf16[256,512]{1,0:T(8,128)(2,1)S(1)} collective-permute-done((bf16[256,512]{1,0:T(8,128)(2,1)S(1)}, bf16[256,512]{1,0:T(8,128)(2,1)S(1)}, u32[]{:S(2)}, u32[]{:S(2)}) %collective-permute-start.12) | collective-permute-done | bytes 262176 | tf_op jit(solution)/shard_map/ppermute | solution.py:516
  36.5 2.0 %other.1 = (f32[16,48,256]{2,1,0:T(8,128)S(1)}, f32[16,8,256]{2,1,0:T(8,128)S(1)}) custom-call(bf16[256,512]{1,0:T(8,128)(2,1)S(1)} %collective-permute-done.12.block_ref, bf16[512,512]{1,0:T(8,128)(2,1)S(1)} %get-tuple-element.73.wk_ref, bf16[512,512]{1,0:T(8,128)(2,1)S(1)} %get-tuple-element.74.wv_ref, s32[2,16]{1,0:T(2,128)S(1)} %select_reduce_fusion.plan_ref.plan_in, ...), custom_call_target="tpu_custom_call" | custom-call | flops 536870912 | bytes 3145728 | tf_op jit(solution)/shard_map/other/pallas_call | solution.py:539
  38.5 1.9 %collective-permute-done.10.block_ref = bf16[256,512]{1,0:T(8,128)(2,1)S(1)} collective-permute-done((bf16[256,512]{1,0:T(8,128)(2,1)S(1)}, bf16[256,512]{1,0:T(8,128)(2,1)S(1)}, u32[]{:S(2)}, u32[]{:S(2)}) %collective-permute-start.10) | collective-permute-done | bytes 262176 | tf_op jit(solution)/shard_map/ppermute | solution.py:514
  40.4 0.8 %collective-permute-start.13 = (bf16[256,512]{1,0:T(8,128)(2,1)S(1)}, bf16[256,512]{1,0:T(8,128)(2,1)S(1)}, u32[]{:S(2)}, u32[]{:S(2)}) collective-permute-start(bf16[256,512]{1,0:T(8,128)(2,1)S(1)} %collective-permute-done.10.block_ref), channel_id=1, source_target_pairs={{0,1},{1,0},{2,3},{3,2},{4,5},{5,4},{6,7},{7,6},{8,9},{9,8},{10,11... | collective-permute-start | bytes 786440 | tf_op jit(solution)/shard_map/ppermute | solution.py:563
  41.2 2.1 %pair.1 = (f32[16,48,256]{2,1,0:T(8,128)S(1)}, f32[16,8,256]{2,1,0:T(8,128)S(1)}) custom-call(bf16[256,512]{1,0:T(8,128)(2,1)S(1)} %collective-permute-done.10.block_ref, bf16[512,512]{1,0:T(8,128)(2,1)S(1)} %get-tuple-element.73.wk_ref, bf16[512,512]{1,0:T(8,128)(2,1)S(1)} %get-tuple-element.74.wv_ref, s32[2,16]{1,0:T(2,128)S(1)} %select_reduce_fusion.plan_ref.plan_in, ...), custom_call_target="tpu_custom_call" | custom-call | flops 536870912 | bytes 3145728 | tf_op jit(solution)/shard_map/pair/pallas_call | solution.py:539
  43.4 4.4 %far.1 = bf16[256,512]{1,0:T(8,128)(2,1)} custom-call(bf16[256,512]{1,0:T(8,128)(2,1)S(1)} %collective-permute-done.13.first_ref, bf16[256,512]{1,0:T(8,128)(2,1)S(1)} %collective-permute-done.14.second_ref, bf16[512,512]{1,0:T(8,128)(2,1)S(1)} %get-tuple-element.73.wk_ref, bf16[512,512]{1,0:T(8,128)(2,1)S(1)} %get-tuple-element.74.wv_ref, ...), custom_call_target="tpu_custom_call" | custom-call | flops 8589934592 | bytes 8388608 | tf_op jit(solution)/shard_map/far/pallas_call | solution.py:566
  (40 shorter events, 2.0 us)
Async XLA Ops:
  0.0 9.2 %copy-start.9 = (s32[16]{0:T(128)S(1)}, s32[16]{0:T(128)}, u32[]{:S(2)}) copy-start(s32[16]{0:T(128)} %param.23) | copy-start | bytes 196
  0.0 14.2 %copy-start = (bf16[512,1536]{1,0:T(8,128)(2,1)S(1)}, bf16[512,1536]{1,0:T(8,128)(2,1)}, u32[]{:S(2)}) copy-start(bf16[512,1536]{1,0:T(8,128)(2,1)} %w_ref.2) | copy-start | bytes 4718596
  5.5 3.8 %collective-permute-start.1 = (bf16[672,256]{1,0:T(8,128)(2,1)}, bf16[672,256]{1,0:T(8,128)(2,1)S(1)}, u32[]{:S(2)}, u32[]{:S(2)}) collective-permute-start(bf16[672,256]{1,0:T(8,128)(2,1)} %get-tuple-element.48), channel_id=1, source_target_pairs={{0,1},{1,0},{2,3},{3,2},{4,5},{5,4},{6,7},{7,6},{8,9},{9,8},{10,11... | collective-permute-start | bytes 1032200 | tf_op jit(solution)/shard_map/ppermute | solution.py:446
  6.3 13.7 %collective-permute-start.6 = (bf16[400,256]{1,0:T(8,128)(2,1)}, bf16[400,256]{1,0:T(8,128)(2,1)S(1)}, u32[]{:S(2)}, u32[]{:S(2)}) collective-permute-start(bf16[400,256]{1,0:T(8,128)(2,1)} %get-tuple-element.63), channel_id=1, source_target_pairs={{0,2},{1,3},{2,0},{3,1},{4,6},{5,7},{6,4},{7,5},{8,10},{9,11},{10,... | collective-permute-start | bytes 614408 | tf_op jit(solution)/shard_map/ppermute | solution.py:447
  6.6 5.1 %collective-permute-start = (bf16[272,256]{1,0:T(8,128)(2,1)}, bf16[272,256]{1,0:T(8,128)(2,1)S(1)}, u32[]{:S(2)}, u32[]{:S(2)}) collective-permute-start(bf16[272,256]{1,0:T(8,128)(2,1)} %get-tuple-element.47), channel_id=1, source_target_pairs={{0,4},{1,5},{2,6},{3,7},{4,0},{5,1},{6,2},{7,3},{8,12},{9,13},{10,... | collective-permute-start | bytes 417800 | tf_op jit(solution)/shard_map/ppermute | solution.py:448
  6.7 9.9 %collective-permute-start.3 = (bf16[272,256]{1,0:T(8,128)(2,1)}, bf16[272,256]{1,0:T(8,128)(2,1)S(1)}, u32[]{:S(2)}, u32[]{:S(2)}) collective-permute-start(bf16[272,256]{1,0:T(8,128)(2,1)} %get-tuple-element.53), channel_id=1, source_target_pairs={{0,1},{1,0},{2,3},{3,2},{4,8},{5,9},{6,10},{7,11},{8,4},{9,5},{10,... | collective-permute-start | bytes 417800 | tf_op jit(solution)/shard_map/ppermute | solution.py:449
  9.4 10.6 %collective-permute-start.7 = (bf16[400,256]{1,0:T(8,128)(2,1)}, bf16[400,256]{1,0:T(8,128)(2,1)S(1)}, u32[]{:S(2)}, u32[]{:S(2)}) collective-permute-start(bf16[400,256]{1,0:T(8,128)(2,1)} %get-tuple-element.64), channel_id=1, source_target_pairs={{0,3},{1,2},{2,1},{3,0},{4,7},{5,6},{6,5},{7,4},{8,11},{9,10},{10,... | collective-permute-start | bytes 614408 | tf_op jit(solution)/shard_map/ppermute | solution.py:453
  11.4 5.4 %collective-permute-start.2 = (bf16[272,256]{1,0:T(8,128)(2,1)}, bf16[272,256]{1,0:T(8,128)(2,1)S(1)}, u32[]{:S(2)}, u32[]{:S(2)}) collective-permute-start(bf16[272,256]{1,0:T(8,128)(2,1)} %get-tuple-element.52), channel_id=1, source_target_pairs={{0,5},{1,4},{2,7},{3,6},{4,1},{5,0},{6,3},{7,2},{8,13},{9,12},{10,... | collective-permute-start | bytes 417800 | tf_op jit(solution)/shard_map/ppermute | solution.py:454
  11.7 6.8 %collective-permute-start.4 = (bf16[272,256]{1,0:T(8,128)(2,1)}, bf16[272,256]{1,0:T(8,128)(2,1)S(1)}, u32[]{:S(2)}, u32[]{:S(2)}) collective-permute-start(bf16[272,256]{1,0:T(8,128)(2,1)} %get-tuple-element.54), channel_id=1, source_target_pairs={{0,1},{1,0},{2,3},{3,2},{4,9},{5,8},{6,11},{7,10},{8,5},{9,4},{10,... | collective-permute-start | bytes 417800 | tf_op jit(solution)/shard_map/ppermute | solution.py:455
  15.2 10.3 %copy-start.1 = (bf16[512,512]{1,0:T(8,128)(2,1)S(1)}, bf16[512,512]{1,0:T(8,128)(2,1)}, u32[]{:S(2)}) copy-start(bf16[512,512]{1,0:T(8,128)(2,1)} %refs_6_.1) | copy-start | bytes 1572868
  15.2 10.3 %copy-start.3 = (bf16[256,512]{1,0:T(8,128)(2,1)S(1)}, bf16[256,512]{1,0:T(8,128)(2,1)}, u32[]{:S(2)}) copy-start(bf16[256,512]{1,0:T(8,128)(2,1)} %refs_5_.1) | copy-start | bytes 786436
  15.2 10.3 %copy-start.4 = (f32[512]{0:T(512)S(1)}, f32[512]{0:T(512)}, u32[]{:S(2)}) copy-start(f32[512]{0:T(512)} %param.21) | copy-start | bytes 6148
  18.8 4.7 %collective-permute-start.5 = (bf16[256,256]{1,0:T(8,128)(2,1)S(1)}, bf16[256,256]{1,0:T(8,128)(2,1)S(1)}, u32[]{:S(2)}, u32[]{:S(2)}) collective-permute-start(bf16[256,256]{1,0:T(8,128)(2,1)S(1)} %get-tuple-element.62), channel_id=1, source_target_pairs={{0,2},{1,3},{2,0},{3,1},{4,6},{5,7},{6,4},{7,5},{8,10},{9,11},{10,... | collective-permute-start | bytes 393224 | tf_op jit(solution)/shard_map/ppermute | solution.py:488
  20.2 5.1 %collective-permute-start.8 = (bf16[256,256]{1,0:T(8,128)(2,1)S(1)}, bf16[256,256]{1,0:T(8,128)(2,1)S(1)}, u32[]{:S(2)}, u32[]{:S(2)}) collective-permute-start(bf16[256,256]{1,0:T(8,128)(2,1)S(1)} %get-tuple-element.67), channel_id=1, source_target_pairs={{0,4},{1,5},{2,6},{3,7},{4,0},{5,1},{6,2},{7,3},{8,12},{9,13},{10,... | collective-permute-start | bytes 393224 | tf_op jit(solution)/shard_map/ppermute | solution.py:490
  20.3 5.1 %collective-permute-start.9 = (bf16[256,256]{1,0:T(8,128)(2,1)S(1)}, bf16[256,256]{1,0:T(8,128)(2,1)S(1)}, u32[]{:S(2)}, u32[]{:S(2)}) collective-permute-start(bf16[256,256]{1,0:T(8,128)(2,1)S(1)} %get-tuple-element.68), channel_id=1, source_target_pairs={{0,1},{1,0},{2,3},{3,2},{4,8},{5,9},{6,10},{7,11},{8,4},{9,5},{10,... | collective-permute-start | bytes 393224 | tf_op jit(solution)/shard_map/ppermute | solution.py:491
  25.9 2.1 %collective-permute-start.11 = (bf16[256,512]{1,0:T(8,128)(2,1)S(1)}, bf16[256,512]{1,0:T(8,128)(2,1)S(1)}, u32[]{:S(2)}, u32[]{:S(2)}) collective-permute-start(bf16[256,512]{1,0:T(8,128)(2,1)S(1)} %get-tuple-element.70.own_ref), channel_id=1, source_target_pairs={{0,1},{1,0},{2,3},{3,2},{4,5},{5,4},{6,7},{7,6},{8,9},{9,8},{10,11... | collective-permute-start | bytes 786440 | tf_op jit(solution)/shard_map/ppermute | solution.py:513
  26.9 13.5 %collective-permute-start.10 = (bf16[256,512]{1,0:T(8,128)(2,1)S(1)}, bf16[256,512]{1,0:T(8,128)(2,1)S(1)}, u32[]{:S(2)}, u32[]{:S(2)}) collective-permute-start(bf16[256,512]{1,0:T(8,128)(2,1)S(1)} %get-tuple-element.70.own_ref), channel_id=1, source_target_pairs={{0,2},{1,3},{2,0},{3,1},{4,6},{5,7},{6,4},{7,5},{8,10},{9,11},{10,... | collective-permute-start | bytes 786440 | tf_op jit(solution)/shard_map/ppermute | solution.py:514
  28.0 8.5 %collective-permute-start.12 = (bf16[256,512]{1,0:T(8,128)(2,1)S(1)}, bf16[256,512]{1,0:T(8,128)(2,1)S(1)}, u32[]{:S(2)}, u32[]{:S(2)}) collective-permute-start(bf16[256,512]{1,0:T(8,128)(2,1)S(1)} %get-tuple-element.70.own_ref), channel_id=1, source_target_pairs={{0,1},{1,0},{2,4},{3,5},{4,2},{5,3},{6,8},{7,9},{8,6},{9,7},{10,12... | collective-permute-start | bytes 786440 | tf_op jit(solution)/shard_map/ppermute | solution.py:516
  36.5 6.9 %copy-start.6 = (bf16[2048,512]{1,0:T(8,128)(2,1)S(1)}, bf16[2048,512]{1,0:T(8,128)(2,1)}, u32[]{:S(2)}) copy-start(bf16[2048,512]{1,0:T(8,128)(2,1)} %down_ref.1) | copy-start | bytes 6291460
  38.5 4.9 %copy-start.5 = (bf16[512,2048]{1,0:T(8,128)(2,1)S(1)}, bf16[512,2048]{1,0:T(8,128)(2,1)}, u32[]{:S(2)}) copy-start(bf16[512,2048]{1,0:T(8,128)(2,1)} %up_ref.1) | copy-start | bytes 6291460
  38.5 4.9 %copy-start.7 = (bf16[512,512]{1,0:T(8,128)(2,1)S(1)}, bf16[512,512]{1,0:T(8,128)(2,1)}, u32[]{:S(2)}) copy-start(bf16[512,512]{1,0:T(8,128)(2,1)} %w_out_ref.1) | copy-start | bytes 1572868
  38.5 4.9 %copy-start.8 = (f32[512]{0:T(512)S(1)}, f32[512]{0:T(512)}, u32[]{:S(2)}) copy-start(f32[512]{0:T(512)} %param.25) | copy-start | bytes 6148
  40.4 3.0 %collective-permute-start.13 = (bf16[256,512]{1,0:T(8,128)(2,1)S(1)}, bf16[256,512]{1,0:T(8,128)(2,1)S(1)}, u32[]{:S(2)}, u32[]{:S(2)}) collective-permute-start(bf16[256,512]{1,0:T(8,128)(2,1)S(1)} %collective-permute-done.10.block_ref), channel_id=1, source_target_pairs={{0,1},{1,0},{2,3},{3,2},{4,5},{5,4},{6,7},{7,6},{8,9},{9,8},{10,11... | collective-permute-start | bytes 786440 | tf_op jit(solution)/shard_map/ppermute | solution.py:563
  41.2 2.2 %collective-permute-start.14 = (bf16[256,512]{1,0:T(8,128)(2,1)S(1)}, bf16[256,512]{1,0:T(8,128)(2,1)S(1)}, u32[]{:S(2)}, u32[]{:S(2)}) collective-permute-start(bf16[256,512]{1,0:T(8,128)(2,1)S(1)} %collective-permute-done.12.block_ref), channel_id=1, source_target_pairs={{0,1},{1,0},{2,3},{3,2},{4,5},{5,4},{6,7},{7,6},{8,9},{9,8},{10,11... | collective-permute-start | bytes 786440 | tf_op jit(solution)/shard_map/ppermute | solution.py:560
  (1 other events, 1.0 us)

commit v16 on v15

--- a/solution.py
+++ b/solution.py
@@ -14,7 +14,7 @@
 NEAR = 128
 TILE = 16
 CAP = 128
-GRID_PARTS = 2
+GRID_PARTS = 1
 MOST = 56
 GROUP = 4
 
@@ -351,13 +351,12 @@
     by_even = odd == lax.rem(inner // 2 + 1, 2)
     project_keys(jnp.where(by_even, first_ref[...], second_ref[...]), wk_ref, wv_ref, key_ref, value_ref, 0)
     gap_ref[...] = gaps(2 * odd - 1, 0, nodes, nodes)
-    for i in range(HEADS // (2 * GROUP)):
-        heads = range(2 * GROUP * i, 2 * GROUP * (i + 1))
-        keys, values = [key_ref[h // per_group] for h in heads], [value_ref[h] for h in heads]
-        for h, sums, _ in extend(
-            heads, keys, values, gap_ref, query_ref, sums_ref, top_ref, scale
-        ):
-            attended_ref[h] = (sums[0:head_dim] / sums[head_dim : head_dim + 1]).astype(jnp.bfloat16)
+    heads = range(HEADS)
+    keys, values = [key_ref[h // per_group] for h in heads], [value_ref[h] for h in heads]
+    for h, sums, _ in extend(
+        heads, keys, values, gap_ref, query_ref, sums_ref, top_ref, scale
+    ):
+        attended_ref[h] = (sums[0:head_dim] / sums[head_dim : head_dim + 1]).astype(jnp.bfloat16)
 
     attended = attended_ref[...].reshape(width, nodes)
     mixed = lax.dot_general(
@@ -365,10 +364,8 @@
     )
     total = state_ref[...] + mixed
     normed = layer_norm(total, gain_ref[...]).astype(jnp.bfloat16)
-    chunk = math.gcd(up_ref.shape[1], 1024)
-    for start in range(0, up_ref.shape[1], chunk):
-        hidden = silu(dot(normed, up_ref[:, start : start + chunk])).astype(jnp.bfloat16)
-        total = total + dot(hidden, down_ref[start : start + chunk, :])
+    hidden = silu(dot(normed, up_ref[...])).astype(jnp.bfloat16)
+    total = total + dot(hidden, down_ref[...])
     out_ref[...] = total.astype(jnp.bfloat16)
 
 

time: 48 us -> 47.8 us (level)
  no operation moved by 1% of the time
where the time goes in v16:
time: 47.8 us; the launch traced here: 47.5 us
  Pallas kernels  21.1 us (44%)
  starting transfers between devices  12.7 us (27%)
  waiting for transfers between devices  12.2 us (26%)
  local copies, waits for them, and re-layouts  1.02 us (2%)
    pallas_call x1, Pallas kernels, local(): pl.pallas_call(functools.partial(message_kernel, pairs), out_shape=outgoi...  5.22 us
    pallas_call x1, Pallas kernels, local(): pl.pallas_call(near_kernel, out_shape=[jax.ShapeDtypeStruct((HEADS, LANES...  4.84 us
    pallas_call x1, Pallas kernels, local(): pl.pallas_call(far_kernel, out_shape=jax.ShapeDtypeStruct((nodes, width),...  4.41 us
    pallas_call x2, Pallas kernels, outer(): pl.pallas_call(functools.partial(outer_kernel, by_pair), out_shape=[jax.S...  4.12 us
    ppermute x1, waiting for transfers between devices, local(): lax.ppermute(part, NODES, chip_trade(p + 1))  2.78 us
    ppermute x1, waiting for transfers between devices, local(): odd = lax.ppermute(normed, NODES, chips_trade(1))  2.76 us
    ppermute x1, starting transfers between devices, local(): odd = lax.ppermute(odd, NODES, bands_trade(1))  2.41 us
    ppermute x1, starting transfers between devices, local(): odd_other = lax.ppermute(odd_other, NODES, bands_trade(1, 1))  2.35 us
  transfers between devices with their start and end apart: 15, of which 9 were waited for; matrix products, arithmetic and copies ran while one was open for 1% of the time, Pallas kernels for 23%

profile of v16, /device:TPU:15, one launch (start us, length us, event | category | flops | bytes accessed | tf_op | source)
XLA Modules:
  0.0 47.5 jit_solution(4676929645142002596)
XLA Ops:
  0.0 5.2 %messages.1 = (bf16[272,256]{1,0:T(8,128)(2,1)}, bf16[272,256]{1,0:T(8,128)(2,1)}, bf16[272,256]{1,0:T(8,128)(2,1)}, bf16[272,256]{1,0:T(8,128)(2,1)}, bf16[400,...) custom-call(bf16[1024,512]{1,0:T(8,128)(2,1)} %grid_ref.1, ...), custom_call_target="tpu_custom_call" | custom-call | flops 2147483648 | bytes 4194304 | tf_op jit(solution)/shard_map/messages/pallas_call | solution.py:408
  5.2 0.7 %collective-permute-start.1 = (bf16[672,256]{1,0:T(8,128)(2,1)}, bf16[672,256]{1,0:T(8,128)(2,1)S(1)}, u32[]{:S(2)}, u32[]{:S(2)}) collective-permute-start(bf16[672,256]{1,0:T(8,128)(2,1)} %get-tuple-element.48), channel_id=1, source_target_pairs={{0,1},{1,0},{2,3},{3,2},{4,5},{5,4},{6,7},{7,6},{8,9},{9,8},{10,11... | collective-permute-start | bytes 1032200 | tf_op jit(solution)/shard_map/ppermute | solution.py:443
  6.4 2.4 %collective-permute-start.3 = (bf16[272,256]{1,0:T(8,128)(2,1)}, bf16[272,256]{1,0:T(8,128)(2,1)S(1)}, u32[]{:S(2)}, u32[]{:S(2)}) collective-permute-start(bf16[272,256]{1,0:T(8,128)(2,1)} %get-tuple-element.53), channel_id=1, source_target_pairs={{0,1},{1,0},{2,3},{3,2},{4,8},{5,9},{6,10},{7,11},{8,4},{9,5},{10,... | collective-permute-start | bytes 417800 | tf_op jit(solution)/shard_map/ppermute | solution.py:446
  9.0 2.1 %collective-permute-start.7 = (bf16[400,256]{1,0:T(8,128)(2,1)}, bf16[400,256]{1,0:T(8,128)(2,1)S(1)}, u32[]{:S(2)}, u32[]{:S(2)}) collective-permute-start(bf16[400,256]{1,0:T(8,128)(2,1)} %get-tuple-element.64), channel_id=1, source_target_pairs={{0,3},{1,2},{2,1},{3,0},{4,7},{5,6},{6,5},{7,4},{8,11},{9,10},{10,... | collective-permute-start | bytes 614408 | tf_op jit(solution)/shard_map/ppermute | solution.py:450
  11.4 2.3 %collective-permute-start.4 = (bf16[272,256]{1,0:T(8,128)(2,1)}, bf16[272,256]{1,0:T(8,128)(2,1)S(1)}, u32[]{:S(2)}, u32[]{:S(2)}) collective-permute-start(bf16[272,256]{1,0:T(8,128)(2,1)} %get-tuple-element.54), channel_id=1, source_target_pairs={{0,1},{1,0},{2,3},{3,2},{4,9},{5,8},{6,11},{7,10},{8,5},{9,4},{10,... | collective-permute-start | bytes 417800 | tf_op jit(solution)/shard_map/ppermute | solution.py:452
  13.9 1.0 %copy-done.2 = bf16[672,256]{1,0:T(8,128)(2,1)S(1)} copy-done((bf16[672,256]{1,0:T(8,128)(2,1)S(1)}, bf16[672,256]{1,0:T(8,128)(2,1)}, u32[]{:S(2)}) %copy-start.2) | copy-done | bytes 344088
  14.8 1.5 %early.1 = (bf16[512,512]{1,0:T(8,128)(2,1)S(1)}, bf16[512,512]{1,0:T(8,128)(2,1)S(1)}, bf16[512,512]{1,0:T(8,128)(2,1)S(1)}, f32[2,256,256]{2,1,0:T(8,128)S(1)}, f32[3,256,256]{2,1,0:T(8,128)S(1)}) custom-call(bf16[512,1536]{1,0:T(8,128)(2,1)S(1)} %copy-done, bf16[672,256]{1,0:T(8,128)(2,1)S(1)} %copy-done.2, ...), custom_call_target="tpu_custom_call" | custom-call | flops 268435456 | bytes 4194304 | tf_op jit(solution)/shard_map/early/pallas_call | solution.py:462
  16.5 1.7 %collective-permute-done.4.refs_3_ = bf16[272,256]{1,0:T(8,128)(2,1)S(1)} collective-permute-done((bf16[272,256]{1,0:T(8,128)(2,1)}, bf16[272,256]{1,0:T(8,128)(2,1)S(1)}, u32[]{:S(2)}, u32[]{:S(2)}) %collective-permute-start.4) | collective-permute-done | bytes 139296 | tf_op jit(solution)/shard_map/ppermute | solution.py:452
  18.5 1.1 %collective-permute-start.5 = (bf16[256,256]{1,0:T(8,128)(2,1)S(1)}, bf16[256,256]{1,0:T(8,128)(2,1)S(1)}, u32[]{:S(2)}, u32[]{:S(2)}) collective-permute-start(bf16[256,256]{1,0:T(8,128)(2,1)S(1)} %get-tuple-element.62), channel_id=1, source_target_pairs={{0,2},{1,3},{2,0},{3,1},{4,6},{5,7},{6,4},{7,5},{8,10},{9,11},{10,... | collective-permute-start | bytes 393224 | tf_op jit(solution)/shard_map/ppermute | solution.py:485
  20.0 0.5 %collective-permute-start.9 = (bf16[256,256]{1,0:T(8,128)(2,1)S(1)}, bf16[256,256]{1,0:T(8,128)(2,1)S(1)}, u32[]{:S(2)}, u32[]{:S(2)}) collective-permute-start(bf16[256,256]{1,0:T(8,128)(2,1)S(1)} %get-tuple-element.68), channel_id=1, source_target_pairs={{0,1},{1,0},{2,3},{3,2},{4,8},{5,9},{6,10},{7,11},{8,4},{9,5},{10,... | collective-permute-start | bytes 393224 | tf_op jit(solution)/shard_map/ppermute | solution.py:488
  20.5 2.8 %collective-permute-done.5.refs_1_ = bf16[256,256]{1,0:T(8,128)(2,1)S(1)} collective-permute-done((bf16[256,256]{1,0:T(8,128)(2,1)S(1)}, bf16[256,256]{1,0:T(8,128)(2,1)S(1)}, u32[]{:S(2)}, u32[]{:S(2)}) %collective-permute-start.5) | collective-permute-done | bytes 131104 | tf_op jit(solution)/shard_map/ppermute | solution.py:485
  23.3 1.8 %collective-permute-done.8.refs_3_ = bf16[256,256]{1,0:T(8,128)(2,1)S(1)} collective-permute-done((bf16[256,256]{1,0:T(8,128)(2,1)S(1)}, bf16[256,256]{1,0:T(8,128)(2,1)S(1)}, u32[]{:S(2)}, u32[]{:S(2)}) %collective-permute-start.8) | collective-permute-done | bytes 131104 | tf_op jit(solution)/shard_map/ppermute | solution.py:487
  25.1 0.5 %merge.1 = (f32[256,512]{1,0:T(8,128)S(1)}, bf16[256,512]{1,0:T(8,128)(2,1)S(1)}) custom-call(f32[256,256]{1,0:T(8,128)S(1)} %get-tuple-element.61.refs_0_, bf16[256,256]{1,0:T(8,128)(2,1)S(1)} %collective-permute-done.5.refs_1_, f32[256,256]{1,0:T(8,128)S(1)} %get-tuple-element.66.refs_2_, bf16[256,256]{1,0:T(8,128)(2,1)S(1)} %collective-permute-done.8.refs_3_, ...), custom_call_target="tpu_custom_call" | custom-call | flops 134217728 | bytes 2097152 | tf_op jit(solution)/shard_map/merge/pallas_call | solution.py:490
  25.6 0.9 %collective-permute-start.11 = (bf16[256,512]{1,0:T(8,128)(2,1)S(1)}, bf16[256,512]{1,0:T(8,128)(2,1)S(1)}, u32[]{:S(2)}, u32[]{:S(2)}) collective-permute-start(bf16[256,512]{1,0:T(8,128)(2,1)S(1)} %get-tuple-element.70.own_ref), channel_id=1, source_target_pairs={{0,1},{1,0},{2,3},{3,2},{4,5},{5,4},{6,7},{7,6},{8,9},{9,8},{10,11... | collective-permute-start | bytes 786440 | tf_op jit(solution)/shard_map/ppermute | solution.py:510
  26.6 0.4 collective-permute-start.10
  27.0 0.7 %collective-permute-done.11.side_ref = bf16[256,512]{1,0:T(8,128)(2,1)S(1)} collective-permute-done((bf16[256,512]{1,0:T(8,128)(2,1)S(1)}, bf16[256,512]{1,0:T(8,128)(2,1)S(1)}, u32[]{:S(2)}, u32[]{:S(2)}) %collective-permute-start.11) | collective-permute-done | bytes 262176 | tf_op jit(solution)/shard_map/ppermute | solution.py:510
  27.7 0.9 %collective-permute-start.12 = (bf16[256,512]{1,0:T(8,128)(2,1)S(1)}, bf16[256,512]{1,0:T(8,128)(2,1)S(1)}, u32[]{:S(2)}, u32[]{:S(2)}) collective-permute-start(bf16[256,512]{1,0:T(8,128)(2,1)S(1)} %get-tuple-element.70.own_ref), channel_id=1, source_target_pairs={{0,1},{1,0},{2,4},{3,5},{4,2},{5,3},{6,8},{7,9},{8,6},{9,7},{10,12... | collective-permute-start | bytes 786440 | tf_op jit(solution)/shard_map/ppermute | solution.py:513
  28.6 4.8 %near.1 = (bf16[16,128,256]{2,1,0:T(8,128)(2,1)S(1)}, f32[16,48,256]{2,1,0:T(8,128)S(1)}, f32[16,8,256]{2,1,0:T(8,128)S(1)}) custom-call(bf16[256,512]{1,0:T(8,128)(2,1)S(1)} %get-tuple-element.70.own_ref, bf16[256,512]{1,0:T(8,128)(2,1)S(1)} %collective-permute-done.11.side_ref, bf16[512,512]{1,0:T(8,128)(2,1)S(1)} %get-tuple-element.72.wq_ref, ...), custom_call_target="tpu_custom_call" | custom-call | flops 8589934592 | bytes 4194304 | tf_op jit(solution)/shard_map/near/pallas_call | solution.py:516
  33.4 2.8 %collective-permute-done.12.block_ref = bf16[256,512]{1,0:T(8,128)(2,1)S(1)} collective-permute-done((bf16[256,512]{1,0:T(8,128)(2,1)S(1)}, bf16[256,512]{1,0:T(8,128)(2,1)S(1)}, u32[]{:S(2)}, u32[]{:S(2)}) %collective-permute-start.12) | collective-permute-done | bytes 262176 | tf_op jit(solution)/shard_map/ppermute | solution.py:513
  36.2 2.0 %other.1 = (f32[16,48,256]{2,1,0:T(8,128)S(1)}, f32[16,8,256]{2,1,0:T(8,128)S(1)}) custom-call(bf16[256,512]{1,0:T(8,128)(2,1)S(1)} %collective-permute-done.12.block_ref, bf16[512,512]{1,0:T(8,128)(2,1)S(1)} %get-tuple-element.73.wk_ref, bf16[512,512]{1,0:T(8,128)(2,1)S(1)} %get-tuple-element.74.wv_ref, s32[2,16]{1,0:T(2,128)S(1)} %select_reduce_fusion.plan_ref.plan_in, ...), custom_call_target="tpu_custom_call" | custom-call | flops 536870912 | bytes 3145728 | tf_op jit(solution)/shard_map/other/pallas_call | solution.py:536
  38.2 1.9 %collective-permute-done.10.block_ref = bf16[256,512]{1,0:T(8,128)(2,1)S(1)} collective-permute-done((bf16[256,512]{1,0:T(8,128)(2,1)S(1)}, bf16[256,512]{1,0:T(8,128)(2,1)S(1)}, u32[]{:S(2)}, u32[]{:S(2)}) %collective-permute-start.10) | collective-permute-done | bytes 262176 | tf_op jit(solution)/shard_map/ppermute | solution.py:511
  40.1 0.8 %collective-permute-start.13 = (bf16[256,512]{1,0:T(8,128)(2,1)S(1)}, bf16[256,512]{1,0:T(8,128)(2,1)S(1)}, u32[]{:S(2)}, u32[]{:S(2)}) collective-permute-start(bf16[256,512]{1,0:T(8,128)(2,1)S(1)} %collective-permute-done.10.block_ref), channel_id=1, source_target_pairs={{0,1},{1,0},{2,3},{3,2},{4,5},{5,4},{6,7},{7,6},{8,9},{9,8},{10,11... | collective-permute-start | bytes 786440 | tf_op jit(solution)/shard_map/ppermute | solution.py:560
  40.9 2.2 %pair.1 = (f32[16,48,256]{2,1,0:T(8,128)S(1)}, f32[16,8,256]{2,1,0:T(8,128)S(1)}) custom-call(bf16[256,512]{1,0:T(8,128)(2,1)S(1)} %collective-permute-done.10.block_ref, bf16[512,512]{1,0:T(8,128)(2,1)S(1)} %get-tuple-element.73.wk_ref, bf16[512,512]{1,0:T(8,128)(2,1)S(1)} %get-tuple-element.74.wv_ref, s32[2,16]{1,0:T(2,128)S(1)} %select_reduce_fusion.plan_ref.plan_in, ...), custom_call_target="tpu_custom_call" | custom-call | flops 536870912 | bytes 3145728 | tf_op jit(solution)/shard_map/pair/pallas_call | solution.py:536
  43.1 4.4 %far.1 = bf16[256,512]{1,0:T(8,128)(2,1)} custom-call(bf16[256,512]{1,0:T(8,128)(2,1)S(1)} %collective-permute-done.13.first_ref, bf16[256,512]{1,0:T(8,128)(2,1)S(1)} %collective-permute-done.14.second_ref, bf16[512,512]{1,0:T(8,128)(2,1)S(1)} %get-tuple-element.73.wk_ref, bf16[512,512]{1,0:T(8,128)(2,1)S(1)} %get-tuple-element.74.wv_ref, ...), custom_call_target="tpu_custom_call" | custom-call | flops 8589934592 | bytes 8388608 | tf_op jit(solution)/shard_map/far/pallas_call | solution.py:563
  (40 shorter events, 2.0 us)
Async XLA Ops:
  0.0 8.8 %copy-start.9 = (s32[16]{0:T(128)S(1)}, s32[16]{0:T(128)}, u32[]{:S(2)}) copy-start(s32[16]{0:T(128)} %param.23) | copy-start | bytes 196
  0.0 13.8 %copy-start = (bf16[512,1536]{1,0:T(8,128)(2,1)S(1)}, bf16[512,1536]{1,0:T(8,128)(2,1)}, u32[]{:S(2)}) copy-start(bf16[512,1536]{1,0:T(8,128)(2,1)} %w_ref.2) | copy-start | bytes 4718596
  5.2 3.8 %collective-permute-start.1 = (bf16[672,256]{1,0:T(8,128)(2,1)}, bf16[672,256]{1,0:T(8,128)(2,1)S(1)}, u32[]{:S(2)}, u32[]{:S(2)}) collective-permute-start(bf16[672,256]{1,0:T(8,128)(2,1)} %get-tuple-element.48), channel_id=1, source_target_pairs={{0,1},{1,0},{2,3},{3,2},{4,5},{5,4},{6,7},{7,6},{8,9},{9,8},{10,11... | collective-permute-start | bytes 1032200 | tf_op jit(solution)/shard_map/ppermute | solution.py:443
  6.0 13.7 %collective-permute-start.6 = (bf16[400,256]{1,0:T(8,128)(2,1)}, bf16[400,256]{1,0:T(8,128)(2,1)S(1)}, u32[]{:S(2)}, u32[]{:S(2)}) collective-permute-start(bf16[400,256]{1,0:T(8,128)(2,1)} %get-tuple-element.63), channel_id=1, source_target_pairs={{0,2},{1,3},{2,0},{3,1},{4,6},{5,7},{6,4},{7,5},{8,10},{9,11},{10,... | collective-permute-start | bytes 614408 | tf_op jit(solution)/shard_map/ppermute | solution.py:444
  6.2 5.1 %collective-permute-start = (bf16[272,256]{1,0:T(8,128)(2,1)}, bf16[272,256]{1,0:T(8,128)(2,1)S(1)}, u32[]{:S(2)}, u32[]{:S(2)}) collective-permute-start(bf16[272,256]{1,0:T(8,128)(2,1)} %get-tuple-element.47), channel_id=1, source_target_pairs={{0,4},{1,5},{2,6},{3,7},{4,0},{5,1},{6,2},{7,3},{8,12},{9,13},{10,... | collective-permute-start | bytes 417800 | tf_op jit(solution)/shard_map/ppermute | solution.py:445
  6.4 9.9 %collective-permute-start.3 = (bf16[272,256]{1,0:T(8,128)(2,1)}, bf16[272,256]{1,0:T(8,128)(2,1)S(1)}, u32[]{:S(2)}, u32[]{:S(2)}) collective-permute-start(bf16[272,256]{1,0:T(8,128)(2,1)} %get-tuple-element.53), channel_id=1, source_target_pairs={{0,1},{1,0},{2,3},{3,2},{4,8},{5,9},{6,10},{7,11},{8,4},{9,5},{10,... | collective-permute-start | bytes 417800 | tf_op jit(solution)/shard_map/ppermute | solution.py:446
  9.0 10.6 %collective-permute-start.7 = (bf16[400,256]{1,0:T(8,128)(2,1)}, bf16[400,256]{1,0:T(8,128)(2,1)S(1)}, u32[]{:S(2)}, u32[]{:S(2)}) collective-permute-start(bf16[400,256]{1,0:T(8,128)(2,1)} %get-tuple-element.64), channel_id=1, source_target_pairs={{0,3},{1,2},{2,1},{3,0},{4,7},{5,6},{6,5},{7,4},{8,11},{9,10},{10,... | collective-permute-start | bytes 614408 | tf_op jit(solution)/shard_map/ppermute | solution.py:450
  11.1 5.4 %collective-permute-start.2 = (bf16[272,256]{1,0:T(8,128)(2,1)}, bf16[272,256]{1,0:T(8,128)(2,1)S(1)}, u32[]{:S(2)}, u32[]{:S(2)}) collective-permute-start(bf16[272,256]{1,0:T(8,128)(2,1)} %get-tuple-element.52), channel_id=1, source_target_pairs={{0,5},{1,4},{2,7},{3,6},{4,1},{5,0},{6,3},{7,2},{8,13},{9,12},{10,... | collective-permute-start | bytes 417800 | tf_op jit(solution)/shard_map/ppermute | solution.py:451
  11.4 6.8 %collective-permute-start.4 = (bf16[272,256]{1,0:T(8,128)(2,1)}, bf16[272,256]{1,0:T(8,128)(2,1)S(1)}, u32[]{:S(2)}, u32[]{:S(2)}) collective-permute-start(bf16[272,256]{1,0:T(8,128)(2,1)} %get-tuple-element.54), channel_id=1, source_target_pairs={{0,1},{1,0},{2,3},{3,2},{4,9},{5,8},{6,11},{7,10},{8,5},{9,4},{10,... | collective-permute-start | bytes 417800 | tf_op jit(solution)/shard_map/ppermute | solution.py:452
  14.8 10.3 %copy-start.1 = (bf16[512,512]{1,0:T(8,128)(2,1)S(1)}, bf16[512,512]{1,0:T(8,128)(2,1)}, u32[]{:S(2)}) copy-start(bf16[512,512]{1,0:T(8,128)(2,1)} %refs_6_.1) | copy-start | bytes 1572868
  14.8 10.3 %copy-start.3 = (bf16[256,512]{1,0:T(8,128)(2,1)S(1)}, bf16[256,512]{1,0:T(8,128)(2,1)}, u32[]{:S(2)}) copy-start(bf16[256,512]{1,0:T(8,128)(2,1)} %refs_5_.1) | copy-start | bytes 786436
  14.8 10.3 %copy-start.4 = (f32[512]{0:T(512)S(1)}, f32[512]{0:T(512)}, u32[]{:S(2)}) copy-start(f32[512]{0:T(512)} %param.21) | copy-start | bytes 6148
  18.5 4.7 %collective-permute-start.5 = (bf16[256,256]{1,0:T(8,128)(2,1)S(1)}, bf16[256,256]{1,0:T(8,128)(2,1)S(1)}, u32[]{:S(2)}, u32[]{:S(2)}) collective-permute-start(bf16[256,256]{1,0:T(8,128)(2,1)S(1)} %get-tuple-element.62), channel_id=1, source_target_pairs={{0,2},{1,3},{2,0},{3,1},{4,6},{5,7},{6,4},{7,5},{8,10},{9,11},{10,... | collective-permute-start | bytes 393224 | tf_op jit(solution)/shard_map/ppermute | solution.py:485
  19.9 5.1 %collective-permute-start.8 = (bf16[256,256]{1,0:T(8,128)(2,1)S(1)}, bf16[256,256]{1,0:T(8,128)(2,1)S(1)}, u32[]{:S(2)}, u32[]{:S(2)}) collective-permute-start(bf16[256,256]{1,0:T(8,128)(2,1)S(1)} %get-tuple-element.67), channel_id=1, source_target_pairs={{0,4},{1,5},{2,6},{3,7},{4,0},{5,1},{6,2},{7,3},{8,12},{9,13},{10,... | collective-permute-start | bytes 393224 | tf_op jit(solution)/shard_map/ppermute | solution.py:487
  20.0 5.1 %collective-permute-start.9 = (bf16[256,256]{1,0:T(8,128)(2,1)S(1)}, bf16[256,256]{1,0:T(8,128)(2,1)S(1)}, u32[]{:S(2)}, u32[]{:S(2)}) collective-permute-start(bf16[256,256]{1,0:T(8,128)(2,1)S(1)} %get-tuple-element.68), channel_id=1, source_target_pairs={{0,1},{1,0},{2,3},{3,2},{4,8},{5,9},{6,10},{7,11},{8,4},{9,5},{10,... | collective-permute-start | bytes 393224 | tf_op jit(solution)/shard_map/ppermute | solution.py:488
  25.6 2.1 %collective-permute-start.11 = (bf16[256,512]{1,0:T(8,128)(2,1)S(1)}, bf16[256,512]{1,0:T(8,128)(2,1)S(1)}, u32[]{:S(2)}, u32[]{:S(2)}) collective-permute-start(bf16[256,512]{1,0:T(8,128)(2,1)S(1)} %get-tuple-element.70.own_ref), channel_id=1, source_target_pairs={{0,1},{1,0},{2,3},{3,2},{4,5},{5,4},{6,7},{7,6},{8,9},{9,8},{10,11... | collective-permute-start | bytes 786440 | tf_op jit(solution)/shard_map/ppermute | solution.py:510
  26.6 13.5 %collective-permute-start.10 = (bf16[256,512]{1,0:T(8,128)(2,1)S(1)}, bf16[256,512]{1,0:T(8,128)(2,1)S(1)}, u32[]{:S(2)}, u32[]{:S(2)}) collective-permute-start(bf16[256,512]{1,0:T(8,128)(2,1)S(1)} %get-tuple-element.70.own_ref), channel_id=1, source_target_pairs={{0,2},{1,3},{2,0},{3,1},{4,6},{5,7},{6,4},{7,5},{8,10},{9,11},{10,... | collective-permute-start | bytes 786440 | tf_op jit(solution)/shard_map/ppermute | solution.py:511
  27.7 8.5 %collective-permute-start.12 = (bf16[256,512]{1,0:T(8,128)(2,1)S(1)}, bf16[256,512]{1,0:T(8,128)(2,1)S(1)}, u32[]{:S(2)}, u32[]{:S(2)}) collective-permute-start(bf16[256,512]{1,0:T(8,128)(2,1)S(1)} %get-tuple-element.70.own_ref), channel_id=1, source_target_pairs={{0,1},{1,0},{2,4},{3,5},{4,2},{5,3},{6,8},{7,9},{8,6},{9,7},{10,12... | collective-permute-start | bytes 786440 | tf_op jit(solution)/shard_map/ppermute | solution.py:513
  36.2 6.9 %copy-start.6 = (bf16[2048,512]{1,0:T(8,128)(2,1)S(1)}, bf16[2048,512]{1,0:T(8,128)(2,1)}, u32[]{:S(2)}) copy-start(bf16[2048,512]{1,0:T(8,128)(2,1)} %down_ref.1) | copy-start | bytes 6291460
  38.2 4.9 %copy-start.5 = (bf16[512,2048]{1,0:T(8,128)(2,1)S(1)}, bf16[512,2048]{1,0:T(8,128)(2,1)}, u32[]{:S(2)}) copy-start(bf16[512,2048]{1,0:T(8,128)(2,1)} %up_ref.1) | copy-start | bytes 6291460
  38.2 4.9 %copy-start.7 = (bf16[512,512]{1,0:T(8,128)(2,1)S(1)}, bf16[512,512]{1,0:T(8,128)(2,1)}, u32[]{:S(2)}) copy-start(bf16[512,512]{1,0:T(8,128)(2,1)} %w_out_ref.1) | copy-start | bytes 1572868
  38.2 4.9 %copy-start.8 = (f32[512]{0:T(512)S(1)}, f32[512]{0:T(512)}, u32[]{:S(2)}) copy-start(f32[512]{0:T(512)} %param.25) | copy-start | bytes 6148
  40.1 3.0 %collective-permute-start.13 = (bf16[256,512]{1,0:T(8,128)(2,1)S(1)}, bf16[256,512]{1,0:T(8,128)(2,1)S(1)}, u32[]{:S(2)}, u32[]{:S(2)}) collective-permute-start(bf16[256,512]{1,0:T(8,128)(2,1)S(1)} %collective-permute-done.10.block_ref), channel_id=1, source_target_pairs={{0,1},{1,0},{2,3},{3,2},{4,5},{5,4},{6,7},{7,6},{8,9},{9,8},{10,11... | collective-permute-start | bytes 786440 | tf_op jit(solution)/shard_map/ppermute | solution.py:560
  40.9 2.2 %collective-permute-start.14 = (bf16[256,512]{1,0:T(8,128)(2,1)S(1)}, bf16[256,512]{1,0:T(8,128)(2,1)S(1)}, u32[]{:S(2)}, u32[]{:S(2)}) collective-permute-start(bf16[256,512]{1,0:T(8,128)(2,1)S(1)} %collective-permute-done.12.block_ref), channel_id=1, source_target_pairs={{0,1},{1,0},{2,3},{3,2},{4,5},{5,4},{6,7},{7,6},{8,9},{9,8},{10,11... | collective-permute-start | bytes 786440 | tf_op jit(solution)/shard_map/ppermute | solution.py:557
  (1 other events, 1.0 us)

commit v17 on v16

--- a/solution.py
+++ b/solution.py
@@ -509,7 +509,6 @@
 
     side = lax.ppermute(normed, NODES, beside)
     even = lax.ppermute(normed, NODES, chips_trade(0))
-    side, normed = lax.optimization_barrier((side, normed))
     odd = lax.ppermute(normed, NODES, chips_trade(1))
 
     extra = head_dim + 16

time: 47.8 us -> 48.6 us (1.017)
  waiting for transfers between devices: 12.2 us -> 13.7 us
  Pallas kernels: 21.1 us -> 20.4 us
    ppermute x1, waiting for transfers between devices: 1.86 us -> 4.06 us  [local(): even = lax.ppermute(normed, NODES, chips_trade(0))]
    pallas_call x2, Pallas kernels: 4.12 us -> 3.37 us  [outer(): pl.pallas_call(functools.partial(outer_kernel, by_pair), out_shape=[jax.S...]
    ppermute x1, waiting for transfers between devices: 0.73 us -> 0.04 us  [local(): side = lax.ppermute(normed, NODES, beside)]
  transfers between devices with their start and end apart: 15 -> 15, of which waited for: 9 -> 8; matrix products, arithmetic and copies ran while one was open for 1% -> 1% of each run, Pallas kernels for 23% -> 21%
where the time goes in v17:
time: 48.6 us; the launch traced here: 48 us
  Pallas kernels  20.4 us (42%)
  waiting for transfers between devices  13.7 us (28%)
  starting transfers between devices  12.3 us (25%)
  local copies, waits for them, and re-layouts  1.02 us (2%)
    pallas_call x1, Pallas kernels, local(): pl.pallas_call(functools.partial(message_kernel, pairs), out_shape=outgoi...  5.22 us
    pallas_call x1, Pallas kernels, local(): pl.pallas_call(near_kernel, out_shape=[jax.ShapeDtypeStruct((HEADS, LANES...  4.85 us
    pallas_call x1, Pallas kernels, local(): pl.pallas_call(far_kernel, out_shape=jax.ShapeDtypeStruct((nodes, width),...  4.41 us
    ppermute x1, waiting for transfers between devices, local(): even = lax.ppermute(normed, NODES, chips_trade(0))  4.06 us
    pallas_call x2, Pallas kernels, outer(): pl.pallas_call(functools.partial(outer_kernel, by_pair), out_shape=[jax.S...  3.37 us
    ppermute x1, waiting for transfers between devices, local(): odd = lax.ppermute(normed, NODES, chips_trade(1))  2.82 us
    ppermute x1, waiting for transfers between devices, local(): lax.ppermute(part, NODES, chip_trade(p + 1))  2.78 us
    ppermute x1, starting transfers between devices, local(): odd = lax.ppermute(odd, NODES, bands_trade(1))  2.41 us
  transfers between devices with their start and end apart: 15, of which 8 were waited for; matrix products, arithmetic and copies ran while one was open for 1% of the time, Pallas kernels for 21%

profile of v17, /device:TPU:15, one launch (start us, length us, event | category | flops | bytes accessed | tf_op | source)
XLA Modules:
  0.0 48.0 jit_solution(9840268260452339137)
XLA Ops:
  0.0 5.2 %messages.1 = (bf16[272,256]{1,0:T(8,128)(2,1)}, bf16[272,256]{1,0:T(8,128)(2,1)}, bf16[272,256]{1,0:T(8,128)(2,1)}, bf16[272,256]{1,0:T(8,128)(2,1)}, bf16[400,...) custom-call(bf16[1024,512]{1,0:T(8,128)(2,1)} %grid_ref.1, ...), custom_call_target="tpu_custom_call" | custom-call | flops 2147483648 | bytes 4194304 | tf_op jit(solution)/shard_map/messages/pallas_call | solution.py:408
  5.2 0.7 %collective-permute-start.1 = (bf16[672,256]{1,0:T(8,128)(2,1)}, bf16[672,256]{1,0:T(8,128)(2,1)S(1)}, u32[]{:S(2)}, u32[]{:S(2)}) collective-permute-start(bf16[672,256]{1,0:T(8,128)(2,1)} %get-tuple-element.46), channel_id=1, source_target_pairs={{0,1},{1,0},{2,3},{3,2},{4,5},{5,4},{6,7},{7,6},{8,9},{9,8},{10,11... | collective-permute-start | bytes 1032200 | tf_op jit(solution)/shard_map/ppermute | solution.py:443
  6.4 2.4 %collective-permute-start.3 = (bf16[272,256]{1,0:T(8,128)(2,1)}, bf16[272,256]{1,0:T(8,128)(2,1)S(1)}, u32[]{:S(2)}, u32[]{:S(2)}) collective-permute-start(bf16[272,256]{1,0:T(8,128)(2,1)} %get-tuple-element.51), channel_id=1, source_target_pairs={{0,1},{1,0},{2,3},{3,2},{4,8},{5,9},{6,10},{7,11},{8,4},{9,5},{10,... | collective-permute-start | bytes 417800 | tf_op jit(solution)/shard_map/ppermute | solution.py:446
  9.0 2.1 %collective-permute-start.7 = (bf16[400,256]{1,0:T(8,128)(2,1)}, bf16[400,256]{1,0:T(8,128)(2,1)S(1)}, u32[]{:S(2)}, u32[]{:S(2)}) collective-permute-start(bf16[400,256]{1,0:T(8,128)(2,1)} %get-tuple-element.62), channel_id=1, source_target_pairs={{0,3},{1,2},{2,1},{3,0},{4,7},{5,6},{6,5},{7,4},{8,11},{9,10},{10,... | collective-permute-start | bytes 614408 | tf_op jit(solution)/shard_map/ppermute | solution.py:450
  11.4 2.3 %collective-permute-start.4 = (bf16[272,256]{1,0:T(8,128)(2,1)}, bf16[272,256]{1,0:T(8,128)(2,1)S(1)}, u32[]{:S(2)}, u32[]{:S(2)}) collective-permute-start(bf16[272,256]{1,0:T(8,128)(2,1)} %get-tuple-element.52), channel_id=1, source_target_pairs={{0,1},{1,0},{2,3},{3,2},{4,9},{5,8},{6,11},{7,10},{8,5},{9,4},{10,... | collective-permute-start | bytes 417800 | tf_op jit(solution)/shard_map/ppermute | solution.py:452
  13.9 1.0 %copy-done.2 = bf16[672,256]{1,0:T(8,128)(2,1)S(1)} copy-done((bf16[672,256]{1,0:T(8,128)(2,1)S(1)}, bf16[672,256]{1,0:T(8,128)(2,1)}, u32[]{:S(2)}) %copy-start.2) | copy-done | bytes 344088
  14.8 1.5 %early.1 = (bf16[512,512]{1,0:T(8,128)(2,1)S(1)}, bf16[512,512]{1,0:T(8,128)(2,1)S(1)}, bf16[512,512]{1,0:T(8,128)(2,1)S(1)}, f32[2,256,256]{2,1,0:T(8,128)S(1)}, f32[3,256,256]{2,1,0:T(8,128)S(1)}) custom-call(bf16[512,1536]{1,0:T(8,128)(2,1)S(1)} %copy-done, bf16[672,256]{1,0:T(8,128)(2,1)S(1)} %copy-done.2, ...), custom_call_target="tpu_custom_call" | custom-call | flops 268435456 | bytes 4194304 | tf_op jit(solution)/shard_map/early/pallas_call | solution.py:462
  16.5 1.7 %collective-permute-done.4.refs_3_ = bf16[272,256]{1,0:T(8,128)(2,1)S(1)} collective-permute-done((bf16[272,256]{1,0:T(8,128)(2,1)}, bf16[272,256]{1,0:T(8,128)(2,1)S(1)}, u32[]{:S(2)}, u32[]{:S(2)}) %collective-permute-start.4) | collective-permute-done | bytes 139296 | tf_op jit(solution)/shard_map/ppermute | solution.py:452
  18.2 0.3 left.1
  18.5 1.1 %collective-permute-start.5 = (bf16[256,256]{1,0:T(8,128)(2,1)S(1)}, bf16[256,256]{1,0:T(8,128)(2,1)S(1)}, u32[]{:S(2)}, u32[]{:S(2)}) collective-permute-start(bf16[256,256]{1,0:T(8,128)(2,1)S(1)} %get-tuple-element.60), channel_id=1, source_target_pairs={{0,2},{1,3},{2,0},{3,1},{4,6},{5,7},{6,4},{7,5},{8,10},{9,11},{10,... | collective-permute-start | bytes 393224 | tf_op jit(solution)/shard_map/ppermute | solution.py:485
  20.0 0.5 %collective-permute-start.9 = (bf16[256,256]{1,0:T(8,128)(2,1)S(1)}, bf16[256,256]{1,0:T(8,128)(2,1)S(1)}, u32[]{:S(2)}, u32[]{:S(2)}) collective-permute-start(bf16[256,256]{1,0:T(8,128)(2,1)S(1)} %get-tuple-element.66), channel_id=1, source_target_pairs={{0,1},{1,0},{2,3},{3,2},{4,8},{5,9},{6,10},{7,11},{8,4},{9,5},{10,... | collective-permute-start | bytes 393224 | tf_op jit(solution)/shard_map/ppermute | solution.py:488
  20.5 2.8 %collective-permute-done.5.refs_1_ = bf16[256,256]{1,0:T(8,128)(2,1)S(1)} collective-permute-done((bf16[256,256]{1,0:T(8,128)(2,1)S(1)}, bf16[256,256]{1,0:T(8,128)(2,1)S(1)}, u32[]{:S(2)}, u32[]{:S(2)}) %collective-permute-start.5) | collective-permute-done | bytes 131104 | tf_op jit(solution)/shard_map/ppermute | solution.py:485
  23.3 1.8 %collective-permute-done.8.refs_3_ = bf16[256,256]{1,0:T(8,128)(2,1)S(1)} collective-permute-done((bf16[256,256]{1,0:T(8,128)(2,1)S(1)}, bf16[256,256]{1,0:T(8,128)(2,1)S(1)}, u32[]{:S(2)}, u32[]{:S(2)}) %collective-permute-start.8) | collective-permute-done | bytes 131104 | tf_op jit(solution)/shard_map/ppermute | solution.py:487
  25.1 0.5 %merge.1 = (f32[256,512]{1,0:T(8,128)S(1)}, bf16[256,512]{1,0:T(8,128)(2,1)S(1)}) custom-call(f32[256,256]{1,0:T(8,128)S(1)} %get-tuple-element.59.refs_0_, bf16[256,256]{1,0:T(8,128)(2,1)S(1)} %collective-permute-done.5.refs_1_, f32[256,256]{1,0:T(8,128)S(1)} %get-tuple-element.64.refs_2_, bf16[256,256]{1,0:T(8,128)(2,1)S(1)} %collective-permute-done.8.refs_3_, ...), custom_call_target="tpu_custom_call" | custom-call | flops 134217728 | bytes 2097152 | tf_op jit(solution)/shard_map/merge/pallas_call | solution.py:490
  25.6 0.9 %collective-permute-start.12 = (bf16[256,512]{1,0:T(8,128)(2,1)S(1)}, bf16[256,512]{1,0:T(8,128)(2,1)S(1)}, u32[]{:S(2)}, u32[]{:S(2)}) collective-permute-start(bf16[256,512]{1,0:T(8,128)(2,1)S(1)} %get-tuple-element.67.own_ref), channel_id=1, source_target_pairs={{0,1},{1,0},{2,3},{3,2},{4,5},{5,4},{6,7},{7,6},{8,9},{9,8},{10,11... | collective-permute-start | bytes 786440 | tf_op jit(solution)/shard_map/ppermute | solution.py:510
  26.6 0.8 %collective-permute-start.11 = (bf16[256,512]{1,0:T(8,128)(2,1)S(1)}, bf16[256,512]{1,0:T(8,128)(2,1)S(1)}, u32[]{:S(2)}, u32[]{:S(2)}) collective-permute-start(bf16[256,512]{1,0:T(8,128)(2,1)S(1)} %get-tuple-element.67.own_ref), channel_id=1, source_target_pairs={{0,1},{1,0},{2,4},{3,5},{4,2},{5,3},{6,8},{7,9},{8,6},{9,7},{10,12... | collective-permute-start | bytes 786440 | tf_op jit(solution)/shard_map/ppermute | solution.py:512
  27.4 0.3 collective-permute-start.10
  27.7 4.8 %near.1 = (bf16[16,128,256]{2,1,0:T(8,128)(2,1)S(1)}, f32[16,48,256]{2,1,0:T(8,128)S(1)}, f32[16,8,256]{2,1,0:T(8,128)S(1)}) custom-call(bf16[256,512]{1,0:T(8,128)(2,1)S(1)} %get-tuple-element.67.own_ref, bf16[256,512]{1,0:T(8,128)(2,1)S(1)} %collective-permute-done.12.side_ref, bf16[512,512]{1,0:T(8,128)(2,1)S(1)} %get-tuple-element.68.wq_ref, ...), custom_call_target="tpu_custom_call" | custom-call | flops 8589934592 | bytes 4194304 | tf_op jit(solution)/shard_map/near/pallas_call | solution.py:515
  32.6 2.8 %collective-permute-done.11.block_ref = bf16[256,512]{1,0:T(8,128)(2,1)S(1)} collective-permute-done((bf16[256,512]{1,0:T(8,128)(2,1)S(1)}, bf16[256,512]{1,0:T(8,128)(2,1)S(1)}, u32[]{:S(2)}, u32[]{:S(2)}) %collective-permute-start.11) | collective-permute-done | bytes 262176 | tf_op jit(solution)/shard_map/ppermute | solution.py:512
  35.4 1.6 %other.1 = (f32[16,48,256]{2,1,0:T(8,128)S(1)}, f32[16,8,256]{2,1,0:T(8,128)S(1)}) custom-call(bf16[256,512]{1,0:T(8,128)(2,1)S(1)} %collective-permute-done.11.block_ref, bf16[512,512]{1,0:T(8,128)(2,1)S(1)} %get-tuple-element.69.wk_ref, bf16[512,512]{1,0:T(8,128)(2,1)S(1)} %get-tuple-element.70.wv_ref, s32[2,16]{1,0:T(2,128)S(1)} %select_reduce_fusion.plan_ref.plan_in, ...), custom_call_target="tpu_custom_call" | custom-call | flops 536870912 | bytes 3145728 | tf_op jit(solution)/shard_map/other/pallas_call | solution.py:535
  37.0 4.1 %collective-permute-done.10.block_ref = bf16[256,512]{1,0:T(8,128)(2,1)S(1)} collective-permute-done((bf16[256,512]{1,0:T(8,128)(2,1)S(1)}, bf16[256,512]{1,0:T(8,128)(2,1)S(1)}, u32[]{:S(2)}, u32[]{:S(2)}) %collective-permute-start.10) | collective-permute-done | bytes 262176 | tf_op jit(solution)/shard_map/ppermute | solution.py:511
  41.1 0.6 %collective-permute-start.13 = (bf16[256,512]{1,0:T(8,128)(2,1)S(1)}, bf16[256,512]{1,0:T(8,128)(2,1)S(1)}, u32[]{:S(2)}, u32[]{:S(2)}) collective-permute-start(bf16[256,512]{1,0:T(8,128)(2,1)S(1)} %collective-permute-done.10.block_ref), channel_id=1, source_target_pairs={{0,1},{1,0},{2,3},{3,2},{4,5},{5,4},{6,7},{7,6},{8,9},{9,8},{10,11... | collective-permute-start | bytes 786440 | tf_op jit(solution)/shard_map/ppermute | solution.py:559
  41.7 1.8 %pair.1 = (f32[16,48,256]{2,1,0:T(8,128)S(1)}, f32[16,8,256]{2,1,0:T(8,128)S(1)}) custom-call(bf16[256,512]{1,0:T(8,128)(2,1)S(1)} %collective-permute-done.10.block_ref, bf16[512,512]{1,0:T(8,128)(2,1)S(1)} %get-tuple-element.69.wk_ref, bf16[512,512]{1,0:T(8,128)(2,1)S(1)} %get-tuple-element.70.wv_ref, s32[2,16]{1,0:T(2,128)S(1)} %select_reduce_fusion.plan_ref.plan_in, ...), custom_call_target="tpu_custom_call" | custom-call | flops 536870912 | bytes 3145728 | tf_op jit(solution)/shard_map/pair/pallas_call | solution.py:535
  43.5 4.4 %far.1 = bf16[256,512]{1,0:T(8,128)(2,1)} custom-call(bf16[256,512]{1,0:T(8,128)(2,1)S(1)} %collective-permute-done.13.first_ref, bf16[256,512]{1,0:T(8,128)(2,1)S(1)} %collective-permute-done.14.second_ref, bf16[512,512]{1,0:T(8,128)(2,1)S(1)} %get-tuple-element.69.wk_ref, bf16[512,512]{1,0:T(8,128)(2,1)S(1)} %get-tuple-element.70.wv_ref, ...), custom_call_target="tpu_custom_call" | custom-call | flops 8589934592 | bytes 8388608 | tf_op jit(solution)/shard_map/far/pallas_call | solution.py:562
  (40 shorter events, 1.7 us)
Async XLA Ops:
  0.0 8.8 %copy-start.9 = (s32[16]{0:T(128)S(1)}, s32[16]{0:T(128)}, u32[]{:S(2)}) copy-start(s32[16]{0:T(128)} %param.23) | copy-start | bytes 196
  0.0 13.8 %copy-start = (bf16[512,1536]{1,0:T(8,128)(2,1)S(1)}, bf16[512,1536]{1,0:T(8,128)(2,1)}, u32[]{:S(2)}) copy-start(bf16[512,1536]{1,0:T(8,128)(2,1)} %w_ref.2) | copy-start | bytes 4718596
  5.2 3.8 %collective-permute-start.1 = (bf16[672,256]{1,0:T(8,128)(2,1)}, bf16[672,256]{1,0:T(8,128)(2,1)S(1)}, u32[]{:S(2)}, u32[]{:S(2)}) collective-permute-start(bf16[672,256]{1,0:T(8,128)(2,1)} %get-tuple-element.46), channel_id=1, source_target_pairs={{0,1},{1,0},{2,3},{3,2},{4,5},{5,4},{6,7},{7,6},{8,9},{9,8},{10,11... | collective-permute-start | bytes 1032200 | tf_op jit(solution)/shard_map/ppermute | solution.py:443
  6.0 13.7 %collective-permute-start.6 = (bf16[400,256]{1,0:T(8,128)(2,1)}, bf16[400,256]{1,0:T(8,128)(2,1)S(1)}, u32[]{:S(2)}, u32[]{:S(2)}) collective-permute-start(bf16[400,256]{1,0:T(8,128)(2,1)} %get-tuple-element.61), channel_id=1, source_target_pairs={{0,2},{1,3},{2,0},{3,1},{4,6},{5,7},{6,4},{7,5},{8,10},{9,11},{10,... | collective-permute-start | bytes 614408 | tf_op jit(solution)/shard_map/ppermute | solution.py:444
  6.2 5.1 %collective-permute-start = (bf16[272,256]{1,0:T(8,128)(2,1)}, bf16[272,256]{1,0:T(8,128)(2,1)S(1)}, u32[]{:S(2)}, u32[]{:S(2)}) collective-permute-start(bf16[272,256]{1,0:T(8,128)(2,1)} %get-tuple-element.45), channel_id=1, source_target_pairs={{0,4},{1,5},{2,6},{3,7},{4,0},{5,1},{6,2},{7,3},{8,12},{9,13},{10,... | collective-permute-start | bytes 417800 | tf_op jit(solution)/shard_map/ppermute | solution.py:445
  6.4 9.9 %collective-permute-start.3 = (bf16[272,256]{1,0:T(8,128)(2,1)}, bf16[272,256]{1,0:T(8,128)(2,1)S(1)}, u32[]{:S(2)}, u32[]{:S(2)}) collective-permute-start(bf16[272,256]{1,0:T(8,128)(2,1)} %get-tuple-element.51), channel_id=1, source_target_pairs={{0,1},{1,0},{2,3},{3,2},{4,8},{5,9},{6,10},{7,11},{8,4},{9,5},{10,... | collective-permute-start | bytes 417800 | tf_op jit(solution)/shard_map/ppermute | solution.py:446
  9.0 10.6 %collective-permute-start.7 = (bf16[400,256]{1,0:T(8,128)(2,1)}, bf16[400,256]{1,0:T(8,128)(2,1)S(1)}, u32[]{:S(2)}, u32[]{:S(2)}) collective-permute-start(bf16[400,256]{1,0:T(8,128)(2,1)} %get-tuple-element.62), channel_id=1, source_target_pairs={{0,3},{1,2},{2,1},{3,0},{4,7},{5,6},{6,5},{7,4},{8,11},{9,10},{10,... | collective-permute-start | bytes 614408 | tf_op jit(solution)/shard_map/ppermute | solution.py:450
  11.1 5.4 %collective-permute-start.2 = (bf16[272,256]{1,0:T(8,128)(2,1)}, bf16[272,256]{1,0:T(8,128)(2,1)S(1)}, u32[]{:S(2)}, u32[]{:S(2)}) collective-permute-start(bf16[272,256]{1,0:T(8,128)(2,1)} %get-tuple-element.50), channel_id=1, source_target_pairs={{0,5},{1,4},{2,7},{3,6},{4,1},{5,0},{6,3},{7,2},{8,13},{9,12},{10,... | collective-permute-start | bytes 417800 | tf_op jit(solution)/shard_map/ppermute | solution.py:451
  11.4 6.8 %collective-permute-start.4 = (bf16[272,256]{1,0:T(8,128)(2,1)}, bf16[272,256]{1,0:T(8,128)(2,1)S(1)}, u32[]{:S(2)}, u32[]{:S(2)}) collective-permute-start(bf16[272,256]{1,0:T(8,128)(2,1)} %get-tuple-element.52), channel_id=1, source_target_pairs={{0,1},{1,0},{2,3},{3,2},{4,9},{5,8},{6,11},{7,10},{8,5},{9,4},{10,... | collective-permute-start | bytes 417800 | tf_op jit(solution)/shard_map/ppermute | solution.py:452
  14.8 10.3 %copy-start.1 = (bf16[512,512]{1,0:T(8,128)(2,1)S(1)}, bf16[512,512]{1,0:T(8,128)(2,1)}, u32[]{:S(2)}) copy-start(bf16[512,512]{1,0:T(8,128)(2,1)} %refs_6_.1) | copy-start | bytes 1572868
  14.8 10.3 %copy-start.3 = (bf16[256,512]{1,0:T(8,128)(2,1)S(1)}, bf16[256,512]{1,0:T(8,128)(2,1)}, u32[]{:S(2)}) copy-start(bf16[256,512]{1,0:T(8,128)(2,1)} %refs_5_.1) | copy-start | bytes 786436
  14.8 10.3 %copy-start.4 = (f32[512]{0:T(512)S(1)}, f32[512]{0:T(512)}, u32[]{:S(2)}) copy-start(f32[512]{0:T(512)} %param.21) | copy-start | bytes 6148
  18.5 4.7 %collective-permute-start.5 = (bf16[256,256]{1,0:T(8,128)(2,1)S(1)}, bf16[256,256]{1,0:T(8,128)(2,1)S(1)}, u32[]{:S(2)}, u32[]{:S(2)}) collective-permute-start(bf16[256,256]{1,0:T(8,128)(2,1)S(1)} %get-tuple-element.60), channel_id=1, source_target_pairs={{0,2},{1,3},{2,0},{3,1},{4,6},{5,7},{6,4},{7,5},{8,10},{9,11},{10,... | collective-permute-start | bytes 393224 | tf_op jit(solution)/shard_map/ppermute | solution.py:485
  19.9 5.1 %collective-permute-start.8 = (bf16[256,256]{1,0:T(8,128)(2,1)S(1)}, bf16[256,256]{1,0:T(8,128)(2,1)S(1)}, u32[]{:S(2)}, u32[]{:S(2)}) collective-permute-start(bf16[256,256]{1,0:T(8,128)(2,1)S(1)} %get-tuple-element.65), channel_id=1, source_target_pairs={{0,4},{1,5},{2,6},{3,7},{4,0},{5,1},{6,2},{7,3},{8,12},{9,13},{10,... | collective-permute-start | bytes 393224 | tf_op jit(solution)/shard_map/ppermute | solution.py:487
  20.0 5.1 %collective-permute-start.9 = (bf16[256,256]{1,0:T(8,128)(2,1)S(1)}, bf16[256,256]{1,0:T(8,128)(2,1)S(1)}, u32[]{:S(2)}, u32[]{:S(2)}) collective-permute-start(bf16[256,256]{1,0:T(8,128)(2,1)S(1)} %get-tuple-element.66), channel_id=1, source_target_pairs={{0,1},{1,0},{2,3},{3,2},{4,8},{5,9},{6,10},{7,11},{8,4},{9,5},{10,... | collective-permute-start | bytes 393224 | tf_op jit(solution)/shard_map/ppermute | solution.py:488
  25.6 2.1 %collective-permute-start.12 = (bf16[256,512]{1,0:T(8,128)(2,1)S(1)}, bf16[256,512]{1,0:T(8,128)(2,1)S(1)}, u32[]{:S(2)}, u32[]{:S(2)}) collective-permute-start(bf16[256,512]{1,0:T(8,128)(2,1)S(1)} %get-tuple-element.67.own_ref), channel_id=1, source_target_pairs={{0,1},{1,0},{2,3},{3,2},{4,5},{5,4},{6,7},{7,6},{8,9},{9,8},{10,11... | collective-permute-start | bytes 786440 | tf_op jit(solution)/shard_map/ppermute | solution.py:510
  26.6 8.8 %collective-permute-start.11 = (bf16[256,512]{1,0:T(8,128)(2,1)S(1)}, bf16[256,512]{1,0:T(8,128)(2,1)S(1)}, u32[]{:S(2)}, u32[]{:S(2)}) collective-permute-start(bf16[256,512]{1,0:T(8,128)(2,1)S(1)} %get-tuple-element.67.own_ref), channel_id=1, source_target_pairs={{0,1},{1,0},{2,4},{3,5},{4,2},{5,3},{6,8},{7,9},{8,6},{9,7},{10,12... | collective-permute-start | bytes 786440 | tf_op jit(solution)/shard_map/ppermute | solution.py:512
  27.4 13.7 %collective-permute-start.10 = (bf16[256,512]{1,0:T(8,128)(2,1)S(1)}, bf16[256,512]{1,0:T(8,128)(2,1)S(1)}, u32[]{:S(2)}, u32[]{:S(2)}) collective-permute-start(bf16[256,512]{1,0:T(8,128)(2,1)S(1)} %get-tuple-element.67.own_ref), channel_id=1, source_target_pairs={{0,2},{1,3},{2,0},{3,1},{4,6},{5,7},{6,4},{7,5},{8,10},{9,11},{10,... | collective-permute-start | bytes 786440 | tf_op jit(solution)/shard_map/ppermute | solution.py:511
  35.4 8.1 %copy-start.6 = (bf16[2048,512]{1,0:T(8,128)(2,1)S(1)}, bf16[2048,512]{1,0:T(8,128)(2,1)}, u32[]{:S(2)}) copy-start(bf16[2048,512]{1,0:T(8,128)(2,1)} %down_ref.1) | copy-start | bytes 6291460
  37.0 6.5 %copy-start.5 = (bf16[512,2048]{1,0:T(8,128)(2,1)S(1)}, bf16[512,2048]{1,0:T(8,128)(2,1)}, u32[]{:S(2)}) copy-start(bf16[512,2048]{1,0:T(8,128)(2,1)} %up_ref.1) | copy-start | bytes 6291460
  37.0 6.5 %copy-start.7 = (bf16[512,512]{1,0:T(8,128)(2,1)S(1)}, bf16[512,512]{1,0:T(8,128)(2,1)}, u32[]{:S(2)}) copy-start(bf16[512,512]{1,0:T(8,128)(2,1)} %w_out_ref.1) | copy-start | bytes 1572868
  37.0 6.5 %copy-start.8 = (f32[512]{0:T(512)S(1)}, f32[512]{0:T(512)}, u32[]{:S(2)}) copy-start(f32[512]{0:T(512)} %param.25) | copy-start | bytes 6148
  41.1 2.4 %collective-permute-start.13 = (bf16[256,512]{1,0:T(8,128)(2,1)S(1)}, bf16[256,512]{1,0:T(8,128)(2,1)S(1)}, u32[]{:S(2)}, u32[]{:S(2)}) collective-permute-start(bf16[256,512]{1,0:T(8,128)(2,1)S(1)} %collective-permute-done.10.block_ref), channel_id=1, source_target_pairs={{0,1},{1,0},{2,3},{3,2},{4,5},{5,4},{6,7},{7,6},{8,9},{9,8},{10,11... | collective-permute-start | bytes 786440 | tf_op jit(solution)/shard_map/ppermute | solution.py:559
  41.7 1.8 %collective-permute-start.14 = (bf16[256,512]{1,0:T(8,128)(2,1)S(1)}, bf16[256,512]{1,0:T(8,128)(2,1)S(1)}, u32[]{:S(2)}, u32[]{:S(2)}) collective-permute-start(bf16[256,512]{1,0:T(8,128)(2,1)S(1)} %collective-permute-done.11.block_ref), channel_id=1, source_target_pairs={{0,1},{1,0},{2,3},{3,2},{4,5},{5,4},{6,7},{7,6},{8,9},{9,8},{10,11... | collective-permute-start | bytes 786440 | tf_op jit(solution)/shard_map/ppermute | solution.py:556
  (1 other events, 1.0 us)

commit v18 on v16

--- a/solution.py
+++ b/solution.py
@@ -556,7 +556,7 @@
     odd, near, top = lax.optimization_barrier((odd, near, top))
     second = lax.ppermute(odd, NODES, beside)
     near, top = outer(False, odd, near, top)
-    even, near, top = lax.optimization_barrier((even, near, top))
+    even, second, near, top = lax.optimization_barrier((even, second, near, top))
     first = lax.ppermute(even, NODES, beside)
     near, top = outer(True, even, near, top)
 

time: 47.8 us -> 47.7 us (level)
  waiting for transfers between devices: 12.2 us -> 10.7 us
  starting transfers between devices: 12.7 us -> 14 us
    ppermute x1, waiting for transfers between devices: 1.86 us -> 0.6 us  [local(): even = lax.ppermute(normed, NODES, chips_trade(0))]
    ppermute x1, starting transfers between devices: 0.01 us -> 1.26 us  [local(): second = lax.ppermute(odd, NODES, beside)]
  transfers between devices with their start and end apart: 15 -> 15, of which waited for: 9 -> 9; matrix products, arithmetic and copies ran while one was open for 1% -> 1% of each run, Pallas kernels for 23% -> 24%
where the time goes in v18:
time: 47.7 us; the launch traced here: 47.5 us
  Pallas kernels  21.3 us (45%)
  starting transfers between devices  14 us (29%)
  waiting for transfers between devices  10.7 us (22%)
  local copies, waits for them, and re-layouts  1.02 us (2%)
    pallas_call x1, Pallas kernels, local(): pl.pallas_call(functools.partial(message_kernel, pairs), out_shape=outgoi...  5.22 us
    pallas_call x1, Pallas kernels, local(): pl.pallas_call(near_kernel, out_shape=[jax.ShapeDtypeStruct((HEADS, LANES...  5 us
    pallas_call x1, Pallas kernels, local(): pl.pallas_call(far_kernel, out_shape=jax.ShapeDtypeStruct((nodes, width),...  4.4 us
    pallas_call x2, Pallas kernels, outer(): pl.pallas_call(functools.partial(outer_kernel, by_pair), out_shape=[jax.S...  4.12 us
    ppermute x1, waiting for transfers between devices, local(): lax.ppermute(part, NODES, chip_trade(p + 1))  2.78 us
    ppermute x1, waiting for transfers between devices, local(): odd = lax.ppermute(normed, NODES, chips_trade(1))  2.6 us
    ppermute x1, starting transfers between devices, local(): odd = lax.ppermute(odd, NODES, bands_trade(1))  2.41 us
    ppermute x1, starting transfers between devices, local(): odd_other = lax.ppermute(odd_other, NODES, bands_trade(1, 1))  2.35 us
  transfers between devices with their start and end apart: 15, of which 9 were waited for; matrix products, arithmetic and copies ran while one was open for 1% of the time, Pallas kernels for 24%

profile of v18, /device:TPU:15, one launch (start us, length us, event | category | flops | bytes accessed | tf_op | source)
XLA Modules:
  0.0 47.5 jit_solution(9994558917347114291)
XLA Ops:
  0.0 5.2 %messages.1 = (bf16[272,256]{1,0:T(8,128)(2,1)}, bf16[272,256]{1,0:T(8,128)(2,1)}, bf16[272,256]{1,0:T(8,128)(2,1)}, bf16[272,256]{1,0:T(8,128)(2,1)}, bf16[400,...) custom-call(bf16[1024,512]{1,0:T(8,128)(2,1)} %grid_ref.1, ...), custom_call_target="tpu_custom_call" | custom-call | flops 2147483648 | bytes 4194304 | tf_op jit(solution)/shard_map/messages/pallas_call | solution.py:408
  5.2 0.7 %collective-permute-start.1 = (bf16[672,256]{1,0:T(8,128)(2,1)}, bf16[672,256]{1,0:T(8,128)(2,1)S(1)}, u32[]{:S(2)}, u32[]{:S(2)}) collective-permute-start(bf16[672,256]{1,0:T(8,128)(2,1)} %get-tuple-element.49), channel_id=1, source_target_pairs={{0,1},{1,0},{2,3},{3,2},{4,5},{5,4},{6,7},{7,6},{8,9},{9,8},{10,11... | collective-permute-start | bytes 1032200 | tf_op jit(solution)/shard_map/ppermute | solution.py:443
  6.4 2.4 %collective-permute-start.3 = (bf16[272,256]{1,0:T(8,128)(2,1)}, bf16[272,256]{1,0:T(8,128)(2,1)S(1)}, u32[]{:S(2)}, u32[]{:S(2)}) collective-permute-start(bf16[272,256]{1,0:T(8,128)(2,1)} %get-tuple-element.54), channel_id=1, source_target_pairs={{0,1},{1,0},{2,3},{3,2},{4,8},{5,9},{6,10},{7,11},{8,4},{9,5},{10,... | collective-permute-start | bytes 417800 | tf_op jit(solution)/shard_map/ppermute | solution.py:446
  9.0 2.1 %collective-permute-start.7 = (bf16[400,256]{1,0:T(8,128)(2,1)}, bf16[400,256]{1,0:T(8,128)(2,1)S(1)}, u32[]{:S(2)}, u32[]{:S(2)}) collective-permute-start(bf16[400,256]{1,0:T(8,128)(2,1)} %get-tuple-element.65), channel_id=1, source_target_pairs={{0,3},{1,2},{2,1},{3,0},{4,7},{5,6},{6,5},{7,4},{8,11},{9,10},{10,... | collective-permute-start | bytes 614408 | tf_op jit(solution)/shard_map/ppermute | solution.py:450
  11.4 2.3 %collective-permute-start.4 = (bf16[272,256]{1,0:T(8,128)(2,1)}, bf16[272,256]{1,0:T(8,128)(2,1)S(1)}, u32[]{:S(2)}, u32[]{:S(2)}) collective-permute-start(bf16[272,256]{1,0:T(8,128)(2,1)} %get-tuple-element.55), channel_id=1, source_target_pairs={{0,1},{1,0},{2,3},{3,2},{4,9},{5,8},{6,11},{7,10},{8,5},{9,4},{10,... | collective-permute-start | bytes 417800 | tf_op jit(solution)/shard_map/ppermute | solution.py:452
  13.9 1.0 %copy-done.2 = bf16[672,256]{1,0:T(8,128)(2,1)S(1)} copy-done((bf16[672,256]{1,0:T(8,128)(2,1)S(1)}, bf16[672,256]{1,0:T(8,128)(2,1)}, u32[]{:S(2)}) %copy-start.2) | copy-done | bytes 344088
  14.8 1.5 %early.1 = (bf16[512,512]{1,0:T(8,128)(2,1)S(1)}, bf16[512,512]{1,0:T(8,128)(2,1)S(1)}, bf16[512,512]{1,0:T(8,128)(2,1)S(1)}, f32[2,256,256]{2,1,0:T(8,128)S(1)}, f32[3,256,256]{2,1,0:T(8,128)S(1)}) custom-call(bf16[512,1536]{1,0:T(8,128)(2,1)S(1)} %copy-done, bf16[672,256]{1,0:T(8,128)(2,1)S(1)} %copy-done.2, ...), custom_call_target="tpu_custom_call" | custom-call | flops 268435456 | bytes 4194304 | tf_op jit(solution)/shard_map/early/pallas_call | solution.py:462
  16.5 1.7 %collective-permute-done.4.refs_3_ = bf16[272,256]{1,0:T(8,128)(2,1)S(1)} collective-permute-done((bf16[272,256]{1,0:T(8,128)(2,1)}, bf16[272,256]{1,0:T(8,128)(2,1)S(1)}, u32[]{:S(2)}, u32[]{:S(2)}) %collective-permute-start.4) | collective-permute-done | bytes 139296 | tf_op jit(solution)/shard_map/ppermute | solution.py:452
  18.5 1.1 %collective-permute-start.5 = (bf16[256,256]{1,0:T(8,128)(2,1)S(1)}, bf16[256,256]{1,0:T(8,128)(2,1)S(1)}, u32[]{:S(2)}, u32[]{:S(2)}) collective-permute-start(bf16[256,256]{1,0:T(8,128)(2,1)S(1)} %get-tuple-element.63), channel_id=1, source_target_pairs={{0,2},{1,3},{2,0},{3,1},{4,6},{5,7},{6,4},{7,5},{8,10},{9,11},{10,... | collective-permute-start | bytes 393224 | tf_op jit(solution)/shard_map/ppermute | solution.py:485
  20.0 0.5 %collective-permute-start.9 = (bf16[256,256]{1,0:T(8,128)(2,1)S(1)}, bf16[256,256]{1,0:T(8,128)(2,1)S(1)}, u32[]{:S(2)}, u32[]{:S(2)}) collective-permute-start(bf16[256,256]{1,0:T(8,128)(2,1)S(1)} %get-tuple-element.69), channel_id=1, source_target_pairs={{0,1},{1,0},{2,3},{3,2},{4,8},{5,9},{6,10},{7,11},{8,4},{9,5},{10,... | collective-permute-start | bytes 393224 | tf_op jit(solution)/shard_map/ppermute | solution.py:488
  20.5 2.8 %collective-permute-done.5.refs_1_ = bf16[256,256]{1,0:T(8,128)(2,1)S(1)} collective-permute-done((bf16[256,256]{1,0:T(8,128)(2,1)S(1)}, bf16[256,256]{1,0:T(8,128)(2,1)S(1)}, u32[]{:S(2)}, u32[]{:S(2)}) %collective-permute-start.5) | collective-permute-done | bytes 131104 | tf_op jit(solution)/shard_map/ppermute | solution.py:485
  23.3 1.8 %collective-permute-done.8.refs_3_ = bf16[256,256]{1,0:T(8,128)(2,1)S(1)} collective-permute-done((bf16[256,256]{1,0:T(8,128)(2,1)S(1)}, bf16[256,256]{1,0:T(8,128)(2,1)S(1)}, u32[]{:S(2)}, u32[]{:S(2)}) %collective-permute-start.8) | collective-permute-done | bytes 131104 | tf_op jit(solution)/shard_map/ppermute | solution.py:487
  25.1 0.5 %merge.1 = (f32[256,512]{1,0:T(8,128)S(1)}, bf16[256,512]{1,0:T(8,128)(2,1)S(1)}) custom-call(f32[256,256]{1,0:T(8,128)S(1)} %get-tuple-element.62.refs_0_, bf16[256,256]{1,0:T(8,128)(2,1)S(1)} %collective-permute-done.5.refs_1_, f32[256,256]{1,0:T(8,128)S(1)} %get-tuple-element.67.refs_2_, bf16[256,256]{1,0:T(8,128)(2,1)S(1)} %collective-permute-done.8.refs_3_, ...), custom_call_target="tpu_custom_call" | custom-call | flops 134217728 | bytes 2097152 | tf_op jit(solution)/shard_map/merge/pallas_call | solution.py:490
  25.6 0.9 %collective-permute-start.11 = (bf16[256,512]{1,0:T(8,128)(2,1)S(1)}, bf16[256,512]{1,0:T(8,128)(2,1)S(1)}, u32[]{:S(2)}, u32[]{:S(2)}) collective-permute-start(bf16[256,512]{1,0:T(8,128)(2,1)S(1)} %get-tuple-element.71.own_ref), channel_id=1, source_target_pairs={{0,1},{1,0},{2,3},{3,2},{4,5},{5,4},{6,7},{7,6},{8,9},{9,8},{10,11... | collective-permute-start | bytes 786440 | tf_op jit(solution)/shard_map/ppermute | solution.py:510
  27.0 0.7 %collective-permute-done.11.side_ref = bf16[256,512]{1,0:T(8,128)(2,1)S(1)} collective-permute-done((bf16[256,512]{1,0:T(8,128)(2,1)S(1)}, bf16[256,512]{1,0:T(8,128)(2,1)S(1)}, u32[]{:S(2)}, u32[]{:S(2)}) %collective-permute-start.11) | collective-permute-done | bytes 262176 | tf_op jit(solution)/shard_map/ppermute | solution.py:510
  27.7 0.9 %collective-permute-start.12 = (bf16[256,512]{1,0:T(8,128)(2,1)S(1)}, bf16[256,512]{1,0:T(8,128)(2,1)S(1)}, u32[]{:S(2)}, u32[]{:S(2)}) collective-permute-start(bf16[256,512]{1,0:T(8,128)(2,1)S(1)} %get-tuple-element.71.own_ref), channel_id=1, source_target_pairs={{0,1},{1,0},{2,4},{3,5},{4,2},{5,3},{6,8},{7,9},{8,6},{9,7},{10,12... | collective-permute-start | bytes 786440 | tf_op jit(solution)/shard_map/ppermute | solution.py:513
  28.6 5.0 %near.1 = (bf16[16,128,256]{2,1,0:T(8,128)(2,1)S(1)}, f32[16,48,256]{2,1,0:T(8,128)S(1)}, f32[16,8,256]{2,1,0:T(8,128)S(1)}) custom-call(bf16[256,512]{1,0:T(8,128)(2,1)S(1)} %get-tuple-element.71.own_ref, bf16[256,512]{1,0:T(8,128)(2,1)S(1)} %collective-permute-done.11.side_ref, bf16[512,512]{1,0:T(8,128)(2,1)S(1)} %get-tuple-element.73.wq_ref, ...), custom_call_target="tpu_custom_call" | custom-call | flops 8589934592 | bytes 4194304 | tf_op jit(solution)/shard_map/near/pallas_call | solution.py:516
  33.6 2.6 %collective-permute-done.12.block_ref = bf16[256,512]{1,0:T(8,128)(2,1)S(1)} collective-permute-done((bf16[256,512]{1,0:T(8,128)(2,1)S(1)}, bf16[256,512]{1,0:T(8,128)(2,1)S(1)}, u32[]{:S(2)}, u32[]{:S(2)}) %collective-permute-start.12) | collective-permute-done | bytes 262176 | tf_op jit(solution)/shard_map/ppermute | solution.py:513
  36.2 1.3 %collective-permute-start.13 = (bf16[256,512]{1,0:T(8,128)(2,1)S(1)}, bf16[256,512]{1,0:T(8,128)(2,1)S(1)}, u32[]{:S(2)}, u32[]{:S(2)}) collective-permute-start(bf16[256,512]{1,0:T(8,128)(2,1)S(1)} %collective-permute-done.12.block_ref), channel_id=1, source_target_pairs={{0,1},{1,0},{2,3},{3,2},{4,5},{5,4},{6,7},{7,6},{8,9},{9,8},{10,11... | collective-permute-start | bytes 786440 | tf_op jit(solution)/shard_map/ppermute | solution.py:557
  37.5 2.0 %other.1 = (f32[16,48,256]{2,1,0:T(8,128)S(1)}, f32[16,8,256]{2,1,0:T(8,128)S(1)}) custom-call(bf16[256,512]{1,0:T(8,128)(2,1)S(1)} %collective-permute-done.12.block_ref, bf16[512,512]{1,0:T(8,128)(2,1)S(1)} %get-tuple-element.74.wk_ref, bf16[512,512]{1,0:T(8,128)(2,1)S(1)} %get-tuple-element.75.wv_ref, s32[2,16]{1,0:T(2,128)S(1)} %select_reduce_fusion.plan_ref.plan_in, ...), custom_call_target="tpu_custom_call" | custom-call | flops 536870912 | bytes 3145728 | tf_op jit(solution)/shard_map/other/pallas_call | solution.py:536
  39.5 0.6 %collective-permute-done.10.block_ref = bf16[256,512]{1,0:T(8,128)(2,1)S(1)} collective-permute-done((bf16[256,512]{1,0:T(8,128)(2,1)S(1)}, bf16[256,512]{1,0:T(8,128)(2,1)S(1)}, u32[]{:S(2)}, u32[]{:S(2)}) %collective-permute-start.10) | collective-permute-done | bytes 262176 | tf_op jit(solution)/shard_map/ppermute | solution.py:511
  40.1 0.9 %collective-permute-start.14 = (bf16[256,512]{1,0:T(8,128)(2,1)S(1)}, bf16[256,512]{1,0:T(8,128)(2,1)S(1)}, u32[]{:S(2)}, u32[]{:S(2)}) collective-permute-start(bf16[256,512]{1,0:T(8,128)(2,1)S(1)} %collective-permute-done.10.block_ref), channel_id=1, source_target_pairs={{0,1},{1,0},{2,3},{3,2},{4,5},{5,4},{6,7},{7,6},{8,9},{9,8},{10,11... | collective-permute-start | bytes 786440 | tf_op jit(solution)/shard_map/ppermute | solution.py:560
  40.9 2.1 %pair.1 = (f32[16,48,256]{2,1,0:T(8,128)S(1)}, f32[16,8,256]{2,1,0:T(8,128)S(1)}) custom-call(bf16[256,512]{1,0:T(8,128)(2,1)S(1)} %collective-permute-done.10.block_ref, bf16[512,512]{1,0:T(8,128)(2,1)S(1)} %get-tuple-element.74.wk_ref, bf16[512,512]{1,0:T(8,128)(2,1)S(1)} %get-tuple-element.75.wv_ref, s32[2,16]{1,0:T(2,128)S(1)} %select_reduce_fusion.plan_ref.plan_in, ...), custom_call_target="tpu_custom_call" | custom-call | flops 536870912 | bytes 3145728 | tf_op jit(solution)/shard_map/pair/pallas_call | solution.py:536
  43.1 4.4 %far.1 = bf16[256,512]{1,0:T(8,128)(2,1)} custom-call(bf16[256,512]{1,0:T(8,128)(2,1)S(1)} %collective-permute-done.14.first_ref, bf16[256,512]{1,0:T(8,128)(2,1)S(1)} %collective-permute-done.13.second_ref, bf16[512,512]{1,0:T(8,128)(2,1)S(1)} %get-tuple-element.74.wk_ref, bf16[512,512]{1,0:T(8,128)(2,1)S(1)} %get-tuple-element.75.wv_ref, ...), custom_call_target="tpu_custom_call" | custom-call | flops 8589934592 | bytes 8388608 | tf_op jit(solution)/shard_map/far/pallas_call | solution.py:563
  (40 shorter events, 2.4 us)
Async XLA Ops:
  0.0 8.8 %copy-start.9 = (s32[16]{0:T(128)S(1)}, s32[16]{0:T(128)}, u32[]{:S(2)}) copy-start(s32[16]{0:T(128)} %param.23) | copy-start | bytes 196
  0.0 13.8 %copy-start = (bf16[512,1536]{1,0:T(8,128)(2,1)S(1)}, bf16[512,1536]{1,0:T(8,128)(2,1)}, u32[]{:S(2)}) copy-start(bf16[512,1536]{1,0:T(8,128)(2,1)} %w_ref.2) | copy-start | bytes 4718596
  5.2 3.8 %collective-permute-start.1 = (bf16[672,256]{1,0:T(8,128)(2,1)}, bf16[672,256]{1,0:T(8,128)(2,1)S(1)}, u32[]{:S(2)}, u32[]{:S(2)}) collective-permute-start(bf16[672,256]{1,0:T(8,128)(2,1)} %get-tuple-element.49), channel_id=1, source_target_pairs={{0,1},{1,0},{2,3},{3,2},{4,5},{5,4},{6,7},{7,6},{8,9},{9,8},{10,11... | collective-permute-start | bytes 1032200 | tf_op jit(solution)/shard_map/ppermute | solution.py:443
  6.0 13.7 %collective-permute-start.6 = (bf16[400,256]{1,0:T(8,128)(2,1)}, bf16[400,256]{1,0:T(8,128)(2,1)S(1)}, u32[]{:S(2)}, u32[]{:S(2)}) collective-permute-start(bf16[400,256]{1,0:T(8,128)(2,1)} %get-tuple-element.64), channel_id=1, source_target_pairs={{0,2},{1,3},{2,0},{3,1},{4,6},{5,7},{6,4},{7,5},{8,10},{9,11},{10,... | collective-permute-start | bytes 614408 | tf_op jit(solution)/shard_map/ppermute | solution.py:444
  6.2 5.1 %collective-permute-start = (bf16[272,256]{1,0:T(8,128)(2,1)}, bf16[272,256]{1,0:T(8,128)(2,1)S(1)}, u32[]{:S(2)}, u32[]{:S(2)}) collective-permute-start(bf16[272,256]{1,0:T(8,128)(2,1)} %get-tuple-element.48), channel_id=1, source_target_pairs={{0,4},{1,5},{2,6},{3,7},{4,0},{5,1},{6,2},{7,3},{8,12},{9,13},{10,... | collective-permute-start | bytes 417800 | tf_op jit(solution)/shard_map/ppermute | solution.py:445
  6.4 9.9 %collective-permute-start.3 = (bf16[272,256]{1,0:T(8,128)(2,1)}, bf16[272,256]{1,0:T(8,128)(2,1)S(1)}, u32[]{:S(2)}, u32[]{:S(2)}) collective-permute-start(bf16[272,256]{1,0:T(8,128)(2,1)} %get-tuple-element.54), channel_id=1, source_target_pairs={{0,1},{1,0},{2,3},{3,2},{4,8},{5,9},{6,10},{7,11},{8,4},{9,5},{10,... | collective-permute-start | bytes 417800 | tf_op jit(solution)/shard_map/ppermute | solution.py:446
  9.0 10.6 %collective-permute-start.7 = (bf16[400,256]{1,0:T(8,128)(2,1)}, bf16[400,256]{1,0:T(8,128)(2,1)S(1)}, u32[]{:S(2)}, u32[]{:S(2)}) collective-permute-start(bf16[400,256]{1,0:T(8,128)(2,1)} %get-tuple-element.65), channel_id=1, source_target_pairs={{0,3},{1,2},{2,1},{3,0},{4,7},{5,6},{6,5},{7,4},{8,11},{9,10},{10,... | collective-permute-start | bytes 614408 | tf_op jit(solution)/shard_map/ppermute | solution.py:450
  11.1 5.4 %collective-permute-start.2 = (bf16[272,256]{1,0:T(8,128)(2,1)}, bf16[272,256]{1,0:T(8,128)(2,1)S(1)}, u32[]{:S(2)}, u32[]{:S(2)}) collective-permute-start(bf16[272,256]{1,0:T(8,128)(2,1)} %get-tuple-element.53), channel_id=1, source_target_pairs={{0,5},{1,4},{2,7},{3,6},{4,1},{5,0},{6,3},{7,2},{8,13},{9,12},{10,... | collective-permute-start | bytes 417800 | tf_op jit(solution)/shard_map/ppermute | solution.py:451
  11.4 6.8 %collective-permute-start.4 = (bf16[272,256]{1,0:T(8,128)(2,1)}, bf16[272,256]{1,0:T(8,128)(2,1)S(1)}, u32[]{:S(2)}, u32[]{:S(2)}) collective-permute-start(bf16[272,256]{1,0:T(8,128)(2,1)} %get-tuple-element.55), channel_id=1, source_target_pairs={{0,1},{1,0},{2,3},{3,2},{4,9},{5,8},{6,11},{7,10},{8,5},{9,4},{10,... | collective-permute-start | bytes 417800 | tf_op jit(solution)/shard_map/ppermute | solution.py:452
  14.8 10.3 %copy-start.1 = (bf16[512,512]{1,0:T(8,128)(2,1)S(1)}, bf16[512,512]{1,0:T(8,128)(2,1)}, u32[]{:S(2)}) copy-start(bf16[512,512]{1,0:T(8,128)(2,1)} %refs_6_.1) | copy-start | bytes 1572868
  14.8 10.3 %copy-start.3 = (bf16[256,512]{1,0:T(8,128)(2,1)S(1)}, bf16[256,512]{1,0:T(8,128)(2,1)}, u32[]{:S(2)}) copy-start(bf16[256,512]{1,0:T(8,128)(2,1)} %refs_5_.1) | copy-start | bytes 786436
  14.8 10.3 %copy-start.4 = (f32[512]{0:T(512)S(1)}, f32[512]{0:T(512)}, u32[]{:S(2)}) copy-start(f32[512]{0:T(512)} %param.21) | copy-start | bytes 6148
  18.5 4.7 %collective-permute-start.5 = (bf16[256,256]{1,0:T(8,128)(2,1)S(1)}, bf16[256,256]{1,0:T(8,128)(2,1)S(1)}, u32[]{:S(2)}, u32[]{:S(2)}) collective-permute-start(bf16[256,256]{1,0:T(8,128)(2,1)S(1)} %get-tuple-element.63), channel_id=1, source_target_pairs={{0,2},{1,3},{2,0},{3,1},{4,6},{5,7},{6,4},{7,5},{8,10},{9,11},{10,... | collective-permute-start | bytes 393224 | tf_op jit(solution)/shard_map/ppermute | solution.py:485
  19.9 5.1 %collective-permute-start.8 = (bf16[256,256]{1,0:T(8,128)(2,1)S(1)}, bf16[256,256]{1,0:T(8,128)(2,1)S(1)}, u32[]{:S(2)}, u32[]{:S(2)}) collective-permute-start(bf16[256,256]{1,0:T(8,128)(2,1)S(1)} %get-tuple-element.68), channel_id=1, source_target_pairs={{0,4},{1,5},{2,6},{3,7},{4,0},{5,1},{6,2},{7,3},{8,12},{9,13},{10,... | collective-permute-start | bytes 393224 | tf_op jit(solution)/shard_map/ppermute | solution.py:487
  20.0 5.1 %collective-permute-start.9 = (bf16[256,256]{1,0:T(8,128)(2,1)S(1)}, bf16[256,256]{1,0:T(8,128)(2,1)S(1)}, u32[]{:S(2)}, u32[]{:S(2)}) collective-permute-start(bf16[256,256]{1,0:T(8,128)(2,1)S(1)} %get-tuple-element.69), channel_id=1, source_target_pairs={{0,1},{1,0},{2,3},{3,2},{4,8},{5,9},{6,10},{7,11},{8,4},{9,5},{10,... | collective-permute-start | bytes 393224 | tf_op jit(solution)/shard_map/ppermute | solution.py:488
  25.6 2.1 %collective-permute-start.11 = (bf16[256,512]{1,0:T(8,128)(2,1)S(1)}, bf16[256,512]{1,0:T(8,128)(2,1)S(1)}, u32[]{:S(2)}, u32[]{:S(2)}) collective-permute-start(bf16[256,512]{1,0:T(8,128)(2,1)S(1)} %get-tuple-element.71.own_ref), channel_id=1, source_target_pairs={{0,1},{1,0},{2,3},{3,2},{4,5},{5,4},{6,7},{7,6},{8,9},{9,8},{10,11... | collective-permute-start | bytes 786440 | tf_op jit(solution)/shard_map/ppermute | solution.py:510
  26.6 13.5 %collective-permute-start.10 = (bf16[256,512]{1,0:T(8,128)(2,1)S(1)}, bf16[256,512]{1,0:T(8,128)(2,1)S(1)}, u32[]{:S(2)}, u32[]{:S(2)}) collective-permute-start(bf16[256,512]{1,0:T(8,128)(2,1)S(1)} %get-tuple-element.71.own_ref), channel_id=1, source_target_pairs={{0,2},{1,3},{2,0},{3,1},{4,6},{5,7},{6,4},{7,5},{8,10},{9,11},{10,... | collective-permute-start | bytes 786440 | tf_op jit(solution)/shard_map/ppermute | solution.py:511
  27.7 8.5 %collective-permute-start.12 = (bf16[256,512]{1,0:T(8,128)(2,1)S(1)}, bf16[256,512]{1,0:T(8,128)(2,1)S(1)}, u32[]{:S(2)}, u32[]{:S(2)}) collective-permute-start(bf16[256,512]{1,0:T(8,128)(2,1)S(1)} %get-tuple-element.71.own_ref), channel_id=1, source_target_pairs={{0,1},{1,0},{2,4},{3,5},{4,2},{5,3},{6,8},{7,9},{8,6},{9,7},{10,12... | collective-permute-start | bytes 786440 | tf_op jit(solution)/shard_map/ppermute | solution.py:513
  36.2 3.9 %collective-permute-start.13 = (bf16[256,512]{1,0:T(8,128)(2,1)S(1)}, bf16[256,512]{1,0:T(8,128)(2,1)S(1)}, u32[]{:S(2)}, u32[]{:S(2)}) collective-permute-start(bf16[256,512]{1,0:T(8,128)(2,1)S(1)} %collective-permute-done.12.block_ref), channel_id=1, source_target_pairs={{0,1},{1,0},{2,3},{3,2},{4,5},{5,4},{6,7},{7,6},{8,9},{9,8},{10,11... | collective-permute-start | bytes 786440 | tf_op jit(solution)/shard_map/ppermute | solution.py:557
  37.4 5.6 %copy-start.6 = (bf16[2048,512]{1,0:T(8,128)(2,1)S(1)}, bf16[2048,512]{1,0:T(8,128)(2,1)}, u32[]{:S(2)}) copy-start(bf16[2048,512]{1,0:T(8,128)(2,1)} %down_ref.1) | copy-start | bytes 6291460
  39.4 3.7 %copy-start.5 = (bf16[512,2048]{1,0:T(8,128)(2,1)S(1)}, bf16[512,2048]{1,0:T(8,128)(2,1)}, u32[]{:S(2)}) copy-start(bf16[512,2048]{1,0:T(8,128)(2,1)} %up_ref.1) | copy-start | bytes 6291460
  39.4 3.7 %copy-start.7 = (bf16[512,512]{1,0:T(8,128)(2,1)S(1)}, bf16[512,512]{1,0:T(8,128)(2,1)}, u32[]{:S(2)}) copy-start(bf16[512,512]{1,0:T(8,128)(2,1)} %w_out_ref.1) | copy-start | bytes 1572868
  39.5 3.7 %copy-start.8 = (f32[512]{0:T(512)S(1)}, f32[512]{0:T(512)}, u32[]{:S(2)}) copy-start(f32[512]{0:T(512)} %param.25) | copy-start | bytes 6148
  40.1 3.0 %collective-permute-start.14 = (bf16[256,512]{1,0:T(8,128)(2,1)S(1)}, bf16[256,512]{1,0:T(8,128)(2,1)S(1)}, u32[]{:S(2)}, u32[]{:S(2)}) collective-permute-start(bf16[256,512]{1,0:T(8,128)(2,1)S(1)} %collective-permute-done.10.block_ref), channel_id=1, source_target_pairs={{0,1},{1,0},{2,3},{3,2},{4,5},{5,4},{6,7},{7,6},{8,9},{9,8},{10,11... | collective-permute-start | bytes 786440 | tf_op jit(solution)/shard_map/ppermute | solution.py:560
  (1 other events, 1.0 us)

commit v19 on v18

--- a/solution.py
+++ b/solution.py
@@ -113,17 +113,15 @@
         fetches[k + 1].wait()
         message_ref[span] = silu(dot(grid_vmem[span], w_vmem[...])).astype(jnp.bfloat16)
     sends = []
-    per_core = len(keys) // 2
+    taken = dot(pick_ref[...], message_ref[...]).astype(jnp.bfloat16)
     for k in range(2):
-        first = k * per_core
-        taken = dot(pick_ref[first * cap : (first + per_core) * cap, :], message_ref[...]).astype(jnp.bfloat16)
         for n in reversed(range(count)):
             start = 0
             if runs[n][0][0][0][2] != k:
                 continue
             for chosen, lanes in runs[n]:
                 for key in chosen:
-                    m = keys.index(key) - first
+                    m = keys.index(key)
                     out_vmems[n][start : start + cap, :] = taken[m * cap : (m + 1) * cap, lanes]
                     start += cap
                 start += TILE

time: 47.7 us -> 47.7 us (level)
  Pallas kernels: 21.3 us -> 20.5 us
  waiting for transfers between devices: 10.7 us -> 11.3 us
    pallas_call x2, Pallas kernels: 4.12 us -> 3.36 us  [outer(): pl.pallas_call(functools.partial(outer_kernel, by_pair), out_shape=[jax.S...]
  transfers between devices with their start and end apart: 15 -> 15, of which waited for: 9 -> 9; matrix products, arithmetic and copies ran while one was open for 1% -> 1% of each run, Pallas kernels for 24% -> 22%
where the time goes in v19:
time: 47.7 us; the launch traced here: 47.3 us
  Pallas kernels  20.5 us (43%)
  starting transfers between devices  14 us (29%)
  waiting for transfers between devices  11.3 us (24%)
  local copies, waits for them, and re-layouts  1.02 us (2%)
    pallas_call x1, Pallas kernels, local(): pl.pallas_call(functools.partial(message_kernel, pairs), out_shape=outgoi...  5.31 us
    pallas_call x1, Pallas kernels, local(): pl.pallas_call(near_kernel, out_shape=[jax.ShapeDtypeStruct((HEADS, LANES...  4.84 us
    pallas_call x1, Pallas kernels, local(): pl.pallas_call(far_kernel, out_shape=jax.ShapeDtypeStruct((nodes, width),...  4.41 us
    pallas_call x2, Pallas kernels, outer(): pl.pallas_call(functools.partial(outer_kernel, by_pair), out_shape=[jax.S...  3.36 us
    ppermute x1, waiting for transfers between devices, local(): lax.ppermute(part, NODES, chip_trade(p + 1))  2.79 us
    ppermute x1, waiting for transfers between devices, local(): odd = lax.ppermute(normed, NODES, chips_trade(1))  2.76 us
    ppermute x1, starting transfers between devices, local(): odd = lax.ppermute(odd, NODES, bands_trade(1))  2.41 us
    ppermute x1, starting transfers between devices, local(): odd_other = lax.ppermute(odd_other, NODES, bands_trade(1, 1))  2.35 us
  transfers between devices with their start and end apart: 15, of which 9 were waited for; matrix products, arithmetic and copies ran while one was open for 1% of the time, Pallas kernels for 22%

profile of v19, /device:TPU:15, one launch (start us, length us, event | category | flops | bytes accessed | tf_op | source)
XLA Modules:
  0.0 47.3 jit_solution(8573380325142172848)
XLA Ops:
  0.0 5.3 %messages.1 = (bf16[272,256]{1,0:T(8,128)(2,1)}, bf16[272,256]{1,0:T(8,128)(2,1)}, bf16[272,256]{1,0:T(8,128)(2,1)}, bf16[272,256]{1,0:T(8,128)(2,1)}, bf16[400,...) custom-call(bf16[1024,512]{1,0:T(8,128)(2,1)} %grid_ref.1, ...), custom_call_target="tpu_custom_call" | custom-call | flops 2147483648 | bytes 4194304 | tf_op jit(solution)/shard_map/messages/pallas_call | solution.py:406
  5.3 0.7 %collective-permute-start.1 = (bf16[672,256]{1,0:T(8,128)(2,1)}, bf16[672,256]{1,0:T(8,128)(2,1)S(1)}, u32[]{:S(2)}, u32[]{:S(2)}) collective-permute-start(bf16[672,256]{1,0:T(8,128)(2,1)} %get-tuple-element.49), channel_id=1, source_target_pairs={{0,1},{1,0},{2,3},{3,2},{4,5},{5,4},{6,7},{7,6},{8,9},{9,8},{10,11... | collective-permute-start | bytes 1032200 | tf_op jit(solution)/shard_map/ppermute | solution.py:441
  6.5 2.4 %collective-permute-start.3 = (bf16[272,256]{1,0:T(8,128)(2,1)}, bf16[272,256]{1,0:T(8,128)(2,1)S(1)}, u32[]{:S(2)}, u32[]{:S(2)}) collective-permute-start(bf16[272,256]{1,0:T(8,128)(2,1)} %get-tuple-element.54), channel_id=1, source_target_pairs={{0,1},{1,0},{2,3},{3,2},{4,8},{5,9},{6,10},{7,11},{8,4},{9,5},{10,... | collective-permute-start | bytes 417800 | tf_op jit(solution)/shard_map/ppermute | solution.py:444
  9.1 2.1 %collective-permute-start.7 = (bf16[400,256]{1,0:T(8,128)(2,1)}, bf16[400,256]{1,0:T(8,128)(2,1)S(1)}, u32[]{:S(2)}, u32[]{:S(2)}) collective-permute-start(bf16[400,256]{1,0:T(8,128)(2,1)} %get-tuple-element.65), channel_id=1, source_target_pairs={{0,3},{1,2},{2,1},{3,0},{4,7},{5,6},{6,5},{7,4},{8,11},{9,10},{10,... | collective-permute-start | bytes 614408 | tf_op jit(solution)/shard_map/ppermute | solution.py:448
  11.5 2.3 %collective-permute-start.4 = (bf16[272,256]{1,0:T(8,128)(2,1)}, bf16[272,256]{1,0:T(8,128)(2,1)S(1)}, u32[]{:S(2)}, u32[]{:S(2)}) collective-permute-start(bf16[272,256]{1,0:T(8,128)(2,1)} %get-tuple-element.55), channel_id=1, source_target_pairs={{0,1},{1,0},{2,3},{3,2},{4,9},{5,8},{6,11},{7,10},{8,5},{9,4},{10,... | collective-permute-start | bytes 417800 | tf_op jit(solution)/shard_map/ppermute | solution.py:450
  14.0 1.0 %copy-done.2 = bf16[672,256]{1,0:T(8,128)(2,1)S(1)} copy-done((bf16[672,256]{1,0:T(8,128)(2,1)S(1)}, bf16[672,256]{1,0:T(8,128)(2,1)}, u32[]{:S(2)}) %copy-start.2) | copy-done | bytes 344088
  14.9 1.5 %early.1 = (bf16[512,512]{1,0:T(8,128)(2,1)S(1)}, bf16[512,512]{1,0:T(8,128)(2,1)S(1)}, bf16[512,512]{1,0:T(8,128)(2,1)S(1)}, f32[2,256,256]{2,1,0:T(8,128)S(1)}, f32[3,256,256]{2,1,0:T(8,128)S(1)}) custom-call(bf16[512,1536]{1,0:T(8,128)(2,1)S(1)} %copy-done, bf16[672,256]{1,0:T(8,128)(2,1)S(1)} %copy-done.2, ...), custom_call_target="tpu_custom_call" | custom-call | flops 268435456 | bytes 4194304 | tf_op jit(solution)/shard_map/early/pallas_call | solution.py:460
  16.6 1.7 %collective-permute-done.4.refs_3_ = bf16[272,256]{1,0:T(8,128)(2,1)S(1)} collective-permute-done((bf16[272,256]{1,0:T(8,128)(2,1)}, bf16[272,256]{1,0:T(8,128)(2,1)S(1)}, u32[]{:S(2)}, u32[]{:S(2)}) %collective-permute-start.4) | collective-permute-done | bytes 139296 | tf_op jit(solution)/shard_map/ppermute | solution.py:450
  18.6 1.1 %collective-permute-start.5 = (bf16[256,256]{1,0:T(8,128)(2,1)S(1)}, bf16[256,256]{1,0:T(8,128)(2,1)S(1)}, u32[]{:S(2)}, u32[]{:S(2)}) collective-permute-start(bf16[256,256]{1,0:T(8,128)(2,1)S(1)} %get-tuple-element.63), channel_id=1, source_target_pairs={{0,2},{1,3},{2,0},{3,1},{4,6},{5,7},{6,4},{7,5},{8,10},{9,11},{10,... | collective-permute-start | bytes 393224 | tf_op jit(solution)/shard_map/ppermute | solution.py:483
  20.1 0.5 %collective-permute-start.9 = (bf16[256,256]{1,0:T(8,128)(2,1)S(1)}, bf16[256,256]{1,0:T(8,128)(2,1)S(1)}, u32[]{:S(2)}, u32[]{:S(2)}) collective-permute-start(bf16[256,256]{1,0:T(8,128)(2,1)S(1)} %get-tuple-element.69), channel_id=1, source_target_pairs={{0,1},{1,0},{2,3},{3,2},{4,8},{5,9},{6,10},{7,11},{8,4},{9,5},{10,... | collective-permute-start | bytes 393224 | tf_op jit(solution)/shard_map/ppermute | solution.py:486
  20.6 2.8 %collective-permute-done.5.refs_1_ = bf16[256,256]{1,0:T(8,128)(2,1)S(1)} collective-permute-done((bf16[256,256]{1,0:T(8,128)(2,1)S(1)}, bf16[256,256]{1,0:T(8,128)(2,1)S(1)}, u32[]{:S(2)}, u32[]{:S(2)}) %collective-permute-start.5) | collective-permute-done | bytes 131104 | tf_op jit(solution)/shard_map/ppermute | solution.py:483
  23.4 1.8 %collective-permute-done.8.refs_3_ = bf16[256,256]{1,0:T(8,128)(2,1)S(1)} collective-permute-done((bf16[256,256]{1,0:T(8,128)(2,1)S(1)}, bf16[256,256]{1,0:T(8,128)(2,1)S(1)}, u32[]{:S(2)}, u32[]{:S(2)}) %collective-permute-start.8) | collective-permute-done | bytes 131104 | tf_op jit(solution)/shard_map/ppermute | solution.py:485
  25.2 0.5 %merge.1 = (f32[256,512]{1,0:T(8,128)S(1)}, bf16[256,512]{1,0:T(8,128)(2,1)S(1)}) custom-call(f32[256,256]{1,0:T(8,128)S(1)} %get-tuple-element.62.refs_0_, bf16[256,256]{1,0:T(8,128)(2,1)S(1)} %collective-permute-done.5.refs_1_, f32[256,256]{1,0:T(8,128)S(1)} %get-tuple-element.67.refs_2_, bf16[256,256]{1,0:T(8,128)(2,1)S(1)} %collective-permute-done.8.refs_3_, ...), custom_call_target="tpu_custom_call" | custom-call | flops 134217728 | bytes 2097152 | tf_op jit(solution)/shard_map/merge/pallas_call | solution.py:488
  25.7 0.9 %collective-permute-start.11 = (bf16[256,512]{1,0:T(8,128)(2,1)S(1)}, bf16[256,512]{1,0:T(8,128)(2,1)S(1)}, u32[]{:S(2)}, u32[]{:S(2)}) collective-permute-start(bf16[256,512]{1,0:T(8,128)(2,1)S(1)} %get-tuple-element.71.own_ref), channel_id=1, source_target_pairs={{0,1},{1,0},{2,3},{3,2},{4,5},{5,4},{6,7},{7,6},{8,9},{9,8},{10,11... | collective-permute-start | bytes 786440 | tf_op jit(solution)/shard_map/ppermute | solution.py:508
  27.1 0.7 %collective-permute-done.11.side_ref = bf16[256,512]{1,0:T(8,128)(2,1)S(1)} collective-permute-done((bf16[256,512]{1,0:T(8,128)(2,1)S(1)}, bf16[256,512]{1,0:T(8,128)(2,1)S(1)}, u32[]{:S(2)}, u32[]{:S(2)}) %collective-permute-start.11) | collective-permute-done | bytes 262176 | tf_op jit(solution)/shard_map/ppermute | solution.py:508
  27.8 0.9 %collective-permute-start.12 = (bf16[256,512]{1,0:T(8,128)(2,1)S(1)}, bf16[256,512]{1,0:T(8,128)(2,1)S(1)}, u32[]{:S(2)}, u32[]{:S(2)}) collective-permute-start(bf16[256,512]{1,0:T(8,128)(2,1)S(1)} %get-tuple-element.71.own_ref), channel_id=1, source_target_pairs={{0,1},{1,0},{2,4},{3,5},{4,2},{5,3},{6,8},{7,9},{8,6},{9,7},{10,12... | collective-permute-start | bytes 786440 | tf_op jit(solution)/shard_map/ppermute | solution.py:511
  28.7 4.8 %near.1 = (bf16[16,128,256]{2,1,0:T(8,128)(2,1)S(1)}, f32[16,48,256]{2,1,0:T(8,128)S(1)}, f32[16,8,256]{2,1,0:T(8,128)S(1)}) custom-call(bf16[256,512]{1,0:T(8,128)(2,1)S(1)} %get-tuple-element.71.own_ref, bf16[256,512]{1,0:T(8,128)(2,1)S(1)} %collective-permute-done.11.side_ref, bf16[512,512]{1,0:T(8,128)(2,1)S(1)} %get-tuple-element.73.wq_ref, ...), custom_call_target="tpu_custom_call" | custom-call | flops 8589934592 | bytes 4194304 | tf_op jit(solution)/shard_map/near/pallas_call | solution.py:514
  33.5 2.8 %collective-permute-done.12.block_ref = bf16[256,512]{1,0:T(8,128)(2,1)S(1)} collective-permute-done((bf16[256,512]{1,0:T(8,128)(2,1)S(1)}, bf16[256,512]{1,0:T(8,128)(2,1)S(1)}, u32[]{:S(2)}, u32[]{:S(2)}) %collective-permute-start.12) | collective-permute-done | bytes 262176 | tf_op jit(solution)/shard_map/ppermute | solution.py:511
  36.3 1.3 %collective-permute-start.13 = (bf16[256,512]{1,0:T(8,128)(2,1)S(1)}, bf16[256,512]{1,0:T(8,128)(2,1)S(1)}, u32[]{:S(2)}, u32[]{:S(2)}) collective-permute-start(bf16[256,512]{1,0:T(8,128)(2,1)S(1)} %collective-permute-done.12.block_ref), channel_id=1, source_target_pairs={{0,1},{1,0},{2,3},{3,2},{4,5},{5,4},{6,7},{7,6},{8,9},{9,8},{10,11... | collective-permute-start | bytes 786440 | tf_op jit(solution)/shard_map/ppermute | solution.py:555
  37.5 1.6 %other.1 = (f32[16,48,256]{2,1,0:T(8,128)S(1)}, f32[16,8,256]{2,1,0:T(8,128)S(1)}) custom-call(bf16[256,512]{1,0:T(8,128)(2,1)S(1)} %collective-permute-done.12.block_ref, bf16[512,512]{1,0:T(8,128)(2,1)S(1)} %get-tuple-element.74.wk_ref, bf16[512,512]{1,0:T(8,128)(2,1)S(1)} %get-tuple-element.75.wv_ref, s32[2,16]{1,0:T(2,128)S(1)} %select_reduce_fusion.plan_ref.plan_in, ...), custom_call_target="tpu_custom_call" | custom-call | flops 536870912 | bytes 3145728 | tf_op jit(solution)/shard_map/other/pallas_call | solution.py:534
  39.2 1.0 %collective-permute-done.10.block_ref = bf16[256,512]{1,0:T(8,128)(2,1)S(1)} collective-permute-done((bf16[256,512]{1,0:T(8,128)(2,1)S(1)}, bf16[256,512]{1,0:T(8,128)(2,1)S(1)}, u32[]{:S(2)}, u32[]{:S(2)}) %collective-permute-start.10) | collective-permute-done | bytes 262176 | tf_op jit(solution)/shard_map/ppermute | solution.py:509
  40.2 0.9 %collective-permute-start.14 = (bf16[256,512]{1,0:T(8,128)(2,1)S(1)}, bf16[256,512]{1,0:T(8,128)(2,1)S(1)}, u32[]{:S(2)}, u32[]{:S(2)}) collective-permute-start(bf16[256,512]{1,0:T(8,128)(2,1)S(1)} %collective-permute-done.10.block_ref), channel_id=1, source_target_pairs={{0,1},{1,0},{2,3},{3,2},{4,5},{5,4},{6,7},{7,6},{8,9},{9,8},{10,11... | collective-permute-start | bytes 786440 | tf_op jit(solution)/shard_map/ppermute | solution.py:558
  41.0 1.8 %pair.1 = (f32[16,48,256]{2,1,0:T(8,128)S(1)}, f32[16,8,256]{2,1,0:T(8,128)S(1)}) custom-call(bf16[256,512]{1,0:T(8,128)(2,1)S(1)} %collective-permute-done.10.block_ref, bf16[512,512]{1,0:T(8,128)(2,1)S(1)} %get-tuple-element.74.wk_ref, bf16[512,512]{1,0:T(8,128)(2,1)S(1)} %get-tuple-element.75.wv_ref, s32[2,16]{1,0:T(2,128)S(1)} %select_reduce_fusion.plan_ref.plan_in, ...), custom_call_target="tpu_custom_call" | custom-call | flops 536870912 | bytes 3145728 | tf_op jit(solution)/shard_map/pair/pallas_call | solution.py:534
  42.8 4.4 %far.1 = bf16[256,512]{1,0:T(8,128)(2,1)} custom-call(bf16[256,512]{1,0:T(8,128)(2,1)S(1)} %collective-permute-done.14.first_ref, bf16[256,512]{1,0:T(8,128)(2,1)S(1)} %collective-permute-done.13.second_ref, bf16[512,512]{1,0:T(8,128)(2,1)S(1)} %get-tuple-element.74.wk_ref, bf16[512,512]{1,0:T(8,128)(2,1)S(1)} %get-tuple-element.75.wv_ref, ...), custom_call_target="tpu_custom_call" | custom-call | flops 8589934592 | bytes 8388608 | tf_op jit(solution)/shard_map/far/pallas_call | solution.py:561
  (40 shorter events, 2.4 us)
Async XLA Ops:
  0.0 8.9 %copy-start.9 = (s32[16]{0:T(128)S(1)}, s32[16]{0:T(128)}, u32[]{:S(2)}) copy-start(s32[16]{0:T(128)} %param.23) | copy-start | bytes 196
  0.0 13.9 %copy-start = (bf16[512,1536]{1,0:T(8,128)(2,1)S(1)}, bf16[512,1536]{1,0:T(8,128)(2,1)}, u32[]{:S(2)}) copy-start(bf16[512,1536]{1,0:T(8,128)(2,1)} %w_ref.2) | copy-start | bytes 4718596
  5.3 3.8 %collective-permute-start.1 = (bf16[672,256]{1,0:T(8,128)(2,1)}, bf16[672,256]{1,0:T(8,128)(2,1)S(1)}, u32[]{:S(2)}, u32[]{:S(2)}) collective-permute-start(bf16[672,256]{1,0:T(8,128)(2,1)} %get-tuple-element.49), channel_id=1, source_target_pairs={{0,1},{1,0},{2,3},{3,2},{4,5},{5,4},{6,7},{7,6},{8,9},{9,8},{10,11... | collective-permute-start | bytes 1032200 | tf_op jit(solution)/shard_map/ppermute | solution.py:441
  6.1 13.7 %collective-permute-start.6 = (bf16[400,256]{1,0:T(8,128)(2,1)}, bf16[400,256]{1,0:T(8,128)(2,1)S(1)}, u32[]{:S(2)}, u32[]{:S(2)}) collective-permute-start(bf16[400,256]{1,0:T(8,128)(2,1)} %get-tuple-element.64), channel_id=1, source_target_pairs={{0,2},{1,3},{2,0},{3,1},{4,6},{5,7},{6,4},{7,5},{8,10},{9,11},{10,... | collective-permute-start | bytes 614408 | tf_op jit(solution)/shard_map/ppermute | solution.py:442
  6.3 5.1 %collective-permute-start = (bf16[272,256]{1,0:T(8,128)(2,1)}, bf16[272,256]{1,0:T(8,128)(2,1)S(1)}, u32[]{:S(2)}, u32[]{:S(2)}) collective-permute-start(bf16[272,256]{1,0:T(8,128)(2,1)} %get-tuple-element.48), channel_id=1, source_target_pairs={{0,4},{1,5},{2,6},{3,7},{4,0},{5,1},{6,2},{7,3},{8,12},{9,13},{10,... | collective-permute-start | bytes 417800 | tf_op jit(solution)/shard_map/ppermute | solution.py:443
  6.5 9.9 %collective-permute-start.3 = (bf16[272,256]{1,0:T(8,128)(2,1)}, bf16[272,256]{1,0:T(8,128)(2,1)S(1)}, u32[]{:S(2)}, u32[]{:S(2)}) collective-permute-start(bf16[272,256]{1,0:T(8,128)(2,1)} %get-tuple-element.54), channel_id=1, source_target_pairs={{0,1},{1,0},{2,3},{3,2},{4,8},{5,9},{6,10},{7,11},{8,4},{9,5},{10,... | collective-permute-start | bytes 417800 | tf_op jit(solution)/shard_map/ppermute | solution.py:444
  9.1 10.6 %collective-permute-start.7 = (bf16[400,256]{1,0:T(8,128)(2,1)}, bf16[400,256]{1,0:T(8,128)(2,1)S(1)}, u32[]{:S(2)}, u32[]{:S(2)}) collective-permute-start(bf16[400,256]{1,0:T(8,128)(2,1)} %get-tuple-element.65), channel_id=1, source_target_pairs={{0,3},{1,2},{2,1},{3,0},{4,7},{5,6},{6,5},{7,4},{8,11},{9,10},{10,... | collective-permute-start | bytes 614408 | tf_op jit(solution)/shard_map/ppermute | solution.py:448
  11.2 5.4 %collective-permute-start.2 = (bf16[272,256]{1,0:T(8,128)(2,1)}, bf16[272,256]{1,0:T(8,128)(2,1)S(1)}, u32[]{:S(2)}, u32[]{:S(2)}) collective-permute-start(bf16[272,256]{1,0:T(8,128)(2,1)} %get-tuple-element.53), channel_id=1, source_target_pairs={{0,5},{1,4},{2,7},{3,6},{4,1},{5,0},{6,3},{7,2},{8,13},{9,12},{10,... | collective-permute-start | bytes 417800 | tf_op jit(solution)/shard_map/ppermute | solution.py:449
  11.5 6.8 %collective-permute-start.4 = (bf16[272,256]{1,0:T(8,128)(2,1)}, bf16[272,256]{1,0:T(8,128)(2,1)S(1)}, u32[]{:S(2)}, u32[]{:S(2)}) collective-permute-start(bf16[272,256]{1,0:T(8,128)(2,1)} %get-tuple-element.55), channel_id=1, source_target_pairs={{0,1},{1,0},{2,3},{3,2},{4,9},{5,8},{6,11},{7,10},{8,5},{9,4},{10,... | collective-permute-start | bytes 417800 | tf_op jit(solution)/shard_map/ppermute | solution.py:450
  14.9 10.3 %copy-start.1 = (bf16[512,512]{1,0:T(8,128)(2,1)S(1)}, bf16[512,512]{1,0:T(8,128)(2,1)}, u32[]{:S(2)}) copy-start(bf16[512,512]{1,0:T(8,128)(2,1)} %refs_6_.1) | copy-start | bytes 1572868
  14.9 10.3 %copy-start.3 = (bf16[256,512]{1,0:T(8,128)(2,1)S(1)}, bf16[256,512]{1,0:T(8,128)(2,1)}, u32[]{:S(2)}) copy-start(bf16[256,512]{1,0:T(8,128)(2,1)} %refs_5_.1) | copy-start | bytes 786436
  14.9 10.3 %copy-start.4 = (f32[512]{0:T(512)S(1)}, f32[512]{0:T(512)}, u32[]{:S(2)}) copy-start(f32[512]{0:T(512)} %param.21) | copy-start | bytes 6148
  18.6 4.7 %collective-permute-start.5 = (bf16[256,256]{1,0:T(8,128)(2,1)S(1)}, bf16[256,256]{1,0:T(8,128)(2,1)S(1)}, u32[]{:S(2)}, u32[]{:S(2)}) collective-permute-start(bf16[256,256]{1,0:T(8,128)(2,1)S(1)} %get-tuple-element.63), channel_id=1, source_target_pairs={{0,2},{1,3},{2,0},{3,1},{4,6},{5,7},{6,4},{7,5},{8,10},{9,11},{10,... | collective-permute-start | bytes 393224 | tf_op jit(solution)/shard_map/ppermute | solution.py:483
  20.0 5.1 %collective-permute-start.8 = (bf16[256,256]{1,0:T(8,128)(2,1)S(1)}, bf16[256,256]{1,0:T(8,128)(2,1)S(1)}, u32[]{:S(2)}, u32[]{:S(2)}) collective-permute-start(bf16[256,256]{1,0:T(8,128)(2,1)S(1)} %get-tuple-element.68), channel_id=1, source_target_pairs={{0,4},{1,5},{2,6},{3,7},{4,0},{5,1},{6,2},{7,3},{8,12},{9,13},{10,... | collective-permute-start | bytes 393224 | tf_op jit(solution)/shard_map/ppermute | solution.py:485
  20.1 5.1 %collective-permute-start.9 = (bf16[256,256]{1,0:T(8,128)(2,1)S(1)}, bf16[256,256]{1,0:T(8,128)(2,1)S(1)}, u32[]{:S(2)}, u32[]{:S(2)}) collective-permute-start(bf16[256,256]{1,0:T(8,128)(2,1)S(1)} %get-tuple-element.69), channel_id=1, source_target_pairs={{0,1},{1,0},{2,3},{3,2},{4,8},{5,9},{6,10},{7,11},{8,4},{9,5},{10,... | collective-permute-start | bytes 393224 | tf_op jit(solution)/shard_map/ppermute | solution.py:486
  25.7 2.1 %collective-permute-start.11 = (bf16[256,512]{1,0:T(8,128)(2,1)S(1)}, bf16[256,512]{1,0:T(8,128)(2,1)S(1)}, u32[]{:S(2)}, u32[]{:S(2)}) collective-permute-start(bf16[256,512]{1,0:T(8,128)(2,1)S(1)} %get-tuple-element.71.own_ref), channel_id=1, source_target_pairs={{0,1},{1,0},{2,3},{3,2},{4,5},{5,4},{6,7},{7,6},{8,9},{9,8},{10,11... | collective-permute-start | bytes 786440 | tf_op jit(solution)/shard_map/ppermute | solution.py:508
  26.6 13.5 %collective-permute-start.10 = (bf16[256,512]{1,0:T(8,128)(2,1)S(1)}, bf16[256,512]{1,0:T(8,128)(2,1)S(1)}, u32[]{:S(2)}, u32[]{:S(2)}) collective-permute-start(bf16[256,512]{1,0:T(8,128)(2,1)S(1)} %get-tuple-element.71.own_ref), channel_id=1, source_target_pairs={{0,2},{1,3},{2,0},{3,1},{4,6},{5,7},{6,4},{7,5},{8,10},{9,11},{10,... | collective-permute-start | bytes 786440 | tf_op jit(solution)/shard_map/ppermute | solution.py:509
  27.8 8.5 %collective-permute-start.12 = (bf16[256,512]{1,0:T(8,128)(2,1)S(1)}, bf16[256,512]{1,0:T(8,128)(2,1)S(1)}, u32[]{:S(2)}, u32[]{:S(2)}) collective-permute-start(bf16[256,512]{1,0:T(8,128)(2,1)S(1)} %get-tuple-element.71.own_ref), channel_id=1, source_target_pairs={{0,1},{1,0},{2,4},{3,5},{4,2},{5,3},{6,8},{7,9},{8,6},{9,7},{10,12... | collective-permute-start | bytes 786440 | tf_op jit(solution)/shard_map/ppermute | solution.py:511
  36.3 3.9 %collective-permute-start.13 = (bf16[256,512]{1,0:T(8,128)(2,1)S(1)}, bf16[256,512]{1,0:T(8,128)(2,1)S(1)}, u32[]{:S(2)}, u32[]{:S(2)}) collective-permute-start(bf16[256,512]{1,0:T(8,128)(2,1)S(1)} %collective-permute-done.12.block_ref), channel_id=1, source_target_pairs={{0,1},{1,0},{2,3},{3,2},{4,5},{5,4},{6,7},{7,6},{8,9},{9,8},{10,11... | collective-permute-start | bytes 786440 | tf_op jit(solution)/shard_map/ppermute | solution.py:555
  37.5 5.3 %copy-start.6 = (bf16[2048,512]{1,0:T(8,128)(2,1)S(1)}, bf16[2048,512]{1,0:T(8,128)(2,1)}, u32[]{:S(2)}) copy-start(bf16[2048,512]{1,0:T(8,128)(2,1)} %down_ref.1) | copy-start | bytes 6291460
  39.1 3.7 %copy-start.5 = (bf16[512,2048]{1,0:T(8,128)(2,1)S(1)}, bf16[512,2048]{1,0:T(8,128)(2,1)}, u32[]{:S(2)}) copy-start(bf16[512,2048]{1,0:T(8,128)(2,1)} %up_ref.1) | copy-start | bytes 6291460
  39.2 3.7 %copy-start.7 = (bf16[512,512]{1,0:T(8,128)(2,1)S(1)}, bf16[512,512]{1,0:T(8,128)(2,1)}, u32[]{:S(2)}) copy-start(bf16[512,512]{1,0:T(8,128)(2,1)} %w_out_ref.1) | copy-start | bytes 1572868
  39.2 3.7 %copy-start.8 = (f32[512]{0:T(512)S(1)}, f32[512]{0:T(512)}, u32[]{:S(2)}) copy-start(f32[512]{0:T(512)} %param.25) | copy-start | bytes 6148
  40.2 2.6 %collective-permute-start.14 = (bf16[256,512]{1,0:T(8,128)(2,1)S(1)}, bf16[256,512]{1,0:T(8,128)(2,1)S(1)}, u32[]{:S(2)}, u32[]{:S(2)}) collective-permute-start(bf16[256,512]{1,0:T(8,128)(2,1)S(1)} %collective-permute-done.10.block_ref), channel_id=1, source_target_pairs={{0,1},{1,0},{2,3},{3,2},{4,5},{5,4},{6,7},{7,6},{8,9},{9,8},{10,11... | collective-permute-start | bytes 786440 | tf_op jit(solution)/shard_map/ppermute | solution.py:558
  (1 other events, 1.0 us)
